TPU v7x, 32 devices: a whole 2x2x4 slice. The times are simulated.
32 devices in a mesh: layer: 8 (over z, x), dp: 4 (over y, core).
Axes of the slice: x: 2, y: 2, z: 4, core: 2. Of those that a mesh axis runs over, the one named last changes fastest.
Arguments:
- state_guess: float32 [8, 4, 32, 256], P('layer', 'dp'), may hold values from -6 to 6
- adjoint_guess: float32 [8, 4, 32, 256], P('layer', 'dp'), may hold values from -6 to 6
- conv_weight: bfloat16 [32, 32, 288], P('layer'), may hold values from -0.375 to 0.375
- conv_bias: float32 [32, 32], P('layer'), may hold values from -3 to 3
Outputs:
- state_fixed: float32 [8, 4, 32, 256], P('layer', 'dp')
- adjoint_fixed: float32 [8, 4, 32, 256], P('layer', 'dp')
- weight_grad: float32 [32, 32, 288], P('layer', 'dp')
- bias_grad: float32 [32, 32], P('layer', 'dp')
All inputs are finite; a program needn't handle non-finite values.
Results may differ from a plain program's by a relative error of at most 0.0071.
Values sent between devices are 32-bit elements; how exact they have to be, the bound alone decides.
No kernel may reach another device: no remote copies, remote signals or barrier semaphores. Data moves between devices by JAX's collectives and lax.ppermute only.
A program may use at most 64 MiB of HBM per device.

v0:
```python
import jax
import jax.numpy as jnp
from jax import lax
from jax.sharding import PartitionSpec as P

IMG = 16


step_size = 0.5


def shifted(x, axis, by):
    length = lax.axis_size(axis)
    pairs = [(i, i + by) for i in range(length) if 0 <= i + by < length]
    return lax.ppermute(x, axis, pairs)


def carried_in(part, axis, combine, identity, reverse):
    count = lax.axis_size(axis)
    place = lax.axis_index(axis)
    ahead = count - 1 - place if reverse else place
    gathered = jax.tree.map(lambda a: lax.all_gather(a, axis), part)
    state = jax.tree.map(lambda a, e: jnp.zeros_like(a) + jnp.asarray(e, a.dtype), part, identity)

    def one(step, state):
        source = count - 1 - step if reverse else step
        return combine(
            state, jax.tree.map(lambda a: lax.dynamic_index_in_dim(a, source, 0, False), gathered)
        )

    return lax.fori_loop(0, ahead, one, state)


def gather_taps(values):
    count, chans, pixels = values.shape
    grid = values.reshape(count, chans, IMG, IMG)
    padded = jnp.pad(grid, ((0, 0), (0, 0), (1, 1), (1, 1)))
    taps = [padded[:, :, row : row + IMG, col : col + IMG] for row in range(3) for col in range(3)]
    return jnp.stack(taps, axis=2).reshape(count, chans * 9, pixels)


def spread_taps(grads):
    count, rows, pixels = grads.shape
    chans = rows // 9
    grid = grads.reshape(count, chans, 9, IMG, IMG)
    total = jnp.zeros((count, chans, IMG + 2, IMG + 2), jnp.float32)
    for tap in range(9):
        row, col = (tap // 3, tap % 3)
        total = total + jnp.pad(grid[:, :, tap], ((0, 0), (0, 0), (row, 2 - row), (col, 2 - col)))
    return total[:, :, 1:-1, 1:-1].reshape(count, chans, pixels)


def forward_block(state, weights, biases):
    chans = weights.shape[1]
    gain = jnp.ones(state.shape, jnp.float32)
    saved = []
    for layer in range(weights.shape[0]):
        kernel = weights[layer]
        rounded = state.astype(jnp.bfloat16)
        pre = jnp.einsum(
            "ok,bkp->bop", kernel, gather_taps(rounded), preferred_element_type=jnp.float32
        )
        squash = jnp.tanh(pre + biases[layer][None, :, None])
        center = jnp.diagonal(kernel.reshape(chans, chans, 9)[:, :, 4]).astype(jnp.float32)
        gain = gain * (1.0 + step_size * (1.0 - squash * squash) * center[None, :, None])
        state = state + step_size * squash
        saved.append((rounded, squash))
    return (state, gain, saved)


def backward_step(adjoint, kernel, squash):
    dz = step_size * adjoint * (1.0 - squash * squash)
    dzb = dz.astype(jnp.bfloat16)
    back = jnp.einsum("ok,bop->bkp", kernel, dzb, preferred_element_type=jnp.float32)
    return (adjoint + spread_taps(back), dz, dzb)


def compose(earlier, later):
    return (later[0] * earlier[0], later[0] * earlier[1] + later[1])


def local(state_guess, adjoint_guess, conv_weight, conv_bias):
    start = state_guess[0]
    guess_adj = adjoint_guess[0]
    final, gain, saved = forward_block(start, conv_weight, conv_bias)
    back = guess_adj
    for layer in reversed(range(conv_weight.shape[0])):
        back, dz, dzb = backward_step(back, conv_weight[layer], saved[layer][1])
    identity = (jnp.ones(start.shape, jnp.float32), jnp.zeros(start.shape, jnp.float32))
    next_guess = shifted(start, "layer", -1)
    fwd_res = final - next_guess
    fwd_pre = carried_in((gain, fwd_res), "layer", compose, identity, False)
    state_fixed = start + fwd_pre[1]
    prev_guess = shifted(guess_adj, "layer", 1)
    bwd_res = back - prev_guess
    bwd_pre = carried_in((gain, bwd_res), "layer", compose, identity, True)
    adjoint_fixed = guess_adj + bwd_pre[1]
    adjoint = adjoint_fixed
    wparts = []
    bparts = []
    for layer in reversed(range(conv_weight.shape[0])):
        rounded, squash = saved[layer]
        adjoint, dz, dzb = backward_step(adjoint, conv_weight[layer], squash)
        wlocal = jnp.einsum(
            "bop,bkp->ok", dzb, gather_taps(rounded), preferred_element_type=jnp.float32
        )
        blocal = jnp.sum(dz, axis=(0, 2))
        wparts.append(wlocal)
        bparts.append(blocal)
    weight_grad = jnp.stack(wparts[::-1])
    bias_grad = jnp.stack(bparts[::-1])
    weight_grad, bias_grad = (
        lax.psum_scatter(weight_grad, "dp", scatter_dimension=1, tiled=True),
        lax.psum_scatter(bias_grad, "dp", scatter_dimension=1, tiled=True),
    )
    return (state_fixed[None], adjoint_fixed[None], weight_grad, bias_grad)


def solution(mesh):
    placed = (
        P("layer", "dp", None, None),
        P("layer", "dp", None, None),
        P("layer", None, None),
        P("layer", None),
    )
    return jax.shard_map(
        local,
        mesh=mesh,
        in_specs=placed,
        out_specs=(
            P("layer", "dp", None, None),
            P("layer", "dp", None, None),
            P("layer", "dp", None),
            P("layer", "dp"),
        ),
        check_vma=False,
    )
```

profile of v0, /device:TPU:0, one launch (start us, length us, event | category | flops | bytes accessed | tf_op | source)
XLA Modules:
  0.0 163.3 jit_solution(7077260340957044320)
XLA Ops:
  7.2 1.3 collective-permute-start
  8.5 6.1 %collective-permute-start.1 = (f32[1,32,256]{2,1,0:T(8,128)}, f32[1,32,256]{2,1,0:T(8,128)}, u32[]{:S(2)}, u32[]{:S(2)}) collective-permute-start(f32[1,32,256]{2,1,0:T(8,128)} %bitcast.740), channel_id=1, source_target_pairs={{0,4},{4,8},{8,12},{12,16},{16,20},{20,24},{24,28},{1,5},{5,9},{9,... | collective-permute-start | bytes 98312 | tf_op jit(solution)/shard_map/ppermute | solution.py:15
  14.6 0.9 copy.168
  15.8 0.9 copy.169
  16.7 1.0 reshape.311
  18.4 0.9 copy.174
  19.4 1.0 reshape.313
  21.0 0.9 copy.179
  21.9 1.0 reshape.315
  27.0 0.8 gather_fusion.1
  27.8 1.1 copy.184
  28.9 1.0 reshape.317
  31.2 0.8 fusion.40
  41.5 0.8 add_subtract_fusion
  42.3 31.0 %all-gather.2 = f32[8,32,256]{2,1,0:T(8,128)S(1)} all-gather(f32[1,32,256]{2,1,0:T(8,128)S(1)} %add_subtract_fusion), channel_id=4, replica_groups=mesh['layer'=8,'dp'=4] {'layer'}, dimensions={0}, use_global_device_ids=true | all-gather | bytes 294912 | tf_op jit(solution)/shard_map/all_gather | solution.py:22
  73.3 30.8 %all-gather = f32[8,32,256]{2,1,0:T(8,128)S(1)} all-gather(f32[1,32,256]{2,1,0:T(8,128)S(1)} %copy-done.11), channel_id=2, replica_groups=mesh['layer'=8,'dp'=4] {'layer'}, dimensions={0}, use_global_device_ids=true | all-gather | bytes 294912 | tf_op jit(solution)/shard_map/all_gather | solution.py:22
  105.0 1.0 convolution_bitcast_fusion.2
  106.0 1.7 %reshape.331 = f32[1,32,9,16,16]{4,3,2,1,0:T(8,128)S(1)} reshape(f32[1,288,256]{2,1,0:T(8,128)} %convolution_bitcast_fusion.2) | data formatting | bytes 589824 | tf_op jit(solution)/shard_map/reshape | solution.py:45
  109.5 1.0 convolution_bitcast_fusion.1
  110.4 1.7 %reshape.334 = f32[1,32,9,16,16]{4,3,2,1,0:T(8,128)S(1)} reshape(f32[1,288,256]{2,1,0:T(8,128)} %convolution_bitcast_fusion.1) | data formatting | bytes 589824 | tf_op jit(solution)/shard_map/reshape | solution.py:45
  113.2 1.0 convolution_bitcast_fusion
  114.2 1.7 %reshape.337 = f32[1,32,9,16,16]{4,3,2,1,0:T(8,128)S(1)} reshape(f32[1,288,256]{2,1,0:T(8,128)} %convolution_bitcast_fusion) | data formatting | bytes 589824 | tf_op jit(solution)/shard_map/reshape | solution.py:45
  117.9 5.7 %all-reduce.67 = f32[4,32]{1,0:T(4,128)S(1)} all-reduce(f32[4,32]{1,0:T(4,128)S(1)} %pad_maximum_fusion.1), channel_id=6, replica_groups=mesh['layer'=8,'dp'=4] {'dp'}, use_global_device_ids=true, to_apply=%region_9.10.clone | all-reduce | flops 128 | bytes 1024
  124.3 30.8 %all-gather.1 = f32[8,32,256]{2,1,0:T(8,128)S(1)} all-gather(f32[1,32,256]{2,1,0:T(8,128)S(1)} %copy-done.10), channel_id=3, replica_groups=mesh['layer'=8,'dp'=4] {'layer'}, dimensions={0}, use_global_device_ids=true | all-gather | bytes 294912 | tf_op jit(solution)/shard_map/all_gather | solution.py:22
  (173 shorter events, 23.0 us)
Async XLA Ops:
  7.2 10.7 %copy-start.2 = (f32[1,1,32,256]{3,2,1,0:T(8,128)S(1)}, f32[1,1,32,256]{3,2,1,0:T(8,128)}, u32[]{:S(2)}) copy-start(f32[1,1,32,256]{3,2,1,0:T(8,128)} %param.8) | copy-start | bytes 98308
  7.2 10.6 %copy-start.14 = (f32[4,32]{1,0:T(4,128)S(1)}, f32[4,32]{1,0:T(4,128)}, u32[]{:S(2)}) copy-start(f32[4,32]{1,0:T(4,128)} %param.11) | copy-start | bytes 1540
  7.2 10.6 %copy-start = (bf16[4,32,288]{2,1,0:T(8,128)(2,1)S(1)}, bf16[4,32,288]{2,1,0:T(8,128)(2,1)}, u32[]{:S(2)}) copy-start(bf16[4,32,288]{2,1,0:T(8,128)(2,1)} %param.10) | copy-start | bytes 221188
  7.2 149.3 %reduce-scatter.3.cloned.1.call-start = ((), (), s32[]{:S(2)}) async-start(), calls=%async_computation.1 | async-start | bytes 245760 | tf_op jit(solution)/shard_map/reduce_scatter | solution.py:113
  7.2 24.0 %collective-permute-start = (f32[1,32,256]{2,1,0:T(8,128)}, f32[1,32,256]{2,1,0:T(8,128)S(1)}, u32[]{:S(2)}, u32[]{:S(2)}) collective-permute-start(f32[1,32,256]{2,1,0:T(8,128)} %bitcast.750), channel_id=1, source_target_pairs={{4,0},{8,4},{12,8},{16,12},{20,16},{24,20},{28,24},{5,1},{9,5},{13... | collective-permute-start | bytes 98312 | tf_op jit(solution)/shard_map/ppermute | solution.py:15
  8.5 32.9 %collective-permute-start.1 = (f32[1,32,256]{2,1,0:T(8,128)}, f32[1,32,256]{2,1,0:T(8,128)}, u32[]{:S(2)}, u32[]{:S(2)}) collective-permute-start(f32[1,32,256]{2,1,0:T(8,128)} %bitcast.740), channel_id=1, source_target_pairs={{0,4},{4,8},{8,12},{12,16},{16,20},{20,24},{24,28},{1,5},{5,9},{9,... | collective-permute-start | bytes 98312 | tf_op jit(solution)/shard_map/ppermute | solution.py:15
  25.9 4.0 %copy-start.15 = (u32[32]{0:T(128)S(1)}, u32[32]{0:T(128)}, u32[]{:S(2)}) copy-start(u32[32]{0:T(128)} %constant.266) | copy-start | bytes 388
  26.7 5.3 %copy-start.1 = (f32[1,1,32,256]{3,2,1,0:T(8,128)S(1)}, f32[1,1,32,256]{3,2,1,0:T(8,128)}, u32[]{:S(2)}) copy-start(f32[1,1,32,256]{3,2,1,0:T(8,128)} %param.9) | copy-start | bytes 98308
  32.0 1.2 copy-start.3
  36.1 0.6 copy-start.5
  37.9 0.9 copy-start.6
  38.8 0.6 copy-start.7
  40.6 0.9 copy-start.8
  40.6 32.7 %copy-start.11 = (f32[1,32,256]{2,1,0:T(8,128)S(1)}, f32[1,32,256]{2,1,0:T(8,128)}, u32[]{:S(2)}) copy-start(f32[1,32,256]{2,1,0:T(8,128)} %get-tuple-element.262) | copy-start | bytes 98308
  40.8 63.6 %copy-start.4 = (f32[1,256,32]{1,2,0:T(8,128)S(1)}, f32[1,256,32]{1,2,0:T(8,128)}, u32[]{:S(2)}) copy-start(f32[1,256,32]{1,2,0:T(8,128)} %copy-done.3) | copy-start | bytes 98308
  105.0 3.8 %copy-start.9 = (f32[1,32,256]{2,1,0:T(8,128)}, f32[1,32,256]{2,1,0:T(8,128)S(1)}, u32[]{:S(2)}) copy-start(f32[1,32,256]{2,1,0:T(8,128)S(1)} %get-tuple-element.189) | copy-start | bytes 98308
  116.1 1.7 %copy-start.12 = (f32[32]{0:T(128)S(1)}, f32[32]{0:T(128)}, u32[]{:S(2)}) copy-start(f32[32]{0:T(128)} %get-tuple-element.188) | copy-start | bytes 388
  116.2 1.8 %copy-start.13 = (f32[32]{0:T(128)S(1)}, f32[32]{0:T(128)}, u32[]{:S(2)}) copy-start(f32[32]{0:T(128)} %get-tuple-element.186) | copy-start | bytes 388
  116.4 8.0 %copy-start.10 = (f32[1,32,256]{2,1,0:T(8,128)S(1)}, f32[1,32,256]{2,1,0:T(8,128)}, u32[]{:S(2)}) copy-start(f32[1,32,256]{2,1,0:T(8,128)} %get-tuple-element.261) | copy-start | bytes 98308
Sparse Core Ops, SparseCore 0:
  124.5 18.6 reduce-scatter.2
where the time goes:
time: 164 us; the launch traced here: 163 us
  blocking collectives  98.3 us (60%)
  local copies, waits for them, and re-layouts  28 us (17%)
  between operations  15.4 us (9%)
  other arithmetic  8.04 us (5%)
  starting transfers between devices  7.42 us (5%)
  matrix products  5.84 us (4%)
    all_gather x3, blocking collectives, carried_in(): gathered = jax.tree.map(lambda a: lax.all_gather(a, axis), part)  92.6 us
    reshape x7, local copies, waits for them, and re-layouts, spread_taps(): grid = grads.reshape(count, chans, 9, IMG, IMG)  8.09 us
    ppermute x2, starting transfers between devices, shifted(): return lax.ppermute(x, axis, pairs)  7.38 us
    unnamed x1, blocking collectives  5.67 us
    unnamed x67, local copies, waits for them, and re-layouts  4.37 us
    add x14, other arithmetic, spread_taps(): total + jnp.pad(grid[:, :, tap], ((0, 0), (0, 0), (row, 2 - row), (col, 2...  4.35 us
    another operation x4, local copies, waits for them, and re-layouts  4.18 us
    another operation x8, local copies, waits for them, and re-layouts, gather_taps(): return jnp.stack(taps, axis=2).reshape(count, chans * 9, pixels)  3.99 us
  transfers between devices with their start and end apart: 3, of which 0 were waited for; matrix products, arithmetic and copies ran while one was open for 16% of the time, Pallas kernels for 0%

commit v1 on v0

v1 whole, which is shorter than its diff:
```python
import functools

import jax
import jax.numpy as jnp
from jax import lax
from jax.experimental import pallas as pl
from jax.experimental.pallas import tpu as pltpu
from jax.sharding import PartitionSpec as P

IMG = 16
HW = IMG * IMG
HALF = 128
TAPS = 9
STEP = 0.5
LIMIT = 32 * 1024 * 1024

VMEM = pl.BlockSpec(memory_space=pltpu.VMEM)


def offset_of(tap):
    return (tap // 3 - 1) * IMG + (tap % 3 - 1)


def inside(shape, down, right):
    pixel = lax.broadcasted_iota(jnp.int32, shape, 1)
    col = lax.rem(pixel, IMG)
    ok = None
    for test in (
        (pixel >= IMG) if down < 0 else None,
        (pixel < HW - IMG) if down > 0 else None,
        (col >= 1) if right < 0 else None,
        (col < IMG - 1) if right > 0 else None,
    ):
        if test is not None:
            ok = test if ok is None else jnp.logical_and(ok, test)
    return ok


def taps_of(values):
    out = []
    for tap in range(TAPS):
        by = offset_of(tap)
        if by == 0:
            out.append(values)
            continue
        ok = inside(values.shape, tap // 3 - 1, tap % 3 - 1)
        out.append(jnp.where(ok, pltpu.roll(values, (-by) % HW, 1), 0.0))
    return out


def spread(rows, chans):
    total = None
    for tap in range(TAPS):
        by = offset_of(tap)
        part = rows[tap * chans : (tap + 1) * chans]
        if by != 0:
            ok = inside(part.shape, 1 - tap // 3, 1 - tap % 3)
            part = jnp.where(ok, pltpu.roll(part, by % HW, 1), 0.0)
        total = part if total is None else total + part
    return total


def permutation(chans):
    size = TAPS * chans
    src = lax.broadcasted_iota(jnp.int32, (size, size), 0)
    dst = lax.broadcasted_iota(jnp.int32, (size, size), 1)
    tap = lax.div(dst, chans)
    return jnp.where(src == (dst - tap * chans) * TAPS + tap, 1.0, 0.0).astype(jnp.bfloat16)


def dot(a, b, dims):
    return lax.dot_general(a, b, (dims, ((), ())), preferred_element_type=jnp.float32)


def relax_kernel(state_ref, adj_ref, w_ref, bias_ref, sent_ref, slope_ref, patch_ref, back_w_ref):
    depth, chans, width = w_ref.shape
    perm = permutation(chans)
    start = state_ref[0, 0]
    guess = adj_ref[0, 0]
    row = lax.broadcasted_iota(jnp.int32, (chans, width), 0)
    lane = lax.broadcasted_iota(jnp.int32, (chans, width), 1)
    center = lane == row * TAPS + TAPS // 2
    eye = lax.broadcasted_iota(jnp.int32, (chans, chans), 0) == lax.broadcasted_iota(
        jnp.int32, (chans, chans), 1
    )
    state = start
    gain = None
    slopes = []
    for n in range(depth):
        weight = w_ref[n]
        kc = jnp.sum(jnp.where(center, weight.astype(jnp.float32), 0.0), axis=1, keepdims=True)
        bias = jnp.sum(
            jnp.where(eye, jnp.broadcast_to(bias_ref[n : n + 1, :], (chans, chans)), 0.0),
            axis=1,
            keepdims=True,
        )
        by_tap = dot(weight, perm, ((1,), (0,))).astype(jnp.bfloat16)
        back_w_ref[n] = dot(perm, weight, ((0,), (1,))).astype(jnp.bfloat16)
        rounded = state.astype(jnp.bfloat16).astype(jnp.float32)
        patch = jnp.concatenate([t.astype(jnp.bfloat16) for t in taps_of(rounded)], axis=0)
        patch_ref[n] = dot(perm, patch, ((1,), (0,))).astype(jnp.bfloat16)
        squash = jnp.tanh(dot(by_tap, patch, ((1,), (0,))) + bias)
        slope = STEP * (1.0 - squash * squash)
        factor = 1.0 + slope * kc
        gain = factor if gain is None else gain * factor
        state = state + STEP * squash
        slope_ref[n] = slope
        slopes.append(slope)
    back = guess
    for n in reversed(range(depth)):
        dzb = (back * slopes[n]).astype(jnp.bfloat16)
        back = back + spread(dot(back_w_ref[n], dzb, ((1,), (0,))), chans)
    place = lax.axis_index("layer")
    first = jnp.where(place == 0, 0.0, start)
    last = jnp.where(place == lax.axis_size("layer") - 1, 0.0, guess)
    for k, value in enumerate((gain, back - gain * last, state - gain * first)):
        put_parts(sent_ref, k, value)


def put_parts(ref, k, value):
    chans = value.shape[0]
    for half in range(HW // HALF):
        piece = value[:, half * HALF : (half + 1) * HALF]
        if len(ref.shape) == 3:
            ref[k, half * chans : (half + 1) * chans, :] = piece
        else:
            for part in range(chans // 8):
                ref[half * (chans // 8) + part, k] = piece[part * 8 : part * 8 + 8]


def get_parts(ref, k, chans):
    if len(ref.shape) == 3:
        halves = [ref[k, h * chans : (h + 1) * chans, :] for h in range(HW // HALF)]
    else:
        parts = chans // 8
        halves = [
            jnp.concatenate([ref[h * parts + p, k] for p in range(parts)], axis=0)
            for h in range(HW // HALF)
        ]
    return jnp.concatenate(halves, axis=1)


def scan_kernel(ref, out_ref):
    count = ref.shape[0]
    out_ref[0, 1] = jnp.zeros(ref.shape[2:], jnp.float32)
    out_ref[count - 1, 0] = jnp.zeros(ref.shape[2:], jnp.float32)
    adj = ref[count - 1, 1]
    for j in reversed(range(count - 1)):
        out_ref[j, 0] = adj
        if j:
            adj = ref[j, 0] * adj + ref[j, 1]
    state = ref[0, 2]
    for j in range(1, count):
        out_ref[j, 1] = state
        state = ref[j, 0] * state + ref[j, 2]


def grad_kernel(
    shares,
    fixed_ref,
    guess_ref,
    start_ref,
    slope_ref,
    patch_ref,
    back_w_ref,
    adj_ref,
    state_ref,
    out_ref,
):
    depth, rows, _ = back_w_ref.shape
    chans = rows // TAPS
    own = chans // shares
    place = lax.axis_index("layer")
    last = place == lax.axis_size("layer") - 1
    adj = jnp.where(last, guess_ref[0, 0], get_parts(fixed_ref, 0, chans))
    adj_ref[0, 0] = adj
    state_ref[0, 0] = jnp.where(place == 0, start_ref[0, 0], get_parts(fixed_ref, 1, chans))
    pad = out_ref.shape[2] - rows
    for n in reversed(range(depth)):
        dz = adj * slope_ref[n]
        dzb = dz.astype(jnp.bfloat16)
        grad = dot(dzb, patch_ref[n], ((1,), (1,)))
        bias = jnp.broadcast_to(jnp.sum(dz, axis=1, keepdims=True), (chans, pad))
        for s in range(shares):
            out_ref[s, n * own : (n + 1) * own, :rows] = grad[s * own : (s + 1) * own]
            out_ref[s, n * own : (n + 1) * own, rows:] = bias[s * own : (s + 1) * own]
        if n:
            adj = adj + spread(dot(back_w_ref[n], dzb, ((1,), (0,))), chans)


def total_kernel(ref, grad_ref, bias_ref):
    depth, own, width = grad_ref.shape
    total = ref[0]
    for s in range(1, ref.shape[0]):
        total = total + ref[s]
    eye = lax.broadcasted_iota(jnp.int32, (own, own), 0) == lax.broadcasted_iota(
        jnp.int32, (own, own), 1
    )
    for n in range(depth):
        mine = total[n * own : (n + 1) * own]
        grad_ref[n] = mine[:, :width]
        column = jnp.broadcast_to(mine[:, width : width + 1], (own, own))
        bias_ref[n : n + 1, :] = jnp.sum(jnp.where(eye, column, 0.0), axis=0, keepdims=True)


def call(kernel, out_shape, args):
    many = isinstance(out_shape, (list, tuple))
    return pl.pallas_call(
        kernel,
        out_shape=out_shape,
        in_specs=[VMEM] * len(args),
        out_specs=[VMEM] * len(out_shape) if many else VMEM,
        compiler_params=pltpu.CompilerParams(vmem_limit_bytes=LIMIT),
    )(*args)


def f32(*shape):
    return jax.ShapeDtypeStruct(shape, jnp.float32)


def bf16(*shape):
    return jax.ShapeDtypeStruct(shape, jnp.bfloat16)


def swap(x, axis):
    return lax.all_to_all(x, axis, 0, 0, tiled=True)


def local(state_guess, adjoint_guess, conv_weight, conv_bias):
    depth, chans, width = conv_weight.shape
    blocks = lax.axis_size("layer")
    shares = lax.axis_size("dp")
    rows = HW // HALF * chans
    tiled = rows == 8 * blocks
    items = 3
    sent, slope, patch, back_w = call(
        relax_kernel,
        (
            f32(blocks, items, 8, HALF) if tiled else f32(items, rows, HALF),
            f32(depth, chans, HW),
            bf16(depth, width, HW),
            bf16(depth, width, chans),
        ),
        (state_guess, adjoint_guess, conv_weight, conv_bias),
    )
    if not tiled:
        sent = jnp.moveaxis(sent.reshape(items, blocks, 1, rows * HALF // blocks), 0, 1)
    got = swap(sent, "layer")
    fixed = call(scan_kernel, f32(blocks, 2, *got.shape[2:]), (got,))
    fixed = swap(fixed, "layer")
    if not tiled:
        fixed = jnp.moveaxis(fixed, 1, 0).reshape(2, rows, HALF)
    lanes = -(-(width + 1) // HALF) * HALF
    adjoint_fixed, state_fixed, parts = call(
        functools.partial(grad_kernel, shares),
        (
            f32(*adjoint_guess.shape),
            f32(*state_guess.shape),
            f32(shares, depth * chans // shares, lanes),
        ),
        (fixed, adjoint_guess, state_guess, slope, patch, back_w),
    )
    weight_grad, bias_grad = call(
        total_kernel,
        (f32(depth, chans // shares, width), f32(depth, chans // shares)),
        (swap(parts, "dp"),),
    )
    return (state_fixed, adjoint_fixed, weight_grad, bias_grad)


def solution(mesh):
    placed = (
        P("layer", "dp", None, None),
        P("layer", "dp", None, None),
        P("layer", None, None),
        P("layer", None),
    )
    return jax.shard_map(
        local,
        mesh=mesh,
        in_specs=placed,
        out_specs=(
            P("layer", "dp", None, None),
            P("layer", "dp", None, None),
            P("layer", "dp", None),
            P("layer", "dp"),
        ),
        check_vma=False,
    )
```

time: 164 us -> 40 us (0.24)
  blocking collectives: 98.3 us -> 31.4 us
  local copies, waits for them, and re-layouts: 28 us -> 3.1 us
  between operations: 15.4 us -> 0.67 us
  other arithmetic: 8.04 us -> 0 us
  starting transfers between devices: 7.42 us -> 0 us
  matrix products: 5.84 us -> 0 us
  Pallas kernels: 0 us -> 4.35 us
    all_gather x3 -> x0, blocking collectives: 92.6 us -> none  [carried_in(): gathered = jax.tree.map(lambda a: lax.all_gather(a, axis), part)]
    all_to_all x0 -> x3, blocking collectives: none -> 31.4 us  [swap(): return lax.all_to_all(x, axis, 0, 0, tiled=True)]
    reshape x14 -> x0, local copies, waits for them, and re-layouts: 8.53 us -> none  [the longest x7 8.09 us: spread_taps(): grid = grads.reshape(count, chans, 9, IMG, IMG)]
    another operation x16 -> x0, local copies, waits for them, and re-layouts: 8.33 us -> none
    ppermute x2 -> x0, starting transfers between devices: 7.38 us -> none  [shifted(): return lax.ppermute(x, axis, pairs)]
    dot_general x15 -> x0, matrix products: 5.84 us -> none  [the longest x7 3.84 us: backward_step(): jnp.einsum('ok,bop->bkp', kernel, dzb, preferred_element_type=jnp.float32)]
    unnamed x1 -> x0, blocking collectives: 5.67 us -> none
    add x22 -> x0, other arithmetic: 4.46 us -> none  [the longest x14 4.35 us: spread_taps(): total + jnp.pad(grid[:, :, tap], ((0, 0), (0, 0), (row, 2 - row), (col, 2...]
  transfers between devices with their start and end apart: 3 -> 0, of which waited for: 0 -> 0; matrix products, arithmetic and copies ran while one was open for 16% -> 0% of each run, Pallas kernels for 0% -> 0%
where the time goes in v1:
time: 40 us; the launch traced here: 39.5 us
  blocking collectives  31.4 us (78%)
  Pallas kernels  4.35 us (11%)
  local copies, waits for them, and re-layouts  3.1 us (8%)
  between operations  0.67 us (2%)
    all_to_all x3, blocking collectives, swap(): return lax.all_to_all(x, axis, 0, 0, tiled=True)  31.4 us
    pallas_call x4, Pallas kernels, call(): pl.pallas_call(kernel, out_shape=out_shape, in_specs=[VMEM] * len(args),...  4.35 us
    unnamed x12, local copies, waits for them, and re-layouts  3.1 us

profile of v1, /device:TPU:0, one launch (start us, length us, event | category | flops | bytes accessed | tf_op | source)
XLA Modules:
  0.0 39.5 jit_solution(14167039402368102754)
XLA Ops:
  0.6 0.0 copy-start
  0.6 0.7 %copy-done = f32[1,1,32,256]{3,2,1,0:T(8,128)S(1)} copy-done((f32[1,1,32,256]{3,2,1,0:T(8,128)S(1)}, f32[1,1,32,256]{3,2,1,0:T(8,128)}, u32[]{:S(2)}) %copy-start) | copy-done | bytes 32792
  1.4 0.0 copy-start.2
  1.4 0.8 %copy-done.2 = f32[1,1,32,256]{3,2,1,0:T(8,128)S(1)} copy-done((f32[1,1,32,256]{3,2,1,0:T(8,128)S(1)}, f32[1,1,32,256]{3,2,1,0:T(8,128)}, u32[]{:S(2)}) %copy-start.2) | copy-done | bytes 32792
  2.2 0.0 copy-start.4
  2.2 0.9 %copy-done.4 = bf16[4,32,288]{2,1,0:T(8,128)(2,1)S(1)} copy-done((bf16[4,32,288]{2,1,0:T(8,128)(2,1)S(1)}, bf16[4,32,288]{2,1,0:T(8,128)(2,1)}, u32[]{:S(2)}) %copy-start.4) | copy-done | bytes 73752
  3.0 0.0 copy-start.5
  3.0 0.7 %copy-done.5 = f32[4,32]{1,0:T(4,128)S(1)} copy-done((f32[4,32]{1,0:T(4,128)S(1)}, f32[4,32]{1,0:T(4,128)}, u32[]{:S(2)}) %copy-start.5) | copy-done | bytes 536
  3.7 2.2 %shard_map.75 = (f32[8,3,8,128]{3,2,1,0:T(8,128)S(1)}, f32[4,32,256]{2,1,0:T(8,128)S(1)}, bf16[4,288,256]{2,1,0:T(8,128)(2,1)S(1)}, bf16[4,288,32]{2,1,0:T(8,128)(2,1)S(1)}) custom-call(f32[1,1,32,256]{3,2,1,0:T(8,128)S(1)} %copy-done, f32[1,1,32,256]{3,2,1,0:T(8,128)S(1)} %copy-done.2, bf16[4,32,288]{2,1,0:T(8,128)(2,1)S(1)} %copy-done.4, f32[4,32]{1,0:T(4,128)S(1)} %copy-done.5), custom_call_target="tpu_custom_call" | custom-call | tf_op jit(solution)/shard_map/pallas_call | solution.py:208
  6.0 14.2 %all_to_all.15.ref = f32[8,3,8,128]{3,2,1,0:T(8,128)S(1)} all-to-all(f32[8,3,8,128]{3,2,1,0:T(8,128)S(1)} %get-tuple-element.13), channel_id=1, replica_groups=mesh['layer'=8,'dp'=4] {'layer'}, dimensions={0} | all-to-all | bytes 196608 | tf_op jit(solution)/shard_map/all_to_all | solution.py:226
  20.1 0.0 copy-start.1
  20.2 0.0 copy-start.3
  20.2 9.3 %all_to_all.16.fixed_ref = f32[8,2,8,128]{3,2,1,0:T(8,128)S(1)} all-to-all(f32[8,2,8,128]{3,2,1,0:T(8,128)S(1)} %shard_map.76), channel_id=1, replica_groups=mesh['layer'=8,'dp'=4] {'layer'}, dimensions={0} | all-to-all | bytes 131072 | tf_op jit(solution)/shard_map/all_to_all | solution.py:226
  29.5 0.0 copy-done.1
  29.5 0.0 copy-done.3
  29.5 1.5 %shard_map.77 = (f32[1,1,32,256]{3,2,1,0:T(8,128)}, f32[1,1,32,256]{3,2,1,0:T(8,128)}, f32[4,32,384]{2,1,0:T(8,128)S(1)}) custom-call(f32[8,2,8,128]{3,2,1,0:T(8,128)S(1)} %all_to_all.16.fixed_ref, f32[1,1,32,256]{3,2,1,0:T(8,128)S(1)} %copy-done.3, f32[1,1,32,256]{3,2,1,0:T(8,128)S(1)} %copy-done.1, f32[4,32,256]{2,1,0:T(8,128)S(1)} %get-tuple-element.14.slope_ref, ...), custom_call_target="tpu_custom_call" | custom-call | tf_op jit(solution)/shard_map/pallas_call | solution.py:208
  30.9 7.9 %all_to_all.17.ref = f32[4,32,384]{2,1,0:T(8,128)S(1)} all-to-all(f32[4,32,384]{2,1,0:T(8,128)S(1)} %get-tuple-element.19), channel_id=1, replica_groups=mesh['layer'=8,'dp'=4] {'dp'}, dimensions={0} | all-to-all | bytes 393216 | tf_op jit(solution)/shard_map/all_to_all | solution.py:226
  38.8 0.7 %shard_map.78 = (f32[4,8,288]{2,1,0:T(8,128)}, f32[4,8]{1,0:T(4,128)}) custom-call(f32[4,32,384]{2,1,0:T(8,128)S(1)} %all_to_all.17.ref), custom_call_target="tpu_custom_call" | custom-call | tf_op jit(solution)/shard_map/pallas_call | solution.py:208
  (1 shorter events, 0.0 us)
Async XLA Ops:
  0.6 0.8 %copy-start = (f32[1,1,32,256]{3,2,1,0:T(8,128)S(1)}, f32[1,1,32,256]{3,2,1,0:T(8,128)}, u32[]{:S(2)}) copy-start(f32[1,1,32,256]{3,2,1,0:T(8,128)} %start_ref.1) | copy-start | bytes 98308
  1.4 0.8 %copy-start.2 = (f32[1,1,32,256]{3,2,1,0:T(8,128)S(1)}, f32[1,1,32,256]{3,2,1,0:T(8,128)}, u32[]{:S(2)}) copy-start(f32[1,1,32,256]{3,2,1,0:T(8,128)} %guess_ref.1) | copy-start | bytes 98308
  2.2 0.9 %copy-start.4 = (bf16[4,32,288]{2,1,0:T(8,128)(2,1)S(1)}, bf16[4,32,288]{2,1,0:T(8,128)(2,1)}, u32[]{:S(2)}) copy-start(bf16[4,32,288]{2,1,0:T(8,128)(2,1)} %w_ref.1) | copy-start | bytes 221188
  3.0 0.7 %copy-start.5 = (f32[4,32]{1,0:T(4,128)S(1)}, f32[4,32]{1,0:T(4,128)}, u32[]{:S(2)}) copy-start(f32[4,32]{1,0:T(4,128)} %bias_ref.1) | copy-start | bytes 1540
  20.1 9.3 %copy-start.1 = (f32[1,1,32,256]{3,2,1,0:T(8,128)S(1)}, f32[1,1,32,256]{3,2,1,0:T(8,128)}, u32[]{:S(2)}) copy-start(f32[1,1,32,256]{3,2,1,0:T(8,128)} %start_ref.1) | copy-start | bytes 98308
  20.2 9.3 %copy-start.3 = (f32[1,1,32,256]{3,2,1,0:T(8,128)S(1)}, f32[1,1,32,256]{3,2,1,0:T(8,128)}, u32[]{:S(2)}) copy-start(f32[1,1,32,256]{3,2,1,0:T(8,128)} %guess_ref.1) | copy-start | bytes 98308

commit v2 on v1

--- a/solution.py
+++ b/solution.py
@@ -15,6 +15,7 @@
 LIMIT = 32 * 1024 * 1024
 
 VMEM = pl.BlockSpec(memory_space=pltpu.VMEM)
+HBM = pl.BlockSpec(memory_space=pltpu.HBM)
 
 
 def offset_of(tap):
@@ -72,9 +73,33 @@
     return lax.dot_general(a, b, (dims, ((), ())), preferred_element_type=jnp.float32)
 
 
-def relax_kernel(state_ref, adj_ref, w_ref, bias_ref, sent_ref, slope_ref, patch_ref, back_w_ref):
+def relax_kernel(
+    state_hbm,
+    adj_hbm,
+    w_hbm,
+    bias_hbm,
+    sent_ref,
+    slope_ref,
+    patch_ref,
+    back_w_ref,
+    state_ref,
+    adj_ref,
+    w_ref,
+    bias_ref,
+    sems,
+):
+    copies = [
+        pltpu.make_async_copy(src, dst, sems.at[k])
+        for k, (src, dst) in enumerate(
+            ((w_hbm, w_ref), (state_hbm, state_ref), (bias_hbm, bias_ref), (adj_hbm, adj_ref))
+        )
+    ]
+    for copy in copies:
+        copy.start()
     depth, chans, width = w_ref.shape
     perm = permutation(chans)
+    for copy in copies:
+        copy.wait()
     start = state_ref[0, 0]
     guess = adj_ref[0, 0]
     row = lax.broadcasted_iota(jnp.int32, (chans, width), 0)
@@ -113,86 +138,120 @@
     place = lax.axis_index("layer")
     first = jnp.where(place == 0, 0.0, start)
     last = jnp.where(place == lax.axis_size("layer") - 1, 0.0, guess)
-    for k, value in enumerate((gain, back - gain * last, state - gain * first)):
-        put_parts(sent_ref, k, value)
-
-
-def put_parts(ref, k, value):
-    chans = value.shape[0]
-    for half in range(HW // HALF):
-        piece = value[:, half * HALF : (half + 1) * HALF]
-        if len(ref.shape) == 3:
-            ref[k, half * chans : (half + 1) * chans, :] = piece
-        else:
-            for part in range(chans // 8):
-                ref[half * (chans // 8) + part, k] = piece[part * 8 : part * 8 + 8]
-
-
-def get_parts(ref, k, chans):
-    if len(ref.shape) == 3:
-        halves = [ref[k, h * chans : (h + 1) * chans, :] for h in range(HW // HALF)]
+    sent_ref[0] = gain
+    sent_ref[1] = state - gain * first
+    sent_ref[2] = back - gain * last
+
+
+def joined(bit, total, mine, got):
+    gain, fwd, bwd = total
+    pre_gain, pre, post_gain, post = mine
+    got_gain, got_fwd, got_bwd = got
+    total = (
+        gain * got_gain,
+        jnp.where(bit, gain * got_fwd + fwd, got_gain * fwd + got_fwd),
+        jnp.where(bit, got_gain * bwd + got_bwd, gain * got_bwd + bwd),
+    )
+    mine = (
+        jnp.where(bit, pre_gain * got_gain, pre_gain),
+        jnp.where(bit, pre_gain * got_fwd + pre, pre),
+        jnp.where(bit, post_gain, post_gain * got_gain),
+        jnp.where(bit, post, post_gain * got_bwd + post),
+    )
+    return total, mine
+
+
+def bit_of(axis, step):
+    return lax.rem(lax.div(lax.axis_index(axis), 2**step), 2) == 1
+
+
+def join_kernel(step, final, *refs):
+    if step == 1:
+        total_ref, got_ref, sent_ref, mine_out = refs
+        one = jnp.ones(total_ref.shape[1:], jnp.float32)
+        zero = jnp.zeros(total_ref.shape[1:], jnp.float32)
+        mine = (one, zero, one, zero)
     else:
-        parts = chans // 8
-        halves = [
-            jnp.concatenate([ref[h * parts + p, k] for p in range(parts)], axis=0)
-            for h in range(HW // HALF)
-        ]
-    return jnp.concatenate(halves, axis=1)
-
-
-def scan_kernel(ref, out_ref):
-    count = ref.shape[0]
-    out_ref[0, 1] = jnp.zeros(ref.shape[2:], jnp.float32)
-    out_ref[count - 1, 0] = jnp.zeros(ref.shape[2:], jnp.float32)
-    adj = ref[count - 1, 1]
-    for j in reversed(range(count - 1)):
-        out_ref[j, 0] = adj
-        if j:
-            adj = ref[j, 0] * adj + ref[j, 1]
-    state = ref[0, 2]
-    for j in range(1, count):
-        out_ref[j, 1] = state
-        state = ref[j, 0] * state + ref[j, 2]
+        total_ref, got_ref, mine_ref, sent_ref, mine_out = refs
+        mine = tuple(mine_ref[k] for k in range(4))
+    total = tuple(total_ref[k] for k in range(3))
+    got = tuple(got_ref[k] for k in range(3))
+    total, mine = joined(bit_of("layer", step - 1), total, mine, got)
+    for k in range(4):
+        mine_out[k] = mine[k]
+    if final:
+        sent_ref[...] = jnp.where(bit_of("layer", step), total[2], total[1])
+    else:
+        for k in range(3):
+            sent_ref[k] = total[k]
 
 
 def grad_kernel(
-    shares,
-    fixed_ref,
+    steps,
+    got_ref,
+    mine_ref,
     guess_ref,
     start_ref,
     slope_ref,
     patch_ref,
     back_w_ref,
+    adj_hbm,
+    state_hbm,
+    keep_ref,
+    send_ref,
     adj_ref,
     state_ref,
-    out_ref,
+    sems,
 ):
     depth, rows, _ = back_w_ref.shape
     chans = rows // TAPS
+    shares = 2 * keep_ref.shape[0]
     own = chans // shares
     place = lax.axis_index("layer")
-    last = place == lax.axis_size("layer") - 1
-    adj = jnp.where(last, guess_ref[0, 0], get_parts(fixed_ref, 0, chans))
+    upper = bit_of("layer", steps - 1)
+    got = got_ref[...]
+    fixed = jnp.where(upper, mine_ref[1] + mine_ref[0] * got, mine_ref[1])
+    state_ref[0, 0] = jnp.where(place == 0, start_ref[0, 0], fixed)
+    fixed = jnp.where(upper, mine_ref[3], mine_ref[3] + mine_ref[2] * got)
+    adj = jnp.where(place == lax.axis_size("layer") - 1, guess_ref[0, 0], fixed)
     adj_ref[0, 0] = adj
-    state_ref[0, 0] = jnp.where(place == 0, start_ref[0, 0], get_parts(fixed_ref, 1, chans))
-    pad = out_ref.shape[2] - rows
+    copies = [
+        pltpu.make_async_copy(src, dst, sems.at[k])
+        for k, (src, dst) in enumerate(((adj_ref, adj_hbm), (state_ref, state_hbm)))
+    ]
+    for copy in copies:
+        copy.start()
+    pad = keep_ref.shape[2] - rows
+    odd = bit_of("dp", 0)
     for n in reversed(range(depth)):
         dz = adj * slope_ref[n]
         dzb = dz.astype(jnp.bfloat16)
         grad = dot(dzb, patch_ref[n], ((1,), (1,)))
         bias = jnp.broadcast_to(jnp.sum(dz, axis=1, keepdims=True), (chans, pad))
-        for s in range(shares):
-            out_ref[s, n * own : (n + 1) * own, :rows] = grad[s * own : (s + 1) * own]
-            out_ref[s, n * own : (n + 1) * own, rows:] = bias[s * own : (s + 1) * own]
+        both = jnp.concatenate([grad, bias], axis=1)
+        for s in range(shares // 2):
+            even_part = both[2 * s * own : (2 * s + 1) * own]
+            odd_part = both[(2 * s + 1) * own : (2 * s + 2) * own]
+            keep_ref[s, n * own : (n + 1) * own] = jnp.where(odd, odd_part, even_part)
+            send_ref[s, n * own : (n + 1) * own] = jnp.where(odd, even_part, odd_part)
         if n:
             adj = adj + spread(dot(back_w_ref[n], dzb, ((1,), (0,))), chans)
-
-
-def total_kernel(ref, grad_ref, bias_ref):
+    for copy in copies:
+        copy.wait()
+
+
+def halve_kernel(step, mine_ref, got_ref, keep_ref, send_ref):
+    odd = bit_of("dp", step)
+    for s in range(keep_ref.shape[0]):
+        even_part = mine_ref[2 * s] + got_ref[2 * s]
+        odd_part = mine_ref[2 * s + 1] + got_ref[2 * s + 1]
+        keep_ref[s] = jnp.where(odd, odd_part, even_part)
+        send_ref[s] = jnp.where(odd, even_part, odd_part)
+
+
+def total_kernel(mine_ref, got_ref, grad_ref, bias_ref):
     depth, own, width = grad_ref.shape
-    total = ref[0]
-    for s in range(1, ref.shape[0]):
-        total = total + ref[s]
+    total = mine_ref[0] + got_ref[0]
     eye = lax.broadcasted_iota(jnp.int32, (own, own), 0) == lax.broadcasted_iota(
         jnp.int32, (own, own), 1
     )
@@ -203,15 +262,15 @@
         bias_ref[n : n + 1, :] = jnp.sum(jnp.where(eye, column, 0.0), axis=0, keepdims=True)
 
 
-def call(kernel, out_shape, args):
-    many = isinstance(out_shape, (list, tuple))
+def call(kernel, out_shape, args, hbm_in=(), hbm_out=(), scratch=()):
     return pl.pallas_call(
         kernel,
         out_shape=out_shape,
-        in_specs=[VMEM] * len(args),
-        out_specs=[VMEM] * len(out_shape) if many else VMEM,
+        in_specs=[HBM if k in hbm_in else VMEM for k in range(len(args))],
+        out_specs=[HBM if k in hbm_out else VMEM for k in range(len(out_shape))],
+        scratch_shapes=list(scratch),
         compiler_params=pltpu.CompilerParams(vmem_limit_bytes=LIMIT),
-    )(*args)
+    )(*(pltpu.with_memory_space_constraint(a, pltpu.HBM) if k in hbm_in else a for k, a in enumerate(args)))
 
 
 def f32(*shape):
@@ -222,48 +281,67 @@
     return jax.ShapeDtypeStruct(shape, jnp.bfloat16)
 
 
-def swap(x, axis):
-    return lax.all_to_all(x, axis, 0, 0, tiled=True)
+def exchange(x, axis, step):
+    pairs = [(i, i ^ (1 << step)) for i in range(lax.axis_size(axis))]
+    return lax.ppermute(x, axis, pairs)
 
 
 def local(state_guess, adjoint_guess, conv_weight, conv_bias):
     depth, chans, width = conv_weight.shape
-    blocks = lax.axis_size("layer")
     shares = lax.axis_size("dp")
-    rows = HW // HALF * chans
-    tiled = rows == 8 * blocks
-    items = 3
-    sent, slope, patch, back_w = call(
+    steps = lax.axis_size("layer").bit_length() - 1
+    args = (state_guess, adjoint_guess, conv_weight, conv_bias)
+    total, slope, patch, back_w = call(
         relax_kernel,
         (
-            f32(blocks, items, 8, HALF) if tiled else f32(items, rows, HALF),
+            f32(3, chans, HW),
             f32(depth, chans, HW),
             bf16(depth, width, HW),
             bf16(depth, width, chans),
         ),
-        (state_guess, adjoint_guess, conv_weight, conv_bias),
-    )
-    if not tiled:
-        sent = jnp.moveaxis(sent.reshape(items, blocks, 1, rows * HALF // blocks), 0, 1)
-    got = swap(sent, "layer")
-    fixed = call(scan_kernel, f32(blocks, 2, *got.shape[2:]), (got,))
-    fixed = swap(fixed, "layer")
-    if not tiled:
-        fixed = jnp.moveaxis(fixed, 1, 0).reshape(2, rows, HALF)
+        args,
+        hbm_in=range(4),
+        scratch=[pltpu.VMEM(a.shape, a.dtype) for a in args] + [pltpu.SemaphoreType.DMA((4,))],
+    )
+    mine = ()
+    for step in range(1, steps):
+        got = exchange(total, "layer", step - 1)
+        final = step == steps - 1
+        total, *mine = call(
+            functools.partial(join_kernel, step, final),
+            (f32(chans, HW) if final else f32(3, chans, HW), f32(4, chans, HW)),
+            (total, got, *mine),
+        )
+    got = exchange(total, "layer", steps - 1)
     lanes = -(-(width + 1) // HALF) * HALF
-    adjoint_fixed, state_fixed, parts = call(
-        functools.partial(grad_kernel, shares),
+    part = (depth * chans // shares, lanes)
+    guess = pltpu.VMEM(adjoint_guess.shape, jnp.float32)
+    adjoint_fixed, state_fixed, keep, send = call(
+        functools.partial(grad_kernel, steps),
         (
             f32(*adjoint_guess.shape),
             f32(*state_guess.shape),
-            f32(shares, depth * chans // shares, lanes),
+            f32(shares // 2, *part),
+            f32(shares // 2, *part),
         ),
-        (fixed, adjoint_guess, state_guess, slope, patch, back_w),
-    )
+        (got, *mine, adjoint_guess, state_guess, slope, patch, back_w),
+        hbm_out=(0, 1),
+        scratch=[guess, guess, pltpu.SemaphoreType.DMA((2,))],
+    )
+    left = shares // 2
+    step = 0
+    while left > 1:
+        left //= 2
+        step += 1
+        keep, send = call(
+            functools.partial(halve_kernel, step),
+            (f32(left, *part), f32(left, *part)),
+            (keep, exchange(send, "dp", step - 1)),
+        )
     weight_grad, bias_grad = call(
         total_kernel,
         (f32(depth, chans // shares, width), f32(depth, chans // shares)),
-        (swap(parts, "dp"),),
+        (keep, exchange(send, "dp", step)),
     )
     return (state_fixed, adjoint_fixed, weight_grad, bias_grad)
 

time: 40 us -> 27 us (0.68)
  blocking collectives: 31.4 us -> 0 us
  waiting for transfers between devices: 0 us -> 10.9 us
  starting transfers between devices: 0 us -> 9.95 us
  local copies, waits for them, and re-layouts: 3.1 us -> 0.01 us
  Pallas kernels: 4.35 us -> 5.33 us
    all_to_all x3 -> x0, blocking collectives: 31.4 us -> none  [swap(): return lax.all_to_all(x, axis, 0, 0, tiled=True)]
    ppermute x0 -> x5, waiting for transfers between devices: none -> 10.9 us  [exchange(): return lax.ppermute(x, axis, pairs)]
    ppermute x0 -> x5, starting transfers between devices: none -> 9.95 us  [exchange(): return lax.ppermute(x, axis, pairs)]
    unnamed x12 -> x4, local copies, waits for them, and re-layouts: 3.1 us -> 0.01 us
    pallas_call x4 -> x6, Pallas kernels: 4.35 us -> 5.33 us  [call(): pl.pallas_call(kernel, out_shape=out_shape, in_specs=[HBM if k in hbm_in...]
  transfers between devices with their start and end apart: 0 -> 5, of which waited for: 0 -> 5; matrix products, arithmetic and copies ran while one was open for 0% -> 0% of each run, Pallas kernels for 0% -> 0%
where the time goes in v2:
time: 27 us; the launch traced here: 26.9 us
  waiting for transfers between devices  10.9 us (40%)
  starting transfers between devices  9.95 us (37%)
  Pallas kernels  5.33 us (20%)
  between operations  0.68 us (3%)
    ppermute x5, waiting for transfers between devices, exchange(): return lax.ppermute(x, axis, pairs)  10.9 us
    ppermute x5, starting transfers between devices, exchange(): return lax.ppermute(x, axis, pairs)  9.95 us
    pallas_call x6, Pallas kernels, call(): pl.pallas_call(kernel, out_shape=out_shape, in_specs=[HBM if k in hbm_in...  5.33 us
  transfers between devices with their start and end apart: 5, of which 5 were waited for; matrix products, arithmetic and copies ran while one was open for 0% of the time, Pallas kernels for 0%

profile of v2, /device:TPU:0, one launch (start us, length us, event | category | flops | bytes accessed | tf_op | source)
XLA Modules:
  0.0 26.9 jit_solution(12691726709149352358)
XLA Ops:
  0.6 3.1 %shard_map.75 = (f32[3,32,256]{2,1,0:T(8,128)S(1)}, f32[4,32,256]{2,1,0:T(8,128)S(1)}, bf16[4,288,256]{2,1,0:T(8,128)(2,1)S(1)}, bf16[4,288,32]{2,1,0:T(8,128)(2,1)S(1)}) custom-call(f32[1,1,32,256]{3,2,1,0:T(8,128)} %start_ref.1, f32[1,1,32,256]{3,2,1,0:T(8,128)} %guess_ref.1, bf16[4,32,288]{2,1,0:T(8,128)(2,1)} %w_hbm.1, f32[4,32]{1,0:T(4,128)} %bias_hbm.1), custom_call_target="tpu_custom_call" | custom-call | tf_op jit(solution)/shard_map/pallas_call | solution.py:266
  3.8 3.0 %collective-permute-start = (f32[3,32,256]{2,1,0:T(8,128)S(1)}, f32[3,32,256]{2,1,0:T(8,128)S(1)}, u32[]{:S(2)}, u32[]{:S(2)}) collective-permute-start(f32[3,32,256]{2,1,0:T(8,128)S(1)} %get-tuple-element.20.refs_0_), channel_id=1, source_target_pairs={{0,4},{4,0},{8,12},{12,8},{16,20},{20,16},{24,28},{28,24},{1,5},{5... | collective-permute-start | bytes 294920 | tf_op jit(solution)/shard_map/ppermute | solution.py:286
  6.8 2.8 %collective-permute-done.refs_1_ = f32[3,32,256]{2,1,0:T(8,128)S(1)} collective-permute-done((f32[3,32,256]{2,1,0:T(8,128)S(1)}, f32[3,32,256]{2,1,0:T(8,128)S(1)}, u32[]{:S(2)}, u32[]{:S(2)}) %collective-permute-start) | collective-permute-done | bytes 98336 | tf_op jit(solution)/shard_map/ppermute | solution.py:286
  9.6 2.0 %collective-permute-start.1 = (f32[3,32,256]{2,1,0:T(8,128)S(1)}, f32[3,32,256]{2,1,0:T(8,128)S(1)}, u32[]{:S(2)}, u32[]{:S(2)}) collective-permute-start(f32[3,32,256]{2,1,0:T(8,128)S(1)} %get-tuple-element.21.refs_0_), channel_id=1, source_target_pairs={{0,8},{4,12},{8,0},{12,4},{16,24},{20,28},{24,16},{28,20},{1,9},{5... | collective-permute-start | bytes 294920 | tf_op jit(solution)/shard_map/ppermute | solution.py:286
  11.6 2.7 %collective-permute-done.1.refs_1_ = f32[3,32,256]{2,1,0:T(8,128)S(1)} collective-permute-done((f32[3,32,256]{2,1,0:T(8,128)S(1)}, f32[3,32,256]{2,1,0:T(8,128)S(1)}, u32[]{:S(2)}, u32[]{:S(2)}) %collective-permute-start.1) | collective-permute-done | bytes 98336 | tf_op jit(solution)/shard_map/ppermute | solution.py:286
  14.3 0.0 copy-start
  14.3 0.0 copy-start.1
  14.3 3.0 %collective-permute-start.2 = (f32[32,256]{1,0:T(8,128)S(1)}, f32[32,256]{1,0:T(8,128)S(1)}, u32[]{:S(2)}, u32[]{:S(2)}) collective-permute-start(f32[32,256]{1,0:T(8,128)S(1)} %get-tuple-element.23), channel_id=1, source_target_pairs={{0,16},{4,20},{8,24},{12,28},{16,0},{20,4},{24,8},{28,12},{1,17},{... | collective-permute-start | bytes 98312 | tf_op jit(solution)/shard_map/ppermute | solution.py:286
  17.3 1.9 %collective-permute-done.2.got_ref = f32[32,256]{1,0:T(8,128)S(1)} collective-permute-done((f32[32,256]{1,0:T(8,128)S(1)}, f32[32,256]{1,0:T(8,128)S(1)}, u32[]{:S(2)}, u32[]{:S(2)}) %collective-permute-start.2) | collective-permute-done | bytes 32800 | tf_op jit(solution)/shard_map/ppermute | solution.py:286
  19.2 0.0 copy-done
  19.2 0.0 copy-done.1
  19.2 1.5 %shard_map.78 = (f32[1,1,32,256]{3,2,1,0:T(8,128)}, f32[1,1,32,256]{3,2,1,0:T(8,128)}, f32[2,32,384]{2,1,0:T(8,128)S(1)}, f32[2,32,384]{2,1,0:T(8,128)S(1)}) custom-call(f32[32,256]{1,0:T(8,128)S(1)} %collective-permute-done.2.got_ref, f32[4,32,256]{2,1,0:T(8,128)S(1)} %get-tuple-element.24.mine_ref, f32[1,1,32,256]{3,2,1,0:T(8,128)S(1)} %copy-done.1, ...), custom_call_target="tpu_custom_call" | custom-call | tf_op jit(solution)/shard_map/pallas_call | solution.py:266
  20.7 0.1 collective-permute-start.3
  20.8 1.3 %collective-permute-done.3.got_ref = f32[2,32,384]{2,1,0:T(8,128)S(1)} collective-permute-done((f32[2,32,384]{2,1,0:T(8,128)S(1)}, f32[2,32,384]{2,1,0:T(8,128)S(1)}, u32[]{:S(2)}, u32[]{:S(2)}) %collective-permute-start.3) | collective-permute-done | bytes 98336 | tf_op jit(solution)/shard_map/ppermute | solution.py:286
  22.1 1.9 %collective-permute-start.4 = (f32[1,32,384]{2,1,0:T(8,128)S(1)}, f32[1,32,384]{2,1,0:T(8,128)S(1)}, u32[]{:S(2)}, u32[]{:S(2)}) collective-permute-start(f32[1,32,384]{2,1,0:T(8,128)S(1)} %get-tuple-element.33), channel_id=1, source_target_pairs={{0,2},{1,3},{2,0},{3,1},{4,6},{5,7},{6,4},{7,5},{8,10},{9,11},{10,... | collective-permute-start | bytes 147464 | tf_op jit(solution)/shard_map/ppermute | solution.py:286
  24.0 2.2 %collective-permute-done.4.got_ref = f32[1,32,384]{2,1,0:T(8,128)S(1)} collective-permute-done((f32[1,32,384]{2,1,0:T(8,128)S(1)}, f32[1,32,384]{2,1,0:T(8,128)S(1)}, u32[]{:S(2)}, u32[]{:S(2)}) %collective-permute-start.4) | collective-permute-done | bytes 49184 | tf_op jit(solution)/shard_map/ppermute | solution.py:286
  26.2 0.7 %shard_map.80 = (f32[4,8,288]{2,1,0:T(8,128)}, f32[4,8]{1,0:T(4,128)}) custom-call(f32[1,32,384]{2,1,0:T(8,128)S(1)} %get-tuple-element.32.mine_ref, f32[1,32,384]{2,1,0:T(8,128)S(1)} %collective-permute-done.4.got_ref), custom_call_target="tpu_custom_call" | custom-call | tf_op jit(solution)/shard_map/pallas_call | solution.py:266
  (3 shorter events, 0.1 us)
Async XLA Ops:
  3.8 5.8 %collective-permute-start = (f32[3,32,256]{2,1,0:T(8,128)S(1)}, f32[3,32,256]{2,1,0:T(8,128)S(1)}, u32[]{:S(2)}, u32[]{:S(2)}) collective-permute-start(f32[3,32,256]{2,1,0:T(8,128)S(1)} %get-tuple-element.20.refs_0_), channel_id=1, source_target_pairs={{0,4},{4,0},{8,12},{12,8},{16,20},{20,16},{24,28},{28,24},{1,5},{5... | collective-permute-start | bytes 294920 | tf_op jit(solution)/shard_map/ppermute | solution.py:286
  9.6 4.7 %collective-permute-start.1 = (f32[3,32,256]{2,1,0:T(8,128)S(1)}, f32[3,32,256]{2,1,0:T(8,128)S(1)}, u32[]{:S(2)}, u32[]{:S(2)}) collective-permute-start(f32[3,32,256]{2,1,0:T(8,128)S(1)} %get-tuple-element.21.refs_0_), channel_id=1, source_target_pairs={{0,8},{4,12},{8,0},{12,4},{16,24},{20,28},{24,16},{28,20},{1,9},{5... | collective-permute-start | bytes 294920 | tf_op jit(solution)/shard_map/ppermute | solution.py:286
  14.3 4.9 %copy-start = (f32[1,1,32,256]{3,2,1,0:T(8,128)S(1)}, f32[1,1,32,256]{3,2,1,0:T(8,128)}, u32[]{:S(2)}) copy-start(f32[1,1,32,256]{3,2,1,0:T(8,128)} %start_ref.1) | copy-start | bytes 98308
  14.3 4.9 %copy-start.1 = (f32[1,1,32,256]{3,2,1,0:T(8,128)S(1)}, f32[1,1,32,256]{3,2,1,0:T(8,128)}, u32[]{:S(2)}) copy-start(f32[1,1,32,256]{3,2,1,0:T(8,128)} %guess_ref.1) | copy-start | bytes 98308
  14.3 4.9 %collective-permute-start.2 = (f32[32,256]{1,0:T(8,128)S(1)}, f32[32,256]{1,0:T(8,128)S(1)}, u32[]{:S(2)}, u32[]{:S(2)}) collective-permute-start(f32[32,256]{1,0:T(8,128)S(1)} %get-tuple-element.23), channel_id=1, source_target_pairs={{0,16},{4,20},{8,24},{12,28},{16,0},{20,4},{24,8},{28,12},{1,17},{... | collective-permute-start | bytes 98312 | tf_op jit(solution)/shard_map/ppermute | solution.py:286
  20.7 1.4 %collective-permute-start.3 = (f32[2,32,384]{2,1,0:T(8,128)S(1)}, f32[2,32,384]{2,1,0:T(8,128)S(1)}, u32[]{:S(2)}, u32[]{:S(2)}) collective-permute-start(f32[2,32,384]{2,1,0:T(8,128)S(1)} %get-tuple-element.31), channel_id=1, source_target_pairs={{0,1},{1,0},{2,3},{3,2},{4,5},{5,4},{6,7},{7,6},{8,9},{9,8},{10,11... | collective-permute-start | bytes 294920 | tf_op jit(solution)/shard_map/ppermute | solution.py:286
  22.1 4.2 %collective-permute-start.4 = (f32[1,32,384]{2,1,0:T(8,128)S(1)}, f32[1,32,384]{2,1,0:T(8,128)S(1)}, u32[]{:S(2)}, u32[]{:S(2)}) collective-permute-start(f32[1,32,384]{2,1,0:T(8,128)S(1)} %get-tuple-element.33), channel_id=1, source_target_pairs={{0,2},{1,3},{2,0},{3,1},{4,6},{5,7},{6,4},{7,5},{8,10},{9,11},{10,... | collective-permute-start | bytes 147464 | tf_op jit(solution)/shard_map/ppermute | solution.py:286

commit v3 on v2

--- a/solution.py
+++ b/solution.py
@@ -18,47 +18,22 @@
 HBM = pl.BlockSpec(memory_space=pltpu.HBM)
 
 
-def offset_of(tap):
-    return (tap // 3 - 1) * IMG + (tap % 3 - 1)
-
-
-def inside(shape, down, right):
-    pixel = lax.broadcasted_iota(jnp.int32, shape, 1)
-    col = lax.rem(pixel, IMG)
-    ok = None
-    for test in (
-        (pixel >= IMG) if down < 0 else None,
-        (pixel < HW - IMG) if down > 0 else None,
-        (col >= 1) if right < 0 else None,
-        (col < IMG - 1) if right > 0 else None,
-    ):
-        if test is not None:
-            ok = test if ok is None else jnp.logical_and(ok, test)
-    return ok
-
-
 def taps_of(values):
+    pixel = lax.broadcasted_iota(jnp.int16, values.shape, 1)
+    col = pixel & (IMG - 1)
+    rows = {-1: pixel >= IMG, 1: pixel < HW - IMG}
+    cols = {-1: col >= 1, 1: col < IMG - 1}
     out = []
     for tap in range(TAPS):
-        by = offset_of(tap)
-        if by == 0:
-            out.append(values)
-            continue
-        ok = inside(values.shape, tap // 3 - 1, tap % 3 - 1)
-        out.append(jnp.where(ok, pltpu.roll(values, (-by) % HW, 1), 0.0))
-    return out
-
-
-def spread(rows, chans):
-    total = None
-    for tap in range(TAPS):
-        by = offset_of(tap)
-        part = rows[tap * chans : (tap + 1) * chans]
-        if by != 0:
-            ok = inside(part.shape, 1 - tap // 3, 1 - tap % 3)
-            part = jnp.where(ok, pltpu.roll(part, by % HW, 1), 0.0)
-        total = part if total is None else total + part
-    return total
+        down, right = tap // 3 - 1, tap % 3 - 1
+        part = values
+        if down or right:
+            part = pltpu.roll(values, -(down * IMG + right) % HW, 1)
+            tests = [rows[down]] if down else []
+            tests += [cols[right]] if right else []
+            part = jnp.where(functools.reduce(jnp.logical_and, tests), part, jnp.zeros_like(part))
+        out.append(part)
+    return jnp.concatenate(out, axis=0)
 
 
 def permutation(chans):
@@ -80,7 +55,7 @@
     bias_hbm,
     sent_ref,
     slope_ref,
-    patch_ref,
+    rounded_ref,
     back_w_ref,
     state_ref,
     adj_ref,
@@ -120,11 +95,13 @@
             keepdims=True,
         )
         by_tap = dot(weight, perm, ((1,), (0,))).astype(jnp.bfloat16)
-        back_w_ref[n] = dot(perm, weight, ((0,), (1,))).astype(jnp.bfloat16)
-        rounded = state.astype(jnp.bfloat16).astype(jnp.float32)
-        patch = jnp.concatenate([t.astype(jnp.bfloat16) for t in taps_of(rounded)], axis=0)
-        patch_ref[n] = dot(perm, patch, ((1,), (0,))).astype(jnp.bfloat16)
-        squash = jnp.tanh(dot(by_tap, patch, ((1,), (0,))) + bias)
+        turned = dot(perm, weight, ((0,), (1,))).astype(jnp.bfloat16)
+        back_w_ref[n] = jnp.concatenate(
+            [turned[t * chans : (t + 1) * chans] for t in reversed(range(TAPS))], axis=1
+        )
+        rounded = state.astype(jnp.bfloat16)
+        rounded_ref[n] = rounded
+        squash = jnp.tanh(dot(by_tap, taps_of(rounded), ((1,), (0,))) + bias)
         slope = STEP * (1.0 - squash * squash)
         factor = 1.0 + slope * kc
         gain = factor if gain is None else gain * factor
@@ -134,13 +111,20 @@
     back = guess
     for n in reversed(range(depth)):
         dzb = (back * slopes[n]).astype(jnp.bfloat16)
-        back = back + spread(dot(back_w_ref[n], dzb, ((1,), (0,))), chans)
+        back = back + dot(back_w_ref[n], taps_of(dzb), ((1,), (0,)))
     place = lax.axis_index("layer")
     first = jnp.where(place == 0, 0.0, start)
     last = jnp.where(place == lax.axis_size("layer") - 1, 0.0, guess)
     sent_ref[0] = gain
     sent_ref[1] = state - gain * first
     sent_ref[2] = back - gain * last
+
+
+def patch_kernel(rounded_ref, patch_ref):
+    depth, chans, _ = rounded_ref.shape
+    perm = permutation(chans)
+    for n in range(depth):
+        patch_ref[n] = dot(perm, taps_of(rounded_ref[n]), ((1,), (0,))).astype(jnp.bfloat16)
 
 
 def joined(bit, total, mine, got):
@@ -203,8 +187,7 @@
     state_ref,
     sems,
 ):
-    depth, rows, _ = back_w_ref.shape
-    chans = rows // TAPS
+    depth, chans, rows = back_w_ref.shape
     shares = 2 * keep_ref.shape[0]
     own = chans // shares
     place = lax.axis_index("layer")
@@ -235,7 +218,7 @@
             keep_ref[s, n * own : (n + 1) * own] = jnp.where(odd, odd_part, even_part)
             send_ref[s, n * own : (n + 1) * own] = jnp.where(odd, even_part, odd_part)
         if n:
-            adj = adj + spread(dot(back_w_ref[n], dzb, ((1,), (0,))), chans)
+            adj = adj + dot(back_w_ref[n], taps_of(dzb), ((1,), (0,)))
     for copy in copies:
         copy.wait()
 
@@ -270,6 +253,7 @@
         out_specs=[HBM if k in hbm_out else VMEM for k in range(len(out_shape))],
         scratch_shapes=list(scratch),
         compiler_params=pltpu.CompilerParams(vmem_limit_bytes=LIMIT),
+        cost_estimate=pl.CostEstimate(flops=2**28, bytes_accessed=2**20, transcendentals=0),
     )(*(pltpu.with_memory_space_constraint(a, pltpu.HBM) if k in hbm_in else a for k, a in enumerate(args)))
 
 
@@ -291,18 +275,19 @@
     shares = lax.axis_size("dp")
     steps = lax.axis_size("layer").bit_length() - 1
     args = (state_guess, adjoint_guess, conv_weight, conv_bias)
-    total, slope, patch, back_w = call(
+    total, slope, rounded, back_w = call(
         relax_kernel,
         (
             f32(3, chans, HW),
             f32(depth, chans, HW),
-            bf16(depth, width, HW),
-            bf16(depth, width, chans),
+            bf16(depth, chans, HW),
+            bf16(depth, chans, width),
         ),
         args,
         hbm_in=range(4),
         scratch=[pltpu.VMEM(a.shape, a.dtype) for a in args] + [pltpu.SemaphoreType.DMA((4,))],
     )
+    (patch,) = call(patch_kernel, (bf16(depth, width, HW),), (rounded,))
     mine = ()
     for step in range(1, steps):
         got = exchange(total, "layer", step - 1)

time: 27 us -> 26.7 us (0.989)
  waiting for transfers between devices: 10.9 us -> 10.3 us
  Pallas kernels: 5.33 us -> 5.61 us
    ppermute x5, waiting for transfers between devices: 10.9 us -> 10.3 us  [exchange(): return lax.ppermute(x, axis, pairs)]
    pallas_call x6 -> x7, Pallas kernels: 5.33 us -> 5.61 us  [call(): pl.pallas_call(kernel, out_shape=out_shape, in_specs=[HBM if k in hbm_in...]
  transfers between devices with their start and end apart: 5 -> 5, of which waited for: 5 -> 5; matrix products, arithmetic and copies ran while one was open for 0% -> 0% of each run, Pallas kernels for 0% -> 2%
where the time goes in v3:
time: 26.7 us; the launch traced here: 26.6 us
  waiting for transfers between devices  10.3 us (39%)
  starting transfers between devices  9.94 us (37%)
  Pallas kernels  5.61 us (21%)
  between operations  0.68 us (3%)
    ppermute x5, waiting for transfers between devices, exchange(): return lax.ppermute(x, axis, pairs)  10.3 us
    ppermute x5, starting transfers between devices, exchange(): return lax.ppermute(x, axis, pairs)  9.94 us
    pallas_call x7, Pallas kernels, call(): pl.pallas_call(kernel, out_shape=out_shape, in_specs=[HBM if k in hbm_in...  5.61 us
  transfers between devices with their start and end apart: 5, of which 5 were waited for; matrix products, arithmetic and copies ran while one was open for 0% of the time, Pallas kernels for 2%

profile of v3, /device:TPU:0, one launch (start us, length us, event | category | flops | bytes accessed | tf_op | source)
XLA Modules:
  0.0 26.6 jit_solution(16151476743998918329)
XLA Ops:
  0.6 2.9 %shard_map.75 = (f32[3,32,256]{2,1,0:T(8,128)S(1)}, f32[4,32,256]{2,1,0:T(8,128)S(1)}, bf16[4,32,256]{2,1,0:T(8,128)(2,1)S(1)}, bf16[4,32,288]{2,1,0:T(8,128)(2,1)S(1)}) custom-call(f32[1,1,32,256]{3,2,1,0:T(8,128)} %start_ref.1, f32[1,1,32,256]{3,2,1,0:T(8,128)} %guess_ref.1, bf16[4,32,288]{2,1,0:T(8,128)(2,1)} %w_hbm.1, f32[4,32]{1,0:T(4,128)} %bias_hbm.1), custom_call_target="tpu_custom_call" | custom-call | flops 268435456 | bytes 1048576 | tf_op jit(solution)/shard_map/pallas_call | solution.py:249
  3.6 3.0 %collective-permute-start = (f32[3,32,256]{2,1,0:T(8,128)S(1)}, f32[3,32,256]{2,1,0:T(8,128)S(1)}, u32[]{:S(2)}, u32[]{:S(2)}) collective-permute-start(f32[3,32,256]{2,1,0:T(8,128)S(1)} %get-tuple-element.20.refs_0_), channel_id=1, source_target_pairs={{0,4},{4,0},{8,12},{12,8},{16,20},{20,16},{24,28},{28,24},{1,5},{5... | collective-permute-start | bytes 294920 | tf_op jit(solution)/shard_map/ppermute | solution.py:270
  6.6 2.8 %collective-permute-done.refs_1_ = f32[3,32,256]{2,1,0:T(8,128)S(1)} collective-permute-done((f32[3,32,256]{2,1,0:T(8,128)S(1)}, f32[3,32,256]{2,1,0:T(8,128)S(1)}, u32[]{:S(2)}, u32[]{:S(2)}) %collective-permute-start) | collective-permute-done | bytes 98336 | tf_op jit(solution)/shard_map/ppermute | solution.py:270
  9.4 2.0 %collective-permute-start.1 = (f32[3,32,256]{2,1,0:T(8,128)S(1)}, f32[3,32,256]{2,1,0:T(8,128)S(1)}, u32[]{:S(2)}, u32[]{:S(2)}) collective-permute-start(f32[3,32,256]{2,1,0:T(8,128)S(1)} %get-tuple-element.21.refs_0_), channel_id=1, source_target_pairs={{0,8},{4,12},{8,0},{12,4},{16,24},{20,28},{24,16},{28,20},{1,9},{5... | collective-permute-start | bytes 294920 | tf_op jit(solution)/shard_map/ppermute | solution.py:270
  11.4 2.7 %collective-permute-done.1.refs_1_ = f32[3,32,256]{2,1,0:T(8,128)S(1)} collective-permute-done((f32[3,32,256]{2,1,0:T(8,128)S(1)}, f32[3,32,256]{2,1,0:T(8,128)S(1)}, u32[]{:S(2)}, u32[]{:S(2)}) %collective-permute-start.1) | collective-permute-done | bytes 98336 | tf_op jit(solution)/shard_map/ppermute | solution.py:270
  14.1 3.0 %collective-permute-start.2 = (f32[32,256]{1,0:T(8,128)S(1)}, f32[32,256]{1,0:T(8,128)S(1)}, u32[]{:S(2)}, u32[]{:S(2)}) collective-permute-start(f32[32,256]{1,0:T(8,128)S(1)} %get-tuple-element.23), channel_id=1, source_target_pairs={{0,16},{4,20},{8,24},{12,28},{16,0},{20,4},{24,8},{28,12},{1,17},{... | collective-permute-start | bytes 98312 | tf_op jit(solution)/shard_map/ppermute | solution.py:270
  17.1 0.0 copy-start
  17.1 0.0 copy-start.1
  17.1 0.6 %shard_map.78.patch_ref = bf16[4,288,256]{2,1,0:T(8,128)(2,1)S(1)} custom-call(bf16[4,32,256]{2,1,0:T(8,128)(2,1)S(1)} %get-tuple-element.26.rounded_ref), custom_call_target="tpu_custom_call" | custom-call | flops 268435456 | bytes 1048576 | tf_op jit(solution)/shard_map/pallas_call | solution.py:249
  17.7 1.3 %collective-permute-done.2.got_ref = f32[32,256]{1,0:T(8,128)S(1)} collective-permute-done((f32[32,256]{1,0:T(8,128)S(1)}, f32[32,256]{1,0:T(8,128)S(1)}, u32[]{:S(2)}, u32[]{:S(2)}) %collective-permute-start.2) | collective-permute-done | bytes 32800 | tf_op jit(solution)/shard_map/ppermute | solution.py:270
  19.0 0.0 copy-done
  19.0 0.0 copy-done.1
  19.0 1.4 %shard_map.79 = (f32[1,1,32,256]{3,2,1,0:T(8,128)}, f32[1,1,32,256]{3,2,1,0:T(8,128)}, f32[2,32,384]{2,1,0:T(8,128)S(1)}, f32[2,32,384]{2,1,0:T(8,128)S(1)}) custom-call(f32[32,256]{1,0:T(8,128)S(1)} %collective-permute-done.2.got_ref, f32[4,32,256]{2,1,0:T(8,128)S(1)} %get-tuple-element.24.mine_ref, f32[1,1,32,256]{3,2,1,0:T(8,128)S(1)} %copy-done.1, ...), custom_call_target="tpu_custom_call" | custom-call | flops 268435456 | bytes 1048576 | tf_op jit(solution)/shard_map/pallas_call | solution.py:249
  20.4 0.1 collective-permute-start.3
  20.5 1.3 %collective-permute-done.3.got_ref = f32[2,32,384]{2,1,0:T(8,128)S(1)} collective-permute-done((f32[2,32,384]{2,1,0:T(8,128)S(1)}, f32[2,32,384]{2,1,0:T(8,128)S(1)}, u32[]{:S(2)}, u32[]{:S(2)}) %collective-permute-start.3) | collective-permute-done | bytes 98336 | tf_op jit(solution)/shard_map/ppermute | solution.py:270
  21.8 1.9 %collective-permute-start.4 = (f32[1,32,384]{2,1,0:T(8,128)S(1)}, f32[1,32,384]{2,1,0:T(8,128)S(1)}, u32[]{:S(2)}, u32[]{:S(2)}) collective-permute-start(f32[1,32,384]{2,1,0:T(8,128)S(1)} %get-tuple-element.33), channel_id=1, source_target_pairs={{0,2},{1,3},{2,0},{3,1},{4,6},{5,7},{6,4},{7,5},{8,10},{9,11},{10,... | collective-permute-start | bytes 147464 | tf_op jit(solution)/shard_map/ppermute | solution.py:270
  23.7 2.2 %collective-permute-done.4.got_ref = f32[1,32,384]{2,1,0:T(8,128)S(1)} collective-permute-done((f32[1,32,384]{2,1,0:T(8,128)S(1)}, f32[1,32,384]{2,1,0:T(8,128)S(1)}, u32[]{:S(2)}, u32[]{:S(2)}) %collective-permute-start.4) | collective-permute-done | bytes 49184 | tf_op jit(solution)/shard_map/ppermute | solution.py:270
  25.9 0.7 %shard_map.81 = (f32[4,8,288]{2,1,0:T(8,128)}, f32[4,8]{1,0:T(4,128)}) custom-call(f32[1,32,384]{2,1,0:T(8,128)S(1)} %get-tuple-element.32.mine_ref, f32[1,32,384]{2,1,0:T(8,128)S(1)} %collective-permute-done.4.got_ref), custom_call_target="tpu_custom_call" | custom-call | flops 268435456 | bytes 1048576 | tf_op jit(solution)/shard_map/pallas_call | solution.py:249
  (3 shorter events, 0.1 us)
Async XLA Ops:
  3.6 5.8 %collective-permute-start = (f32[3,32,256]{2,1,0:T(8,128)S(1)}, f32[3,32,256]{2,1,0:T(8,128)S(1)}, u32[]{:S(2)}, u32[]{:S(2)}) collective-permute-start(f32[3,32,256]{2,1,0:T(8,128)S(1)} %get-tuple-element.20.refs_0_), channel_id=1, source_target_pairs={{0,4},{4,0},{8,12},{12,8},{16,20},{20,16},{24,28},{28,24},{1,5},{5... | collective-permute-start | bytes 294920 | tf_op jit(solution)/shard_map/ppermute | solution.py:270
  9.4 4.7 %collective-permute-start.1 = (f32[3,32,256]{2,1,0:T(8,128)S(1)}, f32[3,32,256]{2,1,0:T(8,128)S(1)}, u32[]{:S(2)}, u32[]{:S(2)}) collective-permute-start(f32[3,32,256]{2,1,0:T(8,128)S(1)} %get-tuple-element.21.refs_0_), channel_id=1, source_target_pairs={{0,8},{4,12},{8,0},{12,4},{16,24},{20,28},{24,16},{28,20},{1,9},{5... | collective-permute-start | bytes 294920 | tf_op jit(solution)/shard_map/ppermute | solution.py:270
  14.1 4.9 %collective-permute-start.2 = (f32[32,256]{1,0:T(8,128)S(1)}, f32[32,256]{1,0:T(8,128)S(1)}, u32[]{:S(2)}, u32[]{:S(2)}) collective-permute-start(f32[32,256]{1,0:T(8,128)S(1)} %get-tuple-element.23), channel_id=1, source_target_pairs={{0,16},{4,20},{8,24},{12,28},{16,0},{20,4},{24,8},{28,12},{1,17},{... | collective-permute-start | bytes 98312 | tf_op jit(solution)/shard_map/ppermute | solution.py:270
  17.1 1.9 %copy-start = (f32[1,1,32,256]{3,2,1,0:T(8,128)S(1)}, f32[1,1,32,256]{3,2,1,0:T(8,128)}, u32[]{:S(2)}) copy-start(f32[1,1,32,256]{3,2,1,0:T(8,128)} %start_ref.1) | copy-start | bytes 98308
  17.1 1.9 %copy-start.1 = (f32[1,1,32,256]{3,2,1,0:T(8,128)S(1)}, f32[1,1,32,256]{3,2,1,0:T(8,128)}, u32[]{:S(2)}) copy-start(f32[1,1,32,256]{3,2,1,0:T(8,128)} %guess_ref.1) | copy-start | bytes 98308
  20.4 1.4 %collective-permute-start.3 = (f32[2,32,384]{2,1,0:T(8,128)S(1)}, f32[2,32,384]{2,1,0:T(8,128)S(1)}, u32[]{:S(2)}, u32[]{:S(2)}) collective-permute-start(f32[2,32,384]{2,1,0:T(8,128)S(1)} %get-tuple-element.31), channel_id=1, source_target_pairs={{0,1},{1,0},{2,3},{3,2},{4,5},{5,4},{6,7},{7,6},{8,9},{9,8},{10,11... | collective-permute-start | bytes 294920 | tf_op jit(solution)/shard_map/ppermute | solution.py:270
  21.8 4.2 %collective-permute-start.4 = (f32[1,32,384]{2,1,0:T(8,128)S(1)}, f32[1,32,384]{2,1,0:T(8,128)S(1)}, u32[]{:S(2)}, u32[]{:S(2)}) collective-permute-start(f32[1,32,384]{2,1,0:T(8,128)S(1)} %get-tuple-element.33), channel_id=1, source_target_pairs={{0,2},{1,3},{2,0},{3,1},{4,6},{5,7},{6,4},{7,5},{8,10},{9,11},{10,... | collective-permute-start | bytes 147464 | tf_op jit(solution)/shard_map/ppermute | solution.py:270

commit v4 on v3

--- a/solution.py
+++ b/solution.py
@@ -18,7 +18,7 @@
 HBM = pl.BlockSpec(memory_space=pltpu.HBM)
 
 
-def taps_of(values):
+def shifts(values):
     pixel = lax.broadcasted_iota(jnp.int16, values.shape, 1)
     col = pixel & (IMG - 1)
     rows = {-1: pixel >= IMG, 1: pixel < HW - IMG}
@@ -26,26 +26,39 @@
     out = []
     for tap in range(TAPS):
         down, right = tap // 3 - 1, tap % 3 - 1
-        part = values
-        if down or right:
-            part = pltpu.roll(values, -(down * IMG + right) % HW, 1)
-            tests = [rows[down]] if down else []
-            tests += [cols[right]] if right else []
-            part = jnp.where(functools.reduce(jnp.logical_and, tests), part, jnp.zeros_like(part))
+        if not down and not right:
+            continue
+        part = pltpu.roll(values, -(down * IMG + right) % HW, 1)
+        tests = [rows[down]] if down else []
+        tests += [cols[right]] if right else []
+        part = jnp.where(functools.reduce(jnp.logical_and, tests), part, jnp.zeros_like(part))
         out.append(part)
-    return jnp.concatenate(out, axis=0)
+    return out
 
 
 def permutation(chans):
     size = TAPS * chans
-    src = lax.broadcasted_iota(jnp.int32, (size, size), 0)
-    dst = lax.broadcasted_iota(jnp.int32, (size, size), 1)
-    tap = lax.div(dst, chans)
-    return jnp.where(src == (dst - tap * chans) * TAPS + tap, 1.0, 0.0).astype(jnp.bfloat16)
+    row = lax.broadcasted_iota(jnp.int32, (size, size), 0)
+    column = lax.broadcasted_iota(jnp.int32, (size, size), 1)
+    block = lax.div(row, chans)
+    chan = row - block * chans
+    tap = jnp.where(block == TAPS - 1, TAPS // 2, block + jnp.where(block >= TAPS // 2, 1, 0))
+    return jnp.where(column == chan * TAPS + tap, 1.0, 0.0).astype(jnp.bfloat16)
 
 
 def dot(a, b, dims):
     return lax.dot_general(a, b, (dims, ((), ())), preferred_element_type=jnp.float32)
+
+
+def convolve(weight, values):
+    chans = values.shape[0]
+    half = (TAPS // 2) * chans
+    near = shifts(values)
+    return (
+        dot(weight[:, 2 * half :], values, ((1,), (0,)))
+        + dot(weight[:, :half], jnp.concatenate(near[: TAPS // 2], axis=0), ((1,), (0,)))
+        + dot(weight[:, half : 2 * half], jnp.concatenate(near[TAPS // 2 :], axis=0), ((1,), (0,)))
+    )
 
 
 def relax_kernel(
@@ -83,25 +96,31 @@
     eye = lax.broadcasted_iota(jnp.int32, (chans, chans), 0) == lax.broadcasted_iota(
         jnp.int32, (chans, chans), 1
     )
+    weights = w_ref[...].reshape(depth * chans, width)
+    by_tap = dot(weights, perm, ((1,), (1,))).astype(jnp.bfloat16)
+    turned = dot(perm, weights, ((1,), (1,))).astype(jnp.bfloat16)
     state = start
     gain = None
     slopes = []
+    backs = []
     for n in range(depth):
-        weight = w_ref[n]
-        kc = jnp.sum(jnp.where(center, weight.astype(jnp.float32), 0.0), axis=1, keepdims=True)
+        mine = slice(n * chans, (n + 1) * chans)
+        kc = jnp.sum(
+            jnp.where(center, w_ref[n].astype(jnp.float32), 0.0), axis=1, keepdims=True
+        )
         bias = jnp.sum(
             jnp.where(eye, jnp.broadcast_to(bias_ref[n : n + 1, :], (chans, chans)), 0.0),
             axis=1,
             keepdims=True,
         )
-        by_tap = dot(weight, perm, ((1,), (0,))).astype(jnp.bfloat16)
-        turned = dot(perm, weight, ((0,), (1,))).astype(jnp.bfloat16)
-        back_w_ref[n] = jnp.concatenate(
-            [turned[t * chans : (t + 1) * chans] for t in reversed(range(TAPS))], axis=1
-        )
+        order = list(reversed(range(TAPS - 1))) + [TAPS - 1]
+        backs.append(
+            jnp.concatenate([turned[t * chans : (t + 1) * chans, mine] for t in order], axis=1)
+        )
+        back_w_ref[n] = backs[n]
         rounded = state.astype(jnp.bfloat16)
         rounded_ref[n] = rounded
-        squash = jnp.tanh(dot(by_tap, taps_of(rounded), ((1,), (0,))) + bias)
+        squash = jnp.tanh(convolve(by_tap[mine], rounded) + bias)
         slope = STEP * (1.0 - squash * squash)
         factor = 1.0 + slope * kc
         gain = factor if gain is None else gain * factor
@@ -111,7 +130,7 @@
     back = guess
     for n in reversed(range(depth)):
         dzb = (back * slopes[n]).astype(jnp.bfloat16)
-        back = back + dot(back_w_ref[n], taps_of(dzb), ((1,), (0,)))
+        back = back + convolve(backs[n], dzb)
     place = lax.axis_index("layer")
     first = jnp.where(place == 0, 0.0, start)
     last = jnp.where(place == lax.axis_size("layer") - 1, 0.0, guess)
@@ -124,7 +143,9 @@
     depth, chans, _ = rounded_ref.shape
     perm = permutation(chans)
     for n in range(depth):
-        patch_ref[n] = dot(perm, taps_of(rounded_ref[n]), ((1,), (0,))).astype(jnp.bfloat16)
+        rounded = rounded_ref[n]
+        patch = jnp.concatenate(shifts(rounded) + [rounded], axis=0)
+        patch_ref[n] = dot(perm, patch, ((0,), (0,))).astype(jnp.bfloat16)
 
 
 def joined(bit, total, mine, got):
@@ -205,36 +226,33 @@
     for copy in copies:
         copy.start()
     pad = keep_ref.shape[2] - rows
-    odd = bit_of("dp", 0)
+    odd, high = bit_of("dp", 0), bit_of("dp", 1)
     for n in reversed(range(depth)):
         dz = adj * slope_ref[n]
         dzb = dz.astype(jnp.bfloat16)
         grad = dot(dzb, patch_ref[n], ((1,), (1,)))
         bias = jnp.broadcast_to(jnp.sum(dz, axis=1, keepdims=True), (chans, pad))
         both = jnp.concatenate([grad, bias], axis=1)
-        for s in range(shares // 2):
-            even_part = both[2 * s * own : (2 * s + 1) * own]
-            odd_part = both[(2 * s + 1) * own : (2 * s + 2) * own]
-            keep_ref[s, n * own : (n + 1) * own] = jnp.where(odd, odd_part, even_part)
-            send_ref[s, n * own : (n + 1) * own] = jnp.where(odd, even_part, odd_part)
+        parts = [both[s * own : (s + 1) * own] for s in range(shares)]
+        parts = [jnp.where(odd, parts[i ^ 1], parts[i]) for i in range(shares)]
+        parts = [jnp.where(high, parts[i ^ 2], parts[i]) for i in range(shares)]
+        where = slice(n * own, (n + 1) * own)
+        keep_ref[0, where], keep_ref[1, where] = parts[0], parts[3]
+        send_ref[0, where], send_ref[1, where] = parts[1], parts[2]
         if n:
-            adj = adj + dot(back_w_ref[n], taps_of(dzb), ((1,), (0,)))
+            adj = adj + convolve(back_w_ref[n], dzb)
     for copy in copies:
         copy.wait()
 
 
-def halve_kernel(step, mine_ref, got_ref, keep_ref, send_ref):
-    odd = bit_of("dp", step)
-    for s in range(keep_ref.shape[0]):
-        even_part = mine_ref[2 * s] + got_ref[2 * s]
-        odd_part = mine_ref[2 * s + 1] + got_ref[2 * s + 1]
-        keep_ref[s] = jnp.where(odd, odd_part, even_part)
-        send_ref[s] = jnp.where(odd, even_part, odd_part)
+def halve_kernel(mine_ref, got_ref, keep_ref, send_ref):
+    keep_ref[...] = mine_ref[0] + got_ref[0]
+    send_ref[...] = mine_ref[1] + got_ref[1]
 
 
 def total_kernel(mine_ref, got_ref, grad_ref, bias_ref):
     depth, own, width = grad_ref.shape
-    total = mine_ref[0] + got_ref[0]
+    total = mine_ref[...] + got_ref[...]
     eye = lax.broadcasted_iota(jnp.int32, (own, own), 0) == lax.broadcasted_iota(
         jnp.int32, (own, own), 1
     )
@@ -265,9 +283,8 @@
     return jax.ShapeDtypeStruct(shape, jnp.bfloat16)
 
 
-def exchange(x, axis, step):
-    pairs = [(i, i ^ (1 << step)) for i in range(lax.axis_size(axis))]
-    return lax.ppermute(x, axis, pairs)
+def exchange(x, axis, mask):
+    return lax.ppermute(x, axis, [(i, i ^ mask) for i in range(lax.axis_size(axis))])
 
 
 def local(state_guess, adjoint_guess, conv_weight, conv_bias):
@@ -290,14 +307,14 @@
     (patch,) = call(patch_kernel, (bf16(depth, width, HW),), (rounded,))
     mine = ()
     for step in range(1, steps):
-        got = exchange(total, "layer", step - 1)
+        got = exchange(total, "layer", 1 << (step - 1))
         final = step == steps - 1
         total, *mine = call(
             functools.partial(join_kernel, step, final),
             (f32(chans, HW) if final else f32(3, chans, HW), f32(4, chans, HW)),
             (total, got, *mine),
         )
-    got = exchange(total, "layer", steps - 1)
+    got = exchange(total, "layer", 1 << (steps - 1))
     lanes = -(-(width + 1) // HALF) * HALF
     part = (depth * chans // shares, lanes)
     guess = pltpu.VMEM(adjoint_guess.shape, jnp.float32)
@@ -313,20 +330,11 @@
         hbm_out=(0, 1),
         scratch=[guess, guess, pltpu.SemaphoreType.DMA((2,))],
     )
-    left = shares // 2
-    step = 0
-    while left > 1:
-        left //= 2
-        step += 1
-        keep, send = call(
-            functools.partial(halve_kernel, step),
-            (f32(left, *part), f32(left, *part)),
-            (keep, exchange(send, "dp", step - 1)),
-        )
+    keep, send = call(halve_kernel, (f32(*part), f32(*part)), (keep, exchange(send, "dp", 1)))
     weight_grad, bias_grad = call(
         total_kernel,
         (f32(depth, chans // shares, width), f32(depth, chans // shares)),
-        (keep, exchange(send, "dp", step)),
+        (keep, exchange(send, "dp", 3)),
     )
     return (state_fixed, adjoint_fixed, weight_grad, bias_grad)
 

time: 26.7 us -> 26.4 us (0.989)
  no operation moved by 1% of the time
where the time goes in v4:
time: 26.4 us; the launch traced here: 26.2 us
  waiting for transfers between devices  10.2 us (39%)
  starting transfers between devices  9.7 us (37%)
  Pallas kernels  5.67 us (21%)
  between operations  0.68 us (3%)
    ppermute x5, waiting for transfers between devices, exchange(): lax.ppermute(x, axis, [(i, i ^ mask) for i in range(lax.axis_size(axis))])  10.2 us
    ppermute x5, starting transfers between devices, exchange(): lax.ppermute(x, axis, [(i, i ^ mask) for i in range(lax.axis_size(axis))])  9.7 us
    pallas_call x7, Pallas kernels, call(): pl.pallas_call(kernel, out_shape=out_shape, in_specs=[HBM if k in hbm_in...  5.67 us
  transfers between devices with their start and end apart: 5, of which 5 were waited for; matrix products, arithmetic and copies ran while one was open for 0% of the time, Pallas kernels for 2%

profile of v4, /device:TPU:0, one launch (start us, length us, event | category | flops | bytes accessed | tf_op | source)
XLA Modules:
  0.0 26.2 jit_solution(6811435316207552367)
XLA Ops:
  0.6 3.0 %shard_map.75 = (f32[3,32,256]{2,1,0:T(8,128)S(1)}, f32[4,32,256]{2,1,0:T(8,128)S(1)}, bf16[4,32,256]{2,1,0:T(8,128)(2,1)S(1)}, bf16[4,32,288]{2,1,0:T(8,128)(2,1)S(1)}) custom-call(f32[1,1,32,256]{3,2,1,0:T(8,128)} %start_ref.1, f32[1,1,32,256]{3,2,1,0:T(8,128)} %guess_ref.1, bf16[4,32,288]{2,1,0:T(8,128)(2,1)} %w_hbm.1, f32[4,32]{1,0:T(4,128)} %bias_hbm.1), custom_call_target="tpu_custom_call" | custom-call | flops 268435456 | bytes 1048576 | tf_op jit(solution)/shard_map/pallas_call | solution.py:267
  3.6 3.0 %collective-permute-start = (f32[3,32,256]{2,1,0:T(8,128)S(1)}, f32[3,32,256]{2,1,0:T(8,128)S(1)}, u32[]{:S(2)}, u32[]{:S(2)}) collective-permute-start(f32[3,32,256]{2,1,0:T(8,128)S(1)} %get-tuple-element.20.refs_0_), channel_id=1, source_target_pairs={{0,4},{4,0},{8,12},{12,8},{16,20},{20,16},{24,28},{28,24},{1,5},{5... | collective-permute-start | bytes 294920 | tf_op jit(solution)/shard_map/ppermute | solution.py:287
  6.6 2.8 %collective-permute-done.refs_1_ = f32[3,32,256]{2,1,0:T(8,128)S(1)} collective-permute-done((f32[3,32,256]{2,1,0:T(8,128)S(1)}, f32[3,32,256]{2,1,0:T(8,128)S(1)}, u32[]{:S(2)}, u32[]{:S(2)}) %collective-permute-start) | collective-permute-done | bytes 98336 | tf_op jit(solution)/shard_map/ppermute | solution.py:287
  9.4 2.0 %collective-permute-start.1 = (f32[3,32,256]{2,1,0:T(8,128)S(1)}, f32[3,32,256]{2,1,0:T(8,128)S(1)}, u32[]{:S(2)}, u32[]{:S(2)}) collective-permute-start(f32[3,32,256]{2,1,0:T(8,128)S(1)} %get-tuple-element.21.refs_0_), channel_id=1, source_target_pairs={{0,8},{4,12},{8,0},{12,4},{16,24},{20,28},{24,16},{28,20},{1,9},{5... | collective-permute-start | bytes 294920 | tf_op jit(solution)/shard_map/ppermute | solution.py:287
  11.4 2.7 %collective-permute-done.1.refs_1_ = f32[3,32,256]{2,1,0:T(8,128)S(1)} collective-permute-done((f32[3,32,256]{2,1,0:T(8,128)S(1)}, f32[3,32,256]{2,1,0:T(8,128)S(1)}, u32[]{:S(2)}, u32[]{:S(2)}) %collective-permute-start.1) | collective-permute-done | bytes 98336 | tf_op jit(solution)/shard_map/ppermute | solution.py:287
  14.2 3.0 %collective-permute-start.2 = (f32[32,256]{1,0:T(8,128)S(1)}, f32[32,256]{1,0:T(8,128)S(1)}, u32[]{:S(2)}, u32[]{:S(2)}) collective-permute-start(f32[32,256]{1,0:T(8,128)S(1)} %get-tuple-element.23), channel_id=1, source_target_pairs={{0,16},{4,20},{8,24},{12,28},{16,0},{20,4},{24,8},{28,12},{1,17},{... | collective-permute-start | bytes 98312 | tf_op jit(solution)/shard_map/ppermute | solution.py:287
  17.1 0.0 copy-start
  17.1 0.0 copy-start.1
  17.1 0.6 %shard_map.78.patch_ref = bf16[4,288,256]{2,1,0:T(8,128)(2,1)S(1)} custom-call(bf16[4,32,256]{2,1,0:T(8,128)(2,1)S(1)} %get-tuple-element.26.rounded_ref), custom_call_target="tpu_custom_call" | custom-call | flops 268435456 | bytes 1048576 | tf_op jit(solution)/shard_map/pallas_call | solution.py:267
  17.7 1.3 %collective-permute-done.2.got_ref = f32[32,256]{1,0:T(8,128)S(1)} collective-permute-done((f32[32,256]{1,0:T(8,128)S(1)}, f32[32,256]{1,0:T(8,128)S(1)}, u32[]{:S(2)}, u32[]{:S(2)}) %collective-permute-start.2) | collective-permute-done | bytes 32800 | tf_op jit(solution)/shard_map/ppermute | solution.py:287
  19.0 0.0 copy-done
  19.0 0.0 copy-done.1
  19.0 1.4 %shard_map.79 = (f32[1,1,32,256]{3,2,1,0:T(8,128)}, f32[1,1,32,256]{3,2,1,0:T(8,128)}, f32[2,32,384]{2,1,0:T(8,128)S(1)}, f32[2,32,384]{2,1,0:T(8,128)S(1)}) custom-call(f32[32,256]{1,0:T(8,128)S(1)} %collective-permute-done.2.got_ref, f32[4,32,256]{2,1,0:T(8,128)S(1)} %get-tuple-element.24.mine_ref, f32[1,1,32,256]{3,2,1,0:T(8,128)S(1)} %copy-done.1, ...), custom_call_target="tpu_custom_call" | custom-call | flops 268435456 | bytes 1048576 | tf_op jit(solution)/shard_map/pallas_call | solution.py:267
  20.4 0.1 collective-permute-start.3
  20.5 1.3 %collective-permute-done.3.got_ref = f32[2,32,384]{2,1,0:T(8,128)S(1)} collective-permute-done((f32[2,32,384]{2,1,0:T(8,128)S(1)}, f32[2,32,384]{2,1,0:T(8,128)S(1)}, u32[]{:S(2)}, u32[]{:S(2)}) %collective-permute-start.3) | collective-permute-done | bytes 98336 | tf_op jit(solution)/shard_map/ppermute | solution.py:287
  21.8 1.7 %collective-permute-start.4 = (f32[32,384]{1,0:T(8,128)S(1)}, f32[32,384]{1,0:T(8,128)S(1)}, u32[]{:S(2)}, u32[]{:S(2)}) collective-permute-start(f32[32,384]{1,0:T(8,128)S(1)} %get-tuple-element.33), channel_id=1, source_target_pairs={{0,3},{1,2},{2,1},{3,0},{4,7},{5,6},{6,5},{7,4},{8,11},{9,10},{10,... | collective-permute-start | bytes 147464 | tf_op jit(solution)/shard_map/ppermute | solution.py:287
  23.5 2.1 %collective-permute-done.4.got_ref = f32[32,384]{1,0:T(8,128)S(1)} collective-permute-done((f32[32,384]{1,0:T(8,128)S(1)}, f32[32,384]{1,0:T(8,128)S(1)}, u32[]{:S(2)}, u32[]{:S(2)}) %collective-permute-start.4) | collective-permute-done | bytes 49184 | tf_op jit(solution)/shard_map/ppermute | solution.py:287
  25.6 0.7 %shard_map.81 = (f32[4,8,288]{2,1,0:T(8,128)}, f32[4,8]{1,0:T(4,128)}) custom-call(f32[32,384]{1,0:T(8,128)S(1)} %get-tuple-element.32.mine_ref, f32[32,384]{1,0:T(8,128)S(1)} %collective-permute-done.4.got_ref), custom_call_target="tpu_custom_call" | custom-call | flops 268435456 | bytes 1048576 | tf_op jit(solution)/shard_map/pallas_call | solution.py:267
  (3 shorter events, 0.1 us)
Async XLA Ops:
  3.6 5.8 %collective-permute-start = (f32[3,32,256]{2,1,0:T(8,128)S(1)}, f32[3,32,256]{2,1,0:T(8,128)S(1)}, u32[]{:S(2)}, u32[]{:S(2)}) collective-permute-start(f32[3,32,256]{2,1,0:T(8,128)S(1)} %get-tuple-element.20.refs_0_), channel_id=1, source_target_pairs={{0,4},{4,0},{8,12},{12,8},{16,20},{20,16},{24,28},{28,24},{1,5},{5... | collective-permute-start | bytes 294920 | tf_op jit(solution)/shard_map/ppermute | solution.py:287
  9.4 4.7 %collective-permute-start.1 = (f32[3,32,256]{2,1,0:T(8,128)S(1)}, f32[3,32,256]{2,1,0:T(8,128)S(1)}, u32[]{:S(2)}, u32[]{:S(2)}) collective-permute-start(f32[3,32,256]{2,1,0:T(8,128)S(1)} %get-tuple-element.21.refs_0_), channel_id=1, source_target_pairs={{0,8},{4,12},{8,0},{12,4},{16,24},{20,28},{24,16},{28,20},{1,9},{5... | collective-permute-start | bytes 294920 | tf_op jit(solution)/shard_map/ppermute | solution.py:287
  14.2 4.9 %collective-permute-start.2 = (f32[32,256]{1,0:T(8,128)S(1)}, f32[32,256]{1,0:T(8,128)S(1)}, u32[]{:S(2)}, u32[]{:S(2)}) collective-permute-start(f32[32,256]{1,0:T(8,128)S(1)} %get-tuple-element.23), channel_id=1, source_target_pairs={{0,16},{4,20},{8,24},{12,28},{16,0},{20,4},{24,8},{28,12},{1,17},{... | collective-permute-start | bytes 98312 | tf_op jit(solution)/shard_map/ppermute | solution.py:287
  17.1 1.9 %copy-start = (f32[1,1,32,256]{3,2,1,0:T(8,128)S(1)}, f32[1,1,32,256]{3,2,1,0:T(8,128)}, u32[]{:S(2)}) copy-start(f32[1,1,32,256]{3,2,1,0:T(8,128)} %start_ref.1) | copy-start | bytes 98308
  17.1 1.9 %copy-start.1 = (f32[1,1,32,256]{3,2,1,0:T(8,128)S(1)}, f32[1,1,32,256]{3,2,1,0:T(8,128)}, u32[]{:S(2)}) copy-start(f32[1,1,32,256]{3,2,1,0:T(8,128)} %guess_ref.1) | copy-start | bytes 98308
  20.4 1.4 %collective-permute-start.3 = (f32[2,32,384]{2,1,0:T(8,128)S(1)}, f32[2,32,384]{2,1,0:T(8,128)S(1)}, u32[]{:S(2)}, u32[]{:S(2)}) collective-permute-start(f32[2,32,384]{2,1,0:T(8,128)S(1)} %get-tuple-element.31), channel_id=1, source_target_pairs={{0,1},{1,0},{2,3},{3,2},{4,5},{5,4},{6,7},{7,6},{8,9},{9,8},{10,11... | collective-permute-start | bytes 294920 | tf_op jit(solution)/shard_map/ppermute | solution.py:287
  21.8 3.8 %collective-permute-start.4 = (f32[32,384]{1,0:T(8,128)S(1)}, f32[32,384]{1,0:T(8,128)S(1)}, u32[]{:S(2)}, u32[]{:S(2)}) collective-permute-start(f32[32,384]{1,0:T(8,128)S(1)} %get-tuple-element.33), channel_id=1, source_target_pairs={{0,3},{1,2},{2,1},{3,0},{4,7},{5,6},{6,5},{7,4},{8,11},{9,10},{10,... | collective-permute-start | bytes 147464 | tf_op jit(solution)/shard_map/ppermute | solution.py:287

commit v5 on v4

--- a/solution.py
+++ b/solution.py
@@ -18,32 +18,24 @@
 HBM = pl.BlockSpec(memory_space=pltpu.HBM)
 
 
-def shifts(values):
-    pixel = lax.broadcasted_iota(jnp.int16, values.shape, 1)
+def moved(values, down, right):
+    if not down and not right:
+        return values
+    kind = jnp.int16 if values.dtype == jnp.bfloat16 else jnp.int32
+    pixel = lax.broadcasted_iota(kind, values.shape, 1)
     col = pixel & (IMG - 1)
-    rows = {-1: pixel >= IMG, 1: pixel < HW - IMG}
-    cols = {-1: col >= 1, 1: col < IMG - 1}
-    out = []
-    for tap in range(TAPS):
-        down, right = tap // 3 - 1, tap % 3 - 1
-        if not down and not right:
-            continue
-        part = pltpu.roll(values, -(down * IMG + right) % HW, 1)
-        tests = [rows[down]] if down else []
-        tests += [cols[right]] if right else []
-        part = jnp.where(functools.reduce(jnp.logical_and, tests), part, jnp.zeros_like(part))
-        out.append(part)
-    return out
+    tests = {-1: [pixel >= IMG], 0: [], 1: [pixel < HW - IMG]}[down]
+    tests = tests + {-1: [col >= 1], 0: [], 1: [col < IMG - 1]}[right]
+    part = pltpu.roll(values, -(down * IMG + right) % HW, 1)
+    return jnp.where(functools.reduce(jnp.logical_and, tests), part, jnp.zeros_like(part))
 
 
 def permutation(chans):
     size = TAPS * chans
     row = lax.broadcasted_iota(jnp.int32, (size, size), 0)
     column = lax.broadcasted_iota(jnp.int32, (size, size), 1)
-    block = lax.div(row, chans)
-    chan = row - block * chans
-    tap = jnp.where(block == TAPS - 1, TAPS // 2, block + jnp.where(block >= TAPS // 2, 1, 0))
-    return jnp.where(column == chan * TAPS + tap, 1.0, 0.0).astype(jnp.bfloat16)
+    tap = lax.div(row, chans)
+    return jnp.where(column == (row - tap * chans) * TAPS + tap, 1.0, 0.0).astype(jnp.bfloat16)
 
 
 def dot(a, b, dims):
@@ -52,12 +44,12 @@
 
 def convolve(weight, values):
     chans = values.shape[0]
-    half = (TAPS // 2) * chans
-    near = shifts(values)
+    columns = jnp.concatenate([moved(values, 0, right) for right in (-1, 0, 1)], axis=0)
+    rows = dot(weight, columns, ((1,), (0,)))
     return (
-        dot(weight[:, 2 * half :], values, ((1,), (0,)))
-        + dot(weight[:, :half], jnp.concatenate(near[: TAPS // 2], axis=0), ((1,), (0,)))
-        + dot(weight[:, half : 2 * half], jnp.concatenate(near[TAPS // 2 :], axis=0), ((1,), (0,)))
+        rows[chans : 2 * chans]
+        + moved(rows[:chans], -1, 0)
+        + moved(rows[2 * chans :], 1, 0)
     )
 
 
@@ -113,14 +105,20 @@
             axis=1,
             keepdims=True,
         )
-        order = list(reversed(range(TAPS - 1))) + [TAPS - 1]
+        blocks = [turned[t * chans : (t + 1) * chans, mine] for t in reversed(range(TAPS))]
         backs.append(
-            jnp.concatenate([turned[t * chans : (t + 1) * chans, mine] for t in order], axis=1)
+            jnp.concatenate(
+                [jnp.concatenate(blocks[3 * a : 3 * a + 3], axis=1) for a in range(3)], axis=0
+            )
         )
         back_w_ref[n] = backs[n]
+        span = 3 * chans
+        ahead = jnp.concatenate(
+            [by_tap[mine, a * span : (a + 1) * span] for a in range(3)], axis=0
+        )
         rounded = state.astype(jnp.bfloat16)
         rounded_ref[n] = rounded
-        squash = jnp.tanh(convolve(by_tap[mine], rounded) + bias)
+        squash = jnp.tanh(convolve(ahead, rounded) + bias)
         slope = STEP * (1.0 - squash * squash)
         factor = 1.0 + slope * kc
         gain = factor if gain is None else gain * factor
@@ -144,7 +142,9 @@
     perm = permutation(chans)
     for n in range(depth):
         rounded = rounded_ref[n]
-        patch = jnp.concatenate(shifts(rounded) + [rounded], axis=0)
+        patch = jnp.concatenate(
+            [moved(rounded, tap // 3 - 1, tap % 3 - 1) for tap in range(TAPS)], axis=0
+        )
         patch_ref[n] = dot(perm, patch, ((0,), (0,))).astype(jnp.bfloat16)
 
 
@@ -208,7 +208,8 @@
     state_ref,
     sems,
 ):
-    depth, chans, rows = back_w_ref.shape
+    depth, rows, _ = patch_ref.shape
+    chans = rows // TAPS
     shares = 2 * keep_ref.shape[0]
     own = chans // shares
     place = lax.axis_index("layer")
@@ -298,7 +299,7 @@
             f32(3, chans, HW),
             f32(depth, chans, HW),
             bf16(depth, chans, HW),
-            bf16(depth, chans, width),
+            bf16(depth, 3 * chans, 3 * chans),
         ),
         args,
         hbm_in=range(4),

time: 26.4 us -> 27.1 us (1.027)
  Pallas kernels: 5.67 us -> 6.37 us
    pallas_call x7, Pallas kernels: 5.67 us -> 6.37 us  [call(): pl.pallas_call(kernel, out_shape=out_shape, in_specs=[HBM if k in hbm_in...]
where the time goes in v5:
time: 27.1 us; the launch traced here: 27 us
  waiting for transfers between devices  10.2 us (38%)
  starting transfers between devices  9.7 us (36%)
  Pallas kernels  6.37 us (24%)
  between operations  0.68 us (3%)
    ppermute x5, waiting for transfers between devices, exchange(): lax.ppermute(x, axis, [(i, i ^ mask) for i in range(lax.axis_size(axis))])  10.2 us
    ppermute x5, starting transfers between devices, exchange(): lax.ppermute(x, axis, [(i, i ^ mask) for i in range(lax.axis_size(axis))])  9.7 us
    pallas_call x7, Pallas kernels, call(): pl.pallas_call(kernel, out_shape=out_shape, in_specs=[HBM if k in hbm_in...  6.37 us
  transfers between devices with their start and end apart: 5, of which 5 were waited for; matrix products, arithmetic and copies ran while one was open for 0% of the time, Pallas kernels for 2%

profile of v5, /device:TPU:0, one launch (start us, length us, event | category | flops | bytes accessed | tf_op | source)
XLA Modules:
  0.0 27.0 jit_solution(4965033437281048778)
XLA Ops:
  0.6 3.5 %shard_map.75 = (f32[3,32,256]{2,1,0:T(8,128)S(1)}, f32[4,32,256]{2,1,0:T(8,128)S(1)}, bf16[4,32,256]{2,1,0:T(8,128)(2,1)S(1)}, bf16[4,96,96]{2,1,0:T(8,128)(2,1)S(1)}) custom-call(f32[1,1,32,256]{3,2,1,0:T(8,128)} %start_ref.1, f32[1,1,32,256]{3,2,1,0:T(8,128)} %guess_ref.1, bf16[4,32,288]{2,1,0:T(8,128)(2,1)} %w_hbm.1, f32[4,32]{1,0:T(4,128)} %bias_hbm.1), custom_call_target="tpu_custom_call" | custom-call | flops 268435456 | bytes 1048576 | tf_op jit(solution)/shard_map/pallas_call | solution.py:268
  4.1 3.0 %collective-permute-start = (f32[3,32,256]{2,1,0:T(8,128)S(1)}, f32[3,32,256]{2,1,0:T(8,128)S(1)}, u32[]{:S(2)}, u32[]{:S(2)}) collective-permute-start(f32[3,32,256]{2,1,0:T(8,128)S(1)} %get-tuple-element.20.refs_0_), channel_id=1, source_target_pairs={{0,4},{4,0},{8,12},{12,8},{16,20},{20,16},{24,28},{28,24},{1,5},{5... | collective-permute-start | bytes 294920 | tf_op jit(solution)/shard_map/ppermute | solution.py:288
  7.1 2.8 %collective-permute-done.refs_1_ = f32[3,32,256]{2,1,0:T(8,128)S(1)} collective-permute-done((f32[3,32,256]{2,1,0:T(8,128)S(1)}, f32[3,32,256]{2,1,0:T(8,128)S(1)}, u32[]{:S(2)}, u32[]{:S(2)}) %collective-permute-start) | collective-permute-done | bytes 98336 | tf_op jit(solution)/shard_map/ppermute | solution.py:288
  10.0 2.0 %collective-permute-start.1 = (f32[3,32,256]{2,1,0:T(8,128)S(1)}, f32[3,32,256]{2,1,0:T(8,128)S(1)}, u32[]{:S(2)}, u32[]{:S(2)}) collective-permute-start(f32[3,32,256]{2,1,0:T(8,128)S(1)} %get-tuple-element.21.refs_0_), channel_id=1, source_target_pairs={{0,8},{4,12},{8,0},{12,4},{16,24},{20,28},{24,16},{28,20},{1,9},{5... | collective-permute-start | bytes 294920 | tf_op jit(solution)/shard_map/ppermute | solution.py:288
  11.9 2.7 %collective-permute-done.1.refs_1_ = f32[3,32,256]{2,1,0:T(8,128)S(1)} collective-permute-done((f32[3,32,256]{2,1,0:T(8,128)S(1)}, f32[3,32,256]{2,1,0:T(8,128)S(1)}, u32[]{:S(2)}, u32[]{:S(2)}) %collective-permute-start.1) | collective-permute-done | bytes 98336 | tf_op jit(solution)/shard_map/ppermute | solution.py:288
  14.7 3.0 %collective-permute-start.2 = (f32[32,256]{1,0:T(8,128)S(1)}, f32[32,256]{1,0:T(8,128)S(1)}, u32[]{:S(2)}, u32[]{:S(2)}) collective-permute-start(f32[32,256]{1,0:T(8,128)S(1)} %get-tuple-element.23), channel_id=1, source_target_pairs={{0,16},{4,20},{8,24},{12,28},{16,0},{20,4},{24,8},{28,12},{1,17},{... | collective-permute-start | bytes 98312 | tf_op jit(solution)/shard_map/ppermute | solution.py:288
  17.7 0.0 copy-start
  17.7 0.0 copy-start.1
  17.7 0.6 %shard_map.78.patch_ref = bf16[4,288,256]{2,1,0:T(8,128)(2,1)S(1)} custom-call(bf16[4,32,256]{2,1,0:T(8,128)(2,1)S(1)} %get-tuple-element.26.rounded_ref), custom_call_target="tpu_custom_call" | custom-call | flops 268435456 | bytes 1048576 | tf_op jit(solution)/shard_map/pallas_call | solution.py:268
  18.3 1.3 %collective-permute-done.2.got_ref = f32[32,256]{1,0:T(8,128)S(1)} collective-permute-done((f32[32,256]{1,0:T(8,128)S(1)}, f32[32,256]{1,0:T(8,128)S(1)}, u32[]{:S(2)}, u32[]{:S(2)}) %collective-permute-start.2) | collective-permute-done | bytes 32800 | tf_op jit(solution)/shard_map/ppermute | solution.py:288
  19.6 0.0 copy-done
  19.6 0.0 copy-done.1
  19.6 1.6 %shard_map.79 = (f32[1,1,32,256]{3,2,1,0:T(8,128)}, f32[1,1,32,256]{3,2,1,0:T(8,128)}, f32[2,32,384]{2,1,0:T(8,128)S(1)}, f32[2,32,384]{2,1,0:T(8,128)S(1)}) custom-call(f32[32,256]{1,0:T(8,128)S(1)} %collective-permute-done.2.got_ref, f32[4,32,256]{2,1,0:T(8,128)S(1)} %get-tuple-element.24.mine_ref, f32[1,1,32,256]{3,2,1,0:T(8,128)S(1)} %copy-done.1, ...), custom_call_target="tpu_custom_call" | custom-call | flops 268435456 | bytes 1048576 | tf_op jit(solution)/shard_map/pallas_call | solution.py:268
  21.1 0.1 collective-permute-start.3
  21.2 1.3 %collective-permute-done.3.got_ref = f32[2,32,384]{2,1,0:T(8,128)S(1)} collective-permute-done((f32[2,32,384]{2,1,0:T(8,128)S(1)}, f32[2,32,384]{2,1,0:T(8,128)S(1)}, u32[]{:S(2)}, u32[]{:S(2)}) %collective-permute-start.3) | collective-permute-done | bytes 98336 | tf_op jit(solution)/shard_map/ppermute | solution.py:288
  22.5 1.7 %collective-permute-start.4 = (f32[32,384]{1,0:T(8,128)S(1)}, f32[32,384]{1,0:T(8,128)S(1)}, u32[]{:S(2)}, u32[]{:S(2)}) collective-permute-start(f32[32,384]{1,0:T(8,128)S(1)} %get-tuple-element.33), channel_id=1, source_target_pairs={{0,3},{1,2},{2,1},{3,0},{4,7},{5,6},{6,5},{7,4},{8,11},{9,10},{10,... | collective-permute-start | bytes 147464 | tf_op jit(solution)/shard_map/ppermute | solution.py:288
  24.2 2.1 %collective-permute-done.4.got_ref = f32[32,384]{1,0:T(8,128)S(1)} collective-permute-done((f32[32,384]{1,0:T(8,128)S(1)}, f32[32,384]{1,0:T(8,128)S(1)}, u32[]{:S(2)}, u32[]{:S(2)}) %collective-permute-start.4) | collective-permute-done | bytes 49184 | tf_op jit(solution)/shard_map/ppermute | solution.py:288
  26.3 0.7 %shard_map.81 = (f32[4,8,288]{2,1,0:T(8,128)}, f32[4,8]{1,0:T(4,128)}) custom-call(f32[32,384]{1,0:T(8,128)S(1)} %get-tuple-element.32.mine_ref, f32[32,384]{1,0:T(8,128)S(1)} %collective-permute-done.4.got_ref), custom_call_target="tpu_custom_call" | custom-call | flops 268435456 | bytes 1048576 | tf_op jit(solution)/shard_map/pallas_call | solution.py:268
  (3 shorter events, 0.1 us)
Async XLA Ops:
  4.1 5.8 %collective-permute-start = (f32[3,32,256]{2,1,0:T(8,128)S(1)}, f32[3,32,256]{2,1,0:T(8,128)S(1)}, u32[]{:S(2)}, u32[]{:S(2)}) collective-permute-start(f32[3,32,256]{2,1,0:T(8,128)S(1)} %get-tuple-element.20.refs_0_), channel_id=1, source_target_pairs={{0,4},{4,0},{8,12},{12,8},{16,20},{20,16},{24,28},{28,24},{1,5},{5... | collective-permute-start | bytes 294920 | tf_op jit(solution)/shard_map/ppermute | solution.py:288
  10.0 4.7 %collective-permute-start.1 = (f32[3,32,256]{2,1,0:T(8,128)S(1)}, f32[3,32,256]{2,1,0:T(8,128)S(1)}, u32[]{:S(2)}, u32[]{:S(2)}) collective-permute-start(f32[3,32,256]{2,1,0:T(8,128)S(1)} %get-tuple-element.21.refs_0_), channel_id=1, source_target_pairs={{0,8},{4,12},{8,0},{12,4},{16,24},{20,28},{24,16},{28,20},{1,9},{5... | collective-permute-start | bytes 294920 | tf_op jit(solution)/shard_map/ppermute | solution.py:288
  14.7 4.9 %collective-permute-start.2 = (f32[32,256]{1,0:T(8,128)S(1)}, f32[32,256]{1,0:T(8,128)S(1)}, u32[]{:S(2)}, u32[]{:S(2)}) collective-permute-start(f32[32,256]{1,0:T(8,128)S(1)} %get-tuple-element.23), channel_id=1, source_target_pairs={{0,16},{4,20},{8,24},{12,28},{16,0},{20,4},{24,8},{28,12},{1,17},{... | collective-permute-start | bytes 98312 | tf_op jit(solution)/shard_map/ppermute | solution.py:288
  17.7 1.9 %copy-start = (f32[1,1,32,256]{3,2,1,0:T(8,128)S(1)}, f32[1,1,32,256]{3,2,1,0:T(8,128)}, u32[]{:S(2)}) copy-start(f32[1,1,32,256]{3,2,1,0:T(8,128)} %start_ref.1) | copy-start | bytes 98308
  17.7 1.9 %copy-start.1 = (f32[1,1,32,256]{3,2,1,0:T(8,128)S(1)}, f32[1,1,32,256]{3,2,1,0:T(8,128)}, u32[]{:S(2)}) copy-start(f32[1,1,32,256]{3,2,1,0:T(8,128)} %guess_ref.1) | copy-start | bytes 98308
  21.1 1.4 %collective-permute-start.3 = (f32[2,32,384]{2,1,0:T(8,128)S(1)}, f32[2,32,384]{2,1,0:T(8,128)S(1)}, u32[]{:S(2)}, u32[]{:S(2)}) collective-permute-start(f32[2,32,384]{2,1,0:T(8,128)S(1)} %get-tuple-element.31), channel_id=1, source_target_pairs={{0,1},{1,0},{2,3},{3,2},{4,5},{5,4},{6,7},{7,6},{8,9},{9,8},{10,11... | collective-permute-start | bytes 294920 | tf_op jit(solution)/shard_map/ppermute | solution.py:288
  22.5 3.8 %collective-permute-start.4 = (f32[32,384]{1,0:T(8,128)S(1)}, f32[32,384]{1,0:T(8,128)S(1)}, u32[]{:S(2)}, u32[]{:S(2)}) collective-permute-start(f32[32,384]{1,0:T(8,128)S(1)} %get-tuple-element.33), channel_id=1, source_target_pairs={{0,3},{1,2},{2,1},{3,0},{4,7},{5,6},{6,5},{7,4},{8,11},{9,10},{10,... | collective-permute-start | bytes 147464 | tf_op jit(solution)/shard_map/ppermute | solution.py:288

commit v6 on v4

--- a/solution.py
+++ b/solution.py
@@ -18,7 +18,7 @@
 HBM = pl.BlockSpec(memory_space=pltpu.HBM)
 
 
-def shifts(values):
+def taps_of(values):
     pixel = lax.broadcasted_iota(jnp.int16, values.shape, 1)
     col = pixel & (IMG - 1)
     rows = {-1: pixel >= IMG, 1: pixel < HW - IMG}
@@ -26,24 +26,22 @@
     out = []
     for tap in range(TAPS):
         down, right = tap // 3 - 1, tap % 3 - 1
-        if not down and not right:
-            continue
-        part = pltpu.roll(values, -(down * IMG + right) % HW, 1)
-        tests = [rows[down]] if down else []
-        tests += [cols[right]] if right else []
-        part = jnp.where(functools.reduce(jnp.logical_and, tests), part, jnp.zeros_like(part))
+        part = values
+        if down or right:
+            part = pltpu.roll(values, -(down * IMG + right) % HW, 1)
+            tests = [rows[down]] if down else []
+            tests += [cols[right]] if right else []
+            part = jnp.where(functools.reduce(jnp.logical_and, tests), part, jnp.zeros_like(part))
         out.append(part)
-    return out
+    return jnp.concatenate(out, axis=0)
 
 
 def permutation(chans):
     size = TAPS * chans
     row = lax.broadcasted_iota(jnp.int32, (size, size), 0)
     column = lax.broadcasted_iota(jnp.int32, (size, size), 1)
-    block = lax.div(row, chans)
-    chan = row - block * chans
-    tap = jnp.where(block == TAPS - 1, TAPS // 2, block + jnp.where(block >= TAPS // 2, 1, 0))
-    return jnp.where(column == chan * TAPS + tap, 1.0, 0.0).astype(jnp.bfloat16)
+    tap = lax.div(row, chans)
+    return jnp.where(column == (row - tap * chans) * TAPS + tap, 1.0, 0.0).astype(jnp.bfloat16)
 
 
 def dot(a, b, dims):
@@ -51,14 +49,7 @@
 
 
 def convolve(weight, values):
-    chans = values.shape[0]
-    half = (TAPS // 2) * chans
-    near = shifts(values)
-    return (
-        dot(weight[:, 2 * half :], values, ((1,), (0,)))
-        + dot(weight[:, :half], jnp.concatenate(near[: TAPS // 2], axis=0), ((1,), (0,)))
-        + dot(weight[:, half : 2 * half], jnp.concatenate(near[TAPS // 2 :], axis=0), ((1,), (0,)))
-    )
+    return dot(weight, taps_of(values), ((1,), (0,)))
 
 
 def relax_kernel(
@@ -74,6 +65,9 @@
     adj_ref,
     w_ref,
     bias_ref,
+    perm_ref,
+    by_tap_ref,
+    column_ref,
     sems,
 ):
     copies = [
@@ -85,52 +79,46 @@
     for copy in copies:
         copy.start()
     depth, chans, width = w_ref.shape
-    perm = permutation(chans)
-    for copy in copies:
-        copy.wait()
-    start = state_ref[0, 0]
-    guess = adj_ref[0, 0]
+    perm_ref[...] = permutation(chans)
     row = lax.broadcasted_iota(jnp.int32, (chans, width), 0)
     lane = lax.broadcasted_iota(jnp.int32, (chans, width), 1)
     center = lane == row * TAPS + TAPS // 2
     eye = lax.broadcasted_iota(jnp.int32, (chans, chans), 0) == lax.broadcasted_iota(
         jnp.int32, (chans, chans), 1
     )
-    weights = w_ref[...].reshape(depth * chans, width)
-    by_tap = dot(weights, perm, ((1,), (1,))).astype(jnp.bfloat16)
-    turned = dot(perm, weights, ((1,), (1,))).astype(jnp.bfloat16)
-    state = start
-    gain = None
-    slopes = []
-    backs = []
+    for copy in copies:
+        copy.wait()
+    start = state_ref[0, 0]
+    guess = adj_ref[0, 0]
+    by_tap = dot(w_ref[...].reshape(depth * chans, width), perm_ref[...], ((1,), (1,)))
+    by_tap_ref[...] = by_tap.astype(jnp.bfloat16).reshape(depth, chans, width)
     for n in range(depth):
-        mine = slice(n * chans, (n + 1) * chans)
-        kc = jnp.sum(
-            jnp.where(center, w_ref[n].astype(jnp.float32), 0.0), axis=1, keepdims=True
-        )
-        bias = jnp.sum(
-            jnp.where(eye, jnp.broadcast_to(bias_ref[n : n + 1, :], (chans, chans)), 0.0),
-            axis=1,
-            keepdims=True,
-        )
-        order = list(reversed(range(TAPS - 1))) + [TAPS - 1]
-        backs.append(
-            jnp.concatenate([turned[t * chans : (t + 1) * chans, mine] for t in order], axis=1)
-        )
-        back_w_ref[n] = backs[n]
+        bias = jnp.broadcast_to(bias_ref[n : n + 1, :], (chans, chans))
+        bias = jnp.sum(jnp.where(eye, bias, 0.0), axis=1, keepdims=True)
+        column_ref[n] = jnp.broadcast_to(bias, (chans, HALF))
+
+    def ahead(n, carry):
+        state, gain = carry
+        weight = w_ref[n]
+        kc = jnp.sum(jnp.where(center, weight.astype(jnp.float32), 0.0), axis=1, keepdims=True)
         rounded = state.astype(jnp.bfloat16)
         rounded_ref[n] = rounded
-        squash = jnp.tanh(convolve(by_tap[mine], rounded) + bias)
+        squash = jnp.tanh(convolve(by_tap_ref[n], rounded) + column_ref[n][:, :1])
         slope = STEP * (1.0 - squash * squash)
-        factor = 1.0 + slope * kc
-        gain = factor if gain is None else gain * factor
-        state = state + STEP * squash
         slope_ref[n] = slope
-        slopes.append(slope)
-    back = guess
-    for n in reversed(range(depth)):
-        dzb = (back * slopes[n]).astype(jnp.bfloat16)
-        back = back + convolve(backs[n], dzb)
+        turned = dot(perm_ref[...], weight, ((1,), (1,))).astype(jnp.bfloat16)
+        back_w_ref[n] = jnp.concatenate(
+            [turned[t * chans : (t + 1) * chans] for t in reversed(range(TAPS))], axis=1
+        )
+        return state + STEP * squash, gain * (1.0 + slope * kc)
+
+    state, gain = lax.fori_loop(0, depth, ahead, (start, jnp.ones_like(start)))
+
+    def behind(i, back):
+        n = depth - 1 - i
+        return back + convolve(back_w_ref[n], (back * slope_ref[n]).astype(jnp.bfloat16))
+
+    back = lax.fori_loop(0, depth, behind, guess)
     place = lax.axis_index("layer")
     first = jnp.where(place == 0, 0.0, start)
     last = jnp.where(place == lax.axis_size("layer") - 1, 0.0, guess)
@@ -144,8 +132,7 @@
     perm = permutation(chans)
     for n in range(depth):
         rounded = rounded_ref[n]
-        patch = jnp.concatenate(shifts(rounded) + [rounded], axis=0)
-        patch_ref[n] = dot(perm, patch, ((0,), (0,))).astype(jnp.bfloat16)
+        patch_ref[n] = dot(perm, taps_of(rounded), ((0,), (0,))).astype(jnp.bfloat16)
 
 
 def joined(bit, total, mine, got):
@@ -227,7 +214,8 @@
         copy.start()
     pad = keep_ref.shape[2] - rows
     odd, high = bit_of("dp", 0), bit_of("dp", 1)
-    for n in reversed(range(depth)):
+
+    def layer(n, adj):
         dz = adj * slope_ref[n]
         dzb = dz.astype(jnp.bfloat16)
         grad = dot(dzb, patch_ref[n], ((1,), (1,)))
@@ -236,11 +224,16 @@
         parts = [both[s * own : (s + 1) * own] for s in range(shares)]
         parts = [jnp.where(odd, parts[i ^ 1], parts[i]) for i in range(shares)]
         parts = [jnp.where(high, parts[i ^ 2], parts[i]) for i in range(shares)]
-        where = slice(n * own, (n + 1) * own)
+        where = pl.ds(pl.multiple_of(n * own, own), own)
         keep_ref[0, where], keep_ref[1, where] = parts[0], parts[3]
         send_ref[0, where], send_ref[1, where] = parts[1], parts[2]
-        if n:
-            adj = adj + convolve(back_w_ref[n], dzb)
+        return dzb
+
+    def behind(i, adj):
+        n = depth - 1 - i
+        return adj + convolve(back_w_ref[n], layer(n, adj))
+
+    layer(0, lax.fori_loop(0, depth - 1, behind, adj))
     for copy in copies:
         copy.wait()
 
@@ -302,7 +295,13 @@
         ),
         args,
         hbm_in=range(4),
-        scratch=[pltpu.VMEM(a.shape, a.dtype) for a in args] + [pltpu.SemaphoreType.DMA((4,))],
+        scratch=[pltpu.VMEM(a.shape, a.dtype) for a in args]
+        + [
+            pltpu.VMEM((width, width), jnp.bfloat16),
+            pltpu.VMEM((depth, chans, width), jnp.bfloat16),
+            pltpu.VMEM((depth, chans, HALF), jnp.float32),
+            pltpu.SemaphoreType.DMA((4,)),
+        ],
     )
     (patch,) = call(patch_kernel, (bf16(depth, width, HW),), (rounded,))
     mine = ()

time: 26.4 us -> 26.5 us (level)
  no operation moved by 1% of the time
where the time goes in v6:
time: 26.5 us; the launch traced here: 26.3 us
  waiting for transfers between devices  10.2 us (38%)
  starting transfers between devices  9.7 us (37%)
  Pallas kernels  5.75 us (22%)
  between operations  0.68 us (3%)
    ppermute x5, waiting for transfers between devices, exchange(): lax.ppermute(x, axis, [(i, i ^ mask) for i in range(lax.axis_size(axis))])  10.2 us
    ppermute x5, starting transfers between devices, exchange(): lax.ppermute(x, axis, [(i, i ^ mask) for i in range(lax.axis_size(axis))])  9.7 us
    pallas_call x7, Pallas kernels, call(): pl.pallas_call(kernel, out_shape=out_shape, in_specs=[HBM if k in hbm_in...  5.75 us
  transfers between devices with their start and end apart: 5, of which 5 were waited for; matrix products, arithmetic and copies ran while one was open for 0% of the time, Pallas kernels for 2%

profile of v6, /device:TPU:0, one launch (start us, length us, event | category | flops | bytes accessed | tf_op | source)
XLA Modules:
  0.0 26.3 jit_solution(17940258980131804927)
XLA Ops:
  0.6 3.5 %shard_map.75 = (f32[3,32,256]{2,1,0:T(8,128)S(1)}, f32[4,32,256]{2,1,0:T(8,128)S(1)}, bf16[4,32,256]{2,1,0:T(8,128)(2,1)S(1)}, bf16[4,32,288]{2,1,0:T(8,128)(2,1)S(1)}) custom-call(f32[1,1,32,256]{3,2,1,0:T(8,128)} %start_ref.1, f32[1,1,32,256]{3,2,1,0:T(8,128)} %guess_ref.1, bf16[4,32,288]{2,1,0:T(8,128)(2,1)} %w_hbm.1, f32[4,32]{1,0:T(4,128)} %bias_hbm.1), custom_call_target="tpu_custom_call" | custom-call | flops 268435456 | bytes 1048576 | tf_op jit(solution)/shard_map/pallas_call | solution.py:260
  4.1 3.0 %collective-permute-start = (f32[3,32,256]{2,1,0:T(8,128)S(1)}, f32[3,32,256]{2,1,0:T(8,128)S(1)}, u32[]{:S(2)}, u32[]{:S(2)}) collective-permute-start(f32[3,32,256]{2,1,0:T(8,128)S(1)} %get-tuple-element.20.refs_0_), channel_id=1, source_target_pairs={{0,4},{4,0},{8,12},{12,8},{16,20},{20,16},{24,28},{28,24},{1,5},{5... | collective-permute-start | bytes 294920 | tf_op jit(solution)/shard_map/ppermute | solution.py:280
  7.1 2.8 %collective-permute-done.refs_1_ = f32[3,32,256]{2,1,0:T(8,128)S(1)} collective-permute-done((f32[3,32,256]{2,1,0:T(8,128)S(1)}, f32[3,32,256]{2,1,0:T(8,128)S(1)}, u32[]{:S(2)}, u32[]{:S(2)}) %collective-permute-start) | collective-permute-done | bytes 98336 | tf_op jit(solution)/shard_map/ppermute | solution.py:280
  10.0 2.0 %collective-permute-start.1 = (f32[3,32,256]{2,1,0:T(8,128)S(1)}, f32[3,32,256]{2,1,0:T(8,128)S(1)}, u32[]{:S(2)}, u32[]{:S(2)}) collective-permute-start(f32[3,32,256]{2,1,0:T(8,128)S(1)} %get-tuple-element.21.refs_0_), channel_id=1, source_target_pairs={{0,8},{4,12},{8,0},{12,4},{16,24},{20,28},{24,16},{28,20},{1,9},{5... | collective-permute-start | bytes 294920 | tf_op jit(solution)/shard_map/ppermute | solution.py:280
  11.9 2.7 %collective-permute-done.1.refs_1_ = f32[3,32,256]{2,1,0:T(8,128)S(1)} collective-permute-done((f32[3,32,256]{2,1,0:T(8,128)S(1)}, f32[3,32,256]{2,1,0:T(8,128)S(1)}, u32[]{:S(2)}, u32[]{:S(2)}) %collective-permute-start.1) | collective-permute-done | bytes 98336 | tf_op jit(solution)/shard_map/ppermute | solution.py:280
  14.7 3.0 %collective-permute-start.2 = (f32[32,256]{1,0:T(8,128)S(1)}, f32[32,256]{1,0:T(8,128)S(1)}, u32[]{:S(2)}, u32[]{:S(2)}) collective-permute-start(f32[32,256]{1,0:T(8,128)S(1)} %get-tuple-element.23), channel_id=1, source_target_pairs={{0,16},{4,20},{8,24},{12,28},{16,0},{20,4},{24,8},{28,12},{1,17},{... | collective-permute-start | bytes 98312 | tf_op jit(solution)/shard_map/ppermute | solution.py:280
  17.7 0.0 copy-start
  17.7 0.0 copy-start.1
  17.7 0.6 %shard_map.78.patch_ref = bf16[4,288,256]{2,1,0:T(8,128)(2,1)S(1)} custom-call(bf16[4,32,256]{2,1,0:T(8,128)(2,1)S(1)} %get-tuple-element.26.rounded_ref), custom_call_target="tpu_custom_call" | custom-call | flops 268435456 | bytes 1048576 | tf_op jit(solution)/shard_map/pallas_call | solution.py:260
  18.3 1.3 %collective-permute-done.2.got_ref = f32[32,256]{1,0:T(8,128)S(1)} collective-permute-done((f32[32,256]{1,0:T(8,128)S(1)}, f32[32,256]{1,0:T(8,128)S(1)}, u32[]{:S(2)}, u32[]{:S(2)}) %collective-permute-start.2) | collective-permute-done | bytes 32800 | tf_op jit(solution)/shard_map/ppermute | solution.py:280
  19.6 0.0 copy-done
  19.6 0.0 copy-done.1
  19.6 0.9 %shard_map.79 = (f32[1,1,32,256]{3,2,1,0:T(8,128)}, f32[1,1,32,256]{3,2,1,0:T(8,128)}, f32[2,32,384]{2,1,0:T(8,128)S(1)}, f32[2,32,384]{2,1,0:T(8,128)S(1)}) custom-call(f32[32,256]{1,0:T(8,128)S(1)} %collective-permute-done.2.got_ref, f32[4,32,256]{2,1,0:T(8,128)S(1)} %get-tuple-element.24.mine_ref, f32[1,1,32,256]{3,2,1,0:T(8,128)S(1)} %copy-done.1, ...), custom_call_target="tpu_custom_call" | custom-call | flops 268435456 | bytes 1048576 | tf_op jit(solution)/shard_map/pallas_call | solution.py:260
  20.5 0.1 collective-permute-start.3
  20.6 1.3 %collective-permute-done.3.got_ref = f32[2,32,384]{2,1,0:T(8,128)S(1)} collective-permute-done((f32[2,32,384]{2,1,0:T(8,128)S(1)}, f32[2,32,384]{2,1,0:T(8,128)S(1)}, u32[]{:S(2)}, u32[]{:S(2)}) %collective-permute-start.3) | collective-permute-done | bytes 98336 | tf_op jit(solution)/shard_map/ppermute | solution.py:280
  21.9 1.7 %collective-permute-start.4 = (f32[32,384]{1,0:T(8,128)S(1)}, f32[32,384]{1,0:T(8,128)S(1)}, u32[]{:S(2)}, u32[]{:S(2)}) collective-permute-start(f32[32,384]{1,0:T(8,128)S(1)} %get-tuple-element.33), channel_id=1, source_target_pairs={{0,3},{1,2},{2,1},{3,0},{4,7},{5,6},{6,5},{7,4},{8,11},{9,10},{10,... | collective-permute-start | bytes 147464 | tf_op jit(solution)/shard_map/ppermute | solution.py:280
  23.6 2.1 %collective-permute-done.4.got_ref = f32[32,384]{1,0:T(8,128)S(1)} collective-permute-done((f32[32,384]{1,0:T(8,128)S(1)}, f32[32,384]{1,0:T(8,128)S(1)}, u32[]{:S(2)}, u32[]{:S(2)}) %collective-permute-start.4) | collective-permute-done | bytes 49184 | tf_op jit(solution)/shard_map/ppermute | solution.py:280
  25.7 0.7 %shard_map.81 = (f32[4,8,288]{2,1,0:T(8,128)}, f32[4,8]{1,0:T(4,128)}) custom-call(f32[32,384]{1,0:T(8,128)S(1)} %get-tuple-element.32.mine_ref, f32[32,384]{1,0:T(8,128)S(1)} %collective-permute-done.4.got_ref), custom_call_target="tpu_custom_call" | custom-call | flops 268435456 | bytes 1048576 | tf_op jit(solution)/shard_map/pallas_call | solution.py:260
  (3 shorter events, 0.1 us)
Async XLA Ops:
  4.1 5.8 %collective-permute-start = (f32[3,32,256]{2,1,0:T(8,128)S(1)}, f32[3,32,256]{2,1,0:T(8,128)S(1)}, u32[]{:S(2)}, u32[]{:S(2)}) collective-permute-start(f32[3,32,256]{2,1,0:T(8,128)S(1)} %get-tuple-element.20.refs_0_), channel_id=1, source_target_pairs={{0,4},{4,0},{8,12},{12,8},{16,20},{20,16},{24,28},{28,24},{1,5},{5... | collective-permute-start | bytes 294920 | tf_op jit(solution)/shard_map/ppermute | solution.py:280
  10.0 4.7 %collective-permute-start.1 = (f32[3,32,256]{2,1,0:T(8,128)S(1)}, f32[3,32,256]{2,1,0:T(8,128)S(1)}, u32[]{:S(2)}, u32[]{:S(2)}) collective-permute-start(f32[3,32,256]{2,1,0:T(8,128)S(1)} %get-tuple-element.21.refs_0_), channel_id=1, source_target_pairs={{0,8},{4,12},{8,0},{12,4},{16,24},{20,28},{24,16},{28,20},{1,9},{5... | collective-permute-start | bytes 294920 | tf_op jit(solution)/shard_map/ppermute | solution.py:280
  14.7 4.9 %collective-permute-start.2 = (f32[32,256]{1,0:T(8,128)S(1)}, f32[32,256]{1,0:T(8,128)S(1)}, u32[]{:S(2)}, u32[]{:S(2)}) collective-permute-start(f32[32,256]{1,0:T(8,128)S(1)} %get-tuple-element.23), channel_id=1, source_target_pairs={{0,16},{4,20},{8,24},{12,28},{16,0},{20,4},{24,8},{28,12},{1,17},{... | collective-permute-start | bytes 98312 | tf_op jit(solution)/shard_map/ppermute | solution.py:280
  17.7 1.9 %copy-start = (f32[1,1,32,256]{3,2,1,0:T(8,128)S(1)}, f32[1,1,32,256]{3,2,1,0:T(8,128)}, u32[]{:S(2)}) copy-start(f32[1,1,32,256]{3,2,1,0:T(8,128)} %start_ref.1) | copy-start | bytes 98308
  17.7 1.9 %copy-start.1 = (f32[1,1,32,256]{3,2,1,0:T(8,128)S(1)}, f32[1,1,32,256]{3,2,1,0:T(8,128)}, u32[]{:S(2)}) copy-start(f32[1,1,32,256]{3,2,1,0:T(8,128)} %guess_ref.1) | copy-start | bytes 98308
  20.5 1.4 %collective-permute-start.3 = (f32[2,32,384]{2,1,0:T(8,128)S(1)}, f32[2,32,384]{2,1,0:T(8,128)S(1)}, u32[]{:S(2)}, u32[]{:S(2)}) collective-permute-start(f32[2,32,384]{2,1,0:T(8,128)S(1)} %get-tuple-element.31), channel_id=1, source_target_pairs={{0,1},{1,0},{2,3},{3,2},{4,5},{5,4},{6,7},{7,6},{8,9},{9,8},{10,11... | collective-permute-start | bytes 294920 | tf_op jit(solution)/shard_map/ppermute | solution.py:280
  21.9 3.8 %collective-permute-start.4 = (f32[32,384]{1,0:T(8,128)S(1)}, f32[32,384]{1,0:T(8,128)S(1)}, u32[]{:S(2)}, u32[]{:S(2)}) collective-permute-start(f32[32,384]{1,0:T(8,128)S(1)} %get-tuple-element.33), channel_id=1, source_target_pairs={{0,3},{1,2},{2,1},{3,0},{4,7},{5,6},{6,5},{7,4},{8,11},{9,10},{10,... | collective-permute-start | bytes 147464 | tf_op jit(solution)/shard_map/ppermute | solution.py:280

commit v7 on v6

--- a/solution.py
+++ b/solution.py
@@ -80,36 +80,36 @@
         copy.start()
     depth, chans, width = w_ref.shape
     perm_ref[...] = permutation(chans)
-    row = lax.broadcasted_iota(jnp.int32, (chans, width), 0)
-    lane = lax.broadcasted_iota(jnp.int32, (chans, width), 1)
-    center = lane == row * TAPS + TAPS // 2
     eye = lax.broadcasted_iota(jnp.int32, (chans, chans), 0) == lax.broadcasted_iota(
         jnp.int32, (chans, chans), 1
     )
     for copy in copies:
         copy.wait()
+    weights = w_ref[...].reshape(depth * chans, width)
+    by_tap = dot(weights, perm_ref[...], ((1,), (1,)))
+    by_tap_ref[...] = by_tap.astype(jnp.bfloat16).reshape(depth, chans, width)
+    turned = dot(perm_ref[...], weights, ((1,), (1,))).astype(jnp.bfloat16)
+    middle = TAPS // 2 * chans
+    for n in range(depth):
+        mine = slice(n * chans, (n + 1) * chans)
+        back_w_ref[n] = jnp.concatenate(
+            [turned[t * chans : (t + 1) * chans, mine] for t in reversed(range(TAPS))], axis=1
+        )
+        bias = jnp.broadcast_to(bias_ref[n : n + 1, :], (chans, chans))
+        for k, square in enumerate((bias, by_tap[mine, middle : middle + chans])):
+            column = jnp.sum(jnp.where(eye, square, 0.0), axis=1, keepdims=True)
+            column_ref[n, k] = jnp.broadcast_to(column, (chans, HALF))
     start = state_ref[0, 0]
     guess = adj_ref[0, 0]
-    by_tap = dot(w_ref[...].reshape(depth * chans, width), perm_ref[...], ((1,), (1,)))
-    by_tap_ref[...] = by_tap.astype(jnp.bfloat16).reshape(depth, chans, width)
-    for n in range(depth):
-        bias = jnp.broadcast_to(bias_ref[n : n + 1, :], (chans, chans))
-        bias = jnp.sum(jnp.where(eye, bias, 0.0), axis=1, keepdims=True)
-        column_ref[n] = jnp.broadcast_to(bias, (chans, HALF))
 
     def ahead(n, carry):
         state, gain = carry
-        weight = w_ref[n]
-        kc = jnp.sum(jnp.where(center, weight.astype(jnp.float32), 0.0), axis=1, keepdims=True)
+        bias, kc = (jnp.concatenate([column_ref[n, k]] * (HW // HALF), axis=1) for k in range(2))
         rounded = state.astype(jnp.bfloat16)
         rounded_ref[n] = rounded
-        squash = jnp.tanh(convolve(by_tap_ref[n], rounded) + column_ref[n][:, :1])
+        squash = jnp.tanh(convolve(by_tap_ref[n], rounded) + bias)
         slope = STEP * (1.0 - squash * squash)
         slope_ref[n] = slope
-        turned = dot(perm_ref[...], weight, ((1,), (1,))).astype(jnp.bfloat16)
-        back_w_ref[n] = jnp.concatenate(
-            [turned[t * chans : (t + 1) * chans] for t in reversed(range(TAPS))], axis=1
-        )
         return state + STEP * squash, gain * (1.0 + slope * kc)
 
     state, gain = lax.fori_loop(0, depth, ahead, (start, jnp.ones_like(start)))
@@ -127,12 +127,14 @@
     sent_ref[2] = back - gain * last
 
 
-def patch_kernel(rounded_ref, patch_ref):
+def patch_kernel(rounded_ref, patch_ref, perm_ref):
     depth, chans, _ = rounded_ref.shape
-    perm = permutation(chans)
-    for n in range(depth):
-        rounded = rounded_ref[n]
-        patch_ref[n] = dot(perm, taps_of(rounded), ((0,), (0,))).astype(jnp.bfloat16)
+    perm_ref[...] = permutation(chans)
+
+    @pl.loop(0, depth)
+    def _(n):
+        patch = taps_of(rounded_ref[n])
+        patch_ref[n] = dot(perm_ref[...], patch, ((0,), (0,))).astype(jnp.bfloat16)
 
 
 def joined(bit, total, mine, got):
@@ -299,11 +301,16 @@
         + [
             pltpu.VMEM((width, width), jnp.bfloat16),
             pltpu.VMEM((depth, chans, width), jnp.bfloat16),
-            pltpu.VMEM((depth, chans, HALF), jnp.float32),
+            pltpu.VMEM((depth, 2, chans, HALF), jnp.float32),
             pltpu.SemaphoreType.DMA((4,)),
         ],
     )
-    (patch,) = call(patch_kernel, (bf16(depth, width, HW),), (rounded,))
+    (patch,) = call(
+        patch_kernel,
+        (bf16(depth, width, HW),),
+        (rounded,),
+        scratch=[pltpu.VMEM((width, width), jnp.bfloat16)],
+    )
     mine = ()
     for step in range(1, steps):
         got = exchange(total, "layer", 1 << (step - 1))

time: 26.5 us -> 26.2 us (0.989)
  waiting for transfers between devices: 10.2 us -> 9.43 us
  Pallas kernels: 5.75 us -> 6.26 us
    ppermute x5, waiting for transfers between devices: 10.2 us -> 9.43 us  [exchange(): lax.ppermute(x, axis, [(i, i ^ mask) for i in range(lax.axis_size(axis))])]
    pallas_call x7, Pallas kernels: 5.75 us -> 6.26 us  [call(): pl.pallas_call(kernel, out_shape=out_shape, in_specs=[HBM if k in hbm_in...]
  transfers between devices with their start and end apart: 5 -> 5, of which waited for: 5 -> 5; matrix products, arithmetic and copies ran while one was open for 0% -> 0% of each run, Pallas kernels for 2% -> 5%
where the time goes in v7:
time: 26.2 us; the launch traced here: 26.1 us
  starting transfers between devices  9.7 us (37%)
  waiting for transfers between devices  9.43 us (36%)
  Pallas kernels  6.26 us (24%)
  between operations  0.68 us (3%)
    ppermute x5, starting transfers between devices, exchange(): lax.ppermute(x, axis, [(i, i ^ mask) for i in range(lax.axis_size(axis))])  9.7 us
    ppermute x5, waiting for transfers between devices, exchange(): lax.ppermute(x, axis, [(i, i ^ mask) for i in range(lax.axis_size(axis))])  9.43 us
    pallas_call x7, Pallas kernels, call(): pl.pallas_call(kernel, out_shape=out_shape, in_specs=[HBM if k in hbm_in...  6.26 us
  transfers between devices with their start and end apart: 5, of which 5 were waited for; matrix products, arithmetic and copies ran while one was open for 0% of the time, Pallas kernels for 5%

profile of v7, /device:TPU:0, one launch (start us, length us, event | category | flops | bytes accessed | tf_op | source)
XLA Modules:
  0.0 26.1 jit_solution(11770407380620912492)
XLA Ops:
  0.6 3.2 %shard_map.75 = (f32[3,32,256]{2,1,0:T(8,128)S(1)}, f32[4,32,256]{2,1,0:T(8,128)S(1)}, bf16[4,32,256]{2,1,0:T(8,128)(2,1)S(1)}, bf16[4,32,288]{2,1,0:T(8,128)(2,1)S(1)}) custom-call(f32[1,1,32,256]{3,2,1,0:T(8,128)} %start_ref.1, f32[1,1,32,256]{3,2,1,0:T(8,128)} %guess_ref.1, bf16[4,32,288]{2,1,0:T(8,128)(2,1)} %w_hbm.1, f32[4,32]{1,0:T(4,128)} %bias_hbm.1), custom_call_target="tpu_custom_call" | custom-call | flops 268435456 | bytes 1048576 | tf_op jit(solution)/shard_map/pallas_call | solution.py:262
  3.9 3.0 %collective-permute-start = (f32[3,32,256]{2,1,0:T(8,128)S(1)}, f32[3,32,256]{2,1,0:T(8,128)S(1)}, u32[]{:S(2)}, u32[]{:S(2)}) collective-permute-start(f32[3,32,256]{2,1,0:T(8,128)S(1)} %get-tuple-element.20.refs_0_), channel_id=1, source_target_pairs={{0,4},{4,0},{8,12},{12,8},{16,20},{20,16},{24,28},{28,24},{1,5},{5... | collective-permute-start | bytes 294920 | tf_op jit(solution)/shard_map/ppermute | solution.py:282
  6.9 2.8 %collective-permute-done.refs_1_ = f32[3,32,256]{2,1,0:T(8,128)S(1)} collective-permute-done((f32[3,32,256]{2,1,0:T(8,128)S(1)}, f32[3,32,256]{2,1,0:T(8,128)S(1)}, u32[]{:S(2)}, u32[]{:S(2)}) %collective-permute-start) | collective-permute-done | bytes 98336 | tf_op jit(solution)/shard_map/ppermute | solution.py:282
  9.7 2.0 %collective-permute-start.1 = (f32[3,32,256]{2,1,0:T(8,128)S(1)}, f32[3,32,256]{2,1,0:T(8,128)S(1)}, u32[]{:S(2)}, u32[]{:S(2)}) collective-permute-start(f32[3,32,256]{2,1,0:T(8,128)S(1)} %get-tuple-element.21.refs_0_), channel_id=1, source_target_pairs={{0,8},{4,12},{8,0},{12,4},{16,24},{20,28},{24,16},{28,20},{1,9},{5... | collective-permute-start | bytes 294920 | tf_op jit(solution)/shard_map/ppermute | solution.py:282
  11.7 2.7 %collective-permute-done.1.refs_1_ = f32[3,32,256]{2,1,0:T(8,128)S(1)} collective-permute-done((f32[3,32,256]{2,1,0:T(8,128)S(1)}, f32[3,32,256]{2,1,0:T(8,128)S(1)}, u32[]{:S(2)}, u32[]{:S(2)}) %collective-permute-start.1) | collective-permute-done | bytes 98336 | tf_op jit(solution)/shard_map/ppermute | solution.py:282
  14.4 3.0 %collective-permute-start.2 = (f32[32,256]{1,0:T(8,128)S(1)}, f32[32,256]{1,0:T(8,128)S(1)}, u32[]{:S(2)}, u32[]{:S(2)}) collective-permute-start(f32[32,256]{1,0:T(8,128)S(1)} %get-tuple-element.23), channel_id=1, source_target_pairs={{0,16},{4,20},{8,24},{12,28},{16,0},{20,4},{24,8},{28,12},{1,17},{... | collective-permute-start | bytes 98312 | tf_op jit(solution)/shard_map/ppermute | solution.py:282
  17.4 0.0 copy-start
  17.4 0.0 copy-start.1
  17.4 1.4 %shard_map.78.patch_ref = bf16[4,288,256]{2,1,0:T(8,128)(2,1)S(1)} custom-call(bf16[4,32,256]{2,1,0:T(8,128)(2,1)S(1)} %get-tuple-element.26.rounded_ref), custom_call_target="tpu_custom_call" | custom-call | flops 268435456 | bytes 1048576 | tf_op jit(solution)/shard_map/pallas_call | solution.py:262
  18.8 0.5 %collective-permute-done.2.got_ref = f32[32,256]{1,0:T(8,128)S(1)} collective-permute-done((f32[32,256]{1,0:T(8,128)S(1)}, f32[32,256]{1,0:T(8,128)S(1)}, u32[]{:S(2)}, u32[]{:S(2)}) %collective-permute-start.2) | collective-permute-done | bytes 32800 | tf_op jit(solution)/shard_map/ppermute | solution.py:282
  19.3 0.0 copy-done
  19.3 0.0 copy-done.1
  19.3 0.9 %shard_map.79 = (f32[1,1,32,256]{3,2,1,0:T(8,128)}, f32[1,1,32,256]{3,2,1,0:T(8,128)}, f32[2,32,384]{2,1,0:T(8,128)S(1)}, f32[2,32,384]{2,1,0:T(8,128)S(1)}) custom-call(f32[32,256]{1,0:T(8,128)S(1)} %collective-permute-done.2.got_ref, f32[4,32,256]{2,1,0:T(8,128)S(1)} %get-tuple-element.24.mine_ref, f32[1,1,32,256]{3,2,1,0:T(8,128)S(1)} %copy-done.1, ...), custom_call_target="tpu_custom_call" | custom-call | flops 268435456 | bytes 1048576 | tf_op jit(solution)/shard_map/pallas_call | solution.py:262
  20.3 0.1 collective-permute-start.3
  20.3 1.3 %collective-permute-done.3.got_ref = f32[2,32,384]{2,1,0:T(8,128)S(1)} collective-permute-done((f32[2,32,384]{2,1,0:T(8,128)S(1)}, f32[2,32,384]{2,1,0:T(8,128)S(1)}, u32[]{:S(2)}, u32[]{:S(2)}) %collective-permute-start.3) | collective-permute-done | bytes 98336 | tf_op jit(solution)/shard_map/ppermute | solution.py:282
  21.6 1.7 %collective-permute-start.4 = (f32[32,384]{1,0:T(8,128)S(1)}, f32[32,384]{1,0:T(8,128)S(1)}, u32[]{:S(2)}, u32[]{:S(2)}) collective-permute-start(f32[32,384]{1,0:T(8,128)S(1)} %get-tuple-element.33), channel_id=1, source_target_pairs={{0,3},{1,2},{2,1},{3,0},{4,7},{5,6},{6,5},{7,4},{8,11},{9,10},{10,... | collective-permute-start | bytes 147464 | tf_op jit(solution)/shard_map/ppermute | solution.py:282
  23.3 2.1 %collective-permute-done.4.got_ref = f32[32,384]{1,0:T(8,128)S(1)} collective-permute-done((f32[32,384]{1,0:T(8,128)S(1)}, f32[32,384]{1,0:T(8,128)S(1)}, u32[]{:S(2)}, u32[]{:S(2)}) %collective-permute-start.4) | collective-permute-done | bytes 49184 | tf_op jit(solution)/shard_map/ppermute | solution.py:282
  25.4 0.7 %shard_map.81 = (f32[4,8,288]{2,1,0:T(8,128)}, f32[4,8]{1,0:T(4,128)}) custom-call(f32[32,384]{1,0:T(8,128)S(1)} %get-tuple-element.32.mine_ref, f32[32,384]{1,0:T(8,128)S(1)} %collective-permute-done.4.got_ref), custom_call_target="tpu_custom_call" | custom-call | flops 268435456 | bytes 1048576 | tf_op jit(solution)/shard_map/pallas_call | solution.py:262
  (3 shorter events, 0.1 us)
Async XLA Ops:
  3.9 5.8 %collective-permute-start = (f32[3,32,256]{2,1,0:T(8,128)S(1)}, f32[3,32,256]{2,1,0:T(8,128)S(1)}, u32[]{:S(2)}, u32[]{:S(2)}) collective-permute-start(f32[3,32,256]{2,1,0:T(8,128)S(1)} %get-tuple-element.20.refs_0_), channel_id=1, source_target_pairs={{0,4},{4,0},{8,12},{12,8},{16,20},{20,16},{24,28},{28,24},{1,5},{5... | collective-permute-start | bytes 294920 | tf_op jit(solution)/shard_map/ppermute | solution.py:282
  9.7 4.7 %collective-permute-start.1 = (f32[3,32,256]{2,1,0:T(8,128)S(1)}, f32[3,32,256]{2,1,0:T(8,128)S(1)}, u32[]{:S(2)}, u32[]{:S(2)}) collective-permute-start(f32[3,32,256]{2,1,0:T(8,128)S(1)} %get-tuple-element.21.refs_0_), channel_id=1, source_target_pairs={{0,8},{4,12},{8,0},{12,4},{16,24},{20,28},{24,16},{28,20},{1,9},{5... | collective-permute-start | bytes 294920 | tf_op jit(solution)/shard_map/ppermute | solution.py:282
  14.4 4.9 %collective-permute-start.2 = (f32[32,256]{1,0:T(8,128)S(1)}, f32[32,256]{1,0:T(8,128)S(1)}, u32[]{:S(2)}, u32[]{:S(2)}) collective-permute-start(f32[32,256]{1,0:T(8,128)S(1)} %get-tuple-element.23), channel_id=1, source_target_pairs={{0,16},{4,20},{8,24},{12,28},{16,0},{20,4},{24,8},{28,12},{1,17},{... | collective-permute-start | bytes 98312 | tf_op jit(solution)/shard_map/ppermute | solution.py:282
  17.4 1.9 %copy-start = (f32[1,1,32,256]{3,2,1,0:T(8,128)S(1)}, f32[1,1,32,256]{3,2,1,0:T(8,128)}, u32[]{:S(2)}) copy-start(f32[1,1,32,256]{3,2,1,0:T(8,128)} %start_ref.1) | copy-start | bytes 98308
  17.4 1.9 %copy-start.1 = (f32[1,1,32,256]{3,2,1,0:T(8,128)S(1)}, f32[1,1,32,256]{3,2,1,0:T(8,128)}, u32[]{:S(2)}) copy-start(f32[1,1,32,256]{3,2,1,0:T(8,128)} %guess_ref.1) | copy-start | bytes 98308
  20.3 1.4 %collective-permute-start.3 = (f32[2,32,384]{2,1,0:T(8,128)S(1)}, f32[2,32,384]{2,1,0:T(8,128)S(1)}, u32[]{:S(2)}, u32[]{:S(2)}) collective-permute-start(f32[2,32,384]{2,1,0:T(8,128)S(1)} %get-tuple-element.31), channel_id=1, source_target_pairs={{0,1},{1,0},{2,3},{3,2},{4,5},{5,4},{6,7},{7,6},{8,9},{9,8},{10,11... | collective-permute-start | bytes 294920 | tf_op jit(solution)/shard_map/ppermute | solution.py:282
  21.6 3.8 %collective-permute-start.4 = (f32[32,384]{1,0:T(8,128)S(1)}, f32[32,384]{1,0:T(8,128)S(1)}, u32[]{:S(2)}, u32[]{:S(2)}) collective-permute-start(f32[32,384]{1,0:T(8,128)S(1)} %get-tuple-element.33), channel_id=1, source_target_pairs={{0,3},{1,2},{2,1},{3,0},{4,7},{5,6},{6,5},{7,4},{8,11},{9,10},{10,... | collective-permute-start | bytes 147464 | tf_op jit(solution)/shard_map/ppermute | solution.py:282

commit v8 on v6

--- a/solution.py
+++ b/solution.py
@@ -65,9 +65,6 @@
     adj_ref,
     w_ref,
     bias_ref,
-    perm_ref,
-    by_tap_ref,
-    column_ref,
     sems,
 ):
     copies = [
@@ -79,46 +76,46 @@
     for copy in copies:
         copy.start()
     depth, chans, width = w_ref.shape
-    perm_ref[...] = permutation(chans)
-    row = lax.broadcasted_iota(jnp.int32, (chans, width), 0)
-    lane = lax.broadcasted_iota(jnp.int32, (chans, width), 1)
-    center = lane == row * TAPS + TAPS // 2
+    perm = permutation(chans)
     eye = lax.broadcasted_iota(jnp.int32, (chans, chans), 0) == lax.broadcasted_iota(
         jnp.int32, (chans, chans), 1
     )
     for copy in copies:
         copy.wait()
+    weights = w_ref[...].reshape(depth * chans, width)
+    by_tap = dot(weights, perm, ((1,), (1,)))
+    turned = dot(perm, weights, ((1,), (1,))).astype(jnp.bfloat16)
+    middle = TAPS // 2 * chans
     start = state_ref[0, 0]
     guess = adj_ref[0, 0]
-    by_tap = dot(w_ref[...].reshape(depth * chans, width), perm_ref[...], ((1,), (1,)))
-    by_tap_ref[...] = by_tap.astype(jnp.bfloat16).reshape(depth, chans, width)
+    state = start
+    gain = None
+    slopes = []
+    backs = []
     for n in range(depth):
+        mine = slice(n * chans, (n + 1) * chans)
         bias = jnp.broadcast_to(bias_ref[n : n + 1, :], (chans, chans))
-        bias = jnp.sum(jnp.where(eye, bias, 0.0), axis=1, keepdims=True)
-        column_ref[n] = jnp.broadcast_to(bias, (chans, HALF))
-
-    def ahead(n, carry):
-        state, gain = carry
-        weight = w_ref[n]
-        kc = jnp.sum(jnp.where(center, weight.astype(jnp.float32), 0.0), axis=1, keepdims=True)
+        bias, kc = (
+            jnp.sum(jnp.where(eye, square, 0.0), axis=1, keepdims=True)
+            for square in (bias, by_tap[mine, middle : middle + chans])
+        )
         rounded = state.astype(jnp.bfloat16)
         rounded_ref[n] = rounded
-        squash = jnp.tanh(convolve(by_tap_ref[n], rounded) + column_ref[n][:, :1])
+        squash = jnp.tanh(convolve(by_tap[mine].astype(jnp.bfloat16), rounded) + bias)
         slope = STEP * (1.0 - squash * squash)
         slope_ref[n] = slope
-        turned = dot(perm_ref[...], weight, ((1,), (1,))).astype(jnp.bfloat16)
-        back_w_ref[n] = jnp.concatenate(
-            [turned[t * chans : (t + 1) * chans] for t in reversed(range(TAPS))], axis=1
+        slopes.append(slope)
+        state = state + STEP * squash
+        factor = 1.0 + slope * kc
+        gain = factor if gain is None else gain * factor
+        back_w = jnp.concatenate(
+            [turned[t * chans : (t + 1) * chans, mine] for t in reversed(range(TAPS))], axis=1
         )
-        return state + STEP * squash, gain * (1.0 + slope * kc)
-
-    state, gain = lax.fori_loop(0, depth, ahead, (start, jnp.ones_like(start)))
-
-    def behind(i, back):
-        n = depth - 1 - i
-        return back + convolve(back_w_ref[n], (back * slope_ref[n]).astype(jnp.bfloat16))
-
-    back = lax.fori_loop(0, depth, behind, guess)
+        back_w_ref[n] = back_w
+        backs.append(back_w)
+    back = guess
+    for n in reversed(range(depth)):
+        back = back + convolve(backs[n], (back * slopes[n]).astype(jnp.bfloat16))
     place = lax.axis_index("layer")
     first = jnp.where(place == 0, 0.0, start)
     last = jnp.where(place == lax.axis_size("layer") - 1, 0.0, guess)
@@ -131,8 +128,8 @@
     depth, chans, _ = rounded_ref.shape
     perm = permutation(chans)
     for n in range(depth):
-        rounded = rounded_ref[n]
-        patch_ref[n] = dot(perm, taps_of(rounded), ((0,), (0,))).astype(jnp.bfloat16)
+        patch = taps_of(rounded_ref[n])
+        patch_ref[n] = dot(perm, patch, ((0,), (0,))).astype(jnp.bfloat16)
 
 
 def joined(bit, total, mine, got):
@@ -295,13 +292,7 @@
         ),
         args,
         hbm_in=range(4),
-        scratch=[pltpu.VMEM(a.shape, a.dtype) for a in args]
-        + [
-            pltpu.VMEM((width, width), jnp.bfloat16),
-            pltpu.VMEM((depth, chans, width), jnp.bfloat16),
-            pltpu.VMEM((depth, chans, HALF), jnp.float32),
-            pltpu.SemaphoreType.DMA((4,)),
-        ],
+        scratch=[pltpu.VMEM(a.shape, a.dtype) for a in args] + [pltpu.SemaphoreType.DMA((4,))],
     )
     (patch,) = call(patch_kernel, (bf16(depth, width, HW),), (rounded,))
     mine = ()

time: 26.5 us -> 25.9 us (0.977)
  Pallas kernels: 5.75 us -> 5.22 us
    pallas_call x7, Pallas kernels: 5.75 us -> 5.22 us  [call(): pl.pallas_call(kernel, out_shape=out_shape, in_specs=[HBM if k in hbm_in...]
where the time goes in v8:
time: 25.9 us; the launch traced here: 25.8 us
  waiting for transfers between devices  10.2 us (39%)
  starting transfers between devices  9.7 us (37%)
  Pallas kernels  5.22 us (20%)
  between operations  0.68 us (3%)
    ppermute x5, waiting for transfers between devices, exchange(): lax.ppermute(x, axis, [(i, i ^ mask) for i in range(lax.axis_size(axis))])  10.2 us
    ppermute x5, starting transfers between devices, exchange(): lax.ppermute(x, axis, [(i, i ^ mask) for i in range(lax.axis_size(axis))])  9.7 us
    pallas_call x7, Pallas kernels, call(): pl.pallas_call(kernel, out_shape=out_shape, in_specs=[HBM if k in hbm_in...  5.22 us
  transfers between devices with their start and end apart: 5, of which 5 were waited for; matrix products, arithmetic and copies ran while one was open for 0% of the time, Pallas kernels for 2%

profile of v8, /device:TPU:0, one launch (start us, length us, event | category | flops | bytes accessed | tf_op | source)
XLA Modules:
  0.0 25.8 jit_solution(10787902736820718253)
XLA Ops:
  0.6 2.9 %shard_map.75 = (f32[3,32,256]{2,1,0:T(8,128)S(1)}, f32[4,32,256]{2,1,0:T(8,128)S(1)}, bf16[4,32,256]{2,1,0:T(8,128)(2,1)S(1)}, bf16[4,32,288]{2,1,0:T(8,128)(2,1)S(1)}) custom-call(f32[1,1,32,256]{3,2,1,0:T(8,128)} %start_ref.1, f32[1,1,32,256]{3,2,1,0:T(8,128)} %guess_ref.1, bf16[4,32,288]{2,1,0:T(8,128)(2,1)} %w_hbm.1, f32[4,32]{1,0:T(4,128)} %bias_hbm.1), custom_call_target="tpu_custom_call" | custom-call | flops 268435456 | bytes 1048576 | tf_op jit(solution)/shard_map/pallas_call | solution.py:257
  3.6 3.0 %collective-permute-start = (f32[3,32,256]{2,1,0:T(8,128)S(1)}, f32[3,32,256]{2,1,0:T(8,128)S(1)}, u32[]{:S(2)}, u32[]{:S(2)}) collective-permute-start(f32[3,32,256]{2,1,0:T(8,128)S(1)} %get-tuple-element.20.refs_0_), channel_id=1, source_target_pairs={{0,4},{4,0},{8,12},{12,8},{16,20},{20,16},{24,28},{28,24},{1,5},{5... | collective-permute-start | bytes 294920 | tf_op jit(solution)/shard_map/ppermute | solution.py:277
  6.6 2.8 %collective-permute-done.refs_1_ = f32[3,32,256]{2,1,0:T(8,128)S(1)} collective-permute-done((f32[3,32,256]{2,1,0:T(8,128)S(1)}, f32[3,32,256]{2,1,0:T(8,128)S(1)}, u32[]{:S(2)}, u32[]{:S(2)}) %collective-permute-start) | collective-permute-done | bytes 98336 | tf_op jit(solution)/shard_map/ppermute | solution.py:277
  9.4 2.0 %collective-permute-start.1 = (f32[3,32,256]{2,1,0:T(8,128)S(1)}, f32[3,32,256]{2,1,0:T(8,128)S(1)}, u32[]{:S(2)}, u32[]{:S(2)}) collective-permute-start(f32[3,32,256]{2,1,0:T(8,128)S(1)} %get-tuple-element.21.refs_0_), channel_id=1, source_target_pairs={{0,8},{4,12},{8,0},{12,4},{16,24},{20,28},{24,16},{28,20},{1,9},{5... | collective-permute-start | bytes 294920 | tf_op jit(solution)/shard_map/ppermute | solution.py:277
  11.4 2.7 %collective-permute-done.1.refs_1_ = f32[3,32,256]{2,1,0:T(8,128)S(1)} collective-permute-done((f32[3,32,256]{2,1,0:T(8,128)S(1)}, f32[3,32,256]{2,1,0:T(8,128)S(1)}, u32[]{:S(2)}, u32[]{:S(2)}) %collective-permute-start.1) | collective-permute-done | bytes 98336 | tf_op jit(solution)/shard_map/ppermute | solution.py:277
  14.1 3.0 %collective-permute-start.2 = (f32[32,256]{1,0:T(8,128)S(1)}, f32[32,256]{1,0:T(8,128)S(1)}, u32[]{:S(2)}, u32[]{:S(2)}) collective-permute-start(f32[32,256]{1,0:T(8,128)S(1)} %get-tuple-element.23), channel_id=1, source_target_pairs={{0,16},{4,20},{8,24},{12,28},{16,0},{20,4},{24,8},{28,12},{1,17},{... | collective-permute-start | bytes 98312 | tf_op jit(solution)/shard_map/ppermute | solution.py:277
  17.1 0.0 copy-start
  17.1 0.0 copy-start.1
  17.1 0.6 %shard_map.78.patch_ref = bf16[4,288,256]{2,1,0:T(8,128)(2,1)S(1)} custom-call(bf16[4,32,256]{2,1,0:T(8,128)(2,1)S(1)} %get-tuple-element.26.rounded_ref), custom_call_target="tpu_custom_call" | custom-call | flops 268435456 | bytes 1048576 | tf_op jit(solution)/shard_map/pallas_call | solution.py:257
  17.7 1.3 %collective-permute-done.2.got_ref = f32[32,256]{1,0:T(8,128)S(1)} collective-permute-done((f32[32,256]{1,0:T(8,128)S(1)}, f32[32,256]{1,0:T(8,128)S(1)}, u32[]{:S(2)}, u32[]{:S(2)}) %collective-permute-start.2) | collective-permute-done | bytes 32800 | tf_op jit(solution)/shard_map/ppermute | solution.py:277
  19.0 0.0 copy-done
  19.0 0.0 copy-done.1
  19.0 0.9 %shard_map.79 = (f32[1,1,32,256]{3,2,1,0:T(8,128)}, f32[1,1,32,256]{3,2,1,0:T(8,128)}, f32[2,32,384]{2,1,0:T(8,128)S(1)}, f32[2,32,384]{2,1,0:T(8,128)S(1)}) custom-call(f32[32,256]{1,0:T(8,128)S(1)} %collective-permute-done.2.got_ref, f32[4,32,256]{2,1,0:T(8,128)S(1)} %get-tuple-element.24.mine_ref, f32[1,1,32,256]{3,2,1,0:T(8,128)S(1)} %copy-done.1, ...), custom_call_target="tpu_custom_call" | custom-call | flops 268435456 | bytes 1048576 | tf_op jit(solution)/shard_map/pallas_call | solution.py:257
  20.0 0.1 collective-permute-start.3
  20.0 1.3 %collective-permute-done.3.got_ref = f32[2,32,384]{2,1,0:T(8,128)S(1)} collective-permute-done((f32[2,32,384]{2,1,0:T(8,128)S(1)}, f32[2,32,384]{2,1,0:T(8,128)S(1)}, u32[]{:S(2)}, u32[]{:S(2)}) %collective-permute-start.3) | collective-permute-done | bytes 98336 | tf_op jit(solution)/shard_map/ppermute | solution.py:277
  21.4 1.7 %collective-permute-start.4 = (f32[32,384]{1,0:T(8,128)S(1)}, f32[32,384]{1,0:T(8,128)S(1)}, u32[]{:S(2)}, u32[]{:S(2)}) collective-permute-start(f32[32,384]{1,0:T(8,128)S(1)} %get-tuple-element.33), channel_id=1, source_target_pairs={{0,3},{1,2},{2,1},{3,0},{4,7},{5,6},{6,5},{7,4},{8,11},{9,10},{10,... | collective-permute-start | bytes 147464 | tf_op jit(solution)/shard_map/ppermute | solution.py:277
  23.0 2.1 %collective-permute-done.4.got_ref = f32[32,384]{1,0:T(8,128)S(1)} collective-permute-done((f32[32,384]{1,0:T(8,128)S(1)}, f32[32,384]{1,0:T(8,128)S(1)}, u32[]{:S(2)}, u32[]{:S(2)}) %collective-permute-start.4) | collective-permute-done | bytes 49184 | tf_op jit(solution)/shard_map/ppermute | solution.py:277
  25.1 0.7 %shard_map.81 = (f32[4,8,288]{2,1,0:T(8,128)}, f32[4,8]{1,0:T(4,128)}) custom-call(f32[32,384]{1,0:T(8,128)S(1)} %get-tuple-element.32.mine_ref, f32[32,384]{1,0:T(8,128)S(1)} %collective-permute-done.4.got_ref), custom_call_target="tpu_custom_call" | custom-call | flops 268435456 | bytes 1048576 | tf_op jit(solution)/shard_map/pallas_call | solution.py:257
  (3 shorter events, 0.1 us)
Async XLA Ops:
  3.6 5.8 %collective-permute-start = (f32[3,32,256]{2,1,0:T(8,128)S(1)}, f32[3,32,256]{2,1,0:T(8,128)S(1)}, u32[]{:S(2)}, u32[]{:S(2)}) collective-permute-start(f32[3,32,256]{2,1,0:T(8,128)S(1)} %get-tuple-element.20.refs_0_), channel_id=1, source_target_pairs={{0,4},{4,0},{8,12},{12,8},{16,20},{20,16},{24,28},{28,24},{1,5},{5... | collective-permute-start | bytes 294920 | tf_op jit(solution)/shard_map/ppermute | solution.py:277
  9.4 4.7 %collective-permute-start.1 = (f32[3,32,256]{2,1,0:T(8,128)S(1)}, f32[3,32,256]{2,1,0:T(8,128)S(1)}, u32[]{:S(2)}, u32[]{:S(2)}) collective-permute-start(f32[3,32,256]{2,1,0:T(8,128)S(1)} %get-tuple-element.21.refs_0_), channel_id=1, source_target_pairs={{0,8},{4,12},{8,0},{12,4},{16,24},{20,28},{24,16},{28,20},{1,9},{5... | collective-permute-start | bytes 294920 | tf_op jit(solution)/shard_map/ppermute | solution.py:277
  14.1 4.9 %collective-permute-start.2 = (f32[32,256]{1,0:T(8,128)S(1)}, f32[32,256]{1,0:T(8,128)S(1)}, u32[]{:S(2)}, u32[]{:S(2)}) collective-permute-start(f32[32,256]{1,0:T(8,128)S(1)} %get-tuple-element.23), channel_id=1, source_target_pairs={{0,16},{4,20},{8,24},{12,28},{16,0},{20,4},{24,8},{28,12},{1,17},{... | collective-permute-start | bytes 98312 | tf_op jit(solution)/shard_map/ppermute | solution.py:277
  17.1 1.9 %copy-start = (f32[1,1,32,256]{3,2,1,0:T(8,128)S(1)}, f32[1,1,32,256]{3,2,1,0:T(8,128)}, u32[]{:S(2)}) copy-start(f32[1,1,32,256]{3,2,1,0:T(8,128)} %start_ref.1) | copy-start | bytes 98308
  17.1 1.9 %copy-start.1 = (f32[1,1,32,256]{3,2,1,0:T(8,128)S(1)}, f32[1,1,32,256]{3,2,1,0:T(8,128)}, u32[]{:S(2)}) copy-start(f32[1,1,32,256]{3,2,1,0:T(8,128)} %guess_ref.1) | copy-start | bytes 98308
  20.0 1.4 %collective-permute-start.3 = (f32[2,32,384]{2,1,0:T(8,128)S(1)}, f32[2,32,384]{2,1,0:T(8,128)S(1)}, u32[]{:S(2)}, u32[]{:S(2)}) collective-permute-start(f32[2,32,384]{2,1,0:T(8,128)S(1)} %get-tuple-element.31), channel_id=1, source_target_pairs={{0,1},{1,0},{2,3},{3,2},{4,5},{5,4},{6,7},{7,6},{8,9},{9,8},{10,11... | collective-permute-start | bytes 294920 | tf_op jit(solution)/shard_map/ppermute | solution.py:277
  21.4 3.8 %collective-permute-start.4 = (f32[32,384]{1,0:T(8,128)S(1)}, f32[32,384]{1,0:T(8,128)S(1)}, u32[]{:S(2)}, u32[]{:S(2)}) collective-permute-start(f32[32,384]{1,0:T(8,128)S(1)} %get-tuple-element.33), channel_id=1, source_target_pairs={{0,3},{1,2},{2,1},{3,0},{4,7},{5,6},{6,5},{7,4},{8,11},{9,10},{10,... | collective-permute-start | bytes 147464 | tf_op jit(solution)/shard_map/ppermute | solution.py:277

commit v9 on v8

--- a/solution.py
+++ b/solution.py
@@ -52,26 +52,10 @@
     return dot(weight, taps_of(values), ((1,), (0,)))
 
 
-def relax_kernel(
-    state_hbm,
-    adj_hbm,
-    w_hbm,
-    bias_hbm,
-    sent_ref,
-    slope_ref,
-    rounded_ref,
-    back_w_ref,
-    state_ref,
-    adj_ref,
-    w_ref,
-    bias_ref,
-    sems,
-):
+def weight_kernel(w_hbm, bias_hbm, by_tap_ref, back_w_ref, column_ref, w_ref, bias_ref, sems):
     copies = [
         pltpu.make_async_copy(src, dst, sems.at[k])
-        for k, (src, dst) in enumerate(
-            ((w_hbm, w_ref), (state_hbm, state_ref), (bias_hbm, bias_ref), (adj_hbm, adj_ref))
-        )
+        for k, (src, dst) in enumerate(((w_hbm, w_ref), (bias_hbm, bias_ref)))
     ]
     for copy in copies:
         copy.start()
@@ -85,37 +69,42 @@
     weights = w_ref[...].reshape(depth * chans, width)
     by_tap = dot(weights, perm, ((1,), (1,)))
     turned = dot(perm, weights, ((1,), (1,))).astype(jnp.bfloat16)
+    by_tap_ref[...] = by_tap.astype(jnp.bfloat16).reshape(depth, chans, width)
     middle = TAPS // 2 * chans
+    for n in range(depth):
+        mine = slice(n * chans, (n + 1) * chans)
+        back_w_ref[n] = jnp.concatenate(
+            [turned[t * chans : (t + 1) * chans, mine] for t in reversed(range(TAPS))], axis=1
+        )
+        bias = jnp.broadcast_to(bias_ref[n : n + 1, :], (chans, chans))
+        for k, square in enumerate((bias, by_tap[mine, middle : middle + chans])):
+            column = jnp.sum(jnp.where(eye, square, 0.0), axis=1, keepdims=True)
+            column_ref[n, k] = jnp.broadcast_to(column, (chans, HALF))
+
+
+def relax_kernel(
+    state_ref, adj_ref, by_tap_ref, back_w_ref, column_ref, sent_ref, slope_ref, rounded_ref
+):
+    depth = by_tap_ref.shape[0]
     start = state_ref[0, 0]
     guess = adj_ref[0, 0]
     state = start
     gain = None
     slopes = []
-    backs = []
     for n in range(depth):
-        mine = slice(n * chans, (n + 1) * chans)
-        bias = jnp.broadcast_to(bias_ref[n : n + 1, :], (chans, chans))
-        bias, kc = (
-            jnp.sum(jnp.where(eye, square, 0.0), axis=1, keepdims=True)
-            for square in (bias, by_tap[mine, middle : middle + chans])
-        )
+        bias, kc = (jnp.concatenate([column_ref[n, k]] * (HW // HALF), axis=1) for k in range(2))
         rounded = state.astype(jnp.bfloat16)
         rounded_ref[n] = rounded
-        squash = jnp.tanh(convolve(by_tap[mine].astype(jnp.bfloat16), rounded) + bias)
+        squash = jnp.tanh(convolve(by_tap_ref[n], rounded) + bias)
         slope = STEP * (1.0 - squash * squash)
         slope_ref[n] = slope
         slopes.append(slope)
         state = state + STEP * squash
         factor = 1.0 + slope * kc
         gain = factor if gain is None else gain * factor
-        back_w = jnp.concatenate(
-            [turned[t * chans : (t + 1) * chans, mine] for t in reversed(range(TAPS))], axis=1
-        )
-        back_w_ref[n] = back_w
-        backs.append(back_w)
     back = guess
     for n in reversed(range(depth)):
-        back = back + convolve(backs[n], (back * slopes[n]).astype(jnp.bfloat16))
+        back = back + convolve(back_w_ref[n], (back * slopes[n]).astype(jnp.bfloat16))
     place = lax.axis_index("layer")
     first = jnp.where(place == 0, 0.0, start)
     last = jnp.where(place == lax.axis_size("layer") - 1, 0.0, guess)
@@ -184,13 +173,10 @@
     slope_ref,
     patch_ref,
     back_w_ref,
-    adj_hbm,
-    state_hbm,
+    adj_ref,
+    state_ref,
     keep_ref,
     send_ref,
-    adj_ref,
-    state_ref,
-    sems,
 ):
     depth, chans, rows = back_w_ref.shape
     shares = 2 * keep_ref.shape[0]
@@ -203,12 +189,6 @@
     fixed = jnp.where(upper, mine_ref[3], mine_ref[3] + mine_ref[2] * got)
     adj = jnp.where(place == lax.axis_size("layer") - 1, guess_ref[0, 0], fixed)
     adj_ref[0, 0] = adj
-    copies = [
-        pltpu.make_async_copy(src, dst, sems.at[k])
-        for k, (src, dst) in enumerate(((adj_ref, adj_hbm), (state_ref, state_hbm)))
-    ]
-    for copy in copies:
-        copy.start()
     pad = keep_ref.shape[2] - rows
     odd, high = bit_of("dp", 0), bit_of("dp", 1)
 
@@ -231,16 +211,24 @@
         return adj + convolve(back_w_ref[n], layer(n, adj))
 
     layer(0, lax.fori_loop(0, depth - 1, behind, adj))
-    for copy in copies:
-        copy.wait()
-
-
-def halve_kernel(mine_ref, got_ref, keep_ref, send_ref):
+
+
+def halve_kernel(mine_ref, got_ref, adj_ref, state_ref, keep_ref, send_ref, adj_out, state_out):
     keep_ref[...] = mine_ref[0] + got_ref[0]
     send_ref[...] = mine_ref[1] + got_ref[1]
-
-
-def total_kernel(mine_ref, got_ref, grad_ref, bias_ref):
+    adj_out[...] = adj_ref[...]
+    state_out[...] = state_ref[...]
+
+
+def total_kernel(
+    mine_ref, got_ref, adj_ref, state_ref, grad_ref, bias_ref, adj_hbm, state_hbm, sems
+):
+    copies = [
+        pltpu.make_async_copy(src, dst, sems.at[k])
+        for k, (src, dst) in enumerate(((adj_ref, adj_hbm), (state_ref, state_hbm)))
+    ]
+    for copy in copies:
+        copy.start()
     depth, own, width = grad_ref.shape
     total = mine_ref[...] + got_ref[...]
     eye = lax.broadcasted_iota(jnp.int32, (own, own), 0) == lax.broadcasted_iota(
@@ -251,6 +239,8 @@
         grad_ref[n] = mine[:, :width]
         column = jnp.broadcast_to(mine[:, width : width + 1], (own, own))
         bias_ref[n : n + 1, :] = jnp.sum(jnp.where(eye, column, 0.0), axis=0, keepdims=True)
+    for copy in copies:
+        copy.wait()
 
 
 def call(kernel, out_shape, args, hbm_in=(), hbm_out=(), scratch=()):
@@ -273,58 +263,78 @@
     return jax.ShapeDtypeStruct(shape, jnp.bfloat16)
 
 
-def exchange(x, axis, mask):
-    return lax.ppermute(x, axis, [(i, i ^ mask) for i in range(lax.axis_size(axis))])
+def exchange(x, partner):
+    blocks, shares = lax.axis_size("layer"), lax.axis_size("dp")
+    pairs = []
+    for layer in range(blocks):
+        for dp in range(shares):
+            to = partner(layer, dp)
+            pairs.append((layer * shares + dp, to[0] * shares + to[1]))
+    return lax.ppermute(x, ("layer", "dp"), pairs)
+
+
+def across(x, step):
+    return exchange(x, lambda layer, dp: (layer ^ (1 << step), dp ^ 1))
+
+
+def image_swap(x):
+    return exchange(x, lambda layer, dp: (layer, dp ^ (layer.bit_count() % 2)))
 
 
 def local(state_guess, adjoint_guess, conv_weight, conv_bias):
     depth, chans, width = conv_weight.shape
     shares = lax.axis_size("dp")
     steps = lax.axis_size("layer").bit_length() - 1
-    args = (state_guess, adjoint_guess, conv_weight, conv_bias)
-    total, slope, rounded, back_w = call(
+    state_guess = image_swap(state_guess)
+    adjoint_guess = image_swap(adjoint_guess)
+    by_tap, back_w, columns = call(
+        weight_kernel,
+        (bf16(depth, chans, width), bf16(depth, chans, width), f32(depth, 2, chans, HALF)),
+        (conv_weight, conv_bias),
+        hbm_in=(0, 1),
+        scratch=[
+            pltpu.VMEM(conv_weight.shape, conv_weight.dtype),
+            pltpu.VMEM(conv_bias.shape, conv_bias.dtype),
+            pltpu.SemaphoreType.DMA((2,)),
+        ],
+    )
+    total, slope, rounded = call(
         relax_kernel,
-        (
-            f32(3, chans, HW),
-            f32(depth, chans, HW),
-            bf16(depth, chans, HW),
-            bf16(depth, chans, width),
-        ),
-        args,
-        hbm_in=range(4),
-        scratch=[pltpu.VMEM(a.shape, a.dtype) for a in args] + [pltpu.SemaphoreType.DMA((4,))],
+        (f32(3, chans, HW), f32(depth, chans, HW), bf16(depth, chans, HW)),
+        (state_guess, adjoint_guess, by_tap, back_w, columns),
     )
     (patch,) = call(patch_kernel, (bf16(depth, width, HW),), (rounded,))
     mine = ()
     for step in range(1, steps):
-        got = exchange(total, "layer", 1 << (step - 1))
+        got = across(total, step - 1)
         final = step == steps - 1
         total, *mine = call(
             functools.partial(join_kernel, step, final),
             (f32(chans, HW) if final else f32(3, chans, HW), f32(4, chans, HW)),
             (total, got, *mine),
         )
-    got = exchange(total, "layer", 1 << (steps - 1))
+    got = across(total, steps - 1)
     lanes = -(-(width + 1) // HALF) * HALF
     part = (depth * chans // shares, lanes)
-    guess = pltpu.VMEM(adjoint_guess.shape, jnp.float32)
+    one = f32(*state_guess.shape)
     adjoint_fixed, state_fixed, keep, send = call(
         functools.partial(grad_kernel, steps),
-        (
-            f32(*adjoint_guess.shape),
-            f32(*state_guess.shape),
-            f32(shares // 2, *part),
-            f32(shares // 2, *part),
-        ),
+        (one, one, f32(shares // 2, *part), f32(shares // 2, *part)),
         (got, *mine, adjoint_guess, state_guess, slope, patch, back_w),
-        hbm_out=(0, 1),
-        scratch=[guess, guess, pltpu.SemaphoreType.DMA((2,))],
-    )
-    keep, send = call(halve_kernel, (f32(*part), f32(*part)), (keep, exchange(send, "dp", 1)))
-    weight_grad, bias_grad = call(
+    )
+    got = exchange(send, lambda layer, dp: (layer, dp ^ 1))
+    keep, send, adjoint_fixed, state_fixed = call(
+        halve_kernel,
+        (f32(*part), f32(*part), one, one),
+        (keep, got, adjoint_fixed, state_fixed),
+    )
+    got = exchange(send, lambda layer, dp: (layer, dp ^ 3))
+    weight_grad, bias_grad, adjoint_fixed, state_fixed = call(
         total_kernel,
-        (f32(depth, chans // shares, width), f32(depth, chans // shares)),
-        (keep, exchange(send, "dp", 3)),
+        (f32(depth, chans // shares, width), f32(depth, chans // shares), one, one),
+        (keep, got, image_swap(adjoint_fixed), image_swap(state_fixed)),
+        hbm_out=(2, 3),
+        scratch=[pltpu.SemaphoreType.DMA((2,))],
     )
     return (state_fixed, adjoint_fixed, weight_grad, bias_grad)
 

time: 25.9 us -> 33.5 us (1.29)
  the two profiles are of different devices: /device:TPU:0 before, /device:TPU:27 now
where the time goes in v9:
time: 33.5 us; the launch traced here: 33.1 us
  waiting for transfers between devices  15.4 us (46%)
  starting transfers between devices  11 us (33%)
  Pallas kernels  6 us (18%)
  between operations  0.74 us (2%)
    ppermute x9, waiting for transfers between devices, exchange(): return lax.ppermute(x, ('layer', 'dp'), pairs)  15.4 us
    ppermute x9, starting transfers between devices, exchange(): return lax.ppermute(x, ('layer', 'dp'), pairs)  11 us
    pallas_call x8, Pallas kernels, call(): pl.pallas_call(kernel, out_shape=out_shape, in_specs=[HBM if k in hbm_in...  6 us
  transfers between devices with their start and end apart: 9, of which 6 were waited for; matrix products, arithmetic and copies ran while one was open for 0% of the time, Pallas kernels for 6%

profile of v9, /device:TPU:27, one launch (start us, length us, event | category | flops | bytes accessed | tf_op | source)
XLA Modules:
  0.0 33.1 jit_solution(5263751132314920944)
XLA Ops:
  0.6 2.6 %collective-permute-start = (f32[1,1,32,256]{3,2,1,0:T(8,128)}, f32[1,1,32,256]{3,2,1,0:T(8,128)S(1)}, u32[]{:S(2)}, u32[]{:S(2)}) collective-permute-start(f32[1,1,32,256]{3,2,1,0:T(8,128)} %param.4), channel_id=1, source_target_pairs={{0,0},{1,1},{2,2},{3,3},{4,5},{5,4},{6,7},{7,6},{8,9},{9,8},{10,11... | collective-permute-start | bytes 98312 | tf_op jit(solution)/shard_map/ppermute | solution.py:273
  3.2 1.9 %collective-permute-start.1 = (f32[1,1,32,256]{3,2,1,0:T(8,128)}, f32[1,1,32,256]{3,2,1,0:T(8,128)S(1)}, u32[]{:S(2)}, u32[]{:S(2)}) collective-permute-start(f32[1,1,32,256]{3,2,1,0:T(8,128)} %param.5), channel_id=1, source_target_pairs={{0,0},{1,1},{2,2},{3,3},{4,5},{5,4},{6,7},{7,6},{8,9},{9,8},{10,11... | collective-permute-start | bytes 98312 | tf_op jit(solution)/shard_map/ppermute | solution.py:273
  5.2 1.3 %shard_map.75 = (bf16[4,32,288]{2,1,0:T(8,128)(2,1)S(1)}, bf16[4,32,288]{2,1,0:T(8,128)(2,1)S(1)}, f32[4,2,32,128]{3,2,1,0:T(8,128)S(1)}) custom-call(bf16[4,32,288]{2,1,0:T(8,128)(2,1)} %w_hbm.1, f32[4,32]{1,0:T(4,128)} %bias_hbm.1), custom_call_target="tpu_custom_call" | custom-call | flops 268435456 | bytes 1048576 | tf_op jit(solution)/shard_map/pallas_call | solution.py:247
  6.5 0.0 collective-permute-done.state_ref.start_ref
  6.5 0.1 collective-permute-done.1.adj_ref.guess_ref
  6.5 1.9 %shard_map.76 = (f32[3,32,256]{2,1,0:T(8,128)S(1)}, f32[4,32,256]{2,1,0:T(8,128)S(1)}, bf16[4,32,256]{2,1,0:T(8,128)(2,1)S(1)}) custom-call(f32[1,1,32,256]{3,2,1,0:T(8,128)S(1)} %collective-permute-done.state_ref.start_ref, f32[1,1,32,256]{3,2,1,0:T(8,128)S(1)} %collective-permute-done.1.adj_ref.guess_ref, ...), custom_call_target="tpu_custom_call" | custom-call | flops 268435456 | bytes 1048576 | tf_op jit(solution)/shard_map/pallas_call | solution.py:247
  8.4 0.1 collective-permute-start.2
  8.5 4.9 %collective-permute-done.2.refs_1_ = f32[3,32,256]{2,1,0:T(8,128)S(1)} collective-permute-done((f32[3,32,256]{2,1,0:T(8,128)S(1)}, f32[3,32,256]{2,1,0:T(8,128)S(1)}, u32[]{:S(2)}, u32[]{:S(2)}) %collective-permute-start.2) | collective-permute-done | bytes 98336 | tf_op jit(solution)/shard_map/ppermute | solution.py:273
  13.4 0.1 collective-permute-start.3
  13.5 4.8 %collective-permute-done.3.refs_1_ = f32[3,32,256]{2,1,0:T(8,128)S(1)} collective-permute-done((f32[3,32,256]{2,1,0:T(8,128)S(1)}, f32[3,32,256]{2,1,0:T(8,128)S(1)}, u32[]{:S(2)}, u32[]{:S(2)}) %collective-permute-start.3) | collective-permute-done | bytes 98336 | tf_op jit(solution)/shard_map/ppermute | solution.py:273
  18.3 0.1 collective-permute-start.4
  18.4 0.6 %shard_map.79.patch_ref = bf16[4,288,256]{2,1,0:T(8,128)(2,1)S(1)} custom-call(bf16[4,32,256]{2,1,0:T(8,128)(2,1)S(1)} %get-tuple-element.35.rounded_ref), custom_call_target="tpu_custom_call" | custom-call | flops 268435456 | bytes 1048576 | tf_op jit(solution)/shard_map/pallas_call | solution.py:247
  19.0 3.9 %collective-permute-done.4.got_ref = f32[32,256]{1,0:T(8,128)S(1)} collective-permute-done((f32[32,256]{1,0:T(8,128)S(1)}, f32[32,256]{1,0:T(8,128)S(1)}, u32[]{:S(2)}, u32[]{:S(2)}) %collective-permute-start.4) | collective-permute-done | bytes 32800 | tf_op jit(solution)/shard_map/ppermute | solution.py:273
  22.9 0.9 %shard_map.80 = (f32[1,1,32,256]{3,2,1,0:T(8,128)S(1)}, f32[1,1,32,256]{3,2,1,0:T(8,128)S(1)}, f32[2,32,384]{2,1,0:T(8,128)S(1)}, f32[2,32,384]{2,1,0:T(8,128)S(1)}) custom-call(f32[32,256]{1,0:T(8,128)S(1)} %collective-permute-done.4.got_ref, f32[4,32,256]{2,1,0:T(8,128)S(1)} %get-tuple-element.33.mine_ref, ...), custom_call_target="tpu_custom_call" | custom-call | flops 268435456 | bytes 1048576 | tf_op jit(solution)/shard_map/pallas_call | solution.py:247
  23.7 0.5 %collective-permute-start.5 = (f32[2,32,384]{2,1,0:T(8,128)S(1)}, f32[2,32,384]{2,1,0:T(8,128)S(1)}, u32[]{:S(2)}, u32[]{:S(2)}) collective-permute-start(f32[2,32,384]{2,1,0:T(8,128)S(1)} %get-tuple-element.37), channel_id=1, source_target_pairs={{0,1},{1,0},{2,3},{3,2},{4,5},{5,4},{6,7},{7,6},{8,9},{9,8},{10,11... | collective-permute-start | bytes 294920 | tf_op jit(solution)/shard_map/ppermute | solution.py:273
  24.2 0.9 %collective-permute-done.5.got_ref = f32[2,32,384]{2,1,0:T(8,128)S(1)} collective-permute-done((f32[2,32,384]{2,1,0:T(8,128)S(1)}, f32[2,32,384]{2,1,0:T(8,128)S(1)}, u32[]{:S(2)}, u32[]{:S(2)}) %collective-permute-start.5) | collective-permute-done | bytes 98336 | tf_op jit(solution)/shard_map/ppermute | solution.py:273
  25.2 1.5 %collective-permute-start.6 = (f32[32,384]{1,0:T(8,128)S(1)}, f32[32,384]{1,0:T(8,128)S(1)}, u32[]{:S(2)}, u32[]{:S(2)}) collective-permute-start(f32[32,384]{1,0:T(8,128)S(1)} %get-tuple-element.41), channel_id=1, source_target_pairs={{0,3},{1,2},{2,1},{3,0},{4,7},{5,6},{6,5},{7,4},{8,11},{9,10},{10,... | collective-permute-start | bytes 147464 | tf_op jit(solution)/shard_map/ppermute | solution.py:273
  26.7 2.0 %collective-permute-start.7 = (f32[1,1,32,256]{3,2,1,0:T(8,128)S(1)}, f32[1,1,32,256]{3,2,1,0:T(8,128)S(1)}, u32[]{:S(2)}, u32[]{:S(2)}) collective-permute-start(f32[1,1,32,256]{3,2,1,0:T(8,128)S(1)} %get-tuple-element.42), channel_id=1, source_target_pairs={{0,0},{1,1},{2,2},{3,3},{4,5},{5,4},{6,7},{7,6},{8,9},{9,8},{10,11... | collective-permute-start | bytes 98312 | tf_op jit(solution)/shard_map/ppermute | solution.py:273
  28.8 2.3 %collective-permute-start.8 = (f32[1,1,32,256]{3,2,1,0:T(8,128)S(1)}, f32[1,1,32,256]{3,2,1,0:T(8,128)S(1)}, u32[]{:S(2)}, u32[]{:S(2)}) collective-permute-start(f32[1,1,32,256]{3,2,1,0:T(8,128)S(1)} %get-tuple-element.43), channel_id=1, source_target_pairs={{0,0},{1,1},{2,2},{3,3},{4,5},{5,4},{6,7},{7,6},{8,9},{9,8},{10,11... | collective-permute-start | bytes 98312 | tf_op jit(solution)/shard_map/ppermute | solution.py:273
  31.0 0.0 collective-permute-done.7.adj_ref
  31.0 0.8 %collective-permute-done.8.state_ref = f32[1,1,32,256]{3,2,1,0:T(8,128)S(1)} collective-permute-done((f32[1,1,32,256]{3,2,1,0:T(8,128)S(1)}, f32[1,1,32,256]{3,2,1,0:T(8,128)S(1)}, u32[]{:S(2)}, u32[]{:S(2)}) %collective-permute-start.8) | collective-permute-done | bytes 32800 | tf_op jit(solution)/shard_map/ppermute | solution.py:273
  31.9 0.0 collective-permute-done.6.got_ref
  31.9 1.3 %shard_map.82 = (f32[4,8,288]{2,1,0:T(8,128)}, f32[4,8]{1,0:T(4,128)}, f32[1,1,32,256]{3,2,1,0:T(8,128)}, f32[1,1,32,256]{3,2,1,0:T(8,128)}) custom-call(f32[32,384]{1,0:T(8,128)S(1)} %get-tuple-element.40.mine_ref, f32[32,384]{1,0:T(8,128)S(1)} %collective-permute-done.6.got_ref, f32[1,1,32,256]{3,2,1,0:T(8,128)S(1)} %collective-permute-done.7.adj_ref, ...), custom_call_target="tpu_custom_call" | custom-call | flops 268435456 | bytes 1048576 | tf_op jit(solution)/shard_map/pallas_call | solution.py:247
  (3 shorter events, 0.1 us)
Async XLA Ops:
  0.6 5.8 %collective-permute-start = (f32[1,1,32,256]{3,2,1,0:T(8,128)}, f32[1,1,32,256]{3,2,1,0:T(8,128)S(1)}, u32[]{:S(2)}, u32[]{:S(2)}) collective-permute-start(f32[1,1,32,256]{3,2,1,0:T(8,128)} %param.4), channel_id=1, source_target_pairs={{0,0},{1,1},{2,2},{3,3},{4,5},{5,4},{6,7},{7,6},{8,9},{9,8},{10,11... | collective-permute-start | bytes 98312 | tf_op jit(solution)/shard_map/ppermute | solution.py:273
  3.2 3.3 %collective-permute-start.1 = (f32[1,1,32,256]{3,2,1,0:T(8,128)}, f32[1,1,32,256]{3,2,1,0:T(8,128)S(1)}, u32[]{:S(2)}, u32[]{:S(2)}) collective-permute-start(f32[1,1,32,256]{3,2,1,0:T(8,128)} %param.5), channel_id=1, source_target_pairs={{0,0},{1,1},{2,2},{3,3},{4,5},{5,4},{6,7},{7,6},{8,9},{9,8},{10,11... | collective-permute-start | bytes 98312 | tf_op jit(solution)/shard_map/ppermute | solution.py:273
  8.4 5.0 %collective-permute-start.2 = (f32[3,32,256]{2,1,0:T(8,128)S(1)}, f32[3,32,256]{2,1,0:T(8,128)S(1)}, u32[]{:S(2)}, u32[]{:S(2)}) collective-permute-start(f32[3,32,256]{2,1,0:T(8,128)S(1)} %get-tuple-element.29.refs_0_), channel_id=1, source_target_pairs={{0,5},{1,4},{2,7},{3,6},{4,1},{5,0},{6,3},{7,2},{8,13},{9,12},{10,... | collective-permute-start | bytes 294920 | tf_op jit(solution)/shard_map/ppermute | solution.py:273
  13.4 4.9 %collective-permute-start.3 = (f32[3,32,256]{2,1,0:T(8,128)S(1)}, f32[3,32,256]{2,1,0:T(8,128)S(1)}, u32[]{:S(2)}, u32[]{:S(2)}) collective-permute-start(f32[3,32,256]{2,1,0:T(8,128)S(1)} %get-tuple-element.30.refs_0_), channel_id=1, source_target_pairs={{0,9},{1,8},{2,11},{3,10},{4,13},{5,12},{6,15},{7,14},{8,1},{9,0},... | collective-permute-start | bytes 294920 | tf_op jit(solution)/shard_map/ppermute | solution.py:273
  18.3 4.5 %collective-permute-start.4 = (f32[32,256]{1,0:T(8,128)S(1)}, f32[32,256]{1,0:T(8,128)S(1)}, u32[]{:S(2)}, u32[]{:S(2)}) collective-permute-start(f32[32,256]{1,0:T(8,128)S(1)} %get-tuple-element.32), channel_id=1, source_target_pairs={{0,17},{1,16},{2,19},{3,18},{4,21},{5,20},{6,23},{7,22},{8,25},{9,... | collective-permute-start | bytes 98312 | tf_op jit(solution)/shard_map/ppermute | solution.py:273
  23.7 1.4 %collective-permute-start.5 = (f32[2,32,384]{2,1,0:T(8,128)S(1)}, f32[2,32,384]{2,1,0:T(8,128)S(1)}, u32[]{:S(2)}, u32[]{:S(2)}) collective-permute-start(f32[2,32,384]{2,1,0:T(8,128)S(1)} %get-tuple-element.37), channel_id=1, source_target_pairs={{0,1},{1,0},{2,3},{3,2},{4,5},{5,4},{6,7},{7,6},{8,9},{9,8},{10,11... | collective-permute-start | bytes 294920 | tf_op jit(solution)/shard_map/ppermute | solution.py:273
  25.2 6.7 %collective-permute-start.6 = (f32[32,384]{1,0:T(8,128)S(1)}, f32[32,384]{1,0:T(8,128)S(1)}, u32[]{:S(2)}, u32[]{:S(2)}) collective-permute-start(f32[32,384]{1,0:T(8,128)S(1)} %get-tuple-element.41), channel_id=1, source_target_pairs={{0,3},{1,2},{2,1},{3,0},{4,7},{5,6},{6,5},{7,4},{8,11},{9,10},{10,... | collective-permute-start | bytes 147464 | tf_op jit(solution)/shard_map/ppermute | solution.py:273
  26.7 4.3 %collective-permute-start.7 = (f32[1,1,32,256]{3,2,1,0:T(8,128)S(1)}, f32[1,1,32,256]{3,2,1,0:T(8,128)S(1)}, u32[]{:S(2)}, u32[]{:S(2)}) collective-permute-start(f32[1,1,32,256]{3,2,1,0:T(8,128)S(1)} %get-tuple-element.42), channel_id=1, source_target_pairs={{0,0},{1,1},{2,2},{3,3},{4,5},{5,4},{6,7},{7,6},{8,9},{9,8},{10,11... | collective-permute-start | bytes 98312 | tf_op jit(solution)/shard_map/ppermute | solution.py:273
  28.8 3.1 %collective-permute-start.8 = (f32[1,1,32,256]{3,2,1,0:T(8,128)S(1)}, f32[1,1,32,256]{3,2,1,0:T(8,128)S(1)}, u32[]{:S(2)}, u32[]{:S(2)}) collective-permute-start(f32[1,1,32,256]{3,2,1,0:T(8,128)S(1)} %get-tuple-element.43), channel_id=1, source_target_pairs={{0,0},{1,1},{2,2},{3,3},{4,5},{5,4},{6,7},{7,6},{8,9},{9,8},{10,11... | collective-permute-start | bytes 98312 | tf_op jit(solution)/shard_map/ppermute | solution.py:273

commit v10 on v8

--- a/solution.py
+++ b/solution.py
@@ -18,22 +18,67 @@
 HBM = pl.BlockSpec(memory_space=pltpu.HBM)
 
 
+def picked(low, high, source, from_high):
+    return jnp.where(
+        from_high,
+        jnp.take_along_axis(high, source, axis=1, mode="promise_in_bounds"),
+        jnp.take_along_axis(low, source, axis=1, mode="promise_in_bounds"),
+    )
+
+
+def lanes_of(values):
+    lane = lax.broadcasted_iota(jnp.int32, (values.shape[0], HALF), 1)
+    return lane // IMG, lane % IMG
+
+
+def by_parity(values):
+    line, col = lanes_of(values)
+    low, high = values[:, :HALF], values[:, HALF:]
+    half = IMG // 4
+    return jnp.concatenate(
+        [
+            picked(low, high, (2 * (line % half) + odd) * IMG + col, line >= half)
+            for odd in range(2)
+        ],
+        axis=1,
+    )
+
+
+def in_order(values):
+    line, col = lanes_of(values)
+    even, odd = values[:, :HALF], values[:, HALF:]
+    return jnp.concatenate(
+        [
+            picked(even, odd, (half * (IMG // 4) + line // 2) * IMG + col, line % 2 == 1)
+            for half in range(2)
+        ],
+        axis=1,
+    )
+
+
 def taps_of(values):
-    pixel = lax.broadcasted_iota(jnp.int16, values.shape, 1)
-    col = pixel & (IMG - 1)
-    rows = {-1: pixel >= IMG, 1: pixel < HW - IMG}
-    cols = {-1: col >= 1, 1: col < IMG - 1}
-    out = []
-    for tap in range(TAPS):
-        down, right = tap // 3 - 1, tap % 3 - 1
-        part = values
-        if down or right:
-            part = pltpu.roll(values, -(down * IMG + right) % HW, 1)
-            tests = [rows[down]] if down else []
-            tests += [cols[right]] if right else []
-            part = jnp.where(functools.reduce(jnp.logical_and, tests), part, jnp.zeros_like(part))
-        out.append(part)
-    return jnp.concatenate(out, axis=0)
+    even, odd = values[:, :HALF], values[:, HALF:]
+    lane = lax.broadcasted_iota(jnp.int16, even.shape, 1)
+    col = lane & (IMG - 1)
+    cols = {-1: [col >= 1], 0: [], 1: [col < IMG - 1]}
+
+    def turned(half, lines, right):
+        by = lines * IMG + right
+        if not by:
+            return half
+        tests = cols[right] + {-1: [lane >= IMG], 0: [], 1: [lane < HALF - IMG]}[lines]
+        part = pltpu.roll(half, -by % HALF, 1)
+        return jnp.where(functools.reduce(jnp.logical_and, tests), part, jnp.zeros_like(part))
+
+    above, here, below = [], [], []
+    for right in (-1, 0, 1):
+        same = turned(even, 0, right), turned(odd, 0, right)
+        above.append((turned(odd, -1, right), same[0]))
+        here.append(same)
+        below.append((same[1], turned(even, 1, right)))
+    return jnp.concatenate(
+        [jnp.concatenate(pair, axis=1) for pair in above + here + below], axis=0
+    )
 
 
 def permutation(chans):
@@ -57,6 +102,7 @@
     adj_hbm,
     w_hbm,
     bias_hbm,
+    guess_ref,
     sent_ref,
     slope_ref,
     rounded_ref,
@@ -86,8 +132,9 @@
     by_tap = dot(weights, perm, ((1,), (1,)))
     turned = dot(perm, weights, ((1,), (1,))).astype(jnp.bfloat16)
     middle = TAPS // 2 * chans
-    start = state_ref[0, 0]
-    guess = adj_ref[0, 0]
+    start = by_parity(state_ref[0, 0])
+    guess = by_parity(adj_ref[0, 0])
+    guess_ref[...] = guess
     state = start
     gain = None
     slopes = []
@@ -175,40 +222,36 @@
             sent_ref[k] = total[k]
 
 
+def later_fixed(steps, got_ref, mine_ref):
+    got = jnp.where(bit_of("layer", steps - 1), 0.0, mine_ref[2] * got_ref[...])
+    return mine_ref[3] + got
+
+
+def fixed_kernel(steps, _, got_ref, mine_ref, guess_ref, start_ref, adj_ref, state_ref):
+    place = lax.axis_index("layer")
+    adj = in_order(later_fixed(steps, got_ref, mine_ref))
+    got = jnp.where(bit_of("layer", steps - 1), mine_ref[0] * got_ref[...], 0.0)
+    state = in_order(mine_ref[1] + got)
+    adj_ref[0, 0] = jnp.where(place == lax.axis_size("layer") - 1, guess_ref[0, 0], adj)
+    state_ref[0, 0] = jnp.where(place == 0, start_ref[0, 0], state)
+
+
 def grad_kernel(
     steps,
     got_ref,
     mine_ref,
     guess_ref,
-    start_ref,
     slope_ref,
     patch_ref,
     back_w_ref,
-    adj_hbm,
-    state_hbm,
     keep_ref,
     send_ref,
-    adj_ref,
-    state_ref,
-    sems,
 ):
     depth, chans, rows = back_w_ref.shape
     shares = 2 * keep_ref.shape[0]
     own = chans // shares
-    place = lax.axis_index("layer")
-    upper = bit_of("layer", steps - 1)
-    got = got_ref[...]
-    fixed = jnp.where(upper, mine_ref[1] + mine_ref[0] * got, mine_ref[1])
-    state_ref[0, 0] = jnp.where(place == 0, start_ref[0, 0], fixed)
-    fixed = jnp.where(upper, mine_ref[3], mine_ref[3] + mine_ref[2] * got)
-    adj = jnp.where(place == lax.axis_size("layer") - 1, guess_ref[0, 0], fixed)
-    adj_ref[0, 0] = adj
-    copies = [
-        pltpu.make_async_copy(src, dst, sems.at[k])
-        for k, (src, dst) in enumerate(((adj_ref, adj_hbm), (state_ref, state_hbm)))
-    ]
-    for copy in copies:
-        copy.start()
+    last = lax.axis_index("layer") == lax.axis_size("layer") - 1
+    adj = jnp.where(last, guess_ref[...], later_fixed(steps, got_ref, mine_ref))
     pad = keep_ref.shape[2] - rows
     odd, high = bit_of("dp", 0), bit_of("dp", 1)
 
@@ -231,8 +274,6 @@
         return adj + convolve(back_w_ref[n], layer(n, adj))
 
     layer(0, lax.fori_loop(0, depth - 1, behind, adj))
-    for copy in copies:
-        copy.wait()
 
 
 def halve_kernel(mine_ref, got_ref, keep_ref, send_ref):
@@ -282,9 +323,10 @@
     shares = lax.axis_size("dp")
     steps = lax.axis_size("layer").bit_length() - 1
     args = (state_guess, adjoint_guess, conv_weight, conv_bias)
-    total, slope, rounded, back_w = call(
+    guess, total, slope, rounded, back_w = call(
         relax_kernel,
         (
+            f32(chans, HW),
             f32(3, chans, HW),
             f32(depth, chans, HW),
             bf16(depth, chans, HW),
@@ -307,18 +349,15 @@
     got = exchange(total, "layer", 1 << (steps - 1))
     lanes = -(-(width + 1) // HALF) * HALF
     part = (depth * chans // shares, lanes)
-    guess = pltpu.VMEM(adjoint_guess.shape, jnp.float32)
-    adjoint_fixed, state_fixed, keep, send = call(
+    keep, send = call(
         functools.partial(grad_kernel, steps),
-        (
-            f32(*adjoint_guess.shape),
-            f32(*state_guess.shape),
-            f32(shares // 2, *part),
-            f32(shares // 2, *part),
-        ),
-        (got, *mine, adjoint_guess, state_guess, slope, patch, back_w),
-        hbm_out=(0, 1),
-        scratch=[guess, guess, pltpu.SemaphoreType.DMA((2,))],
+        (f32(shares // 2, *part), f32(shares // 2, *part)),
+        (got, *mine, guess, slope, patch, back_w),
+    )
+    adjoint_fixed, state_fixed = call(
+        functools.partial(fixed_kernel, steps),
+        (f32(*adjoint_guess.shape), f32(*state_guess.shape)),
+        (keep, got, *mine, adjoint_guess, state_guess),
     )
     keep, send = call(halve_kernel, (f32(*part), f32(*part)), (keep, exchange(send, "dp", 1)))
     weight_grad, bias_grad = call(

time: 25.9 us -> 25.9 us (level)
  waiting for transfers between devices: 10.2 us -> 9.49 us
  Pallas kernels: 5.22 us -> 5.8 us
    ppermute x5, waiting for transfers between devices: 10.2 us -> 9.49 us  [exchange(): lax.ppermute(x, axis, [(i, i ^ mask) for i in range(lax.axis_size(axis))])]
    pallas_call x7 -> x8, Pallas kernels: 5.22 us -> 5.8 us  [call(): pl.pallas_call(kernel, out_shape=out_shape, in_specs=[HBM if k in hbm_in...]
  transfers between devices with their start and end apart: 5 -> 5, of which waited for: 5 -> 5; matrix products, arithmetic and copies ran while one was open for 0% -> 0% of each run, Pallas kernels for 2% -> 5%
where the time goes in v10:
time: 25.9 us; the launch traced here: 25.7 us
  starting transfers between devices  9.7 us (37%)
  waiting for transfers between devices  9.49 us (37%)
  Pallas kernels  5.8 us (22%)
  between operations  0.68 us (3%)
    ppermute x5, starting transfers between devices, exchange(): lax.ppermute(x, axis, [(i, i ^ mask) for i in range(lax.axis_size(axis))])  9.7 us
    ppermute x5, waiting for transfers between devices, exchange(): lax.ppermute(x, axis, [(i, i ^ mask) for i in range(lax.axis_size(axis))])  9.49 us
    pallas_call x8, Pallas kernels, call(): pl.pallas_call(kernel, out_shape=out_shape, in_specs=[HBM if k in hbm_in...  5.8 us
  transfers between devices with their start and end apart: 5, of which 5 were waited for; matrix products, arithmetic and copies ran while one was open for 0% of the time, Pallas kernels for 5%

profile of v10, /device:TPU:0, one launch (start us, length us, event | category | flops | bytes accessed | tf_op | source)
XLA Modules:
  0.0 25.7 jit_solution(10599300938891820499)
XLA Ops:
  0.6 2.9 %shard_map.75 = (f32[32,256]{1,0:T(8,128)S(1)}, f32[3,32,256]{2,1,0:T(8,128)S(1)}, f32[4,32,256]{2,1,0:T(8,128)S(1)}, bf16[4,32,256]{2,1,0:T(8,128)(2,1)S(1)}, bf16[4,32,288]{2,1,0:T(8,128)(2,1)S(1)}) custom-call(f32[1,1,32,256]{3,2,1,0:T(8,128)} %start_ref.1, f32[1,1,32,256]{3,2,1,0:T(8,128)} %guess_ref.1, bf16[4,32,288]{2,1,0:T(8,128)(2,1)} %w_hbm.1, ...), custom_call_target="tpu_custom_call" | custom-call | flops 268435456 | bytes 1048576 | tf_op jit(solution)/shard_map/pallas_call | solution.py:298
  3.6 3.0 %collective-permute-start = (f32[3,32,256]{2,1,0:T(8,128)S(1)}, f32[3,32,256]{2,1,0:T(8,128)S(1)}, u32[]{:S(2)}, u32[]{:S(2)}) collective-permute-start(f32[3,32,256]{2,1,0:T(8,128)S(1)} %get-tuple-element.21.refs_0_), channel_id=1, source_target_pairs={{0,4},{4,0},{8,12},{12,8},{16,20},{20,16},{24,28},{28,24},{1,5},{5... | collective-permute-start | bytes 294920 | tf_op jit(solution)/shard_map/ppermute | solution.py:318
  6.6 2.8 %collective-permute-done.refs_1_ = f32[3,32,256]{2,1,0:T(8,128)S(1)} collective-permute-done((f32[3,32,256]{2,1,0:T(8,128)S(1)}, f32[3,32,256]{2,1,0:T(8,128)S(1)}, u32[]{:S(2)}, u32[]{:S(2)}) %collective-permute-start) | collective-permute-done | bytes 98336 | tf_op jit(solution)/shard_map/ppermute | solution.py:318
  9.4 2.0 %collective-permute-start.1 = (f32[3,32,256]{2,1,0:T(8,128)S(1)}, f32[3,32,256]{2,1,0:T(8,128)S(1)}, u32[]{:S(2)}, u32[]{:S(2)}) collective-permute-start(f32[3,32,256]{2,1,0:T(8,128)S(1)} %get-tuple-element.22.refs_0_), channel_id=1, source_target_pairs={{0,8},{4,12},{8,0},{12,4},{16,24},{20,28},{24,16},{28,20},{1,9},{5... | collective-permute-start | bytes 294920 | tf_op jit(solution)/shard_map/ppermute | solution.py:318
  11.4 2.7 %collective-permute-done.1.refs_1_ = f32[3,32,256]{2,1,0:T(8,128)S(1)} collective-permute-done((f32[3,32,256]{2,1,0:T(8,128)S(1)}, f32[3,32,256]{2,1,0:T(8,128)S(1)}, u32[]{:S(2)}, u32[]{:S(2)}) %collective-permute-start.1) | collective-permute-done | bytes 98336 | tf_op jit(solution)/shard_map/ppermute | solution.py:318
  14.1 3.0 %collective-permute-start.2 = (f32[32,256]{1,0:T(8,128)S(1)}, f32[32,256]{1,0:T(8,128)S(1)}, u32[]{:S(2)}, u32[]{:S(2)}) collective-permute-start(f32[32,256]{1,0:T(8,128)S(1)} %get-tuple-element.24), channel_id=1, source_target_pairs={{0,16},{4,20},{8,24},{12,28},{16,0},{20,4},{24,8},{28,12},{1,17},{... | collective-permute-start | bytes 98312 | tf_op jit(solution)/shard_map/ppermute | solution.py:318
  17.1 0.6 %shard_map.78.patch_ref = bf16[4,288,256]{2,1,0:T(8,128)(2,1)S(1)} custom-call(bf16[4,32,256]{2,1,0:T(8,128)(2,1)S(1)} %get-tuple-element.28.rounded_ref), custom_call_target="tpu_custom_call" | custom-call | flops 268435456 | bytes 1048576 | tf_op jit(solution)/shard_map/pallas_call | solution.py:298
  17.7 1.3 %collective-permute-done.2.got_ref = f32[32,256]{1,0:T(8,128)S(1)} collective-permute-done((f32[32,256]{1,0:T(8,128)S(1)}, f32[32,256]{1,0:T(8,128)S(1)}, u32[]{:S(2)}, u32[]{:S(2)}) %collective-permute-start.2) | collective-permute-done | bytes 32800 | tf_op jit(solution)/shard_map/ppermute | solution.py:318
  19.0 0.8 %shard_map.79 = (f32[2,32,384]{2,1,0:T(8,128)S(1)}, f32[2,32,384]{2,1,0:T(8,128)S(1)}) custom-call(f32[32,256]{1,0:T(8,128)S(1)} %collective-permute-done.2.got_ref, f32[4,32,256]{2,1,0:T(8,128)S(1)} %get-tuple-element.25.mine_ref, f32[32,256]{1,0:T(8,128)S(1)} %get-tuple-element.26.guess_ref, f32[4,32,256]{2,1,0:T(8,128)S(1)} %get-tuple-element.27.slope_ref, ...), custom_call_target="tpu_custom_call" | custom-call | flops 268435456 | bytes 1048576 | tf_op jit(solution)/shard_map/pallas_call | solution.py:298
  19.9 0.1 collective-permute-start.3
  19.9 1.3 %collective-permute-done.3.got_ref = f32[2,32,384]{2,1,0:T(8,128)S(1)} collective-permute-done((f32[2,32,384]{2,1,0:T(8,128)S(1)}, f32[2,32,384]{2,1,0:T(8,128)S(1)}, u32[]{:S(2)}, u32[]{:S(2)}) %collective-permute-start.3) | collective-permute-done | bytes 98336 | tf_op jit(solution)/shard_map/ppermute | solution.py:318
  21.2 0.0 copy-start
  21.2 0.0 copy-start.1
  21.2 1.7 %collective-permute-start.4 = (f32[32,384]{1,0:T(8,128)S(1)}, f32[32,384]{1,0:T(8,128)S(1)}, u32[]{:S(2)}, u32[]{:S(2)}) collective-permute-start(f32[32,384]{1,0:T(8,128)S(1)} %get-tuple-element.35), channel_id=1, source_target_pairs={{0,3},{1,2},{2,1},{3,0},{4,7},{5,6},{6,5},{7,4},{8,11},{9,10},{10,... | collective-permute-start | bytes 147464 | tf_op jit(solution)/shard_map/ppermute | solution.py:318
  22.9 0.0 copy-done
  22.9 0.0 copy-done.1
  22.9 0.7 %shard_map.80 = (f32[1,1,32,256]{3,2,1,0:T(8,128)}, f32[1,1,32,256]{3,2,1,0:T(8,128)}) custom-call(f32[2,32,384]{2,1,0:T(8,128)S(1)} %get-tuple-element.30._.mine_ref, f32[32,256]{1,0:T(8,128)S(1)} %collective-permute-done.2.got_ref, f32[4,32,256]{2,1,0:T(8,128)S(1)} %get-tuple-element.25.mine_ref, f32[1,1,32,256]{3,2,1,0:T(8,128)S(1)} %copy-done.1, ...), custom_call_target="tpu_custom_call" | custom-call | flops 268435456 | bytes 1048576 | tf_op jit(solution)/shard_map/pallas_call | solution.py:298
  23.7 1.4 %collective-permute-done.4.got_ref = f32[32,384]{1,0:T(8,128)S(1)} collective-permute-done((f32[32,384]{1,0:T(8,128)S(1)}, f32[32,384]{1,0:T(8,128)S(1)}, u32[]{:S(2)}, u32[]{:S(2)}) %collective-permute-start.4) | collective-permute-done | bytes 49184 | tf_op jit(solution)/shard_map/ppermute | solution.py:318
  25.0 0.7 %shard_map.82 = (f32[4,8,288]{2,1,0:T(8,128)}, f32[4,8]{1,0:T(4,128)}) custom-call(f32[32,384]{1,0:T(8,128)S(1)} %get-tuple-element.34.mine_ref, f32[32,384]{1,0:T(8,128)S(1)} %collective-permute-done.4.got_ref), custom_call_target="tpu_custom_call" | custom-call | flops 268435456 | bytes 1048576 | tf_op jit(solution)/shard_map/pallas_call | solution.py:298
  (3 shorter events, 0.1 us)
Async XLA Ops:
  3.6 5.8 %collective-permute-start = (f32[3,32,256]{2,1,0:T(8,128)S(1)}, f32[3,32,256]{2,1,0:T(8,128)S(1)}, u32[]{:S(2)}, u32[]{:S(2)}) collective-permute-start(f32[3,32,256]{2,1,0:T(8,128)S(1)} %get-tuple-element.21.refs_0_), channel_id=1, source_target_pairs={{0,4},{4,0},{8,12},{12,8},{16,20},{20,16},{24,28},{28,24},{1,5},{5... | collective-permute-start | bytes 294920 | tf_op jit(solution)/shard_map/ppermute | solution.py:318
  9.4 4.7 %collective-permute-start.1 = (f32[3,32,256]{2,1,0:T(8,128)S(1)}, f32[3,32,256]{2,1,0:T(8,128)S(1)}, u32[]{:S(2)}, u32[]{:S(2)}) collective-permute-start(f32[3,32,256]{2,1,0:T(8,128)S(1)} %get-tuple-element.22.refs_0_), channel_id=1, source_target_pairs={{0,8},{4,12},{8,0},{12,4},{16,24},{20,28},{24,16},{28,20},{1,9},{5... | collective-permute-start | bytes 294920 | tf_op jit(solution)/shard_map/ppermute | solution.py:318
  14.1 4.9 %collective-permute-start.2 = (f32[32,256]{1,0:T(8,128)S(1)}, f32[32,256]{1,0:T(8,128)S(1)}, u32[]{:S(2)}, u32[]{:S(2)}) collective-permute-start(f32[32,256]{1,0:T(8,128)S(1)} %get-tuple-element.24), channel_id=1, source_target_pairs={{0,16},{4,20},{8,24},{12,28},{16,0},{20,4},{24,8},{28,12},{1,17},{... | collective-permute-start | bytes 98312 | tf_op jit(solution)/shard_map/ppermute | solution.py:318
  19.9 1.4 %collective-permute-start.3 = (f32[2,32,384]{2,1,0:T(8,128)S(1)}, f32[2,32,384]{2,1,0:T(8,128)S(1)}, u32[]{:S(2)}, u32[]{:S(2)}) collective-permute-start(f32[2,32,384]{2,1,0:T(8,128)S(1)} %get-tuple-element.33), channel_id=1, source_target_pairs={{0,1},{1,0},{2,3},{3,2},{4,5},{5,4},{6,7},{7,6},{8,9},{9,8},{10,11... | collective-permute-start | bytes 294920 | tf_op jit(solution)/shard_map/ppermute | solution.py:318
  21.2 1.7 %copy-start = (f32[1,1,32,256]{3,2,1,0:T(8,128)S(1)}, f32[1,1,32,256]{3,2,1,0:T(8,128)}, u32[]{:S(2)}) copy-start(f32[1,1,32,256]{3,2,1,0:T(8,128)} %start_ref.1) | copy-start | bytes 98308
  21.2 1.7 %copy-start.1 = (f32[1,1,32,256]{3,2,1,0:T(8,128)S(1)}, f32[1,1,32,256]{3,2,1,0:T(8,128)}, u32[]{:S(2)}) copy-start(f32[1,1,32,256]{3,2,1,0:T(8,128)} %guess_ref.1) | copy-start | bytes 98308
  21.2 3.8 %collective-permute-start.4 = (f32[32,384]{1,0:T(8,128)S(1)}, f32[32,384]{1,0:T(8,128)S(1)}, u32[]{:S(2)}, u32[]{:S(2)}) collective-permute-start(f32[32,384]{1,0:T(8,128)S(1)} %get-tuple-element.35), channel_id=1, source_target_pairs={{0,3},{1,2},{2,1},{3,0},{4,7},{5,6},{6,5},{7,4},{8,11},{9,10},{10,... | collective-permute-start | bytes 147464 | tf_op jit(solution)/shard_map/ppermute | solution.py:318

commit v11 on v10

--- a/solution.py
+++ b/solution.py
@@ -201,25 +201,45 @@
     return lax.rem(lax.div(lax.axis_index(axis), 2**step), 2) == 1
 
 
-def join_kernel(step, final, *refs):
+def join_kernel(step, narrow, *refs):
     if step == 1:
-        total_ref, got_ref, sent_ref, mine_out = refs
+        total_ref, got_ref, sent_ref, fwd_out, mine_out = refs
         one = jnp.ones(total_ref.shape[1:], jnp.float32)
         zero = jnp.zeros(total_ref.shape[1:], jnp.float32)
         mine = (one, zero, one, zero)
     else:
-        total_ref, got_ref, mine_ref, sent_ref, mine_out = refs
+        total_ref, got_ref, mine_ref, sent_ref, fwd_out, mine_out = refs
         mine = tuple(mine_ref[k] for k in range(4))
     total = tuple(total_ref[k] for k in range(3))
     got = tuple(got_ref[k] for k in range(3))
-    total, mine = joined(bit_of("layer", step - 1), total, mine, got)
+    (gain, fwd, bwd), mine = joined(bit_of("layer", step - 1), total, mine, got)
     for k in range(4):
         mine_out[k] = mine[k]
-    if final:
-        sent_ref[...] = jnp.where(bit_of("layer", step), total[2], total[1])
+    fwd_out[...] = fwd
+    sent_ref[0] = gain
+    if narrow:
+        first = jnp.logical_not(jnp.logical_or(bit_of("layer", step), bit_of("layer", step + 1)))
+        sent_ref[1] = jnp.where(first, fwd, bwd)
     else:
-        for k in range(3):
-            sent_ref[k] = total[k]
+        sent_ref[1] = fwd
+        sent_ref[2] = bwd
+
+
+def quarters_kernel(steps, total_ref, fwd_ref, got_ref, mine_ref, sent_ref, late_ref, mine_out):
+    odd, upper = bit_of("layer", steps - 2), bit_of("layer", steps - 1)
+    gain, bwd, fwd = total_ref[0], total_ref[1], fwd_ref[...]
+    got_gain, got = got_ref[0], got_ref[1]
+    pre_gain, pre, post_gain, post = (mine_ref[k] for k in range(4))
+    low_fwd = gain * got + fwd
+    up_bwd = jnp.where(odd, got_gain * bwd + got, gain * got + bwd)
+    sent_ref[...] = jnp.where(upper, up_bwd, low_fwd)
+    late_ref[...] = jnp.where(upper, fwd, low_fwd)
+    second = jnp.logical_and(odd, jnp.logical_not(upper))
+    mine_out[0] = pre_gain
+    mine_out[1] = jnp.where(second, pre_gain * got + pre, pre)
+    mine_out[2] = jnp.where(odd, post_gain, post_gain * got_gain)
+    mine_out[3] = jnp.where(odd, post, post_gain * got + post)
+    mine_out[4] = got_gain
 
 
 def later_fixed(steps, got_ref, mine_ref):
@@ -227,11 +247,13 @@
     return mine_ref[3] + got
 
 
-def fixed_kernel(steps, _, got_ref, mine_ref, guess_ref, start_ref, adj_ref, state_ref):
+def fixed_kernel(steps, _, got_ref, late_ref, mine_ref, guess_ref, start_ref, adj_ref, state_ref):
+    odd, upper = bit_of("layer", steps - 2), bit_of("layer", steps - 1)
     place = lax.axis_index("layer")
     adj = in_order(later_fixed(steps, got_ref, mine_ref))
-    got = jnp.where(bit_of("layer", steps - 1), mine_ref[0] * got_ref[...], 0.0)
-    state = in_order(mine_ref[1] + got)
+    late = late_ref[...]
+    came = jnp.where(odd, mine_ref[4] * got_ref[...] + late, late)
+    state = in_order(mine_ref[1] + jnp.where(upper, mine_ref[0] * came, 0.0))
     adj_ref[0, 0] = jnp.where(place == lax.axis_size("layer") - 1, guess_ref[0, 0], adj)
     state_ref[0, 0] = jnp.where(place == 0, start_ref[0, 0], state)
 
@@ -244,16 +266,14 @@
     slope_ref,
     patch_ref,
     back_w_ref,
-    keep_ref,
-    send_ref,
+    parts_ref,
 ):
     depth, chans, rows = back_w_ref.shape
-    shares = 2 * keep_ref.shape[0]
+    shares = parts_ref.shape[0]
     own = chans // shares
     last = lax.axis_index("layer") == lax.axis_size("layer") - 1
     adj = jnp.where(last, guess_ref[...], later_fixed(steps, got_ref, mine_ref))
-    pad = keep_ref.shape[2] - rows
-    odd, high = bit_of("dp", 0), bit_of("dp", 1)
+    pad = parts_ref.shape[2] - rows
 
     def layer(n, adj):
         dz = adj * slope_ref[n]
@@ -261,12 +281,9 @@
         grad = dot(dzb, patch_ref[n], ((1,), (1,)))
         bias = jnp.broadcast_to(jnp.sum(dz, axis=1, keepdims=True), (chans, pad))
         both = jnp.concatenate([grad, bias], axis=1)
-        parts = [both[s * own : (s + 1) * own] for s in range(shares)]
-        parts = [jnp.where(odd, parts[i ^ 1], parts[i]) for i in range(shares)]
-        parts = [jnp.where(high, parts[i ^ 2], parts[i]) for i in range(shares)]
         where = pl.ds(pl.multiple_of(n * own, own), own)
-        keep_ref[0, where], keep_ref[1, where] = parts[0], parts[3]
-        send_ref[0, where], send_ref[1, where] = parts[1], parts[2]
+        for k in range(shares):
+            parts_ref[k, where] = both[k * own : (k + 1) * own]
         return dzb
 
     def behind(i, adj):
@@ -274,6 +291,15 @@
         return adj + convolve(back_w_ref[n], layer(n, adj))
 
     layer(0, lax.fori_loop(0, depth - 1, behind, adj))
+
+
+def deal_kernel(_, parts_ref, keep_ref, send_ref):
+    odd, high = bit_of("dp", 0), bit_of("dp", 1)
+    parts = [parts_ref[i] for i in range(parts_ref.shape[0])]
+    parts = [jnp.where(odd, parts[i ^ 1], parts[i]) for i in range(len(parts))]
+    parts = [jnp.where(high, parts[i ^ 2], parts[i]) for i in range(len(parts))]
+    keep_ref[0], keep_ref[1] = parts[0], parts[3]
+    send_ref[0], send_ref[1] = parts[1], parts[2]
 
 
 def halve_kernel(mine_ref, got_ref, keep_ref, send_ref):
@@ -294,7 +320,7 @@
         bias_ref[n : n + 1, :] = jnp.sum(jnp.where(eye, column, 0.0), axis=0, keepdims=True)
 
 
-def call(kernel, out_shape, args, hbm_in=(), hbm_out=(), scratch=()):
+def call(kernel, out_shape, args, hbm_in=(), hbm_out=(), scratch=(), work=2**28):
     return pl.pallas_call(
         kernel,
         out_shape=out_shape,
@@ -302,7 +328,7 @@
         out_specs=[HBM if k in hbm_out else VMEM for k in range(len(out_shape))],
         scratch_shapes=list(scratch),
         compiler_params=pltpu.CompilerParams(vmem_limit_bytes=LIMIT),
-        cost_estimate=pl.CostEstimate(flops=2**28, bytes_accessed=2**20, transcendentals=0),
+        cost_estimate=pl.CostEstimate(flops=work, bytes_accessed=work // 256, transcendentals=0),
     )(*(pltpu.with_memory_space_constraint(a, pltpu.HBM) if k in hbm_in else a for k, a in enumerate(args)))
 
 
@@ -338,26 +364,42 @@
     )
     (patch,) = call(patch_kernel, (bf16(depth, width, HW),), (rounded,))
     mine = ()
-    for step in range(1, steps):
+    one = f32(chans, HW)
+    for step in range(1, steps - 1):
         got = exchange(total, "layer", 1 << (step - 1))
-        final = step == steps - 1
-        total, *mine = call(
-            functools.partial(join_kernel, step, final),
-            (f32(chans, HW) if final else f32(3, chans, HW), f32(4, chans, HW)),
+        narrow = step == steps - 2
+        total, fwd, *mine = call(
+            functools.partial(join_kernel, step, narrow),
+            (f32(2 if narrow else 3, chans, HW), one, f32(4, chans, HW)),
             (total, got, *mine),
         )
+    got = exchange(total, "layer", 1 << (steps - 2))
+    total, late, *mine = call(
+        functools.partial(quarters_kernel, steps),
+        (one, one, f32(5, chans, HW)),
+        (total, fwd, got, *mine),
+    )
     got = exchange(total, "layer", 1 << (steps - 1))
+    quarter = 1 << (steps - 2)
+    late = lax.ppermute(late, "layer", [(i, i + quarter) for i in range(quarter, 3 * quarter)])
     lanes = -(-(width + 1) // HALF) * HALF
     part = (depth * chans // shares, lanes)
+    (parts,) = call(
+        functools.partial(grad_kernel, steps),
+        (f32(shares, *part),),
+        (got, *mine, guess, slope, patch, back_w),
+        work=0,
+    )
     keep, send = call(
-        functools.partial(grad_kernel, steps),
+        deal_kernel,
         (f32(shares // 2, *part), f32(shares // 2, *part)),
-        (got, *mine, guess, slope, patch, back_w),
+        (late, parts),
+        work=0,
     )
     adjoint_fixed, state_fixed = call(
         functools.partial(fixed_kernel, steps),
         (f32(*adjoint_guess.shape), f32(*state_guess.shape)),
-        (keep, got, *mine, adjoint_guess, state_guess),
+        (keep, got, late, *mine, adjoint_guess, state_guess),
     )
     keep, send = call(halve_kernel, (f32(*part), f32(*part)), (keep, exchange(send, "dp", 1)))
     weight_grad, bias_grad = call(

time: 25.9 us -> 25.6 us (0.988)
  waiting for transfers between devices: 9.49 us -> 8.49 us
  starting transfers between devices: 9.7 us -> 10.4 us
    ppermute x5, waiting for transfers between devices: 9.49 us -> 8.48 us  [exchange(): lax.ppermute(x, axis, [(i, i ^ mask) for i in range(lax.axis_size(axis))])]
    ppermute x0 -> x1, starting transfers between devices: none -> 0.65 us  [local(): lax.ppermute(late, 'layer', [(i, i + quarter) for i in range(quarter, 3 *...]
    pallas_call x8 -> x9, Pallas kernels: 5.8 us -> 5.86 us  [call(): pl.pallas_call(kernel, out_shape=out_shape, in_specs=[HBM if k in hbm_in...]
  transfers between devices with their start and end apart: 5 -> 6, of which waited for: 5 -> 5; matrix products, arithmetic and copies ran while one was open for 0% -> 0% of each run, Pallas kernels for 5% -> 8%
where the time goes in v11:
time: 25.6 us; the launch traced here: 25.4 us
  starting transfers between devices  10.4 us (41%)
  waiting for transfers between devices  8.49 us (33%)
  Pallas kernels  5.86 us (23%)
  between operations  0.7 us (3%)
    ppermute x5, starting transfers between devices, exchange(): lax.ppermute(x, axis, [(i, i ^ mask) for i in range(lax.axis_size(axis))])  9.7 us
    ppermute x5, waiting for transfers between devices, exchange(): lax.ppermute(x, axis, [(i, i ^ mask) for i in range(lax.axis_size(axis))])  8.48 us
    pallas_call x9, Pallas kernels, call(): pl.pallas_call(kernel, out_shape=out_shape, in_specs=[HBM if k in hbm_in...  5.86 us
    ppermute x1, starting transfers between devices, local(): lax.ppermute(late, 'layer', [(i, i + quarter) for i in range(quarter, 3 *...  0.65 us
  transfers between devices with their start and end apart: 6, of which 5 were waited for; matrix products, arithmetic and copies ran while one was open for 0% of the time, Pallas kernels for 8%

profile of v11, /device:TPU:0, one launch (start us, length us, event | category | flops | bytes accessed | tf_op | source)
XLA Modules:
  0.0 25.4 jit_solution(11528396982626154914)
XLA Ops:
  0.6 2.9 %shard_map.75 = (f32[32,256]{1,0:T(8,128)S(1)}, f32[3,32,256]{2,1,0:T(8,128)S(1)}, f32[4,32,256]{2,1,0:T(8,128)S(1)}, bf16[4,32,256]{2,1,0:T(8,128)(2,1)S(1)}, bf16[4,32,288]{2,1,0:T(8,128)(2,1)S(1)}) custom-call(f32[1,1,32,256]{3,2,1,0:T(8,128)} %start_ref.1, f32[1,1,32,256]{3,2,1,0:T(8,128)} %guess_ref.1, bf16[4,32,288]{2,1,0:T(8,128)(2,1)} %w_hbm.1, ...), custom_call_target="tpu_custom_call" | custom-call | flops 268435456 | bytes 1048576 | tf_op jit(solution)/shard_map/pallas_call | solution.py:324
  3.6 3.0 %collective-permute-start = (f32[3,32,256]{2,1,0:T(8,128)S(1)}, f32[3,32,256]{2,1,0:T(8,128)S(1)}, u32[]{:S(2)}, u32[]{:S(2)}) collective-permute-start(f32[3,32,256]{2,1,0:T(8,128)S(1)} %get-tuple-element.23.refs_0_), channel_id=1, source_target_pairs={{0,4},{4,0},{8,12},{12,8},{16,20},{20,16},{24,28},{28,24},{1,5},{5... | collective-permute-start | bytes 294920 | tf_op jit(solution)/shard_map/ppermute | solution.py:344
  6.6 2.8 %collective-permute-done.refs_1_ = f32[3,32,256]{2,1,0:T(8,128)S(1)} collective-permute-done((f32[3,32,256]{2,1,0:T(8,128)S(1)}, f32[3,32,256]{2,1,0:T(8,128)S(1)}, u32[]{:S(2)}, u32[]{:S(2)}) %collective-permute-start) | collective-permute-done | bytes 98336 | tf_op jit(solution)/shard_map/ppermute | solution.py:344
  9.4 2.0 %collective-permute-start.1 = (f32[2,32,256]{2,1,0:T(8,128)S(1)}, f32[2,32,256]{2,1,0:T(8,128)S(1)}, u32[]{:S(2)}, u32[]{:S(2)}) collective-permute-start(f32[2,32,256]{2,1,0:T(8,128)S(1)} %get-tuple-element.24.total_ref), channel_id=1, source_target_pairs={{0,8},{4,12},{8,0},{12,4},{16,24},{20,28},{24,16},{28,20},{1,9},{5... | collective-permute-start | bytes 196616 | tf_op jit(solution)/shard_map/ppermute | solution.py:344
  11.4 2.4 %collective-permute-done.1.got_ref = f32[2,32,256]{2,1,0:T(8,128)S(1)} collective-permute-done((f32[2,32,256]{2,1,0:T(8,128)S(1)}, f32[2,32,256]{2,1,0:T(8,128)S(1)}, u32[]{:S(2)}, u32[]{:S(2)}) %collective-permute-start.1) | collective-permute-done | bytes 65568 | tf_op jit(solution)/shard_map/ppermute | solution.py:344
  13.8 3.0 %collective-permute-start.3 = (f32[32,256]{1,0:T(8,128)S(1)}, f32[32,256]{1,0:T(8,128)S(1)}, u32[]{:S(2)}, u32[]{:S(2)}) collective-permute-start(f32[32,256]{1,0:T(8,128)S(1)} %get-tuple-element.28), channel_id=1, source_target_pairs={{0,16},{4,20},{8,24},{12,28},{16,0},{20,4},{24,8},{28,12},{1,17},{... | collective-permute-start | bytes 98312 | tf_op jit(solution)/shard_map/ppermute | solution.py:344
  16.7 0.7 %collective-permute-start.2 = (f32[32,256]{1,0:T(8,128)S(1)}, f32[32,256]{1,0:T(8,128)S(1)}, u32[]{:S(2)}, u32[]{:S(2)}) collective-permute-start(f32[32,256]{1,0:T(8,128)S(1)} %get-tuple-element.27), channel_id=1, source_target_pairs={{8,16},{12,20},{16,24},{20,28},{9,17},{13,21},{17,25},{21,29},{10,... | collective-permute-start | bytes 98312 | tf_op jit(solution)/shard_map/ppermute | solution.py:384
  17.4 0.6 %shard_map.78.patch_ref = bf16[4,288,256]{2,1,0:T(8,128)(2,1)S(1)} custom-call(bf16[4,32,256]{2,1,0:T(8,128)(2,1)S(1)} %get-tuple-element.32.rounded_ref), custom_call_target="tpu_custom_call" | custom-call | flops 268435456 | bytes 1048576 | tf_op jit(solution)/shard_map/pallas_call | solution.py:324
  18.0 0.7 %collective-permute-done.3.got_ref = f32[32,256]{1,0:T(8,128)S(1)} collective-permute-done((f32[32,256]{1,0:T(8,128)S(1)}, f32[32,256]{1,0:T(8,128)S(1)}, u32[]{:S(2)}, u32[]{:S(2)}) %collective-permute-start.3) | collective-permute-done | bytes 32800 | tf_op jit(solution)/shard_map/ppermute | solution.py:344
  18.6 0.8 %shard_map.79.parts_ref = f32[4,32,384]{2,1,0:T(8,128)S(1)} custom-call(f32[32,256]{1,0:T(8,128)S(1)} %collective-permute-done.3.got_ref, f32[5,32,256]{2,1,0:T(8,128)S(1)} %get-tuple-element.29.mine_ref, f32[32,256]{1,0:T(8,128)S(1)} %get-tuple-element.30.guess_ref, f32[4,32,256]{2,1,0:T(8,128)S(1)} %get-tuple-element.31.slope_ref, ...), custom_call_target="tpu_custom_call" | custom-call | tf_op jit(solution)/shard_map/pallas_call | solution.py:324
  19.5 0.0 collective-permute-done.2._.late_ref
  19.5 0.1 shard_map.80
  19.6 0.1 collective-permute-start.4
  19.7 1.3 %collective-permute-done.4.got_ref = f32[2,32,384]{2,1,0:T(8,128)S(1)} collective-permute-done((f32[2,32,384]{2,1,0:T(8,128)S(1)}, f32[2,32,384]{2,1,0:T(8,128)S(1)}, u32[]{:S(2)}, u32[]{:S(2)}) %collective-permute-start.4) | collective-permute-done | bytes 98336 | tf_op jit(solution)/shard_map/ppermute | solution.py:344
  20.9 0.0 copy-start
  20.9 0.0 copy-start.1
  21.0 1.7 %collective-permute-start.5 = (f32[32,384]{1,0:T(8,128)S(1)}, f32[32,384]{1,0:T(8,128)S(1)}, u32[]{:S(2)}, u32[]{:S(2)}) collective-permute-start(f32[32,384]{1,0:T(8,128)S(1)} %get-tuple-element.39), channel_id=1, source_target_pairs={{0,3},{1,2},{2,1},{3,0},{4,7},{5,6},{6,5},{7,4},{8,11},{9,10},{10,... | collective-permute-start | bytes 147464 | tf_op jit(solution)/shard_map/ppermute | solution.py:344
  22.6 0.0 copy-done
  22.6 0.0 copy-done.1
  22.6 0.7 %shard_map.81 = (f32[1,1,32,256]{3,2,1,0:T(8,128)}, f32[1,1,32,256]{3,2,1,0:T(8,128)}) custom-call(f32[2,32,384]{2,1,0:T(8,128)S(1)} %get-tuple-element.34._.mine_ref, f32[32,256]{1,0:T(8,128)S(1)} %collective-permute-done.3.got_ref, f32[32,256]{1,0:T(8,128)S(1)} %collective-permute-done.2._.late_ref, f32[5,32,256]{2,1,0:T(8,128)S(1)} %get-tuple-element.29.mine_ref, ...), custom_call_target="tpu_custom_call" | custom-call | flops 268435456 | bytes 1048576 | tf_op jit(solution)/shard_map/pallas_call | solution.py:324
  23.4 1.4 %collective-permute-done.5.got_ref = f32[32,384]{1,0:T(8,128)S(1)} collective-permute-done((f32[32,384]{1,0:T(8,128)S(1)}, f32[32,384]{1,0:T(8,128)S(1)}, u32[]{:S(2)}, u32[]{:S(2)}) %collective-permute-start.5) | collective-permute-done | bytes 49184 | tf_op jit(solution)/shard_map/ppermute | solution.py:344
  24.8 0.7 %shard_map.83 = (f32[4,8,288]{2,1,0:T(8,128)}, f32[4,8]{1,0:T(4,128)}) custom-call(f32[32,384]{1,0:T(8,128)S(1)} %get-tuple-element.38.mine_ref, f32[32,384]{1,0:T(8,128)S(1)} %collective-permute-done.5.got_ref), custom_call_target="tpu_custom_call" | custom-call | flops 268435456 | bytes 1048576 | tf_op jit(solution)/shard_map/pallas_call | solution.py:324
  (3 shorter events, 0.1 us)
Async XLA Ops:
  3.6 5.8 %collective-permute-start = (f32[3,32,256]{2,1,0:T(8,128)S(1)}, f32[3,32,256]{2,1,0:T(8,128)S(1)}, u32[]{:S(2)}, u32[]{:S(2)}) collective-permute-start(f32[3,32,256]{2,1,0:T(8,128)S(1)} %get-tuple-element.23.refs_0_), channel_id=1, source_target_pairs={{0,4},{4,0},{8,12},{12,8},{16,20},{20,16},{24,28},{28,24},{1,5},{5... | collective-permute-start | bytes 294920 | tf_op jit(solution)/shard_map/ppermute | solution.py:344
  9.4 4.3 %collective-permute-start.1 = (f32[2,32,256]{2,1,0:T(8,128)S(1)}, f32[2,32,256]{2,1,0:T(8,128)S(1)}, u32[]{:S(2)}, u32[]{:S(2)}) collective-permute-start(f32[2,32,256]{2,1,0:T(8,128)S(1)} %get-tuple-element.24.total_ref), channel_id=1, source_target_pairs={{0,8},{4,12},{8,0},{12,4},{16,24},{20,28},{24,16},{28,20},{1,9},{5... | collective-permute-start | bytes 196616 | tf_op jit(solution)/shard_map/ppermute | solution.py:344
  13.8 4.9 %collective-permute-start.3 = (f32[32,256]{1,0:T(8,128)S(1)}, f32[32,256]{1,0:T(8,128)S(1)}, u32[]{:S(2)}, u32[]{:S(2)}) collective-permute-start(f32[32,256]{1,0:T(8,128)S(1)} %get-tuple-element.28), channel_id=1, source_target_pairs={{0,16},{4,20},{8,24},{12,28},{16,0},{20,4},{24,8},{28,12},{1,17},{... | collective-permute-start | bytes 98312 | tf_op jit(solution)/shard_map/ppermute | solution.py:344
  16.7 2.7 %collective-permute-start.2 = (f32[32,256]{1,0:T(8,128)S(1)}, f32[32,256]{1,0:T(8,128)S(1)}, u32[]{:S(2)}, u32[]{:S(2)}) collective-permute-start(f32[32,256]{1,0:T(8,128)S(1)} %get-tuple-element.27), channel_id=1, source_target_pairs={{8,16},{12,20},{16,24},{20,28},{9,17},{13,21},{17,25},{21,29},{10,... | collective-permute-start | bytes 98312 | tf_op jit(solution)/shard_map/ppermute | solution.py:384
  19.6 1.4 %collective-permute-start.4 = (f32[2,32,384]{2,1,0:T(8,128)S(1)}, f32[2,32,384]{2,1,0:T(8,128)S(1)}, u32[]{:S(2)}, u32[]{:S(2)}) collective-permute-start(f32[2,32,384]{2,1,0:T(8,128)S(1)} %get-tuple-element.37), channel_id=1, source_target_pairs={{0,1},{1,0},{2,3},{3,2},{4,5},{5,4},{6,7},{7,6},{8,9},{9,8},{10,11... | collective-permute-start | bytes 294920 | tf_op jit(solution)/shard_map/ppermute | solution.py:344
  20.9 1.7 %copy-start = (f32[1,1,32,256]{3,2,1,0:T(8,128)S(1)}, f32[1,1,32,256]{3,2,1,0:T(8,128)}, u32[]{:S(2)}) copy-start(f32[1,1,32,256]{3,2,1,0:T(8,128)} %start_ref.1) | copy-start | bytes 98308
  20.9 1.7 %copy-start.1 = (f32[1,1,32,256]{3,2,1,0:T(8,128)S(1)}, f32[1,1,32,256]{3,2,1,0:T(8,128)}, u32[]{:S(2)}) copy-start(f32[1,1,32,256]{3,2,1,0:T(8,128)} %guess_ref.1) | copy-start | bytes 98308
  21.0 3.8 %collective-permute-start.5 = (f32[32,384]{1,0:T(8,128)S(1)}, f32[32,384]{1,0:T(8,128)S(1)}, u32[]{:S(2)}, u32[]{:S(2)}) collective-permute-start(f32[32,384]{1,0:T(8,128)S(1)} %get-tuple-element.39), channel_id=1, source_target_pairs={{0,3},{1,2},{2,1},{3,0},{4,7},{5,6},{6,5},{7,4},{8,11},{9,10},{10,... | collective-permute-start | bytes 147464 | tf_op jit(solution)/shard_map/ppermute | solution.py:344

commit v12 on v11

--- a/solution.py
+++ b/solution.py
@@ -76,9 +76,8 @@
         above.append((turned(odd, -1, right), same[0]))
         here.append(same)
         below.append((same[1], turned(even, 1, right)))
-    return jnp.concatenate(
-        [jnp.concatenate(pair, axis=1) for pair in above + here + below], axis=0
-    )
+    pairs = above + here + below
+    return [jnp.concatenate([pair[half] for pair in pairs], axis=0) for half in range(2)]
 
 
 def permutation(chans):
@@ -94,7 +93,7 @@
 
 
 def convolve(weight, values):
-    return dot(weight, taps_of(values), ((1,), (0,)))
+    return jnp.concatenate([dot(weight, half, ((1,), (0,))) for half in taps_of(values)], axis=1)
 
 
 def relax_kernel(
@@ -126,15 +125,13 @@
     eye = lax.broadcasted_iota(jnp.int32, (chans, chans), 0) == lax.broadcasted_iota(
         jnp.int32, (chans, chans), 1
     )
-    for copy in copies:
+    for copy in copies[:-1]:
         copy.wait()
     weights = w_ref[...].reshape(depth * chans, width)
     by_tap = dot(weights, perm, ((1,), (1,)))
     turned = dot(perm, weights, ((1,), (1,))).astype(jnp.bfloat16)
     middle = TAPS // 2 * chans
     start = by_parity(state_ref[0, 0])
-    guess = by_parity(adj_ref[0, 0])
-    guess_ref[...] = guess
     state = start
     gain = None
     slopes = []
@@ -160,6 +157,9 @@
         )
         back_w_ref[n] = back_w
         backs.append(back_w)
+    copies[-1].wait()
+    guess = by_parity(adj_ref[0, 0])
+    guess_ref[...] = guess
     back = guess
     for n in reversed(range(depth)):
         back = back + convolve(backs[n], (back * slopes[n]).astype(jnp.bfloat16))
@@ -175,8 +175,9 @@
     depth, chans, _ = rounded_ref.shape
     perm = permutation(chans)
     for n in range(depth):
-        patch = taps_of(rounded_ref[n])
-        patch_ref[n] = dot(perm, patch, ((0,), (0,))).astype(jnp.bfloat16)
+        for k, half in enumerate(taps_of(rounded_ref[n])):
+            patch = dot(half, perm, ((0,), (0,))).astype(jnp.bfloat16)
+            patch_ref[n, k * HALF : (k + 1) * HALF] = patch
 
 
 def joined(bit, total, mine, got):
@@ -278,7 +279,7 @@
     def layer(n, adj):
         dz = adj * slope_ref[n]
         dzb = dz.astype(jnp.bfloat16)
-        grad = dot(dzb, patch_ref[n], ((1,), (1,)))
+        grad = dot(dzb, patch_ref[n], ((1,), (0,)))
         bias = jnp.broadcast_to(jnp.sum(dz, axis=1, keepdims=True), (chans, pad))
         both = jnp.concatenate([grad, bias], axis=1)
         where = pl.ds(pl.multiple_of(n * own, own), own)
@@ -362,7 +363,7 @@
         hbm_in=range(4),
         scratch=[pltpu.VMEM(a.shape, a.dtype) for a in args] + [pltpu.SemaphoreType.DMA((4,))],
     )
-    (patch,) = call(patch_kernel, (bf16(depth, width, HW),), (rounded,))
+    (patch,) = call(patch_kernel, (bf16(depth, HW, width),), (rounded,))
     mine = ()
     one = f32(chans, HW)
     for step in range(1, steps - 1):

time: 25.6 us -> 25.6 us (level)
  waiting for transfers between devices: 8.49 us -> 8.07 us
  Pallas kernels: 5.86 us -> 6.25 us
    ppermute x5, waiting for transfers between devices: 8.48 us -> 8.07 us  [exchange(): lax.ppermute(x, axis, [(i, i ^ mask) for i in range(lax.axis_size(axis))])]
    pallas_call x9, Pallas kernels: 5.86 us -> 6.25 us  [call(): pl.pallas_call(kernel, out_shape=out_shape, in_specs=[HBM if k in hbm_in...]
  transfers between devices with their start and end apart: 6 -> 6, of which waited for: 5 -> 5; matrix products, arithmetic and copies ran while one was open for 0% -> 0% of each run, Pallas kernels for 8% -> 10%
where the time goes in v12:
time: 25.6 us; the launch traced here: 25.4 us
  starting transfers between devices  10.4 us (41%)
  waiting for transfers between devices  8.07 us (32%)
  Pallas kernels  6.25 us (24%)
  between operations  0.7 us (3%)
    ppermute x5, starting transfers between devices, exchange(): lax.ppermute(x, axis, [(i, i ^ mask) for i in range(lax.axis_size(axis))])  9.7 us
    ppermute x5, waiting for transfers between devices, exchange(): lax.ppermute(x, axis, [(i, i ^ mask) for i in range(lax.axis_size(axis))])  8.07 us
    pallas_call x9, Pallas kernels, call(): pl.pallas_call(kernel, out_shape=out_shape, in_specs=[HBM if k in hbm_in...  6.25 us
    ppermute x1, starting transfers between devices, local(): lax.ppermute(late, 'layer', [(i, i + quarter) for i in range(quarter, 3 *...  0.65 us
  transfers between devices with their start and end apart: 6, of which 5 were waited for; matrix products, arithmetic and copies ran while one was open for 0% of the time, Pallas kernels for 10%

profile of v12, /device:TPU:0, one launch (start us, length us, event | category | flops | bytes accessed | tf_op | source)
XLA Modules:
  0.0 25.4 jit_solution(16137937718523052247)
XLA Ops:
  0.6 2.9 %shard_map.75 = (f32[32,256]{1,0:T(8,128)S(1)}, f32[3,32,256]{2,1,0:T(8,128)S(1)}, f32[4,32,256]{2,1,0:T(8,128)S(1)}, bf16[4,32,256]{2,1,0:T(8,128)(2,1)S(1)}, bf16[4,32,288]{2,1,0:T(8,128)(2,1)S(1)}) custom-call(f32[1,1,32,256]{3,2,1,0:T(8,128)} %start_ref.1, f32[1,1,32,256]{3,2,1,0:T(8,128)} %guess_ref.1, bf16[4,32,288]{2,1,0:T(8,128)(2,1)} %w_hbm.1, ...), custom_call_target="tpu_custom_call" | custom-call | flops 268435456 | bytes 1048576 | tf_op jit(solution)/shard_map/pallas_call | solution.py:325
  3.6 3.0 %collective-permute-start = (f32[3,32,256]{2,1,0:T(8,128)S(1)}, f32[3,32,256]{2,1,0:T(8,128)S(1)}, u32[]{:S(2)}, u32[]{:S(2)}) collective-permute-start(f32[3,32,256]{2,1,0:T(8,128)S(1)} %get-tuple-element.23.refs_0_), channel_id=1, source_target_pairs={{0,4},{4,0},{8,12},{12,8},{16,20},{20,16},{24,28},{28,24},{1,5},{5... | collective-permute-start | bytes 294920 | tf_op jit(solution)/shard_map/ppermute | solution.py:345
  6.6 2.8 %collective-permute-done.refs_1_ = f32[3,32,256]{2,1,0:T(8,128)S(1)} collective-permute-done((f32[3,32,256]{2,1,0:T(8,128)S(1)}, f32[3,32,256]{2,1,0:T(8,128)S(1)}, u32[]{:S(2)}, u32[]{:S(2)}) %collective-permute-start) | collective-permute-done | bytes 98336 | tf_op jit(solution)/shard_map/ppermute | solution.py:345
  9.4 2.0 %collective-permute-start.1 = (f32[2,32,256]{2,1,0:T(8,128)S(1)}, f32[2,32,256]{2,1,0:T(8,128)S(1)}, u32[]{:S(2)}, u32[]{:S(2)}) collective-permute-start(f32[2,32,256]{2,1,0:T(8,128)S(1)} %get-tuple-element.24.total_ref), channel_id=1, source_target_pairs={{0,8},{4,12},{8,0},{12,4},{16,24},{20,28},{24,16},{28,20},{1,9},{5... | collective-permute-start | bytes 196616 | tf_op jit(solution)/shard_map/ppermute | solution.py:345
  11.4 2.4 %collective-permute-done.1.got_ref = f32[2,32,256]{2,1,0:T(8,128)S(1)} collective-permute-done((f32[2,32,256]{2,1,0:T(8,128)S(1)}, f32[2,32,256]{2,1,0:T(8,128)S(1)}, u32[]{:S(2)}, u32[]{:S(2)}) %collective-permute-start.1) | collective-permute-done | bytes 65568 | tf_op jit(solution)/shard_map/ppermute | solution.py:345
  13.8 3.0 %collective-permute-start.3 = (f32[32,256]{1,0:T(8,128)S(1)}, f32[32,256]{1,0:T(8,128)S(1)}, u32[]{:S(2)}, u32[]{:S(2)}) collective-permute-start(f32[32,256]{1,0:T(8,128)S(1)} %get-tuple-element.28), channel_id=1, source_target_pairs={{0,16},{4,20},{8,24},{12,28},{16,0},{20,4},{24,8},{28,12},{1,17},{... | collective-permute-start | bytes 98312 | tf_op jit(solution)/shard_map/ppermute | solution.py:345
  16.7 0.7 %collective-permute-start.2 = (f32[32,256]{1,0:T(8,128)S(1)}, f32[32,256]{1,0:T(8,128)S(1)}, u32[]{:S(2)}, u32[]{:S(2)}) collective-permute-start(f32[32,256]{1,0:T(8,128)S(1)} %get-tuple-element.27), channel_id=1, source_target_pairs={{8,16},{12,20},{16,24},{20,28},{9,17},{13,21},{17,25},{21,29},{10,... | collective-permute-start | bytes 98312 | tf_op jit(solution)/shard_map/ppermute | solution.py:385
  17.4 1.0 %shard_map.78.patch_ref = bf16[4,256,288]{2,1,0:T(8,128)(2,1)S(1)} custom-call(bf16[4,32,256]{2,1,0:T(8,128)(2,1)S(1)} %get-tuple-element.32.rounded_ref), custom_call_target="tpu_custom_call" | custom-call | flops 268435456 | bytes 1048576 | tf_op jit(solution)/shard_map/pallas_call | solution.py:325
  18.4 0.3 %collective-permute-done.3.got_ref = f32[32,256]{1,0:T(8,128)S(1)} collective-permute-done((f32[32,256]{1,0:T(8,128)S(1)}, f32[32,256]{1,0:T(8,128)S(1)}, u32[]{:S(2)}, u32[]{:S(2)}) %collective-permute-start.3) | collective-permute-done | bytes 32800 | tf_op jit(solution)/shard_map/ppermute | solution.py:345
  18.6 0.8 %shard_map.79.parts_ref = f32[4,32,384]{2,1,0:T(8,128)S(1)} custom-call(f32[32,256]{1,0:T(8,128)S(1)} %collective-permute-done.3.got_ref, f32[5,32,256]{2,1,0:T(8,128)S(1)} %get-tuple-element.29.mine_ref, f32[32,256]{1,0:T(8,128)S(1)} %get-tuple-element.30.guess_ref, f32[4,32,256]{2,1,0:T(8,128)S(1)} %get-tuple-element.31.slope_ref, ...), custom_call_target="tpu_custom_call" | custom-call | tf_op jit(solution)/shard_map/pallas_call | solution.py:325
  19.5 0.0 collective-permute-done.2._.late_ref
  19.5 0.1 collective-permute-start.4
  19.6 1.3 %collective-permute-done.4.got_ref = f32[2,32,384]{2,1,0:T(8,128)S(1)} collective-permute-done((f32[2,32,384]{2,1,0:T(8,128)S(1)}, f32[2,32,384]{2,1,0:T(8,128)S(1)}, u32[]{:S(2)}, u32[]{:S(2)}) %collective-permute-start.4) | collective-permute-done | bytes 98336 | tf_op jit(solution)/shard_map/ppermute | solution.py:345
  20.9 0.0 copy-start
  20.9 0.0 copy-start.1
  20.9 1.7 %collective-permute-start.5 = (f32[32,384]{1,0:T(8,128)S(1)}, f32[32,384]{1,0:T(8,128)S(1)}, u32[]{:S(2)}, u32[]{:S(2)}) collective-permute-start(f32[32,384]{1,0:T(8,128)S(1)} %get-tuple-element.39), channel_id=1, source_target_pairs={{0,3},{1,2},{2,1},{3,0},{4,7},{5,6},{6,5},{7,4},{8,11},{9,10},{10,... | collective-permute-start | bytes 147464 | tf_op jit(solution)/shard_map/ppermute | solution.py:345
  22.6 0.0 copy-done
  22.6 0.0 copy-done.1
  22.6 0.7 %shard_map.81 = (f32[1,1,32,256]{3,2,1,0:T(8,128)}, f32[1,1,32,256]{3,2,1,0:T(8,128)}) custom-call(f32[2,32,384]{2,1,0:T(8,128)S(1)} %get-tuple-element.34._.mine_ref, f32[32,256]{1,0:T(8,128)S(1)} %collective-permute-done.3.got_ref, f32[32,256]{1,0:T(8,128)S(1)} %collective-permute-done.2._.late_ref, f32[5,32,256]{2,1,0:T(8,128)S(1)} %get-tuple-element.29.mine_ref, ...), custom_call_target="tpu_custom_call" | custom-call | flops 268435456 | bytes 1048576 | tf_op jit(solution)/shard_map/pallas_call | solution.py:325
  23.4 1.4 %collective-permute-done.5.got_ref = f32[32,384]{1,0:T(8,128)S(1)} collective-permute-done((f32[32,384]{1,0:T(8,128)S(1)}, f32[32,384]{1,0:T(8,128)S(1)}, u32[]{:S(2)}, u32[]{:S(2)}) %collective-permute-start.5) | collective-permute-done | bytes 49184 | tf_op jit(solution)/shard_map/ppermute | solution.py:345
  24.7 0.7 %shard_map.83 = (f32[4,8,288]{2,1,0:T(8,128)}, f32[4,8]{1,0:T(4,128)}) custom-call(f32[32,384]{1,0:T(8,128)S(1)} %get-tuple-element.38.mine_ref, f32[32,384]{1,0:T(8,128)S(1)} %collective-permute-done.5.got_ref), custom_call_target="tpu_custom_call" | custom-call | flops 268435456 | bytes 1048576 | tf_op jit(solution)/shard_map/pallas_call | solution.py:325
  (4 shorter events, 0.1 us)
Async XLA Ops:
  3.6 5.8 %collective-permute-start = (f32[3,32,256]{2,1,0:T(8,128)S(1)}, f32[3,32,256]{2,1,0:T(8,128)S(1)}, u32[]{:S(2)}, u32[]{:S(2)}) collective-permute-start(f32[3,32,256]{2,1,0:T(8,128)S(1)} %get-tuple-element.23.refs_0_), channel_id=1, source_target_pairs={{0,4},{4,0},{8,12},{12,8},{16,20},{20,16},{24,28},{28,24},{1,5},{5... | collective-permute-start | bytes 294920 | tf_op jit(solution)/shard_map/ppermute | solution.py:345
  9.4 4.3 %collective-permute-start.1 = (f32[2,32,256]{2,1,0:T(8,128)S(1)}, f32[2,32,256]{2,1,0:T(8,128)S(1)}, u32[]{:S(2)}, u32[]{:S(2)}) collective-permute-start(f32[2,32,256]{2,1,0:T(8,128)S(1)} %get-tuple-element.24.total_ref), channel_id=1, source_target_pairs={{0,8},{4,12},{8,0},{12,4},{16,24},{20,28},{24,16},{28,20},{1,9},{5... | collective-permute-start | bytes 196616 | tf_op jit(solution)/shard_map/ppermute | solution.py:345
  13.8 4.9 %collective-permute-start.3 = (f32[32,256]{1,0:T(8,128)S(1)}, f32[32,256]{1,0:T(8,128)S(1)}, u32[]{:S(2)}, u32[]{:S(2)}) collective-permute-start(f32[32,256]{1,0:T(8,128)S(1)} %get-tuple-element.28), channel_id=1, source_target_pairs={{0,16},{4,20},{8,24},{12,28},{16,0},{20,4},{24,8},{28,12},{1,17},{... | collective-permute-start | bytes 98312 | tf_op jit(solution)/shard_map/ppermute | solution.py:345
  16.7 2.7 %collective-permute-start.2 = (f32[32,256]{1,0:T(8,128)S(1)}, f32[32,256]{1,0:T(8,128)S(1)}, u32[]{:S(2)}, u32[]{:S(2)}) collective-permute-start(f32[32,256]{1,0:T(8,128)S(1)} %get-tuple-element.27), channel_id=1, source_target_pairs={{8,16},{12,20},{16,24},{20,28},{9,17},{13,21},{17,25},{21,29},{10,... | collective-permute-start | bytes 98312 | tf_op jit(solution)/shard_map/ppermute | solution.py:385
  19.5 1.4 %collective-permute-start.4 = (f32[2,32,384]{2,1,0:T(8,128)S(1)}, f32[2,32,384]{2,1,0:T(8,128)S(1)}, u32[]{:S(2)}, u32[]{:S(2)}) collective-permute-start(f32[2,32,384]{2,1,0:T(8,128)S(1)} %get-tuple-element.37), channel_id=1, source_target_pairs={{0,1},{1,0},{2,3},{3,2},{4,5},{5,4},{6,7},{7,6},{8,9},{9,8},{10,11... | collective-permute-start | bytes 294920 | tf_op jit(solution)/shard_map/ppermute | solution.py:345
  20.9 1.7 %copy-start = (f32[1,1,32,256]{3,2,1,0:T(8,128)S(1)}, f32[1,1,32,256]{3,2,1,0:T(8,128)}, u32[]{:S(2)}) copy-start(f32[1,1,32,256]{3,2,1,0:T(8,128)} %start_ref.1) | copy-start | bytes 98308
  20.9 1.7 %copy-start.1 = (f32[1,1,32,256]{3,2,1,0:T(8,128)S(1)}, f32[1,1,32,256]{3,2,1,0:T(8,128)}, u32[]{:S(2)}) copy-start(f32[1,1,32,256]{3,2,1,0:T(8,128)} %guess_ref.1) | copy-start | bytes 98308
  20.9 3.8 %collective-permute-start.5 = (f32[32,384]{1,0:T(8,128)S(1)}, f32[32,384]{1,0:T(8,128)S(1)}, u32[]{:S(2)}, u32[]{:S(2)}) collective-permute-start(f32[32,384]{1,0:T(8,128)S(1)} %get-tuple-element.39), channel_id=1, source_target_pairs={{0,3},{1,2},{2,1},{3,0},{4,7},{5,6},{6,5},{7,4},{8,11},{9,10},{10,... | collective-permute-start | bytes 147464 | tf_op jit(solution)/shard_map/ppermute | solution.py:345

commit v13 on v11

--- a/solution.py
+++ b/solution.py
@@ -293,23 +293,18 @@
     layer(0, lax.fori_loop(0, depth - 1, behind, adj))
 
 
-def deal_kernel(_, parts_ref, keep_ref, send_ref):
+def deal_kernel(_, parts_ref, *outs):
     odd, high = bit_of("dp", 0), bit_of("dp", 1)
     parts = [parts_ref[i] for i in range(parts_ref.shape[0])]
     parts = [jnp.where(odd, parts[i ^ 1], parts[i]) for i in range(len(parts))]
     parts = [jnp.where(high, parts[i ^ 2], parts[i]) for i in range(len(parts))]
-    keep_ref[0], keep_ref[1] = parts[0], parts[3]
-    send_ref[0], send_ref[1] = parts[1], parts[2]
-
-
-def halve_kernel(mine_ref, got_ref, keep_ref, send_ref):
-    keep_ref[...] = mine_ref[0] + got_ref[0]
-    send_ref[...] = mine_ref[1] + got_ref[1]
-
-
-def total_kernel(mine_ref, got_ref, grad_ref, bias_ref):
+    for part, out in zip(parts, outs):
+        out[...] = part
+
+
+def total_kernel(mine_ref, both_ref, chip_ref, core_ref, grad_ref, bias_ref):
     depth, own, width = grad_ref.shape
-    total = mine_ref[...] + got_ref[...]
+    total = (mine_ref[...] + core_ref[...]) + (chip_ref[...] + both_ref[...])
     eye = lax.broadcasted_iota(jnp.int32, (own, own), 0) == lax.broadcasted_iota(
         jnp.int32, (own, own), 1
     )
@@ -390,22 +385,19 @@
         (got, *mine, guess, slope, patch, back_w),
         work=0,
     )
-    keep, send = call(
-        deal_kernel,
-        (f32(shares // 2, *part), f32(shares // 2, *part)),
-        (late, parts),
-        work=0,
-    )
+    keep, *sends = call(deal_kernel, (f32(*part),) * shares, (late, parts), work=0)
     adjoint_fixed, state_fixed = call(
         functools.partial(fixed_kernel, steps),
         (f32(*adjoint_guess.shape), f32(*state_guess.shape)),
         (keep, got, late, *mine, adjoint_guess, state_guess),
     )
-    keep, send = call(halve_kernel, (f32(*part), f32(*part)), (keep, exchange(send, "dp", 1)))
+    both = exchange(sends[2], "dp", 3)
+    chip = exchange(sends[1], "dp", 2)
+    core = exchange(sends[0], "dp", 1)
     weight_grad, bias_grad = call(
         total_kernel,
         (f32(depth, chans // shares, width), f32(depth, chans // shares)),
-        (keep, exchange(send, "dp", 3)),
+        (keep, both, chip, core),
     )
     return (state_fixed, adjoint_fixed, weight_grad, bias_grad)
 

time: 25.6 us -> 25 us (0.977)
  waiting for transfers between devices: 8.49 us -> 7.69 us
    ppermute x5 -> x6, waiting for transfers between devices: 8.48 us -> 7.68 us  [exchange(): lax.ppermute(x, axis, [(i, i ^ mask) for i in range(lax.axis_size(axis))])]
    ppermute x5 -> x6, starting transfers between devices: 9.7 us -> 9.99 us  [exchange(): lax.ppermute(x, axis, [(i, i ^ mask) for i in range(lax.axis_size(axis))])]
    pallas_call x9 -> x8, Pallas kernels: 5.86 us -> 5.83 us  [call(): pl.pallas_call(kernel, out_shape=out_shape, in_specs=[HBM if k in hbm_in...]
  transfers between devices with their start and end apart: 6 -> 7, of which waited for: 5 -> 5; matrix products, arithmetic and copies ran while one was open for 0% -> 0% of each run, Pallas kernels for 8% -> 9%
where the time goes in v13:
time: 25 us; the launch traced here: 24.9 us
  starting transfers between devices  10.6 us (42%)
  waiting for transfers between devices  7.69 us (31%)
  Pallas kernels  5.83 us (23%)
  between operations  0.73 us (3%)
    ppermute x6, starting transfers between devices, exchange(): lax.ppermute(x, axis, [(i, i ^ mask) for i in range(lax.axis_size(axis))])  9.99 us
    ppermute x6, waiting for transfers between devices, exchange(): lax.ppermute(x, axis, [(i, i ^ mask) for i in range(lax.axis_size(axis))])  7.68 us
    pallas_call x8, Pallas kernels, call(): pl.pallas_call(kernel, out_shape=out_shape, in_specs=[HBM if k in hbm_in...  5.83 us
    ppermute x1, starting transfers between devices, local(): lax.ppermute(late, 'layer', [(i, i + quarter) for i in range(quarter, 3 *...  0.65 us
  transfers between devices with their start and end apart: 7, of which 5 were waited for; matrix products, arithmetic and copies ran while one was open for 0% of the time, Pallas kernels for 9%

profile of v13, /device:TPU:0, one launch (start us, length us, event | category | flops | bytes accessed | tf_op | source)
XLA Modules:
  0.0 24.9 jit_solution(10117301194209566923)
XLA Ops:
  0.6 2.9 %shard_map.75 = (f32[32,256]{1,0:T(8,128)S(1)}, f32[3,32,256]{2,1,0:T(8,128)S(1)}, f32[4,32,256]{2,1,0:T(8,128)S(1)}, bf16[4,32,256]{2,1,0:T(8,128)(2,1)S(1)}, bf16[4,32,288]{2,1,0:T(8,128)(2,1)S(1)}) custom-call(f32[1,1,32,256]{3,2,1,0:T(8,128)} %start_ref.1, f32[1,1,32,256]{3,2,1,0:T(8,128)} %guess_ref.1, bf16[4,32,288]{2,1,0:T(8,128)(2,1)} %w_hbm.1, ...), custom_call_target="tpu_custom_call" | custom-call | flops 268435456 | bytes 1048576 | tf_op jit(solution)/shard_map/pallas_call | solution.py:319
  3.6 3.0 %collective-permute-start = (f32[3,32,256]{2,1,0:T(8,128)S(1)}, f32[3,32,256]{2,1,0:T(8,128)S(1)}, u32[]{:S(2)}, u32[]{:S(2)}) collective-permute-start(f32[3,32,256]{2,1,0:T(8,128)S(1)} %get-tuple-element.23.refs_0_), channel_id=1, source_target_pairs={{0,4},{4,0},{8,12},{12,8},{16,20},{20,16},{24,28},{28,24},{1,5},{5... | collective-permute-start | bytes 294920 | tf_op jit(solution)/shard_map/ppermute | solution.py:339
  6.6 2.8 %collective-permute-done.refs_1_ = f32[3,32,256]{2,1,0:T(8,128)S(1)} collective-permute-done((f32[3,32,256]{2,1,0:T(8,128)S(1)}, f32[3,32,256]{2,1,0:T(8,128)S(1)}, u32[]{:S(2)}, u32[]{:S(2)}) %collective-permute-start) | collective-permute-done | bytes 98336 | tf_op jit(solution)/shard_map/ppermute | solution.py:339
  9.4 2.0 %collective-permute-start.1 = (f32[2,32,256]{2,1,0:T(8,128)S(1)}, f32[2,32,256]{2,1,0:T(8,128)S(1)}, u32[]{:S(2)}, u32[]{:S(2)}) collective-permute-start(f32[2,32,256]{2,1,0:T(8,128)S(1)} %get-tuple-element.24.total_ref), channel_id=1, source_target_pairs={{0,8},{4,12},{8,0},{12,4},{16,24},{20,28},{24,16},{28,20},{1,9},{5... | collective-permute-start | bytes 196616 | tf_op jit(solution)/shard_map/ppermute | solution.py:339
  11.4 2.4 %collective-permute-done.1.got_ref = f32[2,32,256]{2,1,0:T(8,128)S(1)} collective-permute-done((f32[2,32,256]{2,1,0:T(8,128)S(1)}, f32[2,32,256]{2,1,0:T(8,128)S(1)}, u32[]{:S(2)}, u32[]{:S(2)}) %collective-permute-start.1) | collective-permute-done | bytes 65568 | tf_op jit(solution)/shard_map/ppermute | solution.py:339
  13.8 3.0 %collective-permute-start.3 = (f32[32,256]{1,0:T(8,128)S(1)}, f32[32,256]{1,0:T(8,128)S(1)}, u32[]{:S(2)}, u32[]{:S(2)}) collective-permute-start(f32[32,256]{1,0:T(8,128)S(1)} %get-tuple-element.28), channel_id=1, source_target_pairs={{0,16},{4,20},{8,24},{12,28},{16,0},{20,4},{24,8},{28,12},{1,17},{... | collective-permute-start | bytes 98312 | tf_op jit(solution)/shard_map/ppermute | solution.py:339
  16.7 0.7 %collective-permute-start.2 = (f32[32,256]{1,0:T(8,128)S(1)}, f32[32,256]{1,0:T(8,128)S(1)}, u32[]{:S(2)}, u32[]{:S(2)}) collective-permute-start(f32[32,256]{1,0:T(8,128)S(1)} %get-tuple-element.27), channel_id=1, source_target_pairs={{8,16},{12,20},{16,24},{20,28},{9,17},{13,21},{17,25},{21,29},{10,... | collective-permute-start | bytes 98312 | tf_op jit(solution)/shard_map/ppermute | solution.py:379
  17.4 0.6 %shard_map.78.patch_ref = bf16[4,288,256]{2,1,0:T(8,128)(2,1)S(1)} custom-call(bf16[4,32,256]{2,1,0:T(8,128)(2,1)S(1)} %get-tuple-element.32.rounded_ref), custom_call_target="tpu_custom_call" | custom-call | flops 268435456 | bytes 1048576 | tf_op jit(solution)/shard_map/pallas_call | solution.py:319
  18.0 0.7 %collective-permute-done.3.got_ref = f32[32,256]{1,0:T(8,128)S(1)} collective-permute-done((f32[32,256]{1,0:T(8,128)S(1)}, f32[32,256]{1,0:T(8,128)S(1)}, u32[]{:S(2)}, u32[]{:S(2)}) %collective-permute-start.3) | collective-permute-done | bytes 32800 | tf_op jit(solution)/shard_map/ppermute | solution.py:339
  18.6 0.8 %shard_map.79.parts_ref = f32[4,32,384]{2,1,0:T(8,128)S(1)} custom-call(f32[32,256]{1,0:T(8,128)S(1)} %collective-permute-done.3.got_ref, f32[5,32,256]{2,1,0:T(8,128)S(1)} %get-tuple-element.29.mine_ref, f32[32,256]{1,0:T(8,128)S(1)} %get-tuple-element.30.guess_ref, f32[4,32,256]{2,1,0:T(8,128)S(1)} %get-tuple-element.31.slope_ref, ...), custom_call_target="tpu_custom_call" | custom-call | tf_op jit(solution)/shard_map/pallas_call | solution.py:319
  19.5 0.0 copy-start
  19.5 0.0 copy-start.1
  19.5 0.0 collective-permute-done.2._.late_ref
  19.6 0.1 collective-permute-start.4
  19.7 1.9 %collective-permute-start.5 = (f32[32,384]{1,0:T(8,128)S(1)}, f32[32,384]{1,0:T(8,128)S(1)}, u32[]{:S(2)}, u32[]{:S(2)}) collective-permute-start(f32[32,384]{1,0:T(8,128)S(1)} %get-tuple-element.38), channel_id=1, source_target_pairs={{0,2},{1,3},{2,0},{3,1},{4,6},{5,7},{6,4},{7,5},{8,10},{9,11},{10,... | collective-permute-start | bytes 147464 | tf_op jit(solution)/shard_map/ppermute | solution.py:339
  21.6 0.0 collective-permute-start.6
  21.6 0.0 copy-done
  21.6 0.0 copy-done.1
  21.6 0.7 %shard_map.81 = (f32[1,1,32,256]{3,2,1,0:T(8,128)}, f32[1,1,32,256]{3,2,1,0:T(8,128)}) custom-call(f32[32,384]{1,0:T(8,128)S(1)} %get-tuple-element.34._.mine_ref, f32[32,256]{1,0:T(8,128)S(1)} %collective-permute-done.3.got_ref, f32[32,256]{1,0:T(8,128)S(1)} %collective-permute-done.2._.late_ref, f32[5,32,256]{2,1,0:T(8,128)S(1)} %get-tuple-element.29.mine_ref, ...), custom_call_target="tpu_custom_call" | custom-call | flops 268435456 | bytes 1048576 | tf_op jit(solution)/shard_map/pallas_call | solution.py:319
  22.4 1.0 %collective-permute-done.4.both_ref = f32[32,384]{1,0:T(8,128)S(1)} collective-permute-done((f32[32,384]{1,0:T(8,128)S(1)}, f32[32,384]{1,0:T(8,128)S(1)}, u32[]{:S(2)}, u32[]{:S(2)}) %collective-permute-start.4) | collective-permute-done | bytes 49184 | tf_op jit(solution)/shard_map/ppermute | solution.py:339
  23.4 0.8 %collective-permute-done.5.chip_ref = f32[32,384]{1,0:T(8,128)S(1)} collective-permute-done((f32[32,384]{1,0:T(8,128)S(1)}, f32[32,384]{1,0:T(8,128)S(1)}, u32[]{:S(2)}, u32[]{:S(2)}) %collective-permute-start.5) | collective-permute-done | bytes 49184 | tf_op jit(solution)/shard_map/ppermute | solution.py:339
  24.2 0.0 collective-permute-done.6.core_ref
  24.2 0.7 %shard_map.82 = (f32[4,8,288]{2,1,0:T(8,128)}, f32[4,8]{1,0:T(4,128)}) custom-call(f32[32,384]{1,0:T(8,128)S(1)} %get-tuple-element.34._.mine_ref, f32[32,384]{1,0:T(8,128)S(1)} %collective-permute-done.4.both_ref, f32[32,384]{1,0:T(8,128)S(1)} %collective-permute-done.5.chip_ref, f32[32,384]{1,0:T(8,128)S(1)} %collective-permute-done.6.core_ref), custom_call_target="tpu_custom_call" | custom-call | flops 268435456 | bytes 1048576 | tf_op jit(solution)/shard_map/pallas_call | solution.py:319
  (3 shorter events, 0.1 us)
Async XLA Ops:
  3.6 5.8 %collective-permute-start = (f32[3,32,256]{2,1,0:T(8,128)S(1)}, f32[3,32,256]{2,1,0:T(8,128)S(1)}, u32[]{:S(2)}, u32[]{:S(2)}) collective-permute-start(f32[3,32,256]{2,1,0:T(8,128)S(1)} %get-tuple-element.23.refs_0_), channel_id=1, source_target_pairs={{0,4},{4,0},{8,12},{12,8},{16,20},{20,16},{24,28},{28,24},{1,5},{5... | collective-permute-start | bytes 294920 | tf_op jit(solution)/shard_map/ppermute | solution.py:339
  9.4 4.3 %collective-permute-start.1 = (f32[2,32,256]{2,1,0:T(8,128)S(1)}, f32[2,32,256]{2,1,0:T(8,128)S(1)}, u32[]{:S(2)}, u32[]{:S(2)}) collective-permute-start(f32[2,32,256]{2,1,0:T(8,128)S(1)} %get-tuple-element.24.total_ref), channel_id=1, source_target_pairs={{0,8},{4,12},{8,0},{12,4},{16,24},{20,28},{24,16},{28,20},{1,9},{5... | collective-permute-start | bytes 196616 | tf_op jit(solution)/shard_map/ppermute | solution.py:339
  13.8 4.9 %collective-permute-start.3 = (f32[32,256]{1,0:T(8,128)S(1)}, f32[32,256]{1,0:T(8,128)S(1)}, u32[]{:S(2)}, u32[]{:S(2)}) collective-permute-start(f32[32,256]{1,0:T(8,128)S(1)} %get-tuple-element.28), channel_id=1, source_target_pairs={{0,16},{4,20},{8,24},{12,28},{16,0},{20,4},{24,8},{28,12},{1,17},{... | collective-permute-start | bytes 98312 | tf_op jit(solution)/shard_map/ppermute | solution.py:339
  16.7 2.8 %collective-permute-start.2 = (f32[32,256]{1,0:T(8,128)S(1)}, f32[32,256]{1,0:T(8,128)S(1)}, u32[]{:S(2)}, u32[]{:S(2)}) collective-permute-start(f32[32,256]{1,0:T(8,128)S(1)} %get-tuple-element.27), channel_id=1, source_target_pairs={{8,16},{12,20},{16,24},{20,28},{9,17},{13,21},{17,25},{21,29},{10,... | collective-permute-start | bytes 98312 | tf_op jit(solution)/shard_map/ppermute | solution.py:379
  19.5 2.1 %copy-start = (f32[1,1,32,256]{3,2,1,0:T(8,128)S(1)}, f32[1,1,32,256]{3,2,1,0:T(8,128)}, u32[]{:S(2)}) copy-start(f32[1,1,32,256]{3,2,1,0:T(8,128)} %start_ref.1) | copy-start | bytes 98308
  19.5 2.1 %copy-start.1 = (f32[1,1,32,256]{3,2,1,0:T(8,128)S(1)}, f32[1,1,32,256]{3,2,1,0:T(8,128)}, u32[]{:S(2)}) copy-start(f32[1,1,32,256]{3,2,1,0:T(8,128)} %guess_ref.1) | copy-start | bytes 98308
  19.6 3.8 %collective-permute-start.4 = (f32[32,384]{1,0:T(8,128)S(1)}, f32[32,384]{1,0:T(8,128)S(1)}, u32[]{:S(2)}, u32[]{:S(2)}) collective-permute-start(f32[32,384]{1,0:T(8,128)S(1)} %get-tuple-element.37), channel_id=1, source_target_pairs={{0,3},{1,2},{2,1},{3,0},{4,7},{5,6},{6,5},{7,4},{8,11},{9,10},{10,... | collective-permute-start | bytes 147464 | tf_op jit(solution)/shard_map/ppermute | solution.py:339
  19.7 4.6 %collective-permute-start.5 = (f32[32,384]{1,0:T(8,128)S(1)}, f32[32,384]{1,0:T(8,128)S(1)}, u32[]{:S(2)}, u32[]{:S(2)}) collective-permute-start(f32[32,384]{1,0:T(8,128)S(1)} %get-tuple-element.38), channel_id=1, source_target_pairs={{0,2},{1,3},{2,0},{3,1},{4,6},{5,7},{6,4},{7,5},{8,10},{9,11},{10,... | collective-permute-start | bytes 147464 | tf_op jit(solution)/shard_map/ppermute | solution.py:339
  21.6 2.6 %collective-permute-start.6 = (f32[32,384]{1,0:T(8,128)S(1)}, f32[32,384]{1,0:T(8,128)S(1)}, u32[]{:S(2)}, u32[]{:S(2)}) collective-permute-start(f32[32,384]{1,0:T(8,128)S(1)} %get-tuple-element.39), channel_id=1, source_target_pairs={{0,1},{1,0},{2,3},{3,2},{4,5},{5,4},{6,7},{7,6},{8,9},{9,8},{10,11... | collective-permute-start | bytes 147464 | tf_op jit(solution)/shard_map/ppermute | solution.py:339

commit v14 on v10

--- a/solution.py
+++ b/solution.py
@@ -201,18 +201,7 @@
     return lax.rem(lax.div(lax.axis_index(axis), 2**step), 2) == 1
 
 
-def join_kernel(step, final, *refs):
-    if step == 1:
-        total_ref, got_ref, sent_ref, mine_out = refs
-        one = jnp.ones(total_ref.shape[1:], jnp.float32)
-        zero = jnp.zeros(total_ref.shape[1:], jnp.float32)
-        mine = (one, zero, one, zero)
-    else:
-        total_ref, got_ref, mine_ref, sent_ref, mine_out = refs
-        mine = tuple(mine_ref[k] for k in range(4))
-    total = tuple(total_ref[k] for k in range(3))
-    got = tuple(got_ref[k] for k in range(3))
-    total, mine = joined(bit_of("layer", step - 1), total, mine, got)
+def put_joined(step, final, total, mine, sent_ref, mine_out):
     for k in range(4):
         mine_out[k] = mine[k]
     if final:
@@ -220,6 +209,44 @@
     else:
         for k in range(3):
             sent_ref[k] = total[k]
+
+
+def four_kernel(final, own_ref, first_ref, second_ref, third_ref, sent_ref, mine_out):
+    low, high = bit_of("layer", 0), bit_of("layer", 1)
+    place = lax.rem(lax.axis_index("layer"), 4)
+    maps = [
+        tuple(ref[k] for k in range(3)) for ref in (own_ref, first_ref, second_ref, third_ref)
+    ]
+    for bit, mask in ((low, 1), (high, 2)):
+        maps = [
+            tuple(jnp.where(bit, b, a) for a, b in zip(maps[k], maps[k ^ mask])) for k in range(4)
+        ]
+    one, zero = jnp.ones_like(maps[0][0]), jnp.zeros_like(maps[0][0])
+    gain, fwd, bwd = maps[0]
+    pre_gain, pre, post_gain, post = one, zero, one, zero
+    for k in range(4):
+        here = maps[k]
+        before = k < place
+        pre = jnp.where(before, here[0] * pre + here[1], pre)
+        pre_gain = jnp.where(before, pre_gain * here[0], pre_gain)
+        if k:
+            bwd = bwd + gain * here[2]
+            fwd = here[0] * fwd + here[1]
+            gain = gain * here[0]
+    for k in reversed(range(4)):
+        here = maps[k]
+        after = k > place
+        post = jnp.where(after, here[0] * post + here[2], post)
+        post_gain = jnp.where(after, post_gain * here[0], post_gain)
+    mine = (pre_gain, pre, post_gain, post)
+    put_joined(2, final, (gain, fwd, bwd), mine, sent_ref, mine_out)
+
+
+def join_kernel(step, final, total_ref, got_ref, mine_ref, sent_ref, mine_out):
+    total, got = (tuple(ref[k] for k in range(3)) for ref in (total_ref, got_ref))
+    mine = tuple(mine_ref[k] for k in range(4))
+    total, mine = joined(bit_of("layer", step - 1), total, mine, got)
+    put_joined(step, final, total, mine, sent_ref, mine_out)
 
 
 def later_fixed(steps, got_ref, mine_ref):
@@ -244,15 +271,14 @@
     slope_ref,
     patch_ref,
     back_w_ref,
-    keep_ref,
-    send_ref,
+    *part_refs,
 ):
     depth, chans, rows = back_w_ref.shape
-    shares = 2 * keep_ref.shape[0]
+    shares = len(part_refs)
     own = chans // shares
     last = lax.axis_index("layer") == lax.axis_size("layer") - 1
     adj = jnp.where(last, guess_ref[...], later_fixed(steps, got_ref, mine_ref))
-    pad = keep_ref.shape[2] - rows
+    pad = part_refs[0].shape[1] - rows
     odd, high = bit_of("dp", 0), bit_of("dp", 1)
 
     def layer(n, adj):
@@ -261,12 +287,12 @@
         grad = dot(dzb, patch_ref[n], ((1,), (1,)))
         bias = jnp.broadcast_to(jnp.sum(dz, axis=1, keepdims=True), (chans, pad))
         both = jnp.concatenate([grad, bias], axis=1)
-        parts = [both[s * own : (s + 1) * own] for s in range(shares)]
+        where = pl.ds(pl.multiple_of(n * own, own), own)
+        parts = [both[k * own : (k + 1) * own] for k in range(shares)]
         parts = [jnp.where(odd, parts[i ^ 1], parts[i]) for i in range(shares)]
         parts = [jnp.where(high, parts[i ^ 2], parts[i]) for i in range(shares)]
-        where = pl.ds(pl.multiple_of(n * own, own), own)
-        keep_ref[0, where], keep_ref[1, where] = parts[0], parts[3]
-        send_ref[0, where], send_ref[1, where] = parts[1], parts[2]
+        for part, ref in zip(parts, part_refs):
+            ref[where] = part
         return dzb
 
     def behind(i, adj):
@@ -276,14 +302,9 @@
     layer(0, lax.fori_loop(0, depth - 1, behind, adj))
 
 
-def halve_kernel(mine_ref, got_ref, keep_ref, send_ref):
-    keep_ref[...] = mine_ref[0] + got_ref[0]
-    send_ref[...] = mine_ref[1] + got_ref[1]
-
-
-def total_kernel(mine_ref, got_ref, grad_ref, bias_ref):
+def total_kernel(mine_ref, both_ref, chip_ref, core_ref, grad_ref, bias_ref):
     depth, own, width = grad_ref.shape
-    total = mine_ref[...] + got_ref[...]
+    total = (mine_ref[...] + core_ref[...]) + (chip_ref[...] + both_ref[...])
     eye = lax.broadcasted_iota(jnp.int32, (own, own), 0) == lax.broadcasted_iota(
         jnp.int32, (own, own), 1
     )
@@ -337,33 +358,39 @@
         scratch=[pltpu.VMEM(a.shape, a.dtype) for a in args] + [pltpu.SemaphoreType.DMA((4,))],
     )
     (patch,) = call(patch_kernel, (bf16(depth, width, HW),), (rounded,))
-    mine = ()
-    for step in range(1, steps):
-        got = exchange(total, "layer", 1 << (step - 1))
-        final = step == steps - 1
-        total, *mine = call(
-            functools.partial(join_kernel, step, final),
-            (f32(chans, HW) if final else f32(3, chans, HW), f32(4, chans, HW)),
-            (total, got, *mine),
+    one = f32(chans, HW)
+    shapes = [(f32(3, chans, HW), f32(4, chans, HW))] * (steps - 3) + [(one, f32(4, chans, HW))]
+    total, mine = call(
+        functools.partial(four_kernel, steps == 3),
+        shapes[0],
+        (total, *(exchange(total, "layer", mask) for mask in (1, 2, 3))),
+    )
+    for step in range(3, steps):
+        total, mine = call(
+            functools.partial(join_kernel, step, step == steps - 1),
+            shapes[step - 2],
+            (total, exchange(total, "layer", 1 << (step - 1)), mine),
         )
     got = exchange(total, "layer", 1 << (steps - 1))
     lanes = -(-(width + 1) // HALF) * HALF
     part = (depth * chans // shares, lanes)
-    keep, send = call(
+    keep, *sends = call(
         functools.partial(grad_kernel, steps),
-        (f32(shares // 2, *part), f32(shares // 2, *part)),
-        (got, *mine, guess, slope, patch, back_w),
+        (f32(*part),) * shares,
+        (got, mine, guess, slope, patch, back_w),
     )
     adjoint_fixed, state_fixed = call(
         functools.partial(fixed_kernel, steps),
         (f32(*adjoint_guess.shape), f32(*state_guess.shape)),
-        (keep, got, *mine, adjoint_guess, state_guess),
-    )
-    keep, send = call(halve_kernel, (f32(*part), f32(*part)), (keep, exchange(send, "dp", 1)))
+        (keep, got, mine, adjoint_guess, state_guess),
+    )
+    both = exchange(sends[2], "dp", 3)
+    chip = exchange(sends[1], "dp", 2)
+    core = exchange(sends[0], "dp", 1)
     weight_grad, bias_grad = call(
         total_kernel,
         (f32(depth, chans // shares, width), f32(depth, chans // shares)),
-        (keep, exchange(send, "dp", 3)),
+        (keep, both, chip, core),
     )
     return (state_fixed, adjoint_fixed, weight_grad, bias_grad)
 

time: 25.9 us -> 24.3 us (0.938)
  waiting for transfers between devices: 9.49 us -> 8.33 us
  starting transfers between devices: 9.7 us -> 9.29 us
    ppermute x5 -> x7, waiting for transfers between devices: 9.49 us -> 8.33 us  [exchange(): lax.ppermute(x, axis, [(i, i ^ mask) for i in range(lax.axis_size(axis))])]
    ppermute x5 -> x7, starting transfers between devices: 9.7 us -> 9.29 us  [exchange(): lax.ppermute(x, axis, [(i, i ^ mask) for i in range(lax.axis_size(axis))])]
    pallas_call x8 -> x6, Pallas kernels: 5.8 us -> 5.84 us  [call(): pl.pallas_call(kernel, out_shape=out_shape, in_specs=[HBM if k in hbm_in...]
  transfers between devices with their start and end apart: 5 -> 7, of which waited for: 5 -> 5; matrix products, arithmetic and copies ran while one was open for 0% -> 0% of each run, Pallas kernels for 5% -> 5%
where the time goes in v14:
time: 24.3 us; the launch traced here: 24.1 us
  starting transfers between devices  9.29 us (38%)
  waiting for transfers between devices  8.33 us (34%)
  Pallas kernels  5.84 us (24%)
  between operations  0.68 us (3%)
    ppermute x7, starting transfers between devices, exchange(): lax.ppermute(x, axis, [(i, i ^ mask) for i in range(lax.axis_size(axis))])  9.29 us
    ppermute x7, waiting for transfers between devices, exchange(): lax.ppermute(x, axis, [(i, i ^ mask) for i in range(lax.axis_size(axis))])  8.33 us
    pallas_call x6, Pallas kernels, call(): pl.pallas_call(kernel, out_shape=out_shape, in_specs=[HBM if k in hbm_in...  5.84 us
  transfers between devices with their start and end apart: 7, of which 5 were waited for; matrix products, arithmetic and copies ran while one was open for 0% of the time, Pallas kernels for 5%

profile of v14, /device:TPU:0, one launch (start us, length us, event | category | flops | bytes accessed | tf_op | source)
XLA Modules:
  0.0 24.1 jit_solution(8107623089282715639)
XLA Ops:
  0.6 2.9 %shard_map.75 = (f32[32,256]{1,0:T(8,128)S(1)}, f32[3,32,256]{2,1,0:T(8,128)S(1)}, f32[4,32,256]{2,1,0:T(8,128)S(1)}, bf16[4,32,256]{2,1,0:T(8,128)(2,1)S(1)}, bf16[4,32,288]{2,1,0:T(8,128)(2,1)S(1)}) custom-call(f32[1,1,32,256]{3,2,1,0:T(8,128)} %start_ref.1, f32[1,1,32,256]{3,2,1,0:T(8,128)} %guess_ref.1, bf16[4,32,288]{2,1,0:T(8,128)(2,1)} %w_hbm.1, ...), custom_call_target="tpu_custom_call" | custom-call | flops 268435456 | bytes 1048576 | tf_op jit(solution)/shard_map/pallas_call | solution.py:319
  3.6 4.0 %collective-permute-start.2 = (f32[3,32,256]{2,1,0:T(8,128)S(1)}, f32[3,32,256]{2,1,0:T(8,128)S(1)}, u32[]{:S(2)}, u32[]{:S(2)}) collective-permute-start(f32[3,32,256]{2,1,0:T(8,128)S(1)} %get-tuple-element.19.own_ref), channel_id=1, source_target_pairs={{0,12},{4,8},{8,4},{12,0},{16,28},{20,24},{24,20},{28,16},{1,13},{... | collective-permute-start | bytes 294920 | tf_op jit(solution)/shard_map/ppermute | solution.py:339
  7.6 0.4 %collective-permute-start.1 = (f32[3,32,256]{2,1,0:T(8,128)S(1)}, f32[3,32,256]{2,1,0:T(8,128)S(1)}, u32[]{:S(2)}, u32[]{:S(2)}) collective-permute-start(f32[3,32,256]{2,1,0:T(8,128)S(1)} %get-tuple-element.19.own_ref), channel_id=1, source_target_pairs={{0,8},{4,12},{8,0},{12,4},{16,24},{20,28},{24,16},{28,20},{1,9},{5... | collective-permute-start | bytes 294920 | tf_op jit(solution)/shard_map/ppermute | solution.py:339
  8.0 0.2 collective-permute-start
  8.2 2.9 %collective-permute-done.2.third_ref = f32[3,32,256]{2,1,0:T(8,128)S(1)} collective-permute-done((f32[3,32,256]{2,1,0:T(8,128)S(1)}, f32[3,32,256]{2,1,0:T(8,128)S(1)}, u32[]{:S(2)}, u32[]{:S(2)}) %collective-permute-start.2) | collective-permute-done | bytes 98336 | tf_op jit(solution)/shard_map/ppermute | solution.py:339
  11.1 1.6 %collective-permute-done.1.second_ref = f32[3,32,256]{2,1,0:T(8,128)S(1)} collective-permute-done((f32[3,32,256]{2,1,0:T(8,128)S(1)}, f32[3,32,256]{2,1,0:T(8,128)S(1)}, u32[]{:S(2)}, u32[]{:S(2)}) %collective-permute-start.1) | collective-permute-done | bytes 98336 | tf_op jit(solution)/shard_map/ppermute | solution.py:339
  12.7 0.0 collective-permute-done.first_ref
  12.7 0.1 shard_map.76
  12.8 2.7 %collective-permute-start.3 = (f32[32,256]{1,0:T(8,128)S(1)}, f32[32,256]{1,0:T(8,128)S(1)}, u32[]{:S(2)}, u32[]{:S(2)}) collective-permute-start(f32[32,256]{1,0:T(8,128)S(1)} %get-tuple-element.20), channel_id=1, source_target_pairs={{0,16},{4,20},{8,24},{12,28},{16,0},{20,4},{24,8},{28,12},{1,17},{... | collective-permute-start | bytes 98312 | tf_op jit(solution)/shard_map/ppermute | solution.py:339
  15.5 0.6 %shard_map.77.patch_ref = bf16[4,288,256]{2,1,0:T(8,128)(2,1)S(1)} custom-call(bf16[4,32,256]{2,1,0:T(8,128)(2,1)S(1)} %get-tuple-element.24.rounded_ref), custom_call_target="tpu_custom_call" | custom-call | flops 268435456 | bytes 1048576 | tf_op jit(solution)/shard_map/pallas_call | solution.py:319
  16.1 1.6 %collective-permute-done.3.got_ref = f32[32,256]{1,0:T(8,128)S(1)} collective-permute-done((f32[32,256]{1,0:T(8,128)S(1)}, f32[32,256]{1,0:T(8,128)S(1)}, u32[]{:S(2)}, u32[]{:S(2)}) %collective-permute-start.3) | collective-permute-done | bytes 32800 | tf_op jit(solution)/shard_map/ppermute | solution.py:339
  17.7 0.0 copy-start
  17.7 0.0 copy-start.1
  17.7 0.9 %shard_map.78 = (f32[32,384]{1,0:T(8,128)S(1)}, f32[32,384]{1,0:T(8,128)S(1)}, f32[32,384]{1,0:T(8,128)S(1)}, f32[32,384]{1,0:T(8,128)S(1)}) custom-call(f32[32,256]{1,0:T(8,128)S(1)} %collective-permute-done.3.got_ref, f32[4,32,256]{2,1,0:T(8,128)S(1)} %get-tuple-element.21.mine_ref, f32[32,256]{1,0:T(8,128)S(1)} %get-tuple-element.22.guess_ref, ...), custom_call_target="tpu_custom_call" | custom-call | flops 268435456 | bytes 1048576 | tf_op jit(solution)/shard_map/pallas_call | solution.py:319
  18.6 0.1 collective-permute-start.4
  18.7 1.6 %collective-permute-start.5 = (f32[32,384]{1,0:T(8,128)S(1)}, f32[32,384]{1,0:T(8,128)S(1)}, u32[]{:S(2)}, u32[]{:S(2)}) collective-permute-start(f32[32,384]{1,0:T(8,128)S(1)} %get-tuple-element.30), channel_id=1, source_target_pairs={{0,2},{1,3},{2,0},{3,1},{4,6},{5,7},{6,4},{7,5},{8,10},{9,11},{10,... | collective-permute-start | bytes 147464 | tf_op jit(solution)/shard_map/ppermute | solution.py:339
  20.3 0.2 collective-permute-start.6
  20.5 0.0 copy-done
  20.5 0.0 copy-done.1
  20.5 0.7 %shard_map.79 = (f32[1,1,32,256]{3,2,1,0:T(8,128)}, f32[1,1,32,256]{3,2,1,0:T(8,128)}) custom-call(f32[32,384]{1,0:T(8,128)S(1)} %get-tuple-element.26._.mine_ref, f32[32,256]{1,0:T(8,128)S(1)} %collective-permute-done.3.got_ref, f32[4,32,256]{2,1,0:T(8,128)S(1)} %get-tuple-element.21.mine_ref, f32[1,1,32,256]{3,2,1,0:T(8,128)S(1)} %copy-done.1, ...), custom_call_target="tpu_custom_call" | custom-call | flops 268435456 | bytes 1048576 | tf_op jit(solution)/shard_map/pallas_call | solution.py:319
  21.3 1.3 %collective-permute-done.4.both_ref = f32[32,384]{1,0:T(8,128)S(1)} collective-permute-done((f32[32,384]{1,0:T(8,128)S(1)}, f32[32,384]{1,0:T(8,128)S(1)}, u32[]{:S(2)}, u32[]{:S(2)}) %collective-permute-start.4) | collective-permute-done | bytes 49184 | tf_op jit(solution)/shard_map/ppermute | solution.py:339
  22.6 0.9 %collective-permute-done.5.chip_ref = f32[32,384]{1,0:T(8,128)S(1)} collective-permute-done((f32[32,384]{1,0:T(8,128)S(1)}, f32[32,384]{1,0:T(8,128)S(1)}, u32[]{:S(2)}, u32[]{:S(2)}) %collective-permute-start.5) | collective-permute-done | bytes 49184 | tf_op jit(solution)/shard_map/ppermute | solution.py:339
  23.5 0.0 collective-permute-done.6.core_ref
  23.5 0.7 %shard_map.80 = (f32[4,8,288]{2,1,0:T(8,128)}, f32[4,8]{1,0:T(4,128)}) custom-call(f32[32,384]{1,0:T(8,128)S(1)} %get-tuple-element.26._.mine_ref, f32[32,384]{1,0:T(8,128)S(1)} %collective-permute-done.4.both_ref, f32[32,384]{1,0:T(8,128)S(1)} %collective-permute-done.5.chip_ref, f32[32,384]{1,0:T(8,128)S(1)} %collective-permute-done.6.core_ref), custom_call_target="tpu_custom_call" | custom-call | flops 268435456 | bytes 1048576 | tf_op jit(solution)/shard_map/pallas_call | solution.py:319
Async XLA Ops:
  3.6 7.5 %collective-permute-start.2 = (f32[3,32,256]{2,1,0:T(8,128)S(1)}, f32[3,32,256]{2,1,0:T(8,128)S(1)}, u32[]{:S(2)}, u32[]{:S(2)}) collective-permute-start(f32[3,32,256]{2,1,0:T(8,128)S(1)} %get-tuple-element.19.own_ref), channel_id=1, source_target_pairs={{0,12},{4,8},{8,4},{12,0},{16,28},{20,24},{24,20},{28,16},{1,13},{... | collective-permute-start | bytes 294920 | tf_op jit(solution)/shard_map/ppermute | solution.py:339
  7.6 5.1 %collective-permute-start.1 = (f32[3,32,256]{2,1,0:T(8,128)S(1)}, f32[3,32,256]{2,1,0:T(8,128)S(1)}, u32[]{:S(2)}, u32[]{:S(2)}) collective-permute-start(f32[3,32,256]{2,1,0:T(8,128)S(1)} %get-tuple-element.19.own_ref), channel_id=1, source_target_pairs={{0,8},{4,12},{8,0},{12,4},{16,24},{20,28},{24,16},{28,20},{1,9},{5... | collective-permute-start | bytes 294920 | tf_op jit(solution)/shard_map/ppermute | solution.py:339
  8.0 4.7 %collective-permute-start = (f32[3,32,256]{2,1,0:T(8,128)S(1)}, f32[3,32,256]{2,1,0:T(8,128)S(1)}, u32[]{:S(2)}, u32[]{:S(2)}) collective-permute-start(f32[3,32,256]{2,1,0:T(8,128)S(1)} %get-tuple-element.19.own_ref), channel_id=1, source_target_pairs={{0,4},{4,0},{8,12},{12,8},{16,20},{20,16},{24,28},{28,24},{1,5},{5... | collective-permute-start | bytes 294920 | tf_op jit(solution)/shard_map/ppermute | solution.py:339
  12.8 4.9 %collective-permute-start.3 = (f32[32,256]{1,0:T(8,128)S(1)}, f32[32,256]{1,0:T(8,128)S(1)}, u32[]{:S(2)}, u32[]{:S(2)}) collective-permute-start(f32[32,256]{1,0:T(8,128)S(1)} %get-tuple-element.20), channel_id=1, source_target_pairs={{0,16},{4,20},{8,24},{12,28},{16,0},{20,4},{24,8},{28,12},{1,17},{... | collective-permute-start | bytes 98312 | tf_op jit(solution)/shard_map/ppermute | solution.py:339
  17.7 2.8 %copy-start = (f32[1,1,32,256]{3,2,1,0:T(8,128)S(1)}, f32[1,1,32,256]{3,2,1,0:T(8,128)}, u32[]{:S(2)}) copy-start(f32[1,1,32,256]{3,2,1,0:T(8,128)} %start_ref.1) | copy-start | bytes 98308
  17.7 2.8 %copy-start.1 = (f32[1,1,32,256]{3,2,1,0:T(8,128)S(1)}, f32[1,1,32,256]{3,2,1,0:T(8,128)}, u32[]{:S(2)}) copy-start(f32[1,1,32,256]{3,2,1,0:T(8,128)} %guess_ref.1) | copy-start | bytes 98308
  18.6 4.0 %collective-permute-start.4 = (f32[32,384]{1,0:T(8,128)S(1)}, f32[32,384]{1,0:T(8,128)S(1)}, u32[]{:S(2)}, u32[]{:S(2)}) collective-permute-start(f32[32,384]{1,0:T(8,128)S(1)} %get-tuple-element.29), channel_id=1, source_target_pairs={{0,3},{1,2},{2,1},{3,0},{4,7},{5,6},{6,5},{7,4},{8,11},{9,10},{10,... | collective-permute-start | bytes 147464 | tf_op jit(solution)/shard_map/ppermute | solution.py:339
  18.7 4.8 %collective-permute-start.5 = (f32[32,384]{1,0:T(8,128)S(1)}, f32[32,384]{1,0:T(8,128)S(1)}, u32[]{:S(2)}, u32[]{:S(2)}) collective-permute-start(f32[32,384]{1,0:T(8,128)S(1)} %get-tuple-element.30), channel_id=1, source_target_pairs={{0,2},{1,3},{2,0},{3,1},{4,6},{5,7},{6,4},{7,5},{8,10},{9,11},{10,... | collective-permute-start | bytes 147464 | tf_op jit(solution)/shard_map/ppermute | solution.py:339
  20.3 3.2 %collective-permute-start.6 = (f32[32,384]{1,0:T(8,128)S(1)}, f32[32,384]{1,0:T(8,128)S(1)}, u32[]{:S(2)}, u32[]{:S(2)}) collective-permute-start(f32[32,384]{1,0:T(8,128)S(1)} %get-tuple-element.31), channel_id=1, source_target_pairs={{0,1},{1,0},{2,3},{3,2},{4,5},{5,4},{6,7},{7,6},{8,9},{9,8},{10,11... | collective-permute-start | bytes 147464 | tf_op jit(solution)/shard_map/ppermute | solution.py:339

commit v15 on v14

--- a/solution.py
+++ b/solution.py
@@ -13,6 +13,8 @@
 TAPS = 9
 STEP = 0.5
 LIMIT = 32 * 1024 * 1024
+GRAD_WORK = 2**28
+FIXED_WORK = 2**32
 
 VMEM = pl.BlockSpec(memory_space=pltpu.VMEM)
 HBM = pl.BlockSpec(memory_space=pltpu.HBM)
@@ -104,6 +106,7 @@
     bias_hbm,
     guess_ref,
     sent_ref,
+    ahead_ref,
     slope_ref,
     rounded_ref,
     back_w_ref,
@@ -167,8 +170,8 @@
     first = jnp.where(place == 0, 0.0, start)
     last = jnp.where(place == lax.axis_size("layer") - 1, 0.0, guess)
     sent_ref[0] = gain
-    sent_ref[1] = state - gain * first
-    sent_ref[2] = back - gain * last
+    sent_ref[1] = back - gain * last
+    ahead_ref[...] = state - gain * first
 
 
 def patch_kernel(rounded_ref, patch_ref):
@@ -179,86 +182,92 @@
         patch_ref[n] = dot(perm, patch, ((0,), (0,))).astype(jnp.bfloat16)
 
 
-def joined(bit, total, mine, got):
-    gain, fwd, bwd = total
-    pre_gain, pre, post_gain, post = mine
-    got_gain, got_fwd, got_bwd = got
-    total = (
-        gain * got_gain,
-        jnp.where(bit, gain * got_fwd + fwd, got_gain * fwd + got_fwd),
-        jnp.where(bit, got_gain * bwd + got_bwd, gain * got_bwd + bwd),
-    )
-    mine = (
-        jnp.where(bit, pre_gain * got_gain, pre_gain),
-        jnp.where(bit, pre_gain * got_fwd + pre, pre),
-        jnp.where(bit, post_gain, post_gain * got_gain),
-        jnp.where(bit, post, post_gain * got_bwd + post),
-    )
-    return total, mine
-
-
 def bit_of(axis, step):
     return lax.rem(lax.div(lax.axis_index(axis), 2**step), 2) == 1
 
 
-def put_joined(step, final, total, mine, sent_ref, mine_out):
-    for k in range(4):
-        mine_out[k] = mine[k]
-    if final:
-        sent_ref[...] = jnp.where(bit_of("layer", step), total[2], total[1])
+def in_places(own, first, second, third):
+    values = [own, first, second, third]
+    for step, mask in ((0, 1), (1, 2)):
+        bit = bit_of("layer", step)
+        values = [
+            tuple(jnp.where(bit, b, a) for a, b in zip(values[k], values[k ^ mask]))
+            for k in range(4)
+        ]
+    return values
+
+
+def later_four_kernel(own_ref, first_ref, second_ref, third_ref, sent_ref, mine_out):
+    place = lax.rem(lax.axis_index("layer"), 4)
+    maps = in_places(*((r[0], r[1]) for r in (own_ref, first_ref, second_ref, third_ref)))
+    gain, bwd = maps[0]
+    for here in maps[1:]:
+        bwd = bwd + gain * here[1]
+        gain = gain * here[0]
+    post_gain, post = jnp.ones_like(gain), jnp.zeros_like(gain)
+    for k in reversed(range(1, 4)):
+        after = k > place
+        post = jnp.where(after, maps[k][0] * post + maps[k][1], post)
+        post_gain = jnp.where(after, post_gain * maps[k][0], post_gain)
+    mine_out[0], mine_out[1] = post_gain, post
+    if len(sent_ref.shape) == 3:
+        sent_ref[0], sent_ref[1] = gain, bwd
     else:
-        for k in range(3):
-            sent_ref[k] = total[k]
-
-
-def four_kernel(final, own_ref, first_ref, second_ref, third_ref, sent_ref, mine_out):
-    low, high = bit_of("layer", 0), bit_of("layer", 1)
+        sent_ref[...] = bwd
+
+
+def earlier_four_kernel(*refs):
+    gains, values, (sent_ref, mine_out) = refs[:4], refs[4:8], refs[8:]
     place = lax.rem(lax.axis_index("layer"), 4)
-    maps = [
-        tuple(ref[k] for k in range(3)) for ref in (own_ref, first_ref, second_ref, third_ref)
-    ]
-    for bit, mask in ((low, 1), (high, 2)):
-        maps = [
-            tuple(jnp.where(bit, b, a) for a, b in zip(maps[k], maps[k ^ mask])) for k in range(4)
-        ]
-    one, zero = jnp.ones_like(maps[0][0]), jnp.zeros_like(maps[0][0])
-    gain, fwd, bwd = maps[0]
-    pre_gain, pre, post_gain, post = one, zero, one, zero
-    for k in range(4):
-        here = maps[k]
+    maps = in_places(*((g[0], v[...]) for g, v in zip(gains, values)))
+    fwd = maps[0][1]
+    for here in maps[1:]:
+        fwd = here[0] * fwd + here[1]
+    pre_gain, pre = jnp.ones_like(fwd), jnp.zeros_like(fwd)
+    for k in range(3):
         before = k < place
-        pre = jnp.where(before, here[0] * pre + here[1], pre)
-        pre_gain = jnp.where(before, pre_gain * here[0], pre_gain)
-        if k:
-            bwd = bwd + gain * here[2]
-            fwd = here[0] * fwd + here[1]
-            gain = gain * here[0]
-    for k in reversed(range(4)):
-        here = maps[k]
-        after = k > place
-        post = jnp.where(after, here[0] * post + here[2], post)
-        post_gain = jnp.where(after, post_gain * here[0], post_gain)
-    mine = (pre_gain, pre, post_gain, post)
-    put_joined(2, final, (gain, fwd, bwd), mine, sent_ref, mine_out)
-
-
-def join_kernel(step, final, total_ref, got_ref, mine_ref, sent_ref, mine_out):
-    total, got = (tuple(ref[k] for k in range(3)) for ref in (total_ref, got_ref))
-    mine = tuple(mine_ref[k] for k in range(4))
-    total, mine = joined(bit_of("layer", step - 1), total, mine, got)
-    put_joined(step, final, total, mine, sent_ref, mine_out)
+        pre = jnp.where(before, maps[k][0] * pre + maps[k][1], pre)
+        pre_gain = jnp.where(before, pre_gain * maps[k][0], pre_gain)
+    mine_out[0], mine_out[1] = pre_gain, pre
+    sent_ref[...] = fwd
+
+
+def later_kernel(step, total_ref, got_ref, mine_ref, sent_ref, mine_out):
+    before = bit_of("layer", step)
+    gain, bwd = total_ref[0], total_ref[1]
+    got_gain, got = got_ref[0], got_ref[1]
+    bwd = jnp.where(before, got_gain * bwd + got, gain * got + bwd)
+    if len(sent_ref.shape) == 3:
+        sent_ref[0], sent_ref[1] = gain * got_gain, bwd
+    else:
+        sent_ref[...] = bwd
+    post_gain, post = mine_ref[0], mine_ref[1]
+    mine_out[0] = jnp.where(before, post_gain, post_gain * got_gain)
+    mine_out[1] = jnp.where(before, post, post_gain * got + post)
+
+
+def earlier_kernel(step, total_ref, got_ref, fwd_ref, got_fwd_ref, mine_ref, sent_ref, mine_out):
+    before = bit_of("layer", step)
+    gain, got_gain = total_ref[0], got_ref[0]
+    fwd, got = fwd_ref[...], got_fwd_ref[...]
+    sent_ref[...] = jnp.where(before, gain * got + fwd, got_gain * fwd + got)
+    pre_gain, pre = mine_ref[0], mine_ref[1]
+    mine_out[0] = jnp.where(before, pre_gain * got_gain, pre_gain)
+    mine_out[1] = jnp.where(before, pre_gain * got + pre, pre)
 
 
 def later_fixed(steps, got_ref, mine_ref):
-    got = jnp.where(bit_of("layer", steps - 1), 0.0, mine_ref[2] * got_ref[...])
-    return mine_ref[3] + got
-
-
-def fixed_kernel(steps, _, got_ref, mine_ref, guess_ref, start_ref, adj_ref, state_ref):
+    got = jnp.where(bit_of("layer", steps - 1), 0.0, mine_ref[0] * got_ref[...])
+    return mine_ref[1] + got
+
+
+def fixed_kernel(
+    steps, _, got_ref, mine_ref, late_ref, mine_fwd_ref, guess_ref, start_ref, adj_ref, state_ref
+):
     place = lax.axis_index("layer")
     adj = in_order(later_fixed(steps, got_ref, mine_ref))
-    got = jnp.where(bit_of("layer", steps - 1), mine_ref[0] * got_ref[...], 0.0)
-    state = in_order(mine_ref[1] + got)
+    late = jnp.where(bit_of("layer", steps - 1), mine_fwd_ref[0] * late_ref[...], 0.0)
+    state = in_order(mine_fwd_ref[1] + late)
     adj_ref[0, 0] = jnp.where(place == lax.axis_size("layer") - 1, guess_ref[0, 0], adj)
     state_ref[0, 0] = jnp.where(place == 0, start_ref[0, 0], state)
 
@@ -315,7 +324,7 @@
         bias_ref[n : n + 1, :] = jnp.sum(jnp.where(eye, column, 0.0), axis=0, keepdims=True)
 
 
-def call(kernel, out_shape, args, hbm_in=(), hbm_out=(), scratch=()):
+def call(kernel, out_shape, args, hbm_in=(), hbm_out=(), scratch=(), work=2**28):
     return pl.pallas_call(
         kernel,
         out_shape=out_shape,
@@ -323,7 +332,7 @@
         out_specs=[HBM if k in hbm_out else VMEM for k in range(len(out_shape))],
         scratch_shapes=list(scratch),
         compiler_params=pltpu.CompilerParams(vmem_limit_bytes=LIMIT),
-        cost_estimate=pl.CostEstimate(flops=2**28, bytes_accessed=2**20, transcendentals=0),
+        cost_estimate=pl.CostEstimate(flops=work, bytes_accessed=0, transcendentals=0),
     )(*(pltpu.with_memory_space_constraint(a, pltpu.HBM) if k in hbm_in else a for k, a in enumerate(args)))
 
 
@@ -344,11 +353,12 @@
     shares = lax.axis_size("dp")
     steps = lax.axis_size("layer").bit_length() - 1
     args = (state_guess, adjoint_guess, conv_weight, conv_bias)
-    guess, total, slope, rounded, back_w = call(
+    guess, total, fwd, slope, rounded, back_w = call(
         relax_kernel,
         (
             f32(chans, HW),
-            f32(3, chans, HW),
+            f32(2, chans, HW),
+            f32(chans, HW),
             f32(depth, chans, HW),
             bf16(depth, chans, HW),
             bf16(depth, chans, width),
@@ -358,31 +368,43 @@
         scratch=[pltpu.VMEM(a.shape, a.dtype) for a in args] + [pltpu.SemaphoreType.DMA((4,))],
     )
     (patch,) = call(patch_kernel, (bf16(depth, width, HW),), (rounded,))
-    one = f32(chans, HW)
-    shapes = [(f32(3, chans, HW), f32(4, chans, HW))] * (steps - 3) + [(one, f32(4, chans, HW))]
+    one, pair = f32(chans, HW), f32(2, chans, HW)
+    gots = [exchange(total, "layer", mask) for mask in (1, 2, 3)]
+    got_fwds = [exchange(fwd, "layer", mask) for mask in (1, 2, 3)]
+    fwd, mine_fwd = call(
+        earlier_four_kernel, (one, pair), (total, *gots, fwd, *got_fwds), work=0
+    )
     total, mine = call(
-        functools.partial(four_kernel, steps == 3),
-        shapes[0],
-        (total, *(exchange(total, "layer", mask) for mask in (1, 2, 3))),
-    )
-    for step in range(3, steps):
+        later_four_kernel, (one if steps == 3 else pair, pair), (total, *gots), work=0
+    )
+    for step in range(2, steps - 1):
+        got, got_fwd = (exchange(x, "layer", 1 << step) for x in (total, fwd))
+        fwd, mine_fwd = call(
+            functools.partial(earlier_kernel, step),
+            (one, pair),
+            (total, got, fwd, got_fwd, mine_fwd),
+            work=0,
+        )
         total, mine = call(
-            functools.partial(join_kernel, step, step == steps - 1),
-            shapes[step - 2],
-            (total, exchange(total, "layer", 1 << (step - 1)), mine),
+            functools.partial(later_kernel, step),
+            (one if step == steps - 2 else pair, pair),
+            (total, got, mine),
+            work=0,
         )
-    got = exchange(total, "layer", 1 << (steps - 1))
+    got, late = (exchange(x, "layer", 1 << (steps - 1)) for x in (total, fwd))
     lanes = -(-(width + 1) // HALF) * HALF
     part = (depth * chans // shares, lanes)
     keep, *sends = call(
         functools.partial(grad_kernel, steps),
         (f32(*part),) * shares,
         (got, mine, guess, slope, patch, back_w),
+        work=GRAD_WORK,
     )
     adjoint_fixed, state_fixed = call(
         functools.partial(fixed_kernel, steps),
         (f32(*adjoint_guess.shape), f32(*state_guess.shape)),
-        (keep, got, mine, adjoint_guess, state_guess),
+        (keep, got, mine, late, mine_fwd, adjoint_guess, state_guess),
+        work=FIXED_WORK,
     )
     both = exchange(sends[2], "dp", 3)
     chip = exchange(sends[1], "dp", 2)

time: 24.3 us -> 25.4 us (1.045)
  starting transfers between devices: 9.29 us -> 16 us
  waiting for transfers between devices: 8.33 us -> 2.66 us
    ppermute x7 -> x11, starting transfers between devices: 9.29 us -> 16 us  [exchange(): lax.ppermute(x, axis, [(i, i ^ mask) for i in range(lax.axis_size(axis))])]
    ppermute x7 -> x11, waiting for transfers between devices: 8.33 us -> 2.66 us  [exchange(): lax.ppermute(x, axis, [(i, i ^ mask) for i in range(lax.axis_size(axis))])]
    pallas_call x6 -> x7, Pallas kernels: 5.84 us -> 5.85 us  [call(): pl.pallas_call(kernel, out_shape=out_shape, in_specs=[HBM if k in hbm_in...]
  transfers between devices with their start and end apart: 7 -> 11, of which waited for: 5 -> 4; matrix products, arithmetic and copies ran while one was open for 0% -> 0% of each run, Pallas kernels for 5% -> 9%
where the time goes in v15:
time: 25.4 us; the launch traced here: 25.2 us
  starting transfers between devices  16 us (63%)
  Pallas kernels  5.85 us (23%)
  waiting for transfers between devices  2.66 us (10%)
  between operations  0.71 us (3%)
    ppermute x11, starting transfers between devices, exchange(): lax.ppermute(x, axis, [(i, i ^ mask) for i in range(lax.axis_size(axis))])  16 us
    pallas_call x7, Pallas kernels, call(): pl.pallas_call(kernel, out_shape=out_shape, in_specs=[HBM if k in hbm_in...  5.85 us
    ppermute x11, waiting for transfers between devices, exchange(): lax.ppermute(x, axis, [(i, i ^ mask) for i in range(lax.axis_size(axis))])  2.66 us
  transfers between devices with their start and end apart: 11, of which 4 were waited for; matrix products, arithmetic and copies ran while one was open for 0% of the time, Pallas kernels for 9%

profile of v15, /device:TPU:0, one launch (start us, length us, event | category | flops | bytes accessed | tf_op | source)
XLA Modules:
  0.0 25.2 jit_solution(15421778864219865662)
XLA Ops:
  0.6 2.9 %shard_map.75 = (f32[32,256]{1,0:T(8,128)S(1)}, f32[2,32,256]{2,1,0:T(8,128)S(1)}, f32[32,256]{1,0:T(8,128)S(1)}, f32[4,32,256]{2,1,0:T(8,128)S(1)}, bf16[4,32,2...) custom-call(f32[1,1,32,256]{3,2,1,0:T(8,128)} %start_ref.1, f32[1,1,32,256]{3,2,1,0:T(8,128)} %guess_ref.1, ...), custom_call_target="tpu_custom_call" | custom-call | flops 268435456 | tf_op jit(solution)/shard_map/pallas_call | solution.py:328
  3.6 4.0 %collective-permute-start.2 = (f32[2,32,256]{2,1,0:T(8,128)S(1)}, f32[2,32,256]{2,1,0:T(8,128)S(1)}, u32[]{:S(2)}, u32[]{:S(2)}) collective-permute-start(f32[2,32,256]{2,1,0:T(8,128)S(1)} %get-tuple-element.22.own_ref.refs_0_), channel_id=1, source_target_pairs={{0,12},{4,8},{8,4},{12,0},{16,28},{20,24},{24,20},{28,16},{1,13},{... | collective-permute-start | bytes 196616 | tf_op jit(solution)/shard_map/ppermute | solution.py:348
  7.6 0.5 %collective-permute-start.1 = (f32[2,32,256]{2,1,0:T(8,128)S(1)}, f32[2,32,256]{2,1,0:T(8,128)S(1)}, u32[]{:S(2)}, u32[]{:S(2)}) collective-permute-start(f32[2,32,256]{2,1,0:T(8,128)S(1)} %get-tuple-element.22.own_ref.refs_0_), channel_id=1, source_target_pairs={{0,8},{4,12},{8,0},{12,4},{16,24},{20,28},{24,16},{28,20},{1,9},{5... | collective-permute-start | bytes 196616 | tf_op jit(solution)/shard_map/ppermute | solution.py:348
  8.0 0.2 collective-permute-start
  8.2 2.8 %collective-permute-start.6 = (f32[32,256]{1,0:T(8,128)S(1)}, f32[32,256]{1,0:T(8,128)S(1)}, u32[]{:S(2)}, u32[]{:S(2)}) collective-permute-start(f32[32,256]{1,0:T(8,128)S(1)} %get-tuple-element.30.refs_4_), channel_id=1, source_target_pairs={{0,12},{4,8},{8,4},{12,0},{16,28},{20,24},{24,20},{28,16},{1,13},{... | collective-permute-start | bytes 98312 | tf_op jit(solution)/shard_map/ppermute | solution.py:348
  11.1 0.5 %collective-permute-start.5 = (f32[32,256]{1,0:T(8,128)S(1)}, f32[32,256]{1,0:T(8,128)S(1)}, u32[]{:S(2)}, u32[]{:S(2)}) collective-permute-start(f32[32,256]{1,0:T(8,128)S(1)} %get-tuple-element.30.refs_4_), channel_id=1, source_target_pairs={{0,8},{4,12},{8,0},{12,4},{16,24},{20,28},{24,16},{28,20},{1,9},{5... | collective-permute-start | bytes 98312 | tf_op jit(solution)/shard_map/ppermute | solution.py:348
  11.5 0.7 %collective-permute-start.4 = (f32[32,256]{1,0:T(8,128)S(1)}, f32[32,256]{1,0:T(8,128)S(1)}, u32[]{:S(2)}, u32[]{:S(2)}) collective-permute-start(f32[32,256]{1,0:T(8,128)S(1)} %get-tuple-element.30.refs_4_), channel_id=1, source_target_pairs={{0,4},{4,0},{8,12},{12,8},{16,20},{20,16},{24,28},{28,24},{1,5},{5... | collective-permute-start | bytes 98312 | tf_op jit(solution)/shard_map/ppermute | solution.py:348
  12.3 0.0 collective-permute-done.first_ref.refs_1_
  12.3 0.1 shard_map.76
  12.4 2.7 %collective-permute-start.3 = (f32[32,256]{1,0:T(8,128)S(1)}, f32[32,256]{1,0:T(8,128)S(1)}, u32[]{:S(2)}, u32[]{:S(2)}) collective-permute-start(f32[32,256]{1,0:T(8,128)S(1)} %get-tuple-element.23), channel_id=1, source_target_pairs={{0,16},{4,20},{8,24},{12,28},{16,0},{20,4},{24,8},{28,12},{1,17},{... | collective-permute-start | bytes 98312 | tf_op jit(solution)/shard_map/ppermute | solution.py:348
  15.1 0.1 collective-permute-done.5.refs_6_
  15.2 0.3 %collective-permute-done.4.refs_5_ = f32[32,256]{1,0:T(8,128)S(1)} collective-permute-done((f32[32,256]{1,0:T(8,128)S(1)}, f32[32,256]{1,0:T(8,128)S(1)}, u32[]{:S(2)}, u32[]{:S(2)}) %collective-permute-start.4) | collective-permute-done | bytes 32800 | tf_op jit(solution)/shard_map/ppermute | solution.py:348
  15.4 0.1 shard_map.79
  15.5 2.7 %collective-permute-start.7 = (f32[32,256]{1,0:T(8,128)S(1)}, f32[32,256]{1,0:T(8,128)S(1)}, u32[]{:S(2)}, u32[]{:S(2)}) collective-permute-start(f32[32,256]{1,0:T(8,128)S(1)} %get-tuple-element.31), channel_id=1, source_target_pairs={{0,16},{4,20},{8,24},{12,28},{16,0},{20,4},{24,8},{28,12},{1,17},{... | collective-permute-start | bytes 98312 | tf_op jit(solution)/shard_map/ppermute | solution.py:348
  18.2 0.5 %shard_map.77.patch_ref = bf16[4,288,256]{2,1,0:T(8,128)(2,1)S(1)} custom-call(bf16[4,32,256]{2,1,0:T(8,128)(2,1)S(1)} %get-tuple-element.27.rounded_ref), custom_call_target="tpu_custom_call" | custom-call | flops 268435456 | tf_op jit(solution)/shard_map/pallas_call | solution.py:328
  18.7 0.0 copy-start
  18.7 0.9 %shard_map.78 = (f32[32,384]{1,0:T(8,128)S(1)}, f32[32,384]{1,0:T(8,128)S(1)}, f32[32,384]{1,0:T(8,128)S(1)}, f32[32,384]{1,0:T(8,128)S(1)}) custom-call(f32[32,256]{1,0:T(8,128)S(1)} %collective-permute-done.3.got_ref, f32[2,32,256]{2,1,0:T(8,128)S(1)} %get-tuple-element.24.mine_ref, f32[32,256]{1,0:T(8,128)S(1)} %get-tuple-element.25.guess_ref, ...), custom_call_target="tpu_custom_call" | custom-call | flops 268435456 | tf_op jit(solution)/shard_map/pallas_call | solution.py:328
  19.6 0.1 collective-permute-start.8
  19.7 1.6 %collective-permute-start.9 = (f32[32,384]{1,0:T(8,128)S(1)}, f32[32,384]{1,0:T(8,128)S(1)}, u32[]{:S(2)}, u32[]{:S(2)}) collective-permute-start(f32[32,384]{1,0:T(8,128)S(1)} %get-tuple-element.36), channel_id=1, source_target_pairs={{0,2},{1,3},{2,0},{3,1},{4,6},{5,7},{6,4},{7,5},{8,10},{9,11},{10,... | collective-permute-start | bytes 147464 | tf_op jit(solution)/shard_map/ppermute | solution.py:348
  21.3 0.3 %collective-permute-start.10 = (f32[32,384]{1,0:T(8,128)S(1)}, f32[32,384]{1,0:T(8,128)S(1)}, u32[]{:S(2)}, u32[]{:S(2)}) collective-permute-start(f32[32,384]{1,0:T(8,128)S(1)} %get-tuple-element.37), channel_id=1, source_target_pairs={{0,1},{1,0},{2,3},{3,2},{4,5},{5,4},{6,7},{7,6},{8,9},{9,8},{10,11... | collective-permute-start | bytes 147464 | tf_op jit(solution)/shard_map/ppermute | solution.py:348
  21.6 0.7 %shard_map.80 = (f32[1,1,32,256]{3,2,1,0:T(8,128)}, f32[1,1,32,256]{3,2,1,0:T(8,128)}) custom-call(f32[32,384]{1,0:T(8,128)S(1)} %get-tuple-element.29._.mine_ref, f32[32,256]{1,0:T(8,128)S(1)} %collective-permute-done.3.got_ref, f32[2,32,256]{2,1,0:T(8,128)S(1)} %get-tuple-element.24.mine_ref, f32[32,256]{1,0:T(8,128)S(1)} %collective-permute-done.7.late_ref, ...), custom_call_target="tpu_custom_call" | custom-call | flops 4294967296 | tf_op jit(solution)/shard_map/pallas_call | solution.py:328
  22.3 1.3 %collective-permute-done.8.both_ref = f32[32,384]{1,0:T(8,128)S(1)} collective-permute-done((f32[32,384]{1,0:T(8,128)S(1)}, f32[32,384]{1,0:T(8,128)S(1)}, u32[]{:S(2)}, u32[]{:S(2)}) %collective-permute-start.8) | collective-permute-done | bytes 49184 | tf_op jit(solution)/shard_map/ppermute | solution.py:348
  23.6 0.9 %collective-permute-done.9.chip_ref = f32[32,384]{1,0:T(8,128)S(1)} collective-permute-done((f32[32,384]{1,0:T(8,128)S(1)}, f32[32,384]{1,0:T(8,128)S(1)}, u32[]{:S(2)}, u32[]{:S(2)}) %collective-permute-start.9) | collective-permute-done | bytes 49184 | tf_op jit(solution)/shard_map/ppermute | solution.py:348
  24.6 0.7 %shard_map.81 = (f32[4,8,288]{2,1,0:T(8,128)}, f32[4,8]{1,0:T(4,128)}) custom-call(f32[32,384]{1,0:T(8,128)S(1)} %get-tuple-element.29._.mine_ref, f32[32,384]{1,0:T(8,128)S(1)} %collective-permute-done.8.both_ref, f32[32,384]{1,0:T(8,128)S(1)} %collective-permute-done.9.chip_ref, f32[32,384]{1,0:T(8,128)S(1)} %collective-permute-done.10.core_ref), custom_call_target="tpu_custom_call" | custom-call | flops 268435456 | tf_op jit(solution)/shard_map/pallas_call | solution.py:328
  (9 shorter events, 0.0 us)
Async XLA Ops:
  3.6 8.0 %collective-permute-start.2 = (f32[2,32,256]{2,1,0:T(8,128)S(1)}, f32[2,32,256]{2,1,0:T(8,128)S(1)}, u32[]{:S(2)}, u32[]{:S(2)}) collective-permute-start(f32[2,32,256]{2,1,0:T(8,128)S(1)} %get-tuple-element.22.own_ref.refs_0_), channel_id=1, source_target_pairs={{0,12},{4,8},{8,4},{12,0},{16,28},{20,24},{24,20},{28,16},{1,13},{... | collective-permute-start | bytes 196616 | tf_op jit(solution)/shard_map/ppermute | solution.py:348
  7.6 4.7 %collective-permute-start.1 = (f32[2,32,256]{2,1,0:T(8,128)S(1)}, f32[2,32,256]{2,1,0:T(8,128)S(1)}, u32[]{:S(2)}, u32[]{:S(2)}) collective-permute-start(f32[2,32,256]{2,1,0:T(8,128)S(1)} %get-tuple-element.22.own_ref.refs_0_), channel_id=1, source_target_pairs={{0,8},{4,12},{8,0},{12,4},{16,24},{20,28},{24,16},{28,20},{1,9},{5... | collective-permute-start | bytes 196616 | tf_op jit(solution)/shard_map/ppermute | solution.py:348
  8.0 4.3 %collective-permute-start = (f32[2,32,256]{2,1,0:T(8,128)S(1)}, f32[2,32,256]{2,1,0:T(8,128)S(1)}, u32[]{:S(2)}, u32[]{:S(2)}) collective-permute-start(f32[2,32,256]{2,1,0:T(8,128)S(1)} %get-tuple-element.22.own_ref.refs_0_), channel_id=1, source_target_pairs={{0,4},{4,0},{8,12},{12,8},{16,20},{20,16},{24,28},{28,24},{1,5},{5... | collective-permute-start | bytes 196616 | tf_op jit(solution)/shard_map/ppermute | solution.py:348
  8.2 6.9 %collective-permute-start.6 = (f32[32,256]{1,0:T(8,128)S(1)}, f32[32,256]{1,0:T(8,128)S(1)}, u32[]{:S(2)}, u32[]{:S(2)}) collective-permute-start(f32[32,256]{1,0:T(8,128)S(1)} %get-tuple-element.30.refs_4_), channel_id=1, source_target_pairs={{0,12},{4,8},{8,4},{12,0},{16,28},{20,24},{24,20},{28,16},{1,13},{... | collective-permute-start | bytes 98312 | tf_op jit(solution)/shard_map/ppermute | solution.py:348
  11.1 4.1 %collective-permute-start.5 = (f32[32,256]{1,0:T(8,128)S(1)}, f32[32,256]{1,0:T(8,128)S(1)}, u32[]{:S(2)}, u32[]{:S(2)}) collective-permute-start(f32[32,256]{1,0:T(8,128)S(1)} %get-tuple-element.30.refs_4_), channel_id=1, source_target_pairs={{0,8},{4,12},{8,0},{12,4},{16,24},{20,28},{24,16},{28,20},{1,9},{5... | collective-permute-start | bytes 98312 | tf_op jit(solution)/shard_map/ppermute | solution.py:348
  11.5 3.9 %collective-permute-start.4 = (f32[32,256]{1,0:T(8,128)S(1)}, f32[32,256]{1,0:T(8,128)S(1)}, u32[]{:S(2)}, u32[]{:S(2)}) collective-permute-start(f32[32,256]{1,0:T(8,128)S(1)} %get-tuple-element.30.refs_4_), channel_id=1, source_target_pairs={{0,4},{4,0},{8,12},{12,8},{16,20},{20,16},{24,28},{28,24},{1,5},{5... | collective-permute-start | bytes 98312 | tf_op jit(solution)/shard_map/ppermute | solution.py:348
  12.4 6.4 %collective-permute-start.3 = (f32[32,256]{1,0:T(8,128)S(1)}, f32[32,256]{1,0:T(8,128)S(1)}, u32[]{:S(2)}, u32[]{:S(2)}) collective-permute-start(f32[32,256]{1,0:T(8,128)S(1)} %get-tuple-element.23), channel_id=1, source_target_pairs={{0,16},{4,20},{8,24},{12,28},{16,0},{20,4},{24,8},{28,12},{1,17},{... | collective-permute-start | bytes 98312 | tf_op jit(solution)/shard_map/ppermute | solution.py:348
  15.5 6.0 %collective-permute-start.7 = (f32[32,256]{1,0:T(8,128)S(1)}, f32[32,256]{1,0:T(8,128)S(1)}, u32[]{:S(2)}, u32[]{:S(2)}) collective-permute-start(f32[32,256]{1,0:T(8,128)S(1)} %get-tuple-element.31), channel_id=1, source_target_pairs={{0,16},{4,20},{8,24},{12,28},{16,0},{20,4},{24,8},{28,12},{1,17},{... | collective-permute-start | bytes 98312 | tf_op jit(solution)/shard_map/ppermute | solution.py:348
  18.7 2.8 %copy-start = (f32[1,1,32,256]{3,2,1,0:T(8,128)S(1)}, f32[1,1,32,256]{3,2,1,0:T(8,128)}, u32[]{:S(2)}) copy-start(f32[1,1,32,256]{3,2,1,0:T(8,128)} %start_ref.1) | copy-start | bytes 98308
  18.7 2.8 %copy-start.1 = (f32[1,1,32,256]{3,2,1,0:T(8,128)S(1)}, f32[1,1,32,256]{3,2,1,0:T(8,128)}, u32[]{:S(2)}) copy-start(f32[1,1,32,256]{3,2,1,0:T(8,128)} %guess_ref.1) | copy-start | bytes 98308
  19.6 4.0 %collective-permute-start.8 = (f32[32,384]{1,0:T(8,128)S(1)}, f32[32,384]{1,0:T(8,128)S(1)}, u32[]{:S(2)}, u32[]{:S(2)}) collective-permute-start(f32[32,384]{1,0:T(8,128)S(1)} %get-tuple-element.35), channel_id=1, source_target_pairs={{0,3},{1,2},{2,1},{3,0},{4,7},{5,6},{6,5},{7,4},{8,11},{9,10},{10,... | collective-permute-start | bytes 147464 | tf_op jit(solution)/shard_map/ppermute | solution.py:348
  19.7 4.9 %collective-permute-start.9 = (f32[32,384]{1,0:T(8,128)S(1)}, f32[32,384]{1,0:T(8,128)S(1)}, u32[]{:S(2)}, u32[]{:S(2)}) collective-permute-start(f32[32,384]{1,0:T(8,128)S(1)} %get-tuple-element.36), channel_id=1, source_target_pairs={{0,2},{1,3},{2,0},{3,1},{4,6},{5,7},{6,4},{7,5},{8,10},{9,11},{10,... | collective-permute-start | bytes 147464 | tf_op jit(solution)/shard_map/ppermute | solution.py:348
  21.3 3.3 %collective-permute-start.10 = (f32[32,384]{1,0:T(8,128)S(1)}, f32[32,384]{1,0:T(8,128)S(1)}, u32[]{:S(2)}, u32[]{:S(2)}) collective-permute-start(f32[32,384]{1,0:T(8,128)S(1)} %get-tuple-element.37), channel_id=1, source_target_pairs={{0,1},{1,0},{2,3},{3,2},{4,5},{5,4},{6,7},{7,6},{8,9},{9,8},{10,11... | collective-permute-start | bytes 147464 | tf_op jit(solution)/shard_map/ppermute | solution.py:348

commit v16 on v14

--- a/solution.py
+++ b/solution.py
@@ -171,12 +171,26 @@
     sent_ref[2] = back - gain * last
 
 
-def patch_kernel(rounded_ref, patch_ref):
+def put_patches(rounded_ref, patch_ref):
     depth, chans, _ = rounded_ref.shape
     perm = permutation(chans)
     for n in range(depth):
         patch = taps_of(rounded_ref[n])
         patch_ref[n] = dot(perm, patch, ((0,), (0,))).astype(jnp.bfloat16)
+
+
+def patch_kernel(rounded_ref, early_ref, patch_ref):
+    @pl.when(jnp.logical_not(bit_of("dp", 0)))
+    def _():
+        put_patches(rounded_ref, patch_ref)
+
+
+def early_patch_kernel(rounded_ref, total_ref, patch_ref, sent_ref):
+    sent_ref[...] = total_ref[...]
+
+    @pl.when(bit_of("dp", 0))
+    def _():
+        put_patches(rounded_ref, patch_ref)
 
 
 def joined(bit, total, mine, got):
@@ -315,13 +329,14 @@
         bias_ref[n : n + 1, :] = jnp.sum(jnp.where(eye, column, 0.0), axis=0, keepdims=True)
 
 
-def call(kernel, out_shape, args, hbm_in=(), hbm_out=(), scratch=()):
+def call(kernel, out_shape, args, hbm_in=(), hbm_out=(), scratch=(), aliases={}):
     return pl.pallas_call(
         kernel,
         out_shape=out_shape,
         in_specs=[HBM if k in hbm_in else VMEM for k in range(len(args))],
         out_specs=[HBM if k in hbm_out else VMEM for k in range(len(out_shape))],
         scratch_shapes=list(scratch),
+        input_output_aliases=aliases,
         compiler_params=pltpu.CompilerParams(vmem_limit_bytes=LIMIT),
         cost_estimate=pl.CostEstimate(flops=2**28, bytes_accessed=2**20, transcendentals=0),
     )(*(pltpu.with_memory_space_constraint(a, pltpu.HBM) if k in hbm_in else a for k, a in enumerate(args)))
@@ -357,7 +372,10 @@
         hbm_in=range(4),
         scratch=[pltpu.VMEM(a.shape, a.dtype) for a in args] + [pltpu.SemaphoreType.DMA((4,))],
     )
-    (patch,) = call(patch_kernel, (bf16(depth, width, HW),), (rounded,))
+    early, total = call(
+        early_patch_kernel, (bf16(depth, width, HW), f32(3, chans, HW)), (rounded, total)
+    )
+    (patch,) = call(patch_kernel, (bf16(depth, width, HW),), (rounded, early), aliases={1: 0})
     one = f32(chans, HW)
     shapes = [(f32(3, chans, HW), f32(4, chans, HW))] * (steps - 3) + [(one, f32(4, chans, HW))]
     total, mine = call(

time: 24.3 us -> 24.8 us (1.021)
  waiting for transfers between devices: 8.33 us -> 8.9 us
    ppermute x7, waiting for transfers between devices: 8.33 us -> 8.9 us  [exchange(): lax.ppermute(x, axis, [(i, i ^ mask) for i in range(lax.axis_size(axis))])]
    pallas_call x6 -> x7, Pallas kernels: 5.84 us -> 5.85 us  [call(): pl.pallas_call(kernel, out_shape=out_shape, in_specs=[HBM if k in hbm_in...]
where the time goes in v16:
time: 24.8 us; the launch traced here: 24.7 us
  starting transfers between devices  9.25 us (37%)
  waiting for transfers between devices  8.9 us (36%)
  Pallas kernels  5.85 us (24%)
  between operations  0.69 us (3%)
    ppermute x7, starting transfers between devices, exchange(): lax.ppermute(x, axis, [(i, i ^ mask) for i in range(lax.axis_size(axis))])  9.25 us
    ppermute x7, waiting for transfers between devices, exchange(): lax.ppermute(x, axis, [(i, i ^ mask) for i in range(lax.axis_size(axis))])  8.9 us
    pallas_call x7, Pallas kernels, call(): pl.pallas_call(kernel, out_shape=out_shape, in_specs=[HBM if k in hbm_in...  5.85 us
  transfers between devices with their start and end apart: 7, of which 5 were waited for; matrix products, arithmetic and copies ran while one was open for 0% of the time, Pallas kernels for 5%

profile of v16, /device:TPU:0, one launch (start us, length us, event | category | flops | bytes accessed | tf_op | source)
XLA Modules:
  0.0 24.7 jit_solution(14280931166648716167)
XLA Ops:
  0.6 2.9 %shard_map.75 = (f32[32,256]{1,0:T(8,128)S(1)}, f32[3,32,256]{2,1,0:T(8,128)S(1)}, f32[4,32,256]{2,1,0:T(8,128)S(1)}, bf16[4,32,256]{2,1,0:T(8,128)(2,1)S(1)}, bf16[4,32,288]{2,1,0:T(8,128)(2,1)S(1)}) custom-call(f32[1,1,32,256]{3,2,1,0:T(8,128)} %start_ref.1, f32[1,1,32,256]{3,2,1,0:T(8,128)} %guess_ref.1, bf16[4,32,288]{2,1,0:T(8,128)(2,1)} %w_hbm.1, ...), custom_call_target="tpu_custom_call" | custom-call | flops 268435456 | bytes 1048576 | tf_op jit(solution)/shard_map/pallas_call | solution.py:333
  3.6 4.0 %collective-permute-start.2 = (f32[3,32,256]{2,1,0:T(8,128)S(1)}, f32[3,32,256]{2,1,0:T(8,128)S(1)}, u32[]{:S(2)}, u32[]{:S(2)}) collective-permute-start(f32[3,32,256]{2,1,0:T(8,128)S(1)} %get-tuple-element.23.own_ref), channel_id=1, source_target_pairs={{0,12},{4,8},{8,4},{12,0},{16,28},{20,24},{24,20},{28,16},{1,13},{... | collective-permute-start | bytes 294920 | tf_op jit(solution)/shard_map/ppermute | solution.py:354
  7.6 0.5 %collective-permute-start.1 = (f32[3,32,256]{2,1,0:T(8,128)S(1)}, f32[3,32,256]{2,1,0:T(8,128)S(1)}, u32[]{:S(2)}, u32[]{:S(2)}) collective-permute-start(f32[3,32,256]{2,1,0:T(8,128)S(1)} %get-tuple-element.23.own_ref), channel_id=1, source_target_pairs={{0,8},{4,12},{8,0},{12,4},{16,24},{20,28},{24,16},{28,20},{1,9},{5... | collective-permute-start | bytes 294920 | tf_op jit(solution)/shard_map/ppermute | solution.py:354
  8.1 0.2 collective-permute-start
  8.3 3.0 %collective-permute-done.2.third_ref = f32[3,32,256]{2,1,0:T(8,128)S(1)} collective-permute-done((f32[3,32,256]{2,1,0:T(8,128)S(1)}, f32[3,32,256]{2,1,0:T(8,128)S(1)}, u32[]{:S(2)}, u32[]{:S(2)}) %collective-permute-start.2) | collective-permute-done | bytes 98336 | tf_op jit(solution)/shard_map/ppermute | solution.py:354
  11.3 2.0 %collective-permute-done.1.second_ref = f32[3,32,256]{2,1,0:T(8,128)S(1)} collective-permute-done((f32[3,32,256]{2,1,0:T(8,128)S(1)}, f32[3,32,256]{2,1,0:T(8,128)S(1)}, u32[]{:S(2)}, u32[]{:S(2)}) %collective-permute-start.1) | collective-permute-done | bytes 98336 | tf_op jit(solution)/shard_map/ppermute | solution.py:354
  13.2 0.0 collective-permute-done.first_ref
  13.2 0.1 shard_map.77
  13.3 2.7 %collective-permute-start.3 = (f32[32,256]{1,0:T(8,128)S(1)}, f32[32,256]{1,0:T(8,128)S(1)}, u32[]{:S(2)}, u32[]{:S(2)}) collective-permute-start(f32[32,256]{1,0:T(8,128)S(1)} %get-tuple-element.24), channel_id=1, source_target_pairs={{0,16},{4,20},{8,24},{12,28},{16,0},{20,4},{24,8},{28,12},{1,17},{... | collective-permute-start | bytes 98312 | tf_op jit(solution)/shard_map/ppermute | solution.py:354
  16.0 0.6 %shard_map.78.patch_ref = bf16[4,288,256]{2,1,0:T(8,128)(2,1)S(1)} custom-call(bf16[4,32,256]{2,1,0:T(8,128)(2,1)S(1)} %get-tuple-element.21.rounded_ref, bf16[4,288,256]{2,1,0:T(8,128)(2,1)S(1)} %get-tuple-element.28.early_ref), custom_call_target="tpu_custom_call", output_to_operand_aliasing={{}: (1, {})} | custom-call | flops 268435456 | bytes 1048576 | tf_op jit(solution)/shard_map/pallas_call | solution.py:333
  16.5 1.7 %collective-permute-done.3.got_ref = f32[32,256]{1,0:T(8,128)S(1)} collective-permute-done((f32[32,256]{1,0:T(8,128)S(1)}, f32[32,256]{1,0:T(8,128)S(1)}, u32[]{:S(2)}, u32[]{:S(2)}) %collective-permute-start.3) | collective-permute-done | bytes 32800 | tf_op jit(solution)/shard_map/ppermute | solution.py:354
  18.2 0.0 copy-start
  18.2 0.0 copy-start.1
  18.2 0.9 %shard_map.79 = (f32[32,384]{1,0:T(8,128)S(1)}, f32[32,384]{1,0:T(8,128)S(1)}, f32[32,384]{1,0:T(8,128)S(1)}, f32[32,384]{1,0:T(8,128)S(1)}) custom-call(f32[32,256]{1,0:T(8,128)S(1)} %collective-permute-done.3.got_ref, f32[4,32,256]{2,1,0:T(8,128)S(1)} %get-tuple-element.25.mine_ref, f32[32,256]{1,0:T(8,128)S(1)} %get-tuple-element.26.guess_ref, ...), custom_call_target="tpu_custom_call" | custom-call | flops 268435456 | bytes 1048576 | tf_op jit(solution)/shard_map/pallas_call | solution.py:333
  19.1 0.1 collective-permute-start.4
  19.2 1.6 %collective-permute-start.5 = (f32[32,384]{1,0:T(8,128)S(1)}, f32[32,384]{1,0:T(8,128)S(1)}, u32[]{:S(2)}, u32[]{:S(2)}) collective-permute-start(f32[32,384]{1,0:T(8,128)S(1)} %get-tuple-element.34), channel_id=1, source_target_pairs={{0,2},{1,3},{2,0},{3,1},{4,6},{5,7},{6,4},{7,5},{8,10},{9,11},{10,... | collective-permute-start | bytes 147464 | tf_op jit(solution)/shard_map/ppermute | solution.py:354
  20.7 0.3 %collective-permute-start.6 = (f32[32,384]{1,0:T(8,128)S(1)}, f32[32,384]{1,0:T(8,128)S(1)}, u32[]{:S(2)}, u32[]{:S(2)}) collective-permute-start(f32[32,384]{1,0:T(8,128)S(1)} %get-tuple-element.35), channel_id=1, source_target_pairs={{0,1},{1,0},{2,3},{3,2},{4,5},{5,4},{6,7},{7,6},{8,9},{9,8},{10,11... | collective-permute-start | bytes 147464 | tf_op jit(solution)/shard_map/ppermute | solution.py:354
  21.0 0.0 copy-done
  21.0 0.0 copy-done.1
  21.0 0.7 %shard_map.80 = (f32[1,1,32,256]{3,2,1,0:T(8,128)}, f32[1,1,32,256]{3,2,1,0:T(8,128)}) custom-call(f32[32,384]{1,0:T(8,128)S(1)} %get-tuple-element.30._.mine_ref, f32[32,256]{1,0:T(8,128)S(1)} %collective-permute-done.3.got_ref, f32[4,32,256]{2,1,0:T(8,128)S(1)} %get-tuple-element.25.mine_ref, f32[1,1,32,256]{3,2,1,0:T(8,128)S(1)} %copy-done.1, ...), custom_call_target="tpu_custom_call" | custom-call | flops 268435456 | bytes 1048576 | tf_op jit(solution)/shard_map/pallas_call | solution.py:333
  21.8 1.4 %collective-permute-done.4.both_ref = f32[32,384]{1,0:T(8,128)S(1)} collective-permute-done((f32[32,384]{1,0:T(8,128)S(1)}, f32[32,384]{1,0:T(8,128)S(1)}, u32[]{:S(2)}, u32[]{:S(2)}) %collective-permute-start.4) | collective-permute-done | bytes 49184 | tf_op jit(solution)/shard_map/ppermute | solution.py:354
  23.1 0.9 %collective-permute-done.5.chip_ref = f32[32,384]{1,0:T(8,128)S(1)} collective-permute-done((f32[32,384]{1,0:T(8,128)S(1)}, f32[32,384]{1,0:T(8,128)S(1)}, u32[]{:S(2)}, u32[]{:S(2)}) %collective-permute-start.5) | collective-permute-done | bytes 49184 | tf_op jit(solution)/shard_map/ppermute | solution.py:354
  24.0 0.0 collective-permute-done.6.core_ref
  24.0 0.7 %shard_map.81 = (f32[4,8,288]{2,1,0:T(8,128)}, f32[4,8]{1,0:T(4,128)}) custom-call(f32[32,384]{1,0:T(8,128)S(1)} %get-tuple-element.30._.mine_ref, f32[32,384]{1,0:T(8,128)S(1)} %collective-permute-done.4.both_ref, f32[32,384]{1,0:T(8,128)S(1)} %collective-permute-done.5.chip_ref, f32[32,384]{1,0:T(8,128)S(1)} %collective-permute-done.6.core_ref), custom_call_target="tpu_custom_call" | custom-call | flops 268435456 | bytes 1048576 | tf_op jit(solution)/shard_map/pallas_call | solution.py:333
  (1 shorter events, 0.0 us)
Async XLA Ops:
  3.6 7.7 %collective-permute-start.2 = (f32[3,32,256]{2,1,0:T(8,128)S(1)}, f32[3,32,256]{2,1,0:T(8,128)S(1)}, u32[]{:S(2)}, u32[]{:S(2)}) collective-permute-start(f32[3,32,256]{2,1,0:T(8,128)S(1)} %get-tuple-element.23.own_ref), channel_id=1, source_target_pairs={{0,12},{4,8},{8,4},{12,0},{16,28},{20,24},{24,20},{28,16},{1,13},{... | collective-permute-start | bytes 294920 | tf_op jit(solution)/shard_map/ppermute | solution.py:354
  7.6 5.6 %collective-permute-start.1 = (f32[3,32,256]{2,1,0:T(8,128)S(1)}, f32[3,32,256]{2,1,0:T(8,128)S(1)}, u32[]{:S(2)}, u32[]{:S(2)}) collective-permute-start(f32[3,32,256]{2,1,0:T(8,128)S(1)} %get-tuple-element.23.own_ref), channel_id=1, source_target_pairs={{0,8},{4,12},{8,0},{12,4},{16,24},{20,28},{24,16},{28,20},{1,9},{5... | collective-permute-start | bytes 294920 | tf_op jit(solution)/shard_map/ppermute | solution.py:354
  8.1 5.1 %collective-permute-start = (f32[3,32,256]{2,1,0:T(8,128)S(1)}, f32[3,32,256]{2,1,0:T(8,128)S(1)}, u32[]{:S(2)}, u32[]{:S(2)}) collective-permute-start(f32[3,32,256]{2,1,0:T(8,128)S(1)} %get-tuple-element.23.own_ref), channel_id=1, source_target_pairs={{0,4},{4,0},{8,12},{12,8},{16,20},{20,16},{24,28},{28,24},{1,5},{5... | collective-permute-start | bytes 294920 | tf_op jit(solution)/shard_map/ppermute | solution.py:354
  13.3 4.9 %collective-permute-start.3 = (f32[32,256]{1,0:T(8,128)S(1)}, f32[32,256]{1,0:T(8,128)S(1)}, u32[]{:S(2)}, u32[]{:S(2)}) collective-permute-start(f32[32,256]{1,0:T(8,128)S(1)} %get-tuple-element.24), channel_id=1, source_target_pairs={{0,16},{4,20},{8,24},{12,28},{16,0},{20,4},{24,8},{28,12},{1,17},{... | collective-permute-start | bytes 98312 | tf_op jit(solution)/shard_map/ppermute | solution.py:354
  18.2 2.8 %copy-start = (f32[1,1,32,256]{3,2,1,0:T(8,128)S(1)}, f32[1,1,32,256]{3,2,1,0:T(8,128)}, u32[]{:S(2)}) copy-start(f32[1,1,32,256]{3,2,1,0:T(8,128)} %start_ref.1) | copy-start | bytes 98308
  18.2 2.8 %copy-start.1 = (f32[1,1,32,256]{3,2,1,0:T(8,128)S(1)}, f32[1,1,32,256]{3,2,1,0:T(8,128)}, u32[]{:S(2)}) copy-start(f32[1,1,32,256]{3,2,1,0:T(8,128)} %guess_ref.1) | copy-start | bytes 98308
  19.1 4.0 %collective-permute-start.4 = (f32[32,384]{1,0:T(8,128)S(1)}, f32[32,384]{1,0:T(8,128)S(1)}, u32[]{:S(2)}, u32[]{:S(2)}) collective-permute-start(f32[32,384]{1,0:T(8,128)S(1)} %get-tuple-element.33), channel_id=1, source_target_pairs={{0,3},{1,2},{2,1},{3,0},{4,7},{5,6},{6,5},{7,4},{8,11},{9,10},{10,... | collective-permute-start | bytes 147464 | tf_op jit(solution)/shard_map/ppermute | solution.py:354
  19.2 4.9 %collective-permute-start.5 = (f32[32,384]{1,0:T(8,128)S(1)}, f32[32,384]{1,0:T(8,128)S(1)}, u32[]{:S(2)}, u32[]{:S(2)}) collective-permute-start(f32[32,384]{1,0:T(8,128)S(1)} %get-tuple-element.34), channel_id=1, source_target_pairs={{0,2},{1,3},{2,0},{3,1},{4,6},{5,7},{6,4},{7,5},{8,10},{9,11},{10,... | collective-permute-start | bytes 147464 | tf_op jit(solution)/shard_map/ppermute | solution.py:354
  20.7 3.3 %collective-permute-start.6 = (f32[32,384]{1,0:T(8,128)S(1)}, f32[32,384]{1,0:T(8,128)S(1)}, u32[]{:S(2)}, u32[]{:S(2)}) collective-permute-start(f32[32,384]{1,0:T(8,128)S(1)} %get-tuple-element.35), channel_id=1, source_target_pairs={{0,1},{1,0},{2,3},{3,2},{4,5},{5,4},{6,7},{7,6},{8,9},{9,8},{10,11... | collective-permute-start | bytes 147464 | tf_op jit(solution)/shard_map/ppermute | solution.py:354

commit v17 on v14

--- a/solution.py
+++ b/solution.py
@@ -211,7 +211,7 @@
             sent_ref[k] = total[k]
 
 
-def four_kernel(final, own_ref, first_ref, second_ref, third_ref, sent_ref, mine_out):
+def four_kernel(final, own_ref, second_ref, first_ref, third_ref, sent_ref, mine_out):
     low, high = bit_of("layer", 0), bit_of("layer", 1)
     place = lax.rem(lax.axis_index("layer"), 4)
     maps = [
@@ -302,7 +302,7 @@
     layer(0, lax.fori_loop(0, depth - 1, behind, adj))
 
 
-def total_kernel(mine_ref, both_ref, chip_ref, core_ref, grad_ref, bias_ref):
+def total_kernel(mine_ref, chip_ref, both_ref, core_ref, grad_ref, bias_ref):
     depth, own, width = grad_ref.shape
     total = (mine_ref[...] + core_ref[...]) + (chip_ref[...] + both_ref[...])
     eye = lax.broadcasted_iota(jnp.int32, (own, own), 0) == lax.broadcasted_iota(
@@ -363,7 +363,7 @@
     total, mine = call(
         functools.partial(four_kernel, steps == 3),
         shapes[0],
-        (total, *(exchange(total, "layer", mask) for mask in (1, 2, 3))),
+        (total, *(exchange(total, "layer", mask) for mask in (2, 1, 3))),
     )
     for step in range(3, steps):
         total, mine = call(
@@ -390,7 +390,7 @@
     weight_grad, bias_grad = call(
         total_kernel,
         (f32(depth, chans // shares, width), f32(depth, chans // shares)),
-        (keep, both, chip, core),
+        (keep, chip, both, core),
     )
     return (state_fixed, adjoint_fixed, weight_grad, bias_grad)
 

time: 24.3 us -> 24.8 us (1.021)
  waiting for transfers between devices: 8.33 us -> 8.64 us
    ppermute x7, waiting for transfers between devices: 8.33 us -> 8.64 us  [exchange(): lax.ppermute(x, axis, [(i, i ^ mask) for i in range(lax.axis_size(axis))])]
  transfers between devices with their start and end apart: 7 -> 7, of which waited for: 5 -> 6; matrix products, arithmetic and copies ran while one was open for 0% -> 0% of each run, Pallas kernels for 5% -> 5%
where the time goes in v17:
time: 24.8 us; the launch traced here: 24.7 us
  starting transfers between devices  9.52 us (38%)
  waiting for transfers between devices  8.64 us (35%)
  Pallas kernels  5.83 us (24%)
  between operations  0.67 us (3%)
    ppermute x7, starting transfers between devices, exchange(): lax.ppermute(x, axis, [(i, i ^ mask) for i in range(lax.axis_size(axis))])  9.52 us
    ppermute x7, waiting for transfers between devices, exchange(): lax.ppermute(x, axis, [(i, i ^ mask) for i in range(lax.axis_size(axis))])  8.64 us
    pallas_call x6, Pallas kernels, call(): pl.pallas_call(kernel, out_shape=out_shape, in_specs=[HBM if k in hbm_in...  5.83 us
  transfers between devices with their start and end apart: 7, of which 6 were waited for; matrix products, arithmetic and copies ran while one was open for 0% of the time, Pallas kernels for 5%

profile of v17, /device:TPU:0, one launch (start us, length us, event | category | flops | bytes accessed | tf_op | source)
XLA Modules:
  0.0 24.7 jit_solution(16580884881081949096)
XLA Ops:
  0.6 2.9 %shard_map.75 = (f32[32,256]{1,0:T(8,128)S(1)}, f32[3,32,256]{2,1,0:T(8,128)S(1)}, f32[4,32,256]{2,1,0:T(8,128)S(1)}, bf16[4,32,256]{2,1,0:T(8,128)(2,1)S(1)}, bf16[4,32,288]{2,1,0:T(8,128)(2,1)S(1)}) custom-call(f32[1,1,32,256]{3,2,1,0:T(8,128)} %start_ref.1, f32[1,1,32,256]{3,2,1,0:T(8,128)} %guess_ref.1, bf16[4,32,288]{2,1,0:T(8,128)(2,1)} %w_hbm.1, ...), custom_call_target="tpu_custom_call" | custom-call | flops 268435456 | bytes 1048576 | tf_op jit(solution)/shard_map/pallas_call | solution.py:319
  3.6 4.0 %collective-permute-start.2 = (f32[3,32,256]{2,1,0:T(8,128)S(1)}, f32[3,32,256]{2,1,0:T(8,128)S(1)}, u32[]{:S(2)}, u32[]{:S(2)}) collective-permute-start(f32[3,32,256]{2,1,0:T(8,128)S(1)} %get-tuple-element.19.own_ref), channel_id=1, source_target_pairs={{0,12},{4,8},{8,4},{12,0},{16,28},{20,24},{24,20},{28,16},{1,13},{... | collective-permute-start | bytes 294920 | tf_op jit(solution)/shard_map/ppermute | solution.py:339
  7.6 0.5 %collective-permute-start.1 = (f32[3,32,256]{2,1,0:T(8,128)S(1)}, f32[3,32,256]{2,1,0:T(8,128)S(1)}, u32[]{:S(2)}, u32[]{:S(2)}) collective-permute-start(f32[3,32,256]{2,1,0:T(8,128)S(1)} %get-tuple-element.19.own_ref), channel_id=1, source_target_pairs={{0,4},{4,0},{8,12},{12,8},{16,20},{20,16},{24,28},{28,24},{1,5},{5... | collective-permute-start | bytes 294920 | tf_op jit(solution)/shard_map/ppermute | solution.py:339
  8.1 0.1 collective-permute-start
  8.2 2.5 %collective-permute-done.2.third_ref = f32[3,32,256]{2,1,0:T(8,128)S(1)} collective-permute-done((f32[3,32,256]{2,1,0:T(8,128)S(1)}, f32[3,32,256]{2,1,0:T(8,128)S(1)}, u32[]{:S(2)}, u32[]{:S(2)}) %collective-permute-start.2) | collective-permute-done | bytes 98336 | tf_op jit(solution)/shard_map/ppermute | solution.py:339
  10.8 1.7 %collective-permute-done.1.first_ref = f32[3,32,256]{2,1,0:T(8,128)S(1)} collective-permute-done((f32[3,32,256]{2,1,0:T(8,128)S(1)}, f32[3,32,256]{2,1,0:T(8,128)S(1)}, u32[]{:S(2)}, u32[]{:S(2)}) %collective-permute-start.1) | collective-permute-done | bytes 98336 | tf_op jit(solution)/shard_map/ppermute | solution.py:339
  12.5 0.3 %collective-permute-done.second_ref = f32[3,32,256]{2,1,0:T(8,128)S(1)} collective-permute-done((f32[3,32,256]{2,1,0:T(8,128)S(1)}, f32[3,32,256]{2,1,0:T(8,128)S(1)}, u32[]{:S(2)}, u32[]{:S(2)}) %collective-permute-start) | collective-permute-done | bytes 98336 | tf_op jit(solution)/shard_map/ppermute | solution.py:339
  12.7 0.1 shard_map.76
  12.8 2.7 %collective-permute-start.3 = (f32[32,256]{1,0:T(8,128)S(1)}, f32[32,256]{1,0:T(8,128)S(1)}, u32[]{:S(2)}, u32[]{:S(2)}) collective-permute-start(f32[32,256]{1,0:T(8,128)S(1)} %get-tuple-element.20), channel_id=1, source_target_pairs={{0,16},{4,20},{8,24},{12,28},{16,0},{20,4},{24,8},{28,12},{1,17},{... | collective-permute-start | bytes 98312 | tf_op jit(solution)/shard_map/ppermute | solution.py:339
  15.5 0.5 %shard_map.77.patch_ref = bf16[4,288,256]{2,1,0:T(8,128)(2,1)S(1)} custom-call(bf16[4,32,256]{2,1,0:T(8,128)(2,1)S(1)} %get-tuple-element.24.rounded_ref), custom_call_target="tpu_custom_call" | custom-call | flops 268435456 | bytes 1048576 | tf_op jit(solution)/shard_map/pallas_call | solution.py:319
  16.0 1.9 %collective-permute-done.3.got_ref = f32[32,256]{1,0:T(8,128)S(1)} collective-permute-done((f32[32,256]{1,0:T(8,128)S(1)}, f32[32,256]{1,0:T(8,128)S(1)}, u32[]{:S(2)}, u32[]{:S(2)}) %collective-permute-start.3) | collective-permute-done | bytes 32800 | tf_op jit(solution)/shard_map/ppermute | solution.py:339
  17.9 0.0 copy-start
  17.9 0.0 copy-start.1
  17.9 0.9 %shard_map.78 = (f32[32,384]{1,0:T(8,128)S(1)}, f32[32,384]{1,0:T(8,128)S(1)}, f32[32,384]{1,0:T(8,128)S(1)}, f32[32,384]{1,0:T(8,128)S(1)}) custom-call(f32[32,256]{1,0:T(8,128)S(1)} %collective-permute-done.3.got_ref, f32[4,32,256]{2,1,0:T(8,128)S(1)} %get-tuple-element.21.mine_ref, f32[32,256]{1,0:T(8,128)S(1)} %get-tuple-element.22.guess_ref, ...), custom_call_target="tpu_custom_call" | custom-call | flops 268435456 | bytes 1048576 | tf_op jit(solution)/shard_map/pallas_call | solution.py:319
  18.8 1.6 %collective-permute-start.4 = (f32[32,384]{1,0:T(8,128)S(1)}, f32[32,384]{1,0:T(8,128)S(1)}, u32[]{:S(2)}, u32[]{:S(2)}) collective-permute-start(f32[32,384]{1,0:T(8,128)S(1)} %get-tuple-element.29), channel_id=1, source_target_pairs={{0,2},{1,3},{2,0},{3,1},{4,6},{5,7},{6,4},{7,5},{8,10},{9,11},{10,... | collective-permute-start | bytes 147464 | tf_op jit(solution)/shard_map/ppermute | solution.py:339
  20.4 0.0 collective-permute-start.5
  20.4 0.6 %collective-permute-start.6 = (f32[32,384]{1,0:T(8,128)S(1)}, f32[32,384]{1,0:T(8,128)S(1)}, u32[]{:S(2)}, u32[]{:S(2)}) collective-permute-start(f32[32,384]{1,0:T(8,128)S(1)} %get-tuple-element.31), channel_id=1, source_target_pairs={{0,1},{1,0},{2,3},{3,2},{4,5},{5,4},{6,7},{7,6},{8,9},{9,8},{10,11... | collective-permute-start | bytes 147464 | tf_op jit(solution)/shard_map/ppermute | solution.py:339
  21.0 0.0 copy-done
  21.0 0.0 copy-done.1
  21.0 0.7 %shard_map.79 = (f32[1,1,32,256]{3,2,1,0:T(8,128)}, f32[1,1,32,256]{3,2,1,0:T(8,128)}) custom-call(f32[32,384]{1,0:T(8,128)S(1)} %get-tuple-element.26._.mine_ref, f32[32,256]{1,0:T(8,128)S(1)} %collective-permute-done.3.got_ref, f32[4,32,256]{2,1,0:T(8,128)S(1)} %get-tuple-element.21.mine_ref, f32[1,1,32,256]{3,2,1,0:T(8,128)S(1)} %copy-done.1, ...), custom_call_target="tpu_custom_call" | custom-call | flops 268435456 | bytes 1048576 | tf_op jit(solution)/shard_map/pallas_call | solution.py:319
  21.7 1.2 %collective-permute-done.4.chip_ref = f32[32,384]{1,0:T(8,128)S(1)} collective-permute-done((f32[32,384]{1,0:T(8,128)S(1)}, f32[32,384]{1,0:T(8,128)S(1)}, u32[]{:S(2)}, u32[]{:S(2)}) %collective-permute-start.4) | collective-permute-done | bytes 49184 | tf_op jit(solution)/shard_map/ppermute | solution.py:339
  22.9 1.1 %collective-permute-done.5.both_ref = f32[32,384]{1,0:T(8,128)S(1)} collective-permute-done((f32[32,384]{1,0:T(8,128)S(1)}, f32[32,384]{1,0:T(8,128)S(1)}, u32[]{:S(2)}, u32[]{:S(2)}) %collective-permute-start.5) | collective-permute-done | bytes 49184 | tf_op jit(solution)/shard_map/ppermute | solution.py:339
  24.0 0.0 collective-permute-done.6.core_ref
  24.0 0.7 %shard_map.80 = (f32[4,8,288]{2,1,0:T(8,128)}, f32[4,8]{1,0:T(4,128)}) custom-call(f32[32,384]{1,0:T(8,128)S(1)} %get-tuple-element.26._.mine_ref, f32[32,384]{1,0:T(8,128)S(1)} %collective-permute-done.4.chip_ref, f32[32,384]{1,0:T(8,128)S(1)} %collective-permute-done.5.both_ref, f32[32,384]{1,0:T(8,128)S(1)} %collective-permute-done.6.core_ref), custom_call_target="tpu_custom_call" | custom-call | flops 268435456 | bytes 1048576 | tf_op jit(solution)/shard_map/pallas_call | solution.py:319
Async XLA Ops:
  3.6 7.2 %collective-permute-start.2 = (f32[3,32,256]{2,1,0:T(8,128)S(1)}, f32[3,32,256]{2,1,0:T(8,128)S(1)}, u32[]{:S(2)}, u32[]{:S(2)}) collective-permute-start(f32[3,32,256]{2,1,0:T(8,128)S(1)} %get-tuple-element.19.own_ref), channel_id=1, source_target_pairs={{0,12},{4,8},{8,4},{12,0},{16,28},{20,24},{24,20},{28,16},{1,13},{... | collective-permute-start | bytes 294920 | tf_op jit(solution)/shard_map/ppermute | solution.py:339
  7.6 4.9 %collective-permute-start.1 = (f32[3,32,256]{2,1,0:T(8,128)S(1)}, f32[3,32,256]{2,1,0:T(8,128)S(1)}, u32[]{:S(2)}, u32[]{:S(2)}) collective-permute-start(f32[3,32,256]{2,1,0:T(8,128)S(1)} %get-tuple-element.19.own_ref), channel_id=1, source_target_pairs={{0,4},{4,0},{8,12},{12,8},{16,20},{20,16},{24,28},{28,24},{1,5},{5... | collective-permute-start | bytes 294920 | tf_op jit(solution)/shard_map/ppermute | solution.py:339
  8.1 4.6 %collective-permute-start = (f32[3,32,256]{2,1,0:T(8,128)S(1)}, f32[3,32,256]{2,1,0:T(8,128)S(1)}, u32[]{:S(2)}, u32[]{:S(2)}) collective-permute-start(f32[3,32,256]{2,1,0:T(8,128)S(1)} %get-tuple-element.19.own_ref), channel_id=1, source_target_pairs={{0,8},{4,12},{8,0},{12,4},{16,24},{20,28},{24,16},{28,20},{1,9},{5... | collective-permute-start | bytes 294920 | tf_op jit(solution)/shard_map/ppermute | solution.py:339
  12.8 5.1 %collective-permute-start.3 = (f32[32,256]{1,0:T(8,128)S(1)}, f32[32,256]{1,0:T(8,128)S(1)}, u32[]{:S(2)}, u32[]{:S(2)}) collective-permute-start(f32[32,256]{1,0:T(8,128)S(1)} %get-tuple-element.20), channel_id=1, source_target_pairs={{0,16},{4,20},{8,24},{12,28},{16,0},{20,4},{24,8},{28,12},{1,17},{... | collective-permute-start | bytes 98312 | tf_op jit(solution)/shard_map/ppermute | solution.py:339
  17.9 3.1 %copy-start = (f32[1,1,32,256]{3,2,1,0:T(8,128)S(1)}, f32[1,1,32,256]{3,2,1,0:T(8,128)}, u32[]{:S(2)}) copy-start(f32[1,1,32,256]{3,2,1,0:T(8,128)} %start_ref.1) | copy-start | bytes 98308
  17.9 3.1 %copy-start.1 = (f32[1,1,32,256]{3,2,1,0:T(8,128)S(1)}, f32[1,1,32,256]{3,2,1,0:T(8,128)}, u32[]{:S(2)}) copy-start(f32[1,1,32,256]{3,2,1,0:T(8,128)} %guess_ref.1) | copy-start | bytes 98308
  18.8 4.2 %collective-permute-start.4 = (f32[32,384]{1,0:T(8,128)S(1)}, f32[32,384]{1,0:T(8,128)S(1)}, u32[]{:S(2)}, u32[]{:S(2)}) collective-permute-start(f32[32,384]{1,0:T(8,128)S(1)} %get-tuple-element.29), channel_id=1, source_target_pairs={{0,2},{1,3},{2,0},{3,1},{4,6},{5,7},{6,4},{7,5},{8,10},{9,11},{10,... | collective-permute-start | bytes 147464 | tf_op jit(solution)/shard_map/ppermute | solution.py:339
  20.4 3.6 %collective-permute-start.5 = (f32[32,384]{1,0:T(8,128)S(1)}, f32[32,384]{1,0:T(8,128)S(1)}, u32[]{:S(2)}, u32[]{:S(2)}) collective-permute-start(f32[32,384]{1,0:T(8,128)S(1)} %get-tuple-element.30), channel_id=1, source_target_pairs={{0,3},{1,2},{2,1},{3,0},{4,7},{5,6},{6,5},{7,4},{8,11},{9,10},{10,... | collective-permute-start | bytes 147464 | tf_op jit(solution)/shard_map/ppermute | solution.py:339
  20.4 3.6 %collective-permute-start.6 = (f32[32,384]{1,0:T(8,128)S(1)}, f32[32,384]{1,0:T(8,128)S(1)}, u32[]{:S(2)}, u32[]{:S(2)}) collective-permute-start(f32[32,384]{1,0:T(8,128)S(1)} %get-tuple-element.31), channel_id=1, source_target_pairs={{0,1},{1,0},{2,3},{3,2},{4,5},{5,4},{6,7},{7,6},{8,9},{9,8},{10,11... | collective-permute-start | bytes 147464 | tf_op jit(solution)/shard_map/ppermute | solution.py:339

commit v18 on v17

--- a/solution.py
+++ b/solution.py
@@ -302,7 +302,7 @@
     layer(0, lax.fori_loop(0, depth - 1, behind, adj))
 
 
-def total_kernel(mine_ref, chip_ref, both_ref, core_ref, grad_ref, bias_ref):
+def total_kernel(mine_ref, both_ref, chip_ref, core_ref, grad_ref, bias_ref):
     depth, own, width = grad_ref.shape
     total = (mine_ref[...] + core_ref[...]) + (chip_ref[...] + both_ref[...])
     eye = lax.broadcasted_iota(jnp.int32, (own, own), 0) == lax.broadcasted_iota(
@@ -390,7 +390,7 @@
     weight_grad, bias_grad = call(
         total_kernel,
         (f32(depth, chans // shares, width), f32(depth, chans // shares)),
-        (keep, chip, both, core),
+        (keep, both, chip, core),
     )
     return (state_fixed, adjoint_fixed, weight_grad, bias_grad)
 

time: 24.8 us -> 24.6 us (level)
  starting transfers between devices: 9.52 us -> 9.23 us
    ppermute x7, starting transfers between devices: 9.52 us -> 9.23 us  [exchange(): lax.ppermute(x, axis, [(i, i ^ mask) for i in range(lax.axis_size(axis))])]
where the time goes in v18:
time: 24.6 us; the launch traced here: 24.4 us
  starting transfers between devices  9.23 us (38%)
  waiting for transfers between devices  8.67 us (35%)
  Pallas kernels  5.83 us (24%)
  between operations  0.68 us (3%)
    ppermute x7, starting transfers between devices, exchange(): lax.ppermute(x, axis, [(i, i ^ mask) for i in range(lax.axis_size(axis))])  9.23 us
    ppermute x7, waiting for transfers between devices, exchange(): lax.ppermute(x, axis, [(i, i ^ mask) for i in range(lax.axis_size(axis))])  8.67 us
    pallas_call x6, Pallas kernels, call(): pl.pallas_call(kernel, out_shape=out_shape, in_specs=[HBM if k in hbm_in...  5.83 us
  transfers between devices with their start and end apart: 7, of which 6 were waited for; matrix products, arithmetic and copies ran while one was open for 0% of the time, Pallas kernels for 5%

profile of v18, /device:TPU:0, one launch (start us, length us, event | category | flops | bytes accessed | tf_op | source)
XLA Modules:
  0.0 24.4 jit_solution(12159489406943783583)
XLA Ops:
  0.6 2.9 %shard_map.75 = (f32[32,256]{1,0:T(8,128)S(1)}, f32[3,32,256]{2,1,0:T(8,128)S(1)}, f32[4,32,256]{2,1,0:T(8,128)S(1)}, bf16[4,32,256]{2,1,0:T(8,128)(2,1)S(1)}, bf16[4,32,288]{2,1,0:T(8,128)(2,1)S(1)}) custom-call(f32[1,1,32,256]{3,2,1,0:T(8,128)} %start_ref.1, f32[1,1,32,256]{3,2,1,0:T(8,128)} %guess_ref.1, bf16[4,32,288]{2,1,0:T(8,128)(2,1)} %w_hbm.1, ...), custom_call_target="tpu_custom_call" | custom-call | flops 268435456 | bytes 1048576 | tf_op jit(solution)/shard_map/pallas_call | solution.py:319
  3.6 4.0 %collective-permute-start.2 = (f32[3,32,256]{2,1,0:T(8,128)S(1)}, f32[3,32,256]{2,1,0:T(8,128)S(1)}, u32[]{:S(2)}, u32[]{:S(2)}) collective-permute-start(f32[3,32,256]{2,1,0:T(8,128)S(1)} %get-tuple-element.19.own_ref), channel_id=1, source_target_pairs={{0,12},{4,8},{8,4},{12,0},{16,28},{20,24},{24,20},{28,16},{1,13},{... | collective-permute-start | bytes 294920 | tf_op jit(solution)/shard_map/ppermute | solution.py:339
  7.6 0.5 %collective-permute-start.1 = (f32[3,32,256]{2,1,0:T(8,128)S(1)}, f32[3,32,256]{2,1,0:T(8,128)S(1)}, u32[]{:S(2)}, u32[]{:S(2)}) collective-permute-start(f32[3,32,256]{2,1,0:T(8,128)S(1)} %get-tuple-element.19.own_ref), channel_id=1, source_target_pairs={{0,4},{4,0},{8,12},{12,8},{16,20},{20,16},{24,28},{28,24},{1,5},{5... | collective-permute-start | bytes 294920 | tf_op jit(solution)/shard_map/ppermute | solution.py:339
  8.1 0.1 collective-permute-start
  8.2 2.5 %collective-permute-done.2.third_ref = f32[3,32,256]{2,1,0:T(8,128)S(1)} collective-permute-done((f32[3,32,256]{2,1,0:T(8,128)S(1)}, f32[3,32,256]{2,1,0:T(8,128)S(1)}, u32[]{:S(2)}, u32[]{:S(2)}) %collective-permute-start.2) | collective-permute-done | bytes 98336 | tf_op jit(solution)/shard_map/ppermute | solution.py:339
  10.8 1.7 %collective-permute-done.1.first_ref = f32[3,32,256]{2,1,0:T(8,128)S(1)} collective-permute-done((f32[3,32,256]{2,1,0:T(8,128)S(1)}, f32[3,32,256]{2,1,0:T(8,128)S(1)}, u32[]{:S(2)}, u32[]{:S(2)}) %collective-permute-start.1) | collective-permute-done | bytes 98336 | tf_op jit(solution)/shard_map/ppermute | solution.py:339
  12.5 0.3 %collective-permute-done.second_ref = f32[3,32,256]{2,1,0:T(8,128)S(1)} collective-permute-done((f32[3,32,256]{2,1,0:T(8,128)S(1)}, f32[3,32,256]{2,1,0:T(8,128)S(1)}, u32[]{:S(2)}, u32[]{:S(2)}) %collective-permute-start) | collective-permute-done | bytes 98336 | tf_op jit(solution)/shard_map/ppermute | solution.py:339
  12.7 0.1 shard_map.76
  12.8 2.7 %collective-permute-start.3 = (f32[32,256]{1,0:T(8,128)S(1)}, f32[32,256]{1,0:T(8,128)S(1)}, u32[]{:S(2)}, u32[]{:S(2)}) collective-permute-start(f32[32,256]{1,0:T(8,128)S(1)} %get-tuple-element.20), channel_id=1, source_target_pairs={{0,16},{4,20},{8,24},{12,28},{16,0},{20,4},{24,8},{28,12},{1,17},{... | collective-permute-start | bytes 98312 | tf_op jit(solution)/shard_map/ppermute | solution.py:339
  15.5 0.5 %shard_map.77.patch_ref = bf16[4,288,256]{2,1,0:T(8,128)(2,1)S(1)} custom-call(bf16[4,32,256]{2,1,0:T(8,128)(2,1)S(1)} %get-tuple-element.24.rounded_ref), custom_call_target="tpu_custom_call" | custom-call | flops 268435456 | bytes 1048576 | tf_op jit(solution)/shard_map/pallas_call | solution.py:319
  16.0 1.9 %collective-permute-done.3.got_ref = f32[32,256]{1,0:T(8,128)S(1)} collective-permute-done((f32[32,256]{1,0:T(8,128)S(1)}, f32[32,256]{1,0:T(8,128)S(1)}, u32[]{:S(2)}, u32[]{:S(2)}) %collective-permute-start.3) | collective-permute-done | bytes 32800 | tf_op jit(solution)/shard_map/ppermute | solution.py:339
  17.9 0.0 copy-start
  17.9 0.0 copy-start.1
  17.9 0.9 %shard_map.78 = (f32[32,384]{1,0:T(8,128)S(1)}, f32[32,384]{1,0:T(8,128)S(1)}, f32[32,384]{1,0:T(8,128)S(1)}, f32[32,384]{1,0:T(8,128)S(1)}) custom-call(f32[32,256]{1,0:T(8,128)S(1)} %collective-permute-done.3.got_ref, f32[4,32,256]{2,1,0:T(8,128)S(1)} %get-tuple-element.21.mine_ref, f32[32,256]{1,0:T(8,128)S(1)} %get-tuple-element.22.guess_ref, ...), custom_call_target="tpu_custom_call" | custom-call | flops 268435456 | bytes 1048576 | tf_op jit(solution)/shard_map/pallas_call | solution.py:319
  18.8 0.1 collective-permute-start.4
  18.9 1.6 %collective-permute-start.5 = (f32[32,384]{1,0:T(8,128)S(1)}, f32[32,384]{1,0:T(8,128)S(1)}, u32[]{:S(2)}, u32[]{:S(2)}) collective-permute-start(f32[32,384]{1,0:T(8,128)S(1)} %get-tuple-element.30), channel_id=1, source_target_pairs={{0,2},{1,3},{2,0},{3,1},{4,6},{5,7},{6,4},{7,5},{8,10},{9,11},{10,... | collective-permute-start | bytes 147464 | tf_op jit(solution)/shard_map/ppermute | solution.py:339
  20.4 0.3 %collective-permute-start.6 = (f32[32,384]{1,0:T(8,128)S(1)}, f32[32,384]{1,0:T(8,128)S(1)}, u32[]{:S(2)}, u32[]{:S(2)}) collective-permute-start(f32[32,384]{1,0:T(8,128)S(1)} %get-tuple-element.31), channel_id=1, source_target_pairs={{0,1},{1,0},{2,3},{3,2},{4,5},{5,4},{6,7},{7,6},{8,9},{9,8},{10,11... | collective-permute-start | bytes 147464 | tf_op jit(solution)/shard_map/ppermute | solution.py:339
  20.7 0.0 copy-done
  20.7 0.0 copy-done.1
  20.7 0.7 %shard_map.79 = (f32[1,1,32,256]{3,2,1,0:T(8,128)}, f32[1,1,32,256]{3,2,1,0:T(8,128)}) custom-call(f32[32,384]{1,0:T(8,128)S(1)} %get-tuple-element.26._.mine_ref, f32[32,256]{1,0:T(8,128)S(1)} %collective-permute-done.3.got_ref, f32[4,32,256]{2,1,0:T(8,128)S(1)} %get-tuple-element.21.mine_ref, f32[1,1,32,256]{3,2,1,0:T(8,128)S(1)} %copy-done.1, ...), custom_call_target="tpu_custom_call" | custom-call | flops 268435456 | bytes 1048576 | tf_op jit(solution)/shard_map/pallas_call | solution.py:319
  21.5 1.4 %collective-permute-done.4.both_ref = f32[32,384]{1,0:T(8,128)S(1)} collective-permute-done((f32[32,384]{1,0:T(8,128)S(1)}, f32[32,384]{1,0:T(8,128)S(1)}, u32[]{:S(2)}, u32[]{:S(2)}) %collective-permute-start.4) | collective-permute-done | bytes 49184 | tf_op jit(solution)/shard_map/ppermute | solution.py:339
  22.8 0.9 %collective-permute-done.5.chip_ref = f32[32,384]{1,0:T(8,128)S(1)} collective-permute-done((f32[32,384]{1,0:T(8,128)S(1)}, f32[32,384]{1,0:T(8,128)S(1)}, u32[]{:S(2)}, u32[]{:S(2)}) %collective-permute-start.5) | collective-permute-done | bytes 49184 | tf_op jit(solution)/shard_map/ppermute | solution.py:339
  23.7 0.0 collective-permute-done.6.core_ref
  23.7 0.7 %shard_map.80 = (f32[4,8,288]{2,1,0:T(8,128)}, f32[4,8]{1,0:T(4,128)}) custom-call(f32[32,384]{1,0:T(8,128)S(1)} %get-tuple-element.26._.mine_ref, f32[32,384]{1,0:T(8,128)S(1)} %collective-permute-done.4.both_ref, f32[32,384]{1,0:T(8,128)S(1)} %collective-permute-done.5.chip_ref, f32[32,384]{1,0:T(8,128)S(1)} %collective-permute-done.6.core_ref), custom_call_target="tpu_custom_call" | custom-call | flops 268435456 | bytes 1048576 | tf_op jit(solution)/shard_map/pallas_call | solution.py:319
Async XLA Ops:
  3.6 7.2 %collective-permute-start.2 = (f32[3,32,256]{2,1,0:T(8,128)S(1)}, f32[3,32,256]{2,1,0:T(8,128)S(1)}, u32[]{:S(2)}, u32[]{:S(2)}) collective-permute-start(f32[3,32,256]{2,1,0:T(8,128)S(1)} %get-tuple-element.19.own_ref), channel_id=1, source_target_pairs={{0,12},{4,8},{8,4},{12,0},{16,28},{20,24},{24,20},{28,16},{1,13},{... | collective-permute-start | bytes 294920 | tf_op jit(solution)/shard_map/ppermute | solution.py:339
  7.6 4.9 %collective-permute-start.1 = (f32[3,32,256]{2,1,0:T(8,128)S(1)}, f32[3,32,256]{2,1,0:T(8,128)S(1)}, u32[]{:S(2)}, u32[]{:S(2)}) collective-permute-start(f32[3,32,256]{2,1,0:T(8,128)S(1)} %get-tuple-element.19.own_ref), channel_id=1, source_target_pairs={{0,4},{4,0},{8,12},{12,8},{16,20},{20,16},{24,28},{28,24},{1,5},{5... | collective-permute-start | bytes 294920 | tf_op jit(solution)/shard_map/ppermute | solution.py:339
  8.1 4.6 %collective-permute-start = (f32[3,32,256]{2,1,0:T(8,128)S(1)}, f32[3,32,256]{2,1,0:T(8,128)S(1)}, u32[]{:S(2)}, u32[]{:S(2)}) collective-permute-start(f32[3,32,256]{2,1,0:T(8,128)S(1)} %get-tuple-element.19.own_ref), channel_id=1, source_target_pairs={{0,8},{4,12},{8,0},{12,4},{16,24},{20,28},{24,16},{28,20},{1,9},{5... | collective-permute-start | bytes 294920 | tf_op jit(solution)/shard_map/ppermute | solution.py:339
  12.8 5.1 %collective-permute-start.3 = (f32[32,256]{1,0:T(8,128)S(1)}, f32[32,256]{1,0:T(8,128)S(1)}, u32[]{:S(2)}, u32[]{:S(2)}) collective-permute-start(f32[32,256]{1,0:T(8,128)S(1)} %get-tuple-element.20), channel_id=1, source_target_pairs={{0,16},{4,20},{8,24},{12,28},{16,0},{20,4},{24,8},{28,12},{1,17},{... | collective-permute-start | bytes 98312 | tf_op jit(solution)/shard_map/ppermute | solution.py:339
  17.9 2.8 %copy-start = (f32[1,1,32,256]{3,2,1,0:T(8,128)S(1)}, f32[1,1,32,256]{3,2,1,0:T(8,128)}, u32[]{:S(2)}) copy-start(f32[1,1,32,256]{3,2,1,0:T(8,128)} %start_ref.1) | copy-start | bytes 98308
  17.9 2.8 %copy-start.1 = (f32[1,1,32,256]{3,2,1,0:T(8,128)S(1)}, f32[1,1,32,256]{3,2,1,0:T(8,128)}, u32[]{:S(2)}) copy-start(f32[1,1,32,256]{3,2,1,0:T(8,128)} %guess_ref.1) | copy-start | bytes 98308
  18.8 4.0 %collective-permute-start.4 = (f32[32,384]{1,0:T(8,128)S(1)}, f32[32,384]{1,0:T(8,128)S(1)}, u32[]{:S(2)}, u32[]{:S(2)}) collective-permute-start(f32[32,384]{1,0:T(8,128)S(1)} %get-tuple-element.29), channel_id=1, source_target_pairs={{0,3},{1,2},{2,1},{3,0},{4,7},{5,6},{6,5},{7,4},{8,11},{9,10},{10,... | collective-permute-start | bytes 147464 | tf_op jit(solution)/shard_map/ppermute | solution.py:339
  18.9 4.9 %collective-permute-start.5 = (f32[32,384]{1,0:T(8,128)S(1)}, f32[32,384]{1,0:T(8,128)S(1)}, u32[]{:S(2)}, u32[]{:S(2)}) collective-permute-start(f32[32,384]{1,0:T(8,128)S(1)} %get-tuple-element.30), channel_id=1, source_target_pairs={{0,2},{1,3},{2,0},{3,1},{4,6},{5,7},{6,4},{7,5},{8,10},{9,11},{10,... | collective-permute-start | bytes 147464 | tf_op jit(solution)/shard_map/ppermute | solution.py:339
  20.4 3.3 %collective-permute-start.6 = (f32[32,384]{1,0:T(8,128)S(1)}, f32[32,384]{1,0:T(8,128)S(1)}, u32[]{:S(2)}, u32[]{:S(2)}) collective-permute-start(f32[32,384]{1,0:T(8,128)S(1)} %get-tuple-element.31), channel_id=1, source_target_pairs={{0,1},{1,0},{2,3},{3,2},{4,5},{5,4},{6,7},{7,6},{8,9},{9,8},{10,11... | collective-permute-start | bytes 147464 | tf_op jit(solution)/shard_map/ppermute | solution.py:339

commit v19 on v14

--- a/solution.py
+++ b/solution.py
@@ -130,7 +130,6 @@
         copy.wait()
     weights = w_ref[...].reshape(depth * chans, width)
     by_tap = dot(weights, perm, ((1,), (1,)))
-    turned = dot(perm, weights, ((1,), (1,))).astype(jnp.bfloat16)
     middle = TAPS // 2 * chans
     start = by_parity(state_ref[0, 0])
     guess = by_parity(adj_ref[0, 0])
@@ -155,6 +154,10 @@
         state = state + STEP * squash
         factor = 1.0 + slope * kc
         gain = factor if gain is None else gain * factor
+        if n == 1:
+            turned = dot(perm, weights, ((1,), (1,))).astype(jnp.bfloat16)
+    for n in range(depth):
+        mine = slice(n * chans, (n + 1) * chans)
         back_w = jnp.concatenate(
             [turned[t * chans : (t + 1) * chans, mine] for t in reversed(range(TAPS))], axis=1
         )
@@ -281,9 +284,11 @@
     pad = part_refs[0].shape[1] - rows
     odd, high = bit_of("dp", 0), bit_of("dp", 1)
 
-    def layer(n, adj):
+    def through(n, adj):
         dz = adj * slope_ref[n]
-        dzb = dz.astype(jnp.bfloat16)
+        return dz, dz.astype(jnp.bfloat16)
+
+    def gradients(n, dz, dzb):
         grad = dot(dzb, patch_ref[n], ((1,), (1,)))
         bias = jnp.broadcast_to(jnp.sum(dz, axis=1, keepdims=True), (chans, pad))
         both = jnp.concatenate([grad, bias], axis=1)
@@ -293,13 +298,15 @@
         parts = [jnp.where(high, parts[i ^ 2], parts[i]) for i in range(shares)]
         for part, ref in zip(parts, part_refs):
             ref[where] = part
-        return dzb
 
     def behind(i, adj):
         n = depth - 1 - i
-        return adj + convolve(back_w_ref[n], layer(n, adj))
-
-    layer(0, lax.fori_loop(0, depth - 1, behind, adj))
+        dz, dzb = through(n, adj)
+        adj = adj + convolve(back_w_ref[n], dzb)
+        gradients(n, dz, dzb)
+        return adj
+
+    gradients(0, *through(0, lax.fori_loop(0, depth - 1, behind, adj)))
 
 
 def total_kernel(mine_ref, both_ref, chip_ref, core_ref, grad_ref, bias_ref):

time: 24.3 us -> 24.3 us (level)
  no operation moved by 1% of the time
where the time goes in v19:
time: 24.3 us; the launch traced here: 24.2 us
  starting transfers between devices  9.29 us (38%)
  waiting for transfers between devices  8.33 us (34%)
  Pallas kernels  5.86 us (24%)
  between operations  0.68 us (3%)
    ppermute x7, starting transfers between devices, exchange(): lax.ppermute(x, axis, [(i, i ^ mask) for i in range(lax.axis_size(axis))])  9.29 us
    ppermute x7, waiting for transfers between devices, exchange(): lax.ppermute(x, axis, [(i, i ^ mask) for i in range(lax.axis_size(axis))])  8.33 us
    pallas_call x6, Pallas kernels, call(): pl.pallas_call(kernel, out_shape=out_shape, in_specs=[HBM if k in hbm_in...  5.86 us
  transfers between devices with their start and end apart: 7, of which 5 were waited for; matrix products, arithmetic and copies ran while one was open for 0% of the time, Pallas kernels for 5%

profile of v19, /device:TPU:0, one launch (start us, length us, event | category | flops | bytes accessed | tf_op | source)
XLA Modules:
  0.0 24.2 jit_solution(16960482832031639672)
XLA Ops:
  0.6 2.9 %shard_map.75 = (f32[32,256]{1,0:T(8,128)S(1)}, f32[3,32,256]{2,1,0:T(8,128)S(1)}, f32[4,32,256]{2,1,0:T(8,128)S(1)}, bf16[4,32,256]{2,1,0:T(8,128)(2,1)S(1)}, bf16[4,32,288]{2,1,0:T(8,128)(2,1)S(1)}) custom-call(f32[1,1,32,256]{3,2,1,0:T(8,128)} %start_ref.1, f32[1,1,32,256]{3,2,1,0:T(8,128)} %guess_ref.1, bf16[4,32,288]{2,1,0:T(8,128)(2,1)} %w_hbm.1, ...), custom_call_target="tpu_custom_call" | custom-call | flops 268435456 | bytes 1048576 | tf_op jit(solution)/shard_map/pallas_call | solution.py:326
  3.6 4.0 %collective-permute-start.2 = (f32[3,32,256]{2,1,0:T(8,128)S(1)}, f32[3,32,256]{2,1,0:T(8,128)S(1)}, u32[]{:S(2)}, u32[]{:S(2)}) collective-permute-start(f32[3,32,256]{2,1,0:T(8,128)S(1)} %get-tuple-element.19.own_ref), channel_id=1, source_target_pairs={{0,12},{4,8},{8,4},{12,0},{16,28},{20,24},{24,20},{28,16},{1,13},{... | collective-permute-start | bytes 294920 | tf_op jit(solution)/shard_map/ppermute | solution.py:346
  7.6 0.5 %collective-permute-start.1 = (f32[3,32,256]{2,1,0:T(8,128)S(1)}, f32[3,32,256]{2,1,0:T(8,128)S(1)}, u32[]{:S(2)}, u32[]{:S(2)}) collective-permute-start(f32[3,32,256]{2,1,0:T(8,128)S(1)} %get-tuple-element.19.own_ref), channel_id=1, source_target_pairs={{0,8},{4,12},{8,0},{12,4},{16,24},{20,28},{24,16},{28,20},{1,9},{5... | collective-permute-start | bytes 294920 | tf_op jit(solution)/shard_map/ppermute | solution.py:346
  8.0 0.2 collective-permute-start
  8.2 2.9 %collective-permute-done.2.third_ref = f32[3,32,256]{2,1,0:T(8,128)S(1)} collective-permute-done((f32[3,32,256]{2,1,0:T(8,128)S(1)}, f32[3,32,256]{2,1,0:T(8,128)S(1)}, u32[]{:S(2)}, u32[]{:S(2)}) %collective-permute-start.2) | collective-permute-done | bytes 98336 | tf_op jit(solution)/shard_map/ppermute | solution.py:346
  11.1 1.6 %collective-permute-done.1.second_ref = f32[3,32,256]{2,1,0:T(8,128)S(1)} collective-permute-done((f32[3,32,256]{2,1,0:T(8,128)S(1)}, f32[3,32,256]{2,1,0:T(8,128)S(1)}, u32[]{:S(2)}, u32[]{:S(2)}) %collective-permute-start.1) | collective-permute-done | bytes 98336 | tf_op jit(solution)/shard_map/ppermute | solution.py:346
  12.7 0.0 collective-permute-done.first_ref
  12.7 0.1 shard_map.76
  12.8 2.7 %collective-permute-start.3 = (f32[32,256]{1,0:T(8,128)S(1)}, f32[32,256]{1,0:T(8,128)S(1)}, u32[]{:S(2)}, u32[]{:S(2)}) collective-permute-start(f32[32,256]{1,0:T(8,128)S(1)} %get-tuple-element.20), channel_id=1, source_target_pairs={{0,16},{4,20},{8,24},{12,28},{16,0},{20,4},{24,8},{28,12},{1,17},{... | collective-permute-start | bytes 98312 | tf_op jit(solution)/shard_map/ppermute | solution.py:346
  15.5 0.5 %shard_map.77.patch_ref = bf16[4,288,256]{2,1,0:T(8,128)(2,1)S(1)} custom-call(bf16[4,32,256]{2,1,0:T(8,128)(2,1)S(1)} %get-tuple-element.24.rounded_ref), custom_call_target="tpu_custom_call" | custom-call | flops 268435456 | bytes 1048576 | tf_op jit(solution)/shard_map/pallas_call | solution.py:326
  16.1 1.6 %collective-permute-done.3.got_ref = f32[32,256]{1,0:T(8,128)S(1)} collective-permute-done((f32[32,256]{1,0:T(8,128)S(1)}, f32[32,256]{1,0:T(8,128)S(1)}, u32[]{:S(2)}, u32[]{:S(2)}) %collective-permute-start.3) | collective-permute-done | bytes 32800 | tf_op jit(solution)/shard_map/ppermute | solution.py:346
  17.7 0.0 copy-start
  17.7 0.0 copy-start.1
  17.7 0.9 %shard_map.78 = (f32[32,384]{1,0:T(8,128)S(1)}, f32[32,384]{1,0:T(8,128)S(1)}, f32[32,384]{1,0:T(8,128)S(1)}, f32[32,384]{1,0:T(8,128)S(1)}) custom-call(f32[32,256]{1,0:T(8,128)S(1)} %collective-permute-done.3.got_ref, f32[4,32,256]{2,1,0:T(8,128)S(1)} %get-tuple-element.21.mine_ref, f32[32,256]{1,0:T(8,128)S(1)} %get-tuple-element.22.guess_ref, ...), custom_call_target="tpu_custom_call" | custom-call | flops 268435456 | bytes 1048576 | tf_op jit(solution)/shard_map/pallas_call | solution.py:326
  18.6 0.1 collective-permute-start.4
  18.7 1.6 %collective-permute-start.5 = (f32[32,384]{1,0:T(8,128)S(1)}, f32[32,384]{1,0:T(8,128)S(1)}, u32[]{:S(2)}, u32[]{:S(2)}) collective-permute-start(f32[32,384]{1,0:T(8,128)S(1)} %get-tuple-element.30), channel_id=1, source_target_pairs={{0,2},{1,3},{2,0},{3,1},{4,6},{5,7},{6,4},{7,5},{8,10},{9,11},{10,... | collective-permute-start | bytes 147464 | tf_op jit(solution)/shard_map/ppermute | solution.py:346
  20.3 0.2 collective-permute-start.6
  20.5 0.0 copy-done
  20.5 0.0 copy-done.1
  20.5 0.7 %shard_map.79 = (f32[1,1,32,256]{3,2,1,0:T(8,128)}, f32[1,1,32,256]{3,2,1,0:T(8,128)}) custom-call(f32[32,384]{1,0:T(8,128)S(1)} %get-tuple-element.26._.mine_ref, f32[32,256]{1,0:T(8,128)S(1)} %collective-permute-done.3.got_ref, f32[4,32,256]{2,1,0:T(8,128)S(1)} %get-tuple-element.21.mine_ref, f32[1,1,32,256]{3,2,1,0:T(8,128)S(1)} %copy-done.1, ...), custom_call_target="tpu_custom_call" | custom-call | flops 268435456 | bytes 1048576 | tf_op jit(solution)/shard_map/pallas_call | solution.py:326
  21.3 1.3 %collective-permute-done.4.both_ref = f32[32,384]{1,0:T(8,128)S(1)} collective-permute-done((f32[32,384]{1,0:T(8,128)S(1)}, f32[32,384]{1,0:T(8,128)S(1)}, u32[]{:S(2)}, u32[]{:S(2)}) %collective-permute-start.4) | collective-permute-done | bytes 49184 | tf_op jit(solution)/shard_map/ppermute | solution.py:346
  22.6 0.9 %collective-permute-done.5.chip_ref = f32[32,384]{1,0:T(8,128)S(1)} collective-permute-done((f32[32,384]{1,0:T(8,128)S(1)}, f32[32,384]{1,0:T(8,128)S(1)}, u32[]{:S(2)}, u32[]{:S(2)}) %collective-permute-start.5) | collective-permute-done | bytes 49184 | tf_op jit(solution)/shard_map/ppermute | solution.py:346
  23.5 0.0 collective-permute-done.6.core_ref
  23.5 0.7 %shard_map.80 = (f32[4,8,288]{2,1,0:T(8,128)}, f32[4,8]{1,0:T(4,128)}) custom-call(f32[32,384]{1,0:T(8,128)S(1)} %get-tuple-element.26._.mine_ref, f32[32,384]{1,0:T(8,128)S(1)} %collective-permute-done.4.both_ref, f32[32,384]{1,0:T(8,128)S(1)} %collective-permute-done.5.chip_ref, f32[32,384]{1,0:T(8,128)S(1)} %collective-permute-done.6.core_ref), custom_call_target="tpu_custom_call" | custom-call | flops 268435456 | bytes 1048576 | tf_op jit(solution)/shard_map/pallas_call | solution.py:326
Async XLA Ops:
  3.6 7.5 %collective-permute-start.2 = (f32[3,32,256]{2,1,0:T(8,128)S(1)}, f32[3,32,256]{2,1,0:T(8,128)S(1)}, u32[]{:S(2)}, u32[]{:S(2)}) collective-permute-start(f32[3,32,256]{2,1,0:T(8,128)S(1)} %get-tuple-element.19.own_ref), channel_id=1, source_target_pairs={{0,12},{4,8},{8,4},{12,0},{16,28},{20,24},{24,20},{28,16},{1,13},{... | collective-permute-start | bytes 294920 | tf_op jit(solution)/shard_map/ppermute | solution.py:346
  7.6 5.1 %collective-permute-start.1 = (f32[3,32,256]{2,1,0:T(8,128)S(1)}, f32[3,32,256]{2,1,0:T(8,128)S(1)}, u32[]{:S(2)}, u32[]{:S(2)}) collective-permute-start(f32[3,32,256]{2,1,0:T(8,128)S(1)} %get-tuple-element.19.own_ref), channel_id=1, source_target_pairs={{0,8},{4,12},{8,0},{12,4},{16,24},{20,28},{24,16},{28,20},{1,9},{5... | collective-permute-start | bytes 294920 | tf_op jit(solution)/shard_map/ppermute | solution.py:346
  8.0 4.7 %collective-permute-start = (f32[3,32,256]{2,1,0:T(8,128)S(1)}, f32[3,32,256]{2,1,0:T(8,128)S(1)}, u32[]{:S(2)}, u32[]{:S(2)}) collective-permute-start(f32[3,32,256]{2,1,0:T(8,128)S(1)} %get-tuple-element.19.own_ref), channel_id=1, source_target_pairs={{0,4},{4,0},{8,12},{12,8},{16,20},{20,16},{24,28},{28,24},{1,5},{5... | collective-permute-start | bytes 294920 | tf_op jit(solution)/shard_map/ppermute | solution.py:346
  12.8 4.9 %collective-permute-start.3 = (f32[32,256]{1,0:T(8,128)S(1)}, f32[32,256]{1,0:T(8,128)S(1)}, u32[]{:S(2)}, u32[]{:S(2)}) collective-permute-start(f32[32,256]{1,0:T(8,128)S(1)} %get-tuple-element.20), channel_id=1, source_target_pairs={{0,16},{4,20},{8,24},{12,28},{16,0},{20,4},{24,8},{28,12},{1,17},{... | collective-permute-start | bytes 98312 | tf_op jit(solution)/shard_map/ppermute | solution.py:346
  17.7 2.8 %copy-start = (f32[1,1,32,256]{3,2,1,0:T(8,128)S(1)}, f32[1,1,32,256]{3,2,1,0:T(8,128)}, u32[]{:S(2)}) copy-start(f32[1,1,32,256]{3,2,1,0:T(8,128)} %start_ref.1) | copy-start | bytes 98308
  17.7 2.8 %copy-start.1 = (f32[1,1,32,256]{3,2,1,0:T(8,128)S(1)}, f32[1,1,32,256]{3,2,1,0:T(8,128)}, u32[]{:S(2)}) copy-start(f32[1,1,32,256]{3,2,1,0:T(8,128)} %guess_ref.1) | copy-start | bytes 98308
  18.6 4.0 %collective-permute-start.4 = (f32[32,384]{1,0:T(8,128)S(1)}, f32[32,384]{1,0:T(8,128)S(1)}, u32[]{:S(2)}, u32[]{:S(2)}) collective-permute-start(f32[32,384]{1,0:T(8,128)S(1)} %get-tuple-element.29), channel_id=1, source_target_pairs={{0,3},{1,2},{2,1},{3,0},{4,7},{5,6},{6,5},{7,4},{8,11},{9,10},{10,... | collective-permute-start | bytes 147464 | tf_op jit(solution)/shard_map/ppermute | solution.py:346
  18.7 4.8 %collective-permute-start.5 = (f32[32,384]{1,0:T(8,128)S(1)}, f32[32,384]{1,0:T(8,128)S(1)}, u32[]{:S(2)}, u32[]{:S(2)}) collective-permute-start(f32[32,384]{1,0:T(8,128)S(1)} %get-tuple-element.30), channel_id=1, source_target_pairs={{0,2},{1,3},{2,0},{3,1},{4,6},{5,7},{6,4},{7,5},{8,10},{9,11},{10,... | collective-permute-start | bytes 147464 | tf_op jit(solution)/shard_map/ppermute | solution.py:346
  20.3 3.2 %collective-permute-start.6 = (f32[32,384]{1,0:T(8,128)S(1)}, f32[32,384]{1,0:T(8,128)S(1)}, u32[]{:S(2)}, u32[]{:S(2)}) collective-permute-start(f32[32,384]{1,0:T(8,128)S(1)} %get-tuple-element.31), channel_id=1, source_target_pairs={{0,1},{1,0},{2,3},{3,2},{4,5},{5,4},{6,7},{7,6},{8,9},{9,8},{10,11... | collective-permute-start | bytes 147464 | tf_op jit(solution)/shard_map/ppermute | solution.py:346

commit v20 on v14

--- a/solution.py
+++ b/solution.py
@@ -278,21 +278,29 @@
     own = chans // shares
     last = lax.axis_index("layer") == lax.axis_size("layer") - 1
     adj = jnp.where(last, guess_ref[...], later_fixed(steps, got_ref, mine_ref))
-    pad = part_refs[0].shape[1] - rows
+    full = rows // HALF * HALF
+    block, base = depth * own, depth * own * (full // HALF)
     odd, high = bit_of("dp", 0), bit_of("dp", 1)
 
     def layer(n, adj):
         dz = adj * slope_ref[n]
         dzb = dz.astype(jnp.bfloat16)
         grad = dot(dzb, patch_ref[n], ((1,), (1,)))
-        bias = jnp.broadcast_to(jnp.sum(dz, axis=1, keepdims=True), (chans, pad))
-        both = jnp.concatenate([grad, bias], axis=1)
-        where = pl.ds(pl.multiple_of(n * own, own), own)
+        bias = jnp.broadcast_to(jnp.sum(dz, axis=1, keepdims=True), (chans, HALF))
+        start = pl.multiple_of(n * own, own)
+        rest = jnp.concatenate([grad[:, full:]] * depth, axis=1)
+        both = jnp.concatenate([grad[:, :full], rest, bias], axis=1)
         parts = [both[k * own : (k + 1) * own] for k in range(shares)]
         parts = [jnp.where(odd, parts[i ^ 1], parts[i]) for i in range(shares)]
         parts = [jnp.where(high, parts[i ^ 2], parts[i]) for i in range(shares)]
+        lane = lax.broadcasted_iota(jnp.int32, (own, HALF), 1)
         for part, ref in zip(parts, part_refs):
-            ref[where] = part
+            for k in range(full // HALF):
+                ref[pl.ds(k * block + start, own)] = part[:, k * HALF : (k + 1) * HALF]
+            for k, here in ((0, lane // (rows - full) == n), (1, lane % depth == n)):
+                tile = slice(base + k * own, base + (k + 1) * own)
+                at = full + k * HALF
+                ref[tile] = jnp.where(here, part[:, at : at + HALF], ref[tile])
         return dzb
 
     def behind(i, adj):
@@ -308,10 +316,13 @@
     eye = lax.broadcasted_iota(jnp.int32, (own, own), 0) == lax.broadcasted_iota(
         jnp.int32, (own, own), 1
     )
+    full = width // HALF
+    base, rest = depth * own * full, width - full * HALF
     for n in range(depth):
-        mine = total[n * own : (n + 1) * own]
-        grad_ref[n] = mine[:, :width]
-        column = jnp.broadcast_to(mine[:, width : width + 1], (own, own))
+        pieces = [total[(k * depth + n) * own : (k * depth + n + 1) * own] for k in range(full)]
+        pieces.append(total[base : base + own, n * rest : (n + 1) * rest])
+        grad_ref[n] = jnp.concatenate(pieces, axis=1)
+        column = jnp.broadcast_to(total[base + own : base + 2 * own, n : n + 1], (own, own))
         bias_ref[n : n + 1, :] = jnp.sum(jnp.where(eye, column, 0.0), axis=0, keepdims=True)
 
 
@@ -372,8 +383,8 @@
             (total, exchange(total, "layer", 1 << (step - 1)), mine),
         )
     got = exchange(total, "layer", 1 << (steps - 1))
-    lanes = -(-(width + 1) // HALF) * HALF
-    part = (depth * chans // shares, lanes)
+    own = chans // shares
+    part = (depth * own * (width // HALF) + 2 * own, HALF)
     keep, *sends = call(
         functools.partial(grad_kernel, steps),
         (f32(*part),) * shares,

time: 24.3 us -> 23.9 us (0.984)
  waiting for transfers between devices: 8.33 us -> 7.8 us
    ppermute x7, waiting for transfers between devices: 8.33 us -> 7.8 us  [exchange(): lax.ppermute(x, axis, [(i, i ^ mask) for i in range(lax.axis_size(axis))])]
where the time goes in v20:
time: 23.9 us; the launch traced here: 23.7 us
  starting transfers between devices  9.29 us (39%)
  waiting for transfers between devices  7.8 us (33%)
  Pallas kernels  5.95 us (25%)
  between operations  0.68 us (3%)
    ppermute x7, starting transfers between devices, exchange(): lax.ppermute(x, axis, [(i, i ^ mask) for i in range(lax.axis_size(axis))])  9.29 us
    ppermute x7, waiting for transfers between devices, exchange(): lax.ppermute(x, axis, [(i, i ^ mask) for i in range(lax.axis_size(axis))])  7.8 us
    pallas_call x6, Pallas kernels, call(): pl.pallas_call(kernel, out_shape=out_shape, in_specs=[HBM if k in hbm_in...  5.95 us
  transfers between devices with their start and end apart: 7, of which 5 were waited for; matrix products, arithmetic and copies ran while one was open for 0% of the time, Pallas kernels for 5%

profile of v20, /device:TPU:0, one launch (start us, length us, event | category | flops | bytes accessed | tf_op | source)
XLA Modules:
  0.0 23.7 jit_solution(2358661255885508097)
XLA Ops:
  0.6 2.9 %shard_map.75 = (f32[32,256]{1,0:T(8,128)S(1)}, f32[3,32,256]{2,1,0:T(8,128)S(1)}, f32[4,32,256]{2,1,0:T(8,128)S(1)}, bf16[4,32,256]{2,1,0:T(8,128)(2,1)S(1)}, bf16[4,32,288]{2,1,0:T(8,128)(2,1)S(1)}) custom-call(f32[1,1,32,256]{3,2,1,0:T(8,128)} %start_ref.1, f32[1,1,32,256]{3,2,1,0:T(8,128)} %guess_ref.1, bf16[4,32,288]{2,1,0:T(8,128)(2,1)} %w_hbm.1, ...), custom_call_target="tpu_custom_call" | custom-call | flops 268435456 | bytes 1048576 | tf_op jit(solution)/shard_map/pallas_call | solution.py:330
  3.6 4.0 %collective-permute-start.2 = (f32[3,32,256]{2,1,0:T(8,128)S(1)}, f32[3,32,256]{2,1,0:T(8,128)S(1)}, u32[]{:S(2)}, u32[]{:S(2)}) collective-permute-start(f32[3,32,256]{2,1,0:T(8,128)S(1)} %get-tuple-element.19.own_ref), channel_id=1, source_target_pairs={{0,12},{4,8},{8,4},{12,0},{16,28},{20,24},{24,20},{28,16},{1,13},{... | collective-permute-start | bytes 294920 | tf_op jit(solution)/shard_map/ppermute | solution.py:350
  7.6 0.4 %collective-permute-start.1 = (f32[3,32,256]{2,1,0:T(8,128)S(1)}, f32[3,32,256]{2,1,0:T(8,128)S(1)}, u32[]{:S(2)}, u32[]{:S(2)}) collective-permute-start(f32[3,32,256]{2,1,0:T(8,128)S(1)} %get-tuple-element.19.own_ref), channel_id=1, source_target_pairs={{0,8},{4,12},{8,0},{12,4},{16,24},{20,28},{24,16},{28,20},{1,9},{5... | collective-permute-start | bytes 294920 | tf_op jit(solution)/shard_map/ppermute | solution.py:350
  8.0 0.2 collective-permute-start
  8.2 2.9 %collective-permute-done.2.third_ref = f32[3,32,256]{2,1,0:T(8,128)S(1)} collective-permute-done((f32[3,32,256]{2,1,0:T(8,128)S(1)}, f32[3,32,256]{2,1,0:T(8,128)S(1)}, u32[]{:S(2)}, u32[]{:S(2)}) %collective-permute-start.2) | collective-permute-done | bytes 98336 | tf_op jit(solution)/shard_map/ppermute | solution.py:350
  11.1 1.6 %collective-permute-done.1.second_ref = f32[3,32,256]{2,1,0:T(8,128)S(1)} collective-permute-done((f32[3,32,256]{2,1,0:T(8,128)S(1)}, f32[3,32,256]{2,1,0:T(8,128)S(1)}, u32[]{:S(2)}, u32[]{:S(2)}) %collective-permute-start.1) | collective-permute-done | bytes 98336 | tf_op jit(solution)/shard_map/ppermute | solution.py:350
  12.7 0.0 collective-permute-done.first_ref
  12.7 0.1 shard_map.76
  12.8 2.7 %collective-permute-start.3 = (f32[32,256]{1,0:T(8,128)S(1)}, f32[32,256]{1,0:T(8,128)S(1)}, u32[]{:S(2)}, u32[]{:S(2)}) collective-permute-start(f32[32,256]{1,0:T(8,128)S(1)} %get-tuple-element.20), channel_id=1, source_target_pairs={{0,16},{4,20},{8,24},{12,28},{16,0},{20,4},{24,8},{28,12},{1,17},{... | collective-permute-start | bytes 98312 | tf_op jit(solution)/shard_map/ppermute | solution.py:350
  15.5 0.6 %shard_map.77.patch_ref = bf16[4,288,256]{2,1,0:T(8,128)(2,1)S(1)} custom-call(bf16[4,32,256]{2,1,0:T(8,128)(2,1)S(1)} %get-tuple-element.24.rounded_ref), custom_call_target="tpu_custom_call" | custom-call | flops 268435456 | bytes 1048576 | tf_op jit(solution)/shard_map/pallas_call | solution.py:330
  16.1 1.6 %collective-permute-done.3.got_ref = f32[32,256]{1,0:T(8,128)S(1)} collective-permute-done((f32[32,256]{1,0:T(8,128)S(1)}, f32[32,256]{1,0:T(8,128)S(1)}, u32[]{:S(2)}, u32[]{:S(2)}) %collective-permute-start.3) | collective-permute-done | bytes 32800 | tf_op jit(solution)/shard_map/ppermute | solution.py:350
  17.7 0.0 copy-start
  17.7 0.0 copy-start.1
  17.7 0.9 %shard_map.78 = (f32[80,128]{1,0:T(8,128)S(1)}, f32[80,128]{1,0:T(8,128)S(1)}, f32[80,128]{1,0:T(8,128)S(1)}, f32[80,128]{1,0:T(8,128)S(1)}) custom-call(f32[32,256]{1,0:T(8,128)S(1)} %collective-permute-done.3.got_ref, f32[4,32,256]{2,1,0:T(8,128)S(1)} %get-tuple-element.21.mine_ref, f32[32,256]{1,0:T(8,128)S(1)} %get-tuple-element.22.guess_ref, ...), custom_call_target="tpu_custom_call" | custom-call | flops 268435456 | bytes 1048576 | tf_op jit(solution)/shard_map/pallas_call | solution.py:330
  18.6 0.1 collective-permute-start.4
  18.7 1.6 %collective-permute-start.5 = (f32[80,128]{1,0:T(8,128)S(1)}, f32[80,128]{1,0:T(8,128)S(1)}, u32[]{:S(2)}, u32[]{:S(2)}) collective-permute-start(f32[80,128]{1,0:T(8,128)S(1)} %get-tuple-element.30), channel_id=1, source_target_pairs={{0,2},{1,3},{2,0},{3,1},{4,6},{5,7},{6,4},{7,5},{8,10},{9,11},{10,... | collective-permute-start | bytes 122888 | tf_op jit(solution)/shard_map/ppermute | solution.py:350
  20.4 0.2 collective-permute-start.6
  20.6 0.0 copy-done
  20.6 0.0 copy-done.1
  20.6 0.7 %shard_map.79 = (f32[1,1,32,256]{3,2,1,0:T(8,128)}, f32[1,1,32,256]{3,2,1,0:T(8,128)}) custom-call(f32[80,128]{1,0:T(8,128)S(1)} %get-tuple-element.26._.mine_ref, f32[32,256]{1,0:T(8,128)S(1)} %collective-permute-done.3.got_ref, f32[4,32,256]{2,1,0:T(8,128)S(1)} %get-tuple-element.21.mine_ref, f32[1,1,32,256]{3,2,1,0:T(8,128)S(1)} %copy-done.1, ...), custom_call_target="tpu_custom_call" | custom-call | flops 268435456 | bytes 1048576 | tf_op jit(solution)/shard_map/pallas_call | solution.py:330
  21.3 1.1 %collective-permute-done.4.both_ref = f32[80,128]{1,0:T(8,128)S(1)} collective-permute-done((f32[80,128]{1,0:T(8,128)S(1)}, f32[80,128]{1,0:T(8,128)S(1)}, u32[]{:S(2)}, u32[]{:S(2)}) %collective-permute-start.4) | collective-permute-done | bytes 40992 | tf_op jit(solution)/shard_map/ppermute | solution.py:350
  22.4 0.6 %collective-permute-done.5.chip_ref = f32[80,128]{1,0:T(8,128)S(1)} collective-permute-done((f32[80,128]{1,0:T(8,128)S(1)}, f32[80,128]{1,0:T(8,128)S(1)}, u32[]{:S(2)}, u32[]{:S(2)}) %collective-permute-start.5) | collective-permute-done | bytes 40992 | tf_op jit(solution)/shard_map/ppermute | solution.py:350
  23.0 0.0 collective-permute-done.6.core_ref
  23.0 0.7 %shard_map.80 = (f32[4,8,288]{2,1,0:T(8,128)}, f32[4,8]{1,0:T(4,128)}) custom-call(f32[80,128]{1,0:T(8,128)S(1)} %get-tuple-element.26._.mine_ref, f32[80,128]{1,0:T(8,128)S(1)} %collective-permute-done.4.both_ref, f32[80,128]{1,0:T(8,128)S(1)} %collective-permute-done.5.chip_ref, f32[80,128]{1,0:T(8,128)S(1)} %collective-permute-done.6.core_ref), custom_call_target="tpu_custom_call" | custom-call | flops 268435456 | bytes 1048576 | tf_op jit(solution)/shard_map/pallas_call | solution.py:330
Async XLA Ops:
  3.6 7.5 %collective-permute-start.2 = (f32[3,32,256]{2,1,0:T(8,128)S(1)}, f32[3,32,256]{2,1,0:T(8,128)S(1)}, u32[]{:S(2)}, u32[]{:S(2)}) collective-permute-start(f32[3,32,256]{2,1,0:T(8,128)S(1)} %get-tuple-element.19.own_ref), channel_id=1, source_target_pairs={{0,12},{4,8},{8,4},{12,0},{16,28},{20,24},{24,20},{28,16},{1,13},{... | collective-permute-start | bytes 294920 | tf_op jit(solution)/shard_map/ppermute | solution.py:350
  7.6 5.1 %collective-permute-start.1 = (f32[3,32,256]{2,1,0:T(8,128)S(1)}, f32[3,32,256]{2,1,0:T(8,128)S(1)}, u32[]{:S(2)}, u32[]{:S(2)}) collective-permute-start(f32[3,32,256]{2,1,0:T(8,128)S(1)} %get-tuple-element.19.own_ref), channel_id=1, source_target_pairs={{0,8},{4,12},{8,0},{12,4},{16,24},{20,28},{24,16},{28,20},{1,9},{5... | collective-permute-start | bytes 294920 | tf_op jit(solution)/shard_map/ppermute | solution.py:350
  8.0 4.7 %collective-permute-start = (f32[3,32,256]{2,1,0:T(8,128)S(1)}, f32[3,32,256]{2,1,0:T(8,128)S(1)}, u32[]{:S(2)}, u32[]{:S(2)}) collective-permute-start(f32[3,32,256]{2,1,0:T(8,128)S(1)} %get-tuple-element.19.own_ref), channel_id=1, source_target_pairs={{0,4},{4,0},{8,12},{12,8},{16,20},{20,16},{24,28},{28,24},{1,5},{5... | collective-permute-start | bytes 294920 | tf_op jit(solution)/shard_map/ppermute | solution.py:350
  12.8 4.9 %collective-permute-start.3 = (f32[32,256]{1,0:T(8,128)S(1)}, f32[32,256]{1,0:T(8,128)S(1)}, u32[]{:S(2)}, u32[]{:S(2)}) collective-permute-start(f32[32,256]{1,0:T(8,128)S(1)} %get-tuple-element.20), channel_id=1, source_target_pairs={{0,16},{4,20},{8,24},{12,28},{16,0},{20,4},{24,8},{28,12},{1,17},{... | collective-permute-start | bytes 98312 | tf_op jit(solution)/shard_map/ppermute | solution.py:350
  17.7 2.9 %copy-start = (f32[1,1,32,256]{3,2,1,0:T(8,128)S(1)}, f32[1,1,32,256]{3,2,1,0:T(8,128)}, u32[]{:S(2)}) copy-start(f32[1,1,32,256]{3,2,1,0:T(8,128)} %start_ref.1) | copy-start | bytes 98308
  17.7 2.9 %copy-start.1 = (f32[1,1,32,256]{3,2,1,0:T(8,128)S(1)}, f32[1,1,32,256]{3,2,1,0:T(8,128)}, u32[]{:S(2)}) copy-start(f32[1,1,32,256]{3,2,1,0:T(8,128)} %guess_ref.1) | copy-start | bytes 98308
  18.6 3.8 %collective-permute-start.4 = (f32[80,128]{1,0:T(8,128)S(1)}, f32[80,128]{1,0:T(8,128)S(1)}, u32[]{:S(2)}, u32[]{:S(2)}) collective-permute-start(f32[80,128]{1,0:T(8,128)S(1)} %get-tuple-element.29), channel_id=1, source_target_pairs={{0,3},{1,2},{2,1},{3,0},{4,7},{5,6},{6,5},{7,4},{8,11},{9,10},{10,... | collective-permute-start | bytes 122888 | tf_op jit(solution)/shard_map/ppermute | solution.py:350
  18.7 4.3 %collective-permute-start.5 = (f32[80,128]{1,0:T(8,128)S(1)}, f32[80,128]{1,0:T(8,128)S(1)}, u32[]{:S(2)}, u32[]{:S(2)}) collective-permute-start(f32[80,128]{1,0:T(8,128)S(1)} %get-tuple-element.30), channel_id=1, source_target_pairs={{0,2},{1,3},{2,0},{3,1},{4,6},{5,7},{6,4},{7,5},{8,10},{9,11},{10,... | collective-permute-start | bytes 122888 | tf_op jit(solution)/shard_map/ppermute | solution.py:350
  20.4 2.7 %collective-permute-start.6 = (f32[80,128]{1,0:T(8,128)S(1)}, f32[80,128]{1,0:T(8,128)S(1)}, u32[]{:S(2)}, u32[]{:S(2)}) collective-permute-start(f32[80,128]{1,0:T(8,128)S(1)} %get-tuple-element.31), channel_id=1, source_target_pairs={{0,1},{1,0},{2,3},{3,2},{4,5},{5,4},{6,7},{7,6},{8,9},{9,8},{10,11... | collective-permute-start | bytes 122888 | tf_op jit(solution)/shard_map/ppermute | solution.py:350

commit v21 on v20

--- a/solution.py
+++ b/solution.py
@@ -211,7 +211,7 @@
             sent_ref[k] = total[k]
 
 
-def four_kernel(final, own_ref, first_ref, second_ref, third_ref, sent_ref, mine_out):
+def four_kernel(final, own_ref, second_ref, first_ref, third_ref, sent_ref, mine_out):
     low, high = bit_of("layer", 0), bit_of("layer", 1)
     place = lax.rem(lax.axis_index("layer"), 4)
     maps = [
@@ -374,7 +374,7 @@
     total, mine = call(
         functools.partial(four_kernel, steps == 3),
         shapes[0],
-        (total, *(exchange(total, "layer", mask) for mask in (1, 2, 3))),
+        (total, *(exchange(total, "layer", mask) for mask in (2, 1, 3))),
     )
     for step in range(3, steps):
         total, mine = call(

time: 23.9 us -> 24.1 us (level)
  waiting for transfers between devices: 7.8 us -> 8.14 us
    ppermute x7, waiting for transfers between devices: 7.8 us -> 8.14 us  [exchange(): lax.ppermute(x, axis, [(i, i ^ mask) for i in range(lax.axis_size(axis))])]
  transfers between devices with their start and end apart: 7 -> 7, of which waited for: 5 -> 6; matrix products, arithmetic and copies ran while one was open for 0% -> 0% of each run, Pallas kernels for 5% -> 5%
where the time goes in v21:
time: 24.1 us; the launch traced here: 24 us
  starting transfers between devices  9.23 us (38%)
  waiting for transfers between devices  8.14 us (34%)
  Pallas kernels  5.93 us (25%)
  between operations  0.67 us (3%)
    ppermute x7, starting transfers between devices, exchange(): lax.ppermute(x, axis, [(i, i ^ mask) for i in range(lax.axis_size(axis))])  9.23 us
    ppermute x7, waiting for transfers between devices, exchange(): lax.ppermute(x, axis, [(i, i ^ mask) for i in range(lax.axis_size(axis))])  8.14 us
    pallas_call x6, Pallas kernels, call(): pl.pallas_call(kernel, out_shape=out_shape, in_specs=[HBM if k in hbm_in...  5.93 us
  transfers between devices with their start and end apart: 7, of which 6 were waited for; matrix products, arithmetic and copies ran while one was open for 0% of the time, Pallas kernels for 5%

profile of v21, /device:TPU:0, one launch (start us, length us, event | category | flops | bytes accessed | tf_op | source)
XLA Modules:
  0.0 24.0 jit_solution(15463146459501866490)
XLA Ops:
  0.6 2.9 %shard_map.75 = (f32[32,256]{1,0:T(8,128)S(1)}, f32[3,32,256]{2,1,0:T(8,128)S(1)}, f32[4,32,256]{2,1,0:T(8,128)S(1)}, bf16[4,32,256]{2,1,0:T(8,128)(2,1)S(1)}, bf16[4,32,288]{2,1,0:T(8,128)(2,1)S(1)}) custom-call(f32[1,1,32,256]{3,2,1,0:T(8,128)} %start_ref.1, f32[1,1,32,256]{3,2,1,0:T(8,128)} %guess_ref.1, bf16[4,32,288]{2,1,0:T(8,128)(2,1)} %w_hbm.1, ...), custom_call_target="tpu_custom_call" | custom-call | flops 268435456 | bytes 1048576 | tf_op jit(solution)/shard_map/pallas_call | solution.py:330
  3.6 4.0 %collective-permute-start.2 = (f32[3,32,256]{2,1,0:T(8,128)S(1)}, f32[3,32,256]{2,1,0:T(8,128)S(1)}, u32[]{:S(2)}, u32[]{:S(2)}) collective-permute-start(f32[3,32,256]{2,1,0:T(8,128)S(1)} %get-tuple-element.19.own_ref), channel_id=1, source_target_pairs={{0,12},{4,8},{8,4},{12,0},{16,28},{20,24},{24,20},{28,16},{1,13},{... | collective-permute-start | bytes 294920 | tf_op jit(solution)/shard_map/ppermute | solution.py:350
  7.6 0.5 %collective-permute-start.1 = (f32[3,32,256]{2,1,0:T(8,128)S(1)}, f32[3,32,256]{2,1,0:T(8,128)S(1)}, u32[]{:S(2)}, u32[]{:S(2)}) collective-permute-start(f32[3,32,256]{2,1,0:T(8,128)S(1)} %get-tuple-element.19.own_ref), channel_id=1, source_target_pairs={{0,4},{4,0},{8,12},{12,8},{16,20},{20,16},{24,28},{28,24},{1,5},{5... | collective-permute-start | bytes 294920 | tf_op jit(solution)/shard_map/ppermute | solution.py:350
  8.1 0.1 collective-permute-start
  8.2 2.5 %collective-permute-done.2.third_ref = f32[3,32,256]{2,1,0:T(8,128)S(1)} collective-permute-done((f32[3,32,256]{2,1,0:T(8,128)S(1)}, f32[3,32,256]{2,1,0:T(8,128)S(1)}, u32[]{:S(2)}, u32[]{:S(2)}) %collective-permute-start.2) | collective-permute-done | bytes 98336 | tf_op jit(solution)/shard_map/ppermute | solution.py:350
  10.8 1.7 %collective-permute-done.1.first_ref = f32[3,32,256]{2,1,0:T(8,128)S(1)} collective-permute-done((f32[3,32,256]{2,1,0:T(8,128)S(1)}, f32[3,32,256]{2,1,0:T(8,128)S(1)}, u32[]{:S(2)}, u32[]{:S(2)}) %collective-permute-start.1) | collective-permute-done | bytes 98336 | tf_op jit(solution)/shard_map/ppermute | solution.py:350
  12.5 0.3 %collective-permute-done.second_ref = f32[3,32,256]{2,1,0:T(8,128)S(1)} collective-permute-done((f32[3,32,256]{2,1,0:T(8,128)S(1)}, f32[3,32,256]{2,1,0:T(8,128)S(1)}, u32[]{:S(2)}, u32[]{:S(2)}) %collective-permute-start) | collective-permute-done | bytes 98336 | tf_op jit(solution)/shard_map/ppermute | solution.py:350
  12.7 0.1 shard_map.76
  12.8 2.7 %collective-permute-start.3 = (f32[32,256]{1,0:T(8,128)S(1)}, f32[32,256]{1,0:T(8,128)S(1)}, u32[]{:S(2)}, u32[]{:S(2)}) collective-permute-start(f32[32,256]{1,0:T(8,128)S(1)} %get-tuple-element.20), channel_id=1, source_target_pairs={{0,16},{4,20},{8,24},{12,28},{16,0},{20,4},{24,8},{28,12},{1,17},{... | collective-permute-start | bytes 98312 | tf_op jit(solution)/shard_map/ppermute | solution.py:350
  15.5 0.5 %shard_map.77.patch_ref = bf16[4,288,256]{2,1,0:T(8,128)(2,1)S(1)} custom-call(bf16[4,32,256]{2,1,0:T(8,128)(2,1)S(1)} %get-tuple-element.24.rounded_ref), custom_call_target="tpu_custom_call" | custom-call | flops 268435456 | bytes 1048576 | tf_op jit(solution)/shard_map/pallas_call | solution.py:330
  16.0 1.9 %collective-permute-done.3.got_ref = f32[32,256]{1,0:T(8,128)S(1)} collective-permute-done((f32[32,256]{1,0:T(8,128)S(1)}, f32[32,256]{1,0:T(8,128)S(1)}, u32[]{:S(2)}, u32[]{:S(2)}) %collective-permute-start.3) | collective-permute-done | bytes 32800 | tf_op jit(solution)/shard_map/ppermute | solution.py:350
  17.9 0.0 copy-start
  17.9 0.0 copy-start.1
  17.9 0.9 %shard_map.78 = (f32[80,128]{1,0:T(8,128)S(1)}, f32[80,128]{1,0:T(8,128)S(1)}, f32[80,128]{1,0:T(8,128)S(1)}, f32[80,128]{1,0:T(8,128)S(1)}) custom-call(f32[32,256]{1,0:T(8,128)S(1)} %collective-permute-done.3.got_ref, f32[4,32,256]{2,1,0:T(8,128)S(1)} %get-tuple-element.21.mine_ref, f32[32,256]{1,0:T(8,128)S(1)} %get-tuple-element.22.guess_ref, ...), custom_call_target="tpu_custom_call" | custom-call | flops 268435456 | bytes 1048576 | tf_op jit(solution)/shard_map/pallas_call | solution.py:330
  18.8 0.1 collective-permute-start.4
  18.9 1.6 %collective-permute-start.5 = (f32[80,128]{1,0:T(8,128)S(1)}, f32[80,128]{1,0:T(8,128)S(1)}, u32[]{:S(2)}, u32[]{:S(2)}) collective-permute-start(f32[80,128]{1,0:T(8,128)S(1)} %get-tuple-element.30), channel_id=1, source_target_pairs={{0,2},{1,3},{2,0},{3,1},{4,6},{5,7},{6,4},{7,5},{8,10},{9,11},{10,... | collective-permute-start | bytes 122888 | tf_op jit(solution)/shard_map/ppermute | solution.py:350
  20.5 0.3 %collective-permute-start.6 = (f32[80,128]{1,0:T(8,128)S(1)}, f32[80,128]{1,0:T(8,128)S(1)}, u32[]{:S(2)}, u32[]{:S(2)}) collective-permute-start(f32[80,128]{1,0:T(8,128)S(1)} %get-tuple-element.31), channel_id=1, source_target_pairs={{0,1},{1,0},{2,3},{3,2},{4,5},{5,4},{6,7},{7,6},{8,9},{9,8},{10,11... | collective-permute-start | bytes 122888 | tf_op jit(solution)/shard_map/ppermute | solution.py:350
  20.8 0.0 copy-done
  20.8 0.0 copy-done.1
  20.8 0.7 %shard_map.79 = (f32[1,1,32,256]{3,2,1,0:T(8,128)}, f32[1,1,32,256]{3,2,1,0:T(8,128)}) custom-call(f32[80,128]{1,0:T(8,128)S(1)} %get-tuple-element.26._.mine_ref, f32[32,256]{1,0:T(8,128)S(1)} %collective-permute-done.3.got_ref, f32[4,32,256]{2,1,0:T(8,128)S(1)} %get-tuple-element.21.mine_ref, f32[1,1,32,256]{3,2,1,0:T(8,128)S(1)} %copy-done.1, ...), custom_call_target="tpu_custom_call" | custom-call | flops 268435456 | bytes 1048576 | tf_op jit(solution)/shard_map/pallas_call | solution.py:330
  21.5 1.2 %collective-permute-done.4.both_ref = f32[80,128]{1,0:T(8,128)S(1)} collective-permute-done((f32[80,128]{1,0:T(8,128)S(1)}, f32[80,128]{1,0:T(8,128)S(1)}, u32[]{:S(2)}, u32[]{:S(2)}) %collective-permute-start.4) | collective-permute-done | bytes 40992 | tf_op jit(solution)/shard_map/ppermute | solution.py:350
  22.7 0.6 %collective-permute-done.5.chip_ref = f32[80,128]{1,0:T(8,128)S(1)} collective-permute-done((f32[80,128]{1,0:T(8,128)S(1)}, f32[80,128]{1,0:T(8,128)S(1)}, u32[]{:S(2)}, u32[]{:S(2)}) %collective-permute-start.5) | collective-permute-done | bytes 40992 | tf_op jit(solution)/shard_map/ppermute | solution.py:350
  23.3 0.0 collective-permute-done.6.core_ref
  23.3 0.7 %shard_map.80 = (f32[4,8,288]{2,1,0:T(8,128)}, f32[4,8]{1,0:T(4,128)}) custom-call(f32[80,128]{1,0:T(8,128)S(1)} %get-tuple-element.26._.mine_ref, f32[80,128]{1,0:T(8,128)S(1)} %collective-permute-done.4.both_ref, f32[80,128]{1,0:T(8,128)S(1)} %collective-permute-done.5.chip_ref, f32[80,128]{1,0:T(8,128)S(1)} %collective-permute-done.6.core_ref), custom_call_target="tpu_custom_call" | custom-call | flops 268435456 | bytes 1048576 | tf_op jit(solution)/shard_map/pallas_call | solution.py:330
Async XLA Ops:
  3.6 7.2 %collective-permute-start.2 = (f32[3,32,256]{2,1,0:T(8,128)S(1)}, f32[3,32,256]{2,1,0:T(8,128)S(1)}, u32[]{:S(2)}, u32[]{:S(2)}) collective-permute-start(f32[3,32,256]{2,1,0:T(8,128)S(1)} %get-tuple-element.19.own_ref), channel_id=1, source_target_pairs={{0,12},{4,8},{8,4},{12,0},{16,28},{20,24},{24,20},{28,16},{1,13},{... | collective-permute-start | bytes 294920 | tf_op jit(solution)/shard_map/ppermute | solution.py:350
  7.6 4.9 %collective-permute-start.1 = (f32[3,32,256]{2,1,0:T(8,128)S(1)}, f32[3,32,256]{2,1,0:T(8,128)S(1)}, u32[]{:S(2)}, u32[]{:S(2)}) collective-permute-start(f32[3,32,256]{2,1,0:T(8,128)S(1)} %get-tuple-element.19.own_ref), channel_id=1, source_target_pairs={{0,4},{4,0},{8,12},{12,8},{16,20},{20,16},{24,28},{28,24},{1,5},{5... | collective-permute-start | bytes 294920 | tf_op jit(solution)/shard_map/ppermute | solution.py:350
  8.1 4.6 %collective-permute-start = (f32[3,32,256]{2,1,0:T(8,128)S(1)}, f32[3,32,256]{2,1,0:T(8,128)S(1)}, u32[]{:S(2)}, u32[]{:S(2)}) collective-permute-start(f32[3,32,256]{2,1,0:T(8,128)S(1)} %get-tuple-element.19.own_ref), channel_id=1, source_target_pairs={{0,8},{4,12},{8,0},{12,4},{16,24},{20,28},{24,16},{28,20},{1,9},{5... | collective-permute-start | bytes 294920 | tf_op jit(solution)/shard_map/ppermute | solution.py:350
  12.8 5.1 %collective-permute-start.3 = (f32[32,256]{1,0:T(8,128)S(1)}, f32[32,256]{1,0:T(8,128)S(1)}, u32[]{:S(2)}, u32[]{:S(2)}) collective-permute-start(f32[32,256]{1,0:T(8,128)S(1)} %get-tuple-element.20), channel_id=1, source_target_pairs={{0,16},{4,20},{8,24},{12,28},{16,0},{20,4},{24,8},{28,12},{1,17},{... | collective-permute-start | bytes 98312 | tf_op jit(solution)/shard_map/ppermute | solution.py:350
  17.9 2.9 %copy-start = (f32[1,1,32,256]{3,2,1,0:T(8,128)S(1)}, f32[1,1,32,256]{3,2,1,0:T(8,128)}, u32[]{:S(2)}) copy-start(f32[1,1,32,256]{3,2,1,0:T(8,128)} %start_ref.1) | copy-start | bytes 98308
  17.9 2.9 %copy-start.1 = (f32[1,1,32,256]{3,2,1,0:T(8,128)S(1)}, f32[1,1,32,256]{3,2,1,0:T(8,128)}, u32[]{:S(2)}) copy-start(f32[1,1,32,256]{3,2,1,0:T(8,128)} %guess_ref.1) | copy-start | bytes 98308
  18.8 3.9 %collective-permute-start.4 = (f32[80,128]{1,0:T(8,128)S(1)}, f32[80,128]{1,0:T(8,128)S(1)}, u32[]{:S(2)}, u32[]{:S(2)}) collective-permute-start(f32[80,128]{1,0:T(8,128)S(1)} %get-tuple-element.29), channel_id=1, source_target_pairs={{0,3},{1,2},{2,1},{3,0},{4,7},{5,6},{6,5},{7,4},{8,11},{9,10},{10,... | collective-permute-start | bytes 122888 | tf_op jit(solution)/shard_map/ppermute | solution.py:350
  18.9 4.4 %collective-permute-start.5 = (f32[80,128]{1,0:T(8,128)S(1)}, f32[80,128]{1,0:T(8,128)S(1)}, u32[]{:S(2)}, u32[]{:S(2)}) collective-permute-start(f32[80,128]{1,0:T(8,128)S(1)} %get-tuple-element.30), channel_id=1, source_target_pairs={{0,2},{1,3},{2,0},{3,1},{4,6},{5,7},{6,4},{7,5},{8,10},{9,11},{10,... | collective-permute-start | bytes 122888 | tf_op jit(solution)/shard_map/ppermute | solution.py:350
  20.5 2.8 %collective-permute-start.6 = (f32[80,128]{1,0:T(8,128)S(1)}, f32[80,128]{1,0:T(8,128)S(1)}, u32[]{:S(2)}, u32[]{:S(2)}) collective-permute-start(f32[80,128]{1,0:T(8,128)S(1)} %get-tuple-element.31), channel_id=1, source_target_pairs={{0,1},{1,0},{2,3},{3,2},{4,5},{5,4},{6,7},{7,6},{8,9},{9,8},{10,11... | collective-permute-start | bytes 122888 | tf_op jit(solution)/shard_map/ppermute | solution.py:350
